TPU v7x, 32 devices: a whole 2x2x4 slice. The times are simulated.
32 devices in a mesh: grp: 8 (over z, x), sub: 4 (over y, core).
Axes of the slice: x: 2, y: 2, z: 4, core: 2. Of those that a mesh axis runs over, the one named last changes fastest.
Arguments:
- field: bfloat16 [64, 64, 32, 128], P('grp', 'sub'), may hold values from -6 to 6
- cotangent: bfloat16 [64, 64, 32, 128], P('grp', 'sub'), may hold values from -0.0390625 to 0.0390625
- fine_kernel: bfloat16 [3, 3, 3, 128, 128], replicated, may hold values from -0.109375 to 0.109375
- fine_bias: float32 [128], replicated, may hold values from -3 to 3
- coarse_kernel: bfloat16 [3, 3, 3, 128, 256], replicated, may hold values from -0.109375 to 0.109375
- coarse_bias: float32 [256], replicated, may hold values from -3 to 3
- merge_weight: bfloat16 [256, 128], replicated, may hold values from -0.375 to 0.375
Outputs:
- output: bfloat16 [64, 64, 32, 128], P('grp', 'sub')
- grad_fine_kernel: float32 [3, 3, 3, 128, 128], P(None, None, None, None, 'sub')
- grad_fine_bias: float32 [128], P('sub')
- grad_coarse_kernel: float32 [3, 3, 3, 128, 256], P(None, None, None, None, 'sub')
- grad_coarse_bias: float32 [256], P('sub')
- grad_merge_weight: float32 [256, 128], P('sub')
All inputs are finite; a program needn't handle non-finite values.
Results may differ from a plain program's by a relative error of at most 0.02.
Values may be sent and summed in bfloat16 or wider, within the bound.
No kernel may reach another device: no remote copies, remote signals or barrier semaphores. Data moves between devices by JAX's collectives and lax.ppermute only.
A program may use at most 64 MiB of HBM per device.

v0:
```python
import functools

import jax
import jax.numpy as jnp
from jax import lax
from jax.experimental import pallas as pl
from jax.experimental.pallas import tpu as pltpu
from jax.sharding import PartitionSpec as P

F32 = jnp.float32
BF16 = jnp.bfloat16
VMEM_LIMIT = 48 * 1024 * 1024


def call(body, name, args, outs, scratch=(), flops=0, nbytes=0):
    specs = [pl.BlockSpec(memory_space=pltpu.SMEM)]
    specs += [pl.BlockSpec(memory_space=pltpu.VMEM) for _ in args[1:]]
    return pl.pallas_call(
        body,
        name=name,
        out_shape=[jax.ShapeDtypeStruct(s, t) for s, t in outs],
        in_specs=specs,
        out_specs=[pl.BlockSpec(memory_space=pltpu.VMEM) for _ in outs],
        scratch_shapes=list(scratch),
        compiler_params=pltpu.CompilerParams(vmem_limit_bytes=VMEM_LIMIT),
        cost_estimate=pl.CostEstimate(flops=flops, bytes_accessed=nbytes, transcendentals=0),
    )(*args)


def put_faces(odd, first, second, low, high):
    first[...] = jnp.where(odd, low, high)
    second[...] = jnp.where(odd, high, low)


def get_faces(odd, first, second):
    a, b = first[...], second[...]
    return jnp.where(odd, a, b), jnp.where(odd, b, a)


def sum_cube(rows, planes, ref):
    half = rows // 2
    ref[pl.ds(0, rows), :] = planes
    return ref[pl.ds(0, half, stride=2), :] + ref[pl.ds(1, half, stride=2), :]


def shift_rows(value, step, depth):
    rows = value.shape[0]
    moved = pltpu.roll(value, step % rows, 0)
    place = lax.broadcasted_iota(jnp.int32, value.shape, 0) % depth
    edge = 0 if step == 1 else depth - 1
    return jnp.where(place == edge, 0.0, moved)


def sigmoid(value):
    return 1.0 / (1.0 + jnp.exp(-value))


def prep_body(par, lo, hi, cot, pg, out_a, out_b, tmp):
    bx, by, bz, c = cot.shape
    cx, cy, cz = bx // 2, by // 2, bz // 2
    total = jnp.sum(cot[...].astype(F32).reshape(cx, 2, cy, 2, bz, c), axis=(1, 3))
    grad = sum_cube(cx * cy * bz, total.reshape(cx * cy * bz, c), tmp).astype(BF16)
    pg[...] = grad.reshape(cx, cy, cz, c)
    face = cy * cz
    low = jnp.concatenate([lo[0].reshape(by * bz, c), grad[:face]], axis=0)
    high = jnp.concatenate([hi[0].reshape(by * bz, c), grad[-face:]], axis=0)
    put_faces(par[0] == 1, out_a, out_b, low, high)


def turn_body(par, lo, hi, pg, ra, rb, out_a, out_b):
    bx, _, bz, c = lo.shape
    cx, cy, cz, _ = pg.shape
    xlo, xhi = get_faces(par[0] == 1, ra, rb)
    fine = 2 * cy * bz

    def side(face, row, coarse, crow):
        return jnp.concatenate(
            [
                xlo[row : row + bz],
                face[...].reshape(bx * bz, c),
                xhi[row : row + bz],
                xlo[fine + crow : fine + crow + cz],
                coarse.reshape(cx * cz, c),
                xhi[fine + crow : fine + crow + cz],
            ],
            axis=0,
        )

    low = side(lo, 0, pg[:, 0], 0)
    high = side(hi, fine - bz, pg[:, cy - 1], (cy - 1) * cz)
    put_faces(par[1] == 1, out_a, out_b, low, high)


def fine_body(par, field, ra, rb, ua, ub, w, bias, fpad, hidden, ds, pooled, out_a, out_b, wb, tmp):
    bx, by, bz, c = field.shape
    cx, cy, cz = bx // 2, by // 2, bz // 2
    rows = by * bz
    xlo, xhi = get_faces(par[0] == 1, ra, rb)
    ylo, yhi = get_faces(par[1] == 1, ua, ub)
    fpad[1 : bx + 1, 1 : by + 1] = field[...]
    fpad[0, 1 : by + 1] = xlo[:rows].reshape(by, bz, c)
    fpad[bx + 1, 1 : by + 1] = xhi[:rows].reshape(by, bz, c)
    fpad[:, 0] = ylo[: (bx + 2) * bz].reshape(bx + 2, bz, c)
    fpad[:, by + 1] = yhi[: (bx + 2) * bz].reshape(bx + 2, bz, c)
    for i in range(3):
        for j in range(3):
            for k in range(3):
                wb[pl.ds((3 * i + j) * c, c), pl.ds(k * c, c)] = w[i, j, k]

    def plane(x):
        taps = [fpad[x + i, j : j + by].reshape(rows, c) for i in range(3) for j in range(3)]
        part = jnp.dot(jnp.concatenate(taps, axis=1), wb[...], preferred_element_type=F32)
        pre = (
            part[:, c : 2 * c]
            + shift_rows(part[:, :c], 1, bz)
            + shift_rows(part[:, 2 * c :], -1, bz)
            + bias[...]
        )
        sig = sigmoid(pre)
        hid = (pre * sig).astype(BF16)
        hidden[x] = hid.reshape(by, bz, c)
        ds[x] = (sig * (1.0 + pre * (1.0 - sig))).reshape(by, bz, c)
        return hid.astype(F32)

    def pair(q, carry):
        both = plane(2 * q) + plane(2 * q + 1)
        both = jnp.sum(both.reshape(cy, 2, bz, c), axis=1).reshape(cy * bz, c)
        pooled[q] = (sum_cube(cy * bz, both, tmp) / 8.0).astype(BF16).reshape(cy, cz, c)
        return carry

    lax.fori_loop(0, cx, pair, 0)
    low = pooled[0:2].reshape(2 * cy * cz, c)
    high = pooled[cx - 2 : cx].reshape(2 * cy * cz, c)
    put_faces(par[0] == 1, out_a, out_b, low, high)


def turn2_body(par, pooled, ra, rb, out_a, out_b):
    cx, cy, cz, c = pooled.shape
    xlo, xhi = get_faces(par[0] == 1, ra, rb)
    xlo, xhi = xlo.reshape(2, cy, cz, c), xhi.reshape(2, cy, cz, c)

    def side(y):
        parts = [xlo[:, y : y + 2], pooled[:, y : y + 2], xhi[:, y : y + 2]]
        return jnp.concatenate([p.reshape(-1, c) for p in parts], axis=0)

    put_faces(par[1] == 1, out_a, out_b, side(0), side(cy - 2))


def reverse_bits(value, count):
    out = 0
    for _ in range(count):
        out, value = out * 2 + value % 2, value // 2
    return out


def spread(par, keep, send, n, blocks, piece):
    bits = n.bit_length() - 1
    half = n // 2
    for b in (0, 1):

        @pl.when(par == b)
        def _():
            for s in range(n):
                target = keep if s % 2 == b else send
                for t in range(blocks):
                    value = piece(s, t)
                    size = value.shape[0]
                    target[reverse_bits(s, bits) % half, pl.ds(t * size, size)] = value


def coarse_body(
    n, par, pooled, ra, rb, ua, ub, pg, fa, fb, ga, gb, w, bias, wm,
    slope, coarse, keep, send, cbias, qpad, gpad, wb, st, rhs, acc, ct,
):
    cx, cy, cz, c = pooled.shape
    c2 = wm.shape[0]
    xlo, xhi = get_faces(par[0] == 1, ra, rb)
    ylo, yhi = get_faces(par[1] == 1, ua, ub)
    qpad[2 : cx + 2, 2 : cy + 2] = pooled[...]
    qpad[0:2, 2 : cy + 2] = xlo.reshape(2, cy, cz, c)
    qpad[cx + 2 : cx + 4, 2 : cy + 2] = xhi.reshape(2, cy, cz, c)
    qpad[:, 0:2] = ylo.reshape(cx + 4, 2, cz, c)
    qpad[:, cy + 2 : cy + 4] = yhi.reshape(cx + 4, 2, cz, c)
    face = cy * cz
    glo, ghi = get_faces(par[0] == 1, fa, fb)
    hlo, hhi = get_faces(par[1] == 1, ga, gb)
    gpad[1 : cx + 1, 1 : cy + 1] = pg[...]
    gpad[0, 1 : cy + 1] = glo[-face:].reshape(cy, cz, c)
    gpad[cx + 1, 1 : cy + 1] = ghi[-face:].reshape(cy, cz, c)
    edge = (cx + 2) * cz
    gpad[:, 0] = hlo[-edge:].reshape(cx + 2, cz, c)
    gpad[:, cy + 1] = hhi[-edge:].reshape(cx + 2, cz, c)
    for i in range(3):
        for j in range(3):
            for k in range(3):
                wb[pl.ds((3 * i + j) * c, c), pl.ds(k * c2, c2)] = w[i, j, k]
    wide = cy + 2
    rows = wide * cz

    def plane(x, carry):
        taps = [qpad[x + i, j : j + wide].reshape(rows, c) for i in range(3) for j in range(3)]
        part = jnp.dot(jnp.concatenate(taps, axis=1), wb[...], preferred_element_type=F32)
        pre = (
            part[:, c2 : 2 * c2]
            + shift_rows(part[:, :c2], 1, cz)
            + shift_rows(part[:, 2 * c2 :], -1, cz)
            + bias[...]
        )
        sig = sigmoid(pre)
        back = lax.dot_general(
            gpad[x].reshape(rows, c), wm[...], (((1,), (1,)), ((), ())), preferred_element_type=F32
        )
        slope[x] = (back * (sig * (1.0 + pre * (1.0 - sig)))).astype(BF16).reshape(wide, cz, c2)

        @pl.when((x >= 1) & (x <= cx))
        def _():
            coarse[x - 1] = (pre * sig).astype(BF16).reshape(wide, cz, c2)[1 : cy + 1]

        return carry

    lax.fori_loop(0, cx + 2, plane, 0)
    cells = cx * cy * cz
    mid = slope[1 : cx + 1, 1 : cy + 1].reshape(cells, c2)
    wide_mid = mid.astype(F32)
    st[pl.ds(0, c2), :] = shift_rows(wide_mid, -1, cz).astype(BF16).T
    st[pl.ds(c2, c2), :] = mid.T
    st[pl.ds(2 * c2, c2), :] = shift_rows(wide_mid, 1, cz).astype(BF16).T
    for i in range(3):
        for j in range(3):
            rhs[:, pl.ds((3 * i + j) * c, c)] = qpad[
                1 + i : 1 + i + cx, 1 + j : 1 + j + cy
            ].reshape(cells, c)
    rhs[:, pl.ds(9 * c, c)] = jnp.ones((cells, c), BF16)
    acc[...] = jnp.dot(st[...], rhs[...], preferred_element_type=F32).astype(BF16)
    ct[...] = jnp.dot(
        coarse[...].reshape(cells, c2).T, pg[...].reshape(cells, c), preferred_element_type=F32
    ).astype(BF16)
    cbias[...] = acc[pl.ds(c2, c2), pl.ds(9 * c, c)]
    per = c2 // n

    def piece(s, t):
        if t == 27:
            return ct[pl.ds(s * per, per), :]
        k, tap = t // 9, t % 9
        return acc[pl.ds(k * c2 + s * per, per), pl.ds(tap * c, c)]

    spread(par[2], keep, send, n, 28, piece)


def back_body(n, par, slope, w, cot, ds, fpad, cbias, keep, send, up, st, rhs, acc, wt):
    bx, by, bz, c = cot.shape
    cx, cy, cz = bx // 2, by // 2, bz // 2
    c2 = slope.shape[3]
    cells = cx * cy * cz
    total = jnp.zeros((cells, 3 * c), F32)
    for i in range(3):
        for j in range(3):
            tap = slope[2 - i : 2 - i + cx, 2 - j : 2 - j + cy].reshape(cells, c2)
            total = total + lax.dot_general(
                tap,
                w[i, j].reshape(3 * c, c2),
                (((1,), (1,)), ((), ())),
                preferred_element_type=F32,
            )
    pooled = (
        total[:, c : 2 * c]
        + shift_rows(total[:, :c], -1, cz)
        + shift_rows(total[:, 2 * c :], 1, cz)
    ) * 0.125
    up[pl.ds(0, cells, stride=2), :] = pooled
    up[pl.ds(1, cells, stride=2), :] = pooled
    rows = by * bz
    for x in range(bx):
        base = up[pl.ds((x // 2) * cy * bz, cy * bz), :].reshape(cy, 1, bz, c)
        fine = cot[x].astype(F32).reshape(cy, 2, bz, c) + base
        fs = (fine.reshape(rows, c) * ds[x].reshape(rows, c)).astype(BF16)
        wide = fs.astype(F32)
        st[pl.ds(0, c), pl.ds(x * rows, rows)] = shift_rows(wide, -1, bz).astype(BF16).T
        st[pl.ds(c, c), pl.ds(x * rows, rows)] = fs.T
        st[pl.ds(2 * c, c), pl.ds(x * rows, rows)] = shift_rows(wide, 1, bz).astype(BF16).T
    voxels = bx * rows
    for t in range(0, 10, 2):
        for h in (0, 1):
            i, j = (t + h) // 3, (t + h) % 3
            if t + h == 9:
                rhs[:, pl.ds(h * c, c)] = jnp.ones((voxels, c), BF16)
            else:
                rhs[:, pl.ds(h * c, c)] = fpad[i : i + bx, j : j + by].reshape(voxels, c)
        acc[:, pl.ds(t * c, 2 * c)] = jnp.dot(
            st[...], rhs[...], preferred_element_type=F32
        ).astype(BF16)
    per, cper = c // n, c2 // n
    lane = lax.broadcasted_iota(jnp.int32, (per, c), 1)

    def piece(s, t):
        if t == 27:
            bias = acc[pl.ds(c + s * per, per), pl.ds(9 * c, c)].astype(F32)
            one = cbias[pl.ds(s * cper, per), :].astype(F32)
            two = cbias[pl.ds(s * cper + per, per), :].astype(F32)
            return jnp.where(lane == 0, bias, jnp.where(lane == 1, one, two)).astype(BF16)
        k, tap = t // 9, t % 9
        return acc[pl.ds(k * c + s * per, per), pl.ds(tap * c, c)]

    spread(par[2], keep, send, n, 28, piece)


def merge_body(par, hidden, coarse, wm, out, tmp):
    bx, by, bz, c = hidden.shape
    cx, cy, cz = bx // 2, by // 2, bz // 2
    c2 = coarse.shape[3]
    cells = cx * cy * cz
    proj = jnp.dot(coarse[...].reshape(cells, c2), wm[...], preferred_element_type=F32)
    tmp[pl.ds(0, cells, stride=2), :] = proj
    tmp[pl.ds(1, cells, stride=2), :] = proj
    for x in range(bx):
        base = tmp[pl.ds((x // 2) * cy * bz, cy * bz), :].reshape(cy, 1, bz, c)
        total = hidden[x].astype(F32).reshape(cy, 2, bz, c) + base
        out[x] = total.astype(BF16).reshape(by, bz, c)


def swap(value, axis, bit):
    n = lax.axis_size(axis)
    return lax.ppermute(value, axis, [(i, i ^ (1 << bit)) for i in range(n)])


def swap_faces(first, second, axis):
    n = lax.axis_size(axis)
    one = [p for i in range(0, n - 1, 2) for p in ((i, i + 1), (i + 1, i))]
    two = [p for i in range(1, n - 1, 2) for p in ((i, i + 1), (i + 1, i))]
    return lax.ppermute(first, axis, one), lax.ppermute(second, axis, two)


def add(a, b):
    return (a.astype(F32) + b.astype(F32)).astype(BF16)


def half_of(value, which):
    size = value.shape[0] // 2
    return lax.dynamic_slice_in_dim(value, which * size, size, 0)


def reduce_all(keep, send, sub, grp):
    got = swap(send, "sub", 0)
    for bit in range(1, lax.axis_size("sub").bit_length() - 1):
        mine = (sub >> bit) & 1
        send = add(half_of(keep, 1 - mine), half_of(got, 1 - mine))
        keep = add(half_of(keep, mine), half_of(got, mine))
        got = swap(send, "sub", bit)
    total = add(keep, got)[0]
    order = []
    for bit in range(lax.axis_size("grp").bit_length() - 1):
        mine = (grp >> bit) & 1
        if total.shape[0] % 32:
            total = add(total, swap(total, "grp", bit))
            continue
        got = swap(half_of(total, 1 - mine), "grp", bit)
        total = add(half_of(total, mine), got)
        order.append((bit, mine))
    for bit, mine in reversed(order):
        got = swap(total, "grp", bit)
        first, second = jnp.where(mine == 0, total, got), jnp.where(mine == 0, got, total)
        total = jnp.concatenate([first, second], axis=0)
    return total


def per_device(field, cotangent, fine_kernel, fine_bias, coarse_kernel, coarse_bias, merge_weight):
    grp, sub = lax.axis_index("grp"), lax.axis_index("sub")
    n = lax.axis_size("sub")
    bx, by, bz, c = field.shape
    cx, cy, cz = bx // 2, by // 2, bz // 2
    c2 = merge_weight.shape[0]
    par = jnp.stack([grp % 2, sub % 2, sub % 2]).astype(jnp.int32)
    face = by * bz + cy * cz
    pg, sa, sb = call(
        prep_body,
        "prep",
        (par, field[:1], field[bx - 1 :], cotangent),
        [((cx, cy, cz, c), BF16), ((face, c), BF16), ((face, c), BF16)],
        [pltpu.VMEM((cx * cy * bz, c), F32)],
    )
    xa, xb = swap_faces(sa, sb, "grp")
    edge = (bx + 2) * bz + (cx + 2) * cz
    ta, tb = call(
        turn_body,
        "turn",
        (par, field[:, :1], field[:, by - 1 :], pg, xa, xb),
        [((edge, c), BF16), ((edge, c), BF16)],
    )
    ya, yb = swap_faces(ta, tb, "sub")
    side = 2 * cy * cz
    fpad, hidden, ds, pooled, pa, pb = call(
        fine_body,
        "fine",
        (par, field, xa, xb, ya, yb, fine_kernel, fine_bias.reshape(1, c)),
        [
            ((bx + 2, by + 2, bz, c), BF16),
            ((bx, by, bz, c), BF16),
            ((bx, by, bz, c), F32),
            ((cx, cy, cz, c), BF16),
            ((side, c), BF16),
            ((side, c), BF16),
        ],
        [pltpu.VMEM((9 * c, 3 * c), BF16), pltpu.VMEM((cy * bz, c), F32)],
    )
    pxa, pxb = swap_faces(pa, pb, "grp")
    side = (cx + 4) * 2 * cz
    qa, qb = call(
        turn2_body,
        "turn2",
        (par, pooled, pxa, pxb),
        [((side, c), BF16), ((side, c), BF16)],
    )
    pya, pyb = swap_faces(qa, qb, "sub")
    cells = cx * cy * cz
    part = (n // 2, 28 * (c2 // n), c)
    slope, coarse, ckeep, csend, cbias = call(
        functools.partial(coarse_body, n),
        "coarse",
        (par, pooled, pxa, pxb, pya, pyb, pg, xa, xb, ya, yb, coarse_kernel, coarse_bias.reshape(1, c2), merge_weight),
        [
            ((cx + 2, cy + 2, cz, c2), BF16),
            ((cx, cy, cz, c2), BF16),
            (part, BF16),
            (part, BF16),
            ((c2, c), BF16),
        ],
        [
            pltpu.VMEM((cx + 4, cy + 4, cz, c), BF16),
            pltpu.VMEM((cx + 2, cy + 2, cz, c), BF16),
            pltpu.VMEM((9 * c, 3 * c2), BF16),
            pltpu.VMEM((3 * c2, cells), BF16),
            pltpu.VMEM((cells, 10 * c), BF16),
            pltpu.VMEM((3 * c2, 10 * c), BF16),
            pltpu.VMEM((c2, c), BF16),
        ],
    )
    coarse_sum = reduce_all(ckeep, csend, sub, grp)
    part = (n // 2, 28 * (c // n), c)
    fkeep, fsend = call(
        functools.partial(back_body, n),
        "back",
        (par, slope, coarse_kernel, cotangent, ds, fpad, cbias),
        [(part, BF16), (part, BF16)],
        [
            pltpu.VMEM((cx * cy * bz, c), F32),
            pltpu.VMEM((3 * c, bx * by * bz), BF16),
            pltpu.VMEM((bx * by * bz, 2 * c), BF16),
            pltpu.VMEM((3 * c, 10 * c), BF16),
            pltpu.VMEM((16, 128), BF16),
        ],
    )
    fine_sum = reduce_all(fkeep, fsend, sub, grp)
    (output,) = call(
        merge_body,
        "merge",
        (par, hidden, coarse, merge_weight),
        [((bx, by, bz, c), BF16)],
        [pltpu.VMEM((cx * cy * bz, c), F32)],
    )
    per, cper = c // n, c2 // n
    fine_sum = fine_sum.reshape(28, per, c)
    coarse_sum = coarse_sum.reshape(28, cper, c)

    def kernel_of(total, size):
        shaped = total[:27].reshape(3, 3, 3, size, c)
        return jnp.transpose(shaped, (1, 2, 0, 4, 3)).astype(F32)

    grad_coarse_bias = jnp.concatenate([fine_sum[27, :, 1], fine_sum[27, :, 2]]).astype(F32)
    return (
        output,
        kernel_of(fine_sum, per),
        fine_sum[27, :, 0].astype(F32),
        kernel_of(coarse_sum, cper),
        grad_coarse_bias,
        coarse_sum[27].astype(F32),
    )


def solution(mesh):
    in_specs = (P("grp", "sub", None, None), P("grp", "sub", None, None), P(), P(), P(), P(), P())
    out_specs = (
        P("grp", "sub", None, None),
        P(None, None, None, None, "sub"),
        P("sub"),
        P(None, None, None, None, "sub"),
        P("sub"),
        P("sub", None),
    )
    return jax.shard_map(
        per_device, mesh=mesh, in_specs=in_specs, out_specs=out_specs, check_vma=False
    )
```

profile of v0, /device:TPU:0, one launch (start us, length us, event | category | flops | bytes accessed | tf_op | source)
XLA Modules:
  0.0 135.0 jit_solution(11217982558560954768)
XLA Ops:
  0.7 1.0 fusion.4
  1.7 0.1 pad_add_fusion.par
  1.7 1.2 copy-done.1
  3.0 0.8 prep.1
  3.8 3.0 %collective-permute-start = (bf16[640,128]{1,0:T(8,128)(2,1)S(1)}, bf16[640,128]{1,0:T(8,128)(2,1)S(1)}, u32[]{:S(2)}, u32[]{:S(2)}) collective-permute-start(bf16[640,128]{1,0:T(8,128)(2,1)S(1)} %get-tuple-element.26), channel_id=1, source_target_pairs={{0,4},{4,0},{8,12},{12,8},{16,20},{20,16},{24,28},{28,24},{1,5},{5... | collective-permute-start | bytes 491528 | tf_op jit(solution)/shard_map/ppermute | solution.py:330
  6.8 0.8 collective-permute-start.1
  7.6 0.9 fusion.3
  8.5 5.3 %collective-permute-done.ra.fa = bf16[640,128]{1,0:T(8,128)(2,1)S(1)} collective-permute-done((bf16[640,128]{1,0:T(8,128)(2,1)S(1)}, bf16[640,128]{1,0:T(8,128)(2,1)S(1)}, u32[]{:S(2)}, u32[]{:S(2)}) %collective-permute-start) | collective-permute-done | bytes 163872 | tf_op jit(solution)/shard_map/ppermute | solution.py:330
  13.8 0.6 turn.1
  14.5 0.7 collective-permute-start.3
  15.1 0.6 collective-permute-done.2.ua.ga
  15.8 8.6 %fine.1 = (bf16[10,18,32,128]{3,2,1,0:T(8,128)(2,1)S(1)}, bf16[8,16,32,128]{3,2,1,0:T(8,128)(2,1)S(1)}, f32[8,16,32,128]{3,2,1,0:T(8,128)}, bf16[4,8,16,128]{3,2...) custom-call(s32[3]{0:T(128)S(1)} %pad_add_fusion.par, ...), custom_call_target="tpu_custom_call" | custom-call | tf_op jit(solution)/shard_map/fine/pallas_call | solution.py:18
  24.4 2.4 %collective-permute-start.4 = (bf16[256,128]{1,0:T(8,128)(2,1)S(1)}, bf16[256,128]{1,0:T(8,128)(2,1)S(1)}, u32[]{:S(2)}, u32[]{:S(2)}) collective-permute-start(bf16[256,128]{1,0:T(8,128)(2,1)S(1)} %get-tuple-element.33), channel_id=1, source_target_pairs={{0,4},{4,0},{8,12},{12,8},{16,20},{20,16},{24,28},{28,24},{1,5},{5... | collective-permute-start | bytes 196616 | tf_op jit(solution)/shard_map/ppermute | solution.py:330
  26.9 0.7 collective-permute-start.5
  27.5 1.6 %collective-permute-done.4.ra = bf16[256,128]{1,0:T(8,128)(2,1)S(1)} collective-permute-done((bf16[256,128]{1,0:T(8,128)(2,1)S(1)}, bf16[256,128]{1,0:T(8,128)(2,1)S(1)}, u32[]{:S(2)}, u32[]{:S(2)}) %collective-permute-start.4) | collective-permute-done | bytes 65568 | tf_op jit(solution)/shard_map/ppermute | solution.py:330
  29.1 0.6 turn2.1
  29.7 4.4 %collective-permute-start.6 = (bf16[256,128]{1,0:T(8,128)(2,1)S(1)}, bf16[256,128]{1,0:T(8,128)(2,1)S(1)}, u32[]{:S(2)}, u32[]{:S(2)}) collective-permute-start(bf16[256,128]{1,0:T(8,128)(2,1)S(1)} %get-tuple-element.35), channel_id=1, source_target_pairs={{0,1},{1,0},{2,3},{3,2},{4,5},{5,4},{6,7},{7,6},{8,9},{9,8},{10,11... | collective-permute-start | bytes 196616 | tf_op jit(solution)/shard_map/ppermute | solution.py:330
  34.1 0.7 collective-permute-start.7
  34.8 0.2 collective-permute-done.6.ua
  35.0 5.9 %coarse.1 = (bf16[6,10,16,256]{3,2,1,0:T(8,128)(2,1)S(1)}, bf16[4,8,16,256]{3,2,1,0:T(8,128)(2,1)S(1)}, bf16[2,1792,128]{2,1,0:T(8,128)(2,1)S(1)}, bf16[2,1792,128]{2,1,0:T(8,128)(2,1)S(1)}, bf16[256,128]{1,0:T(8,128)(2,1)S(1)}) custom-call(s32[3]{0:T(128)S(1)} %pad_add_fusion.par, bf16[4,8,16,128]{3,2,1,0:T(8,128)(2,1)S(1)} %get-tuple-element.32.pooled, ...), custom_call_target="tpu_custom_call" | custom-call | tf_op jit(solution)/shard_map/coarse/pallas_call | solution.py:18
  41.0 10.2 %back.1 = (bf16[2,896,128]{2,1,0:T(8,128)(2,1)S(1)}, bf16[2,896,128]{2,1,0:T(8,128)(2,1)S(1)}) custom-call(s32[3]{0:T(128)S(1)} %pad_add_fusion.par, bf16[6,10,16,256]{3,2,1,0:T(8,128)(2,1)S(1)} %get-tuple-element.38.slope, bf16[3,3,3,128,256]{4,3,2,1,0:T(8,128)(2,1)S(1)} %copy-done, bf16[8,16,32,128]{3,2,1,0:T(8,128)(2,1)S(1)} %copy-done.2, ...), custom_call_target="tpu_custom_call" | custom-call | tf_op jit(solution)/shard_map/back/pallas_call | solution.py:18
  51.2 5.1 %collective-permute-start.8 = (bf16[2,896,128]{2,1,0:T(8,128)(2,1)S(1)}, bf16[2,896,128]{2,1,0:T(8,128)(2,1)}, u32[]{:S(2)}, u32[]{:S(2)}) collective-permute-start(bf16[2,896,128]{2,1,0:T(8,128)(2,1)S(1)} %get-tuple-element.43), channel_id=1, source_target_pairs={{0,1},{1,0},{2,3},{3,2},{4,5},{5,4},{6,7},{7,6},{8,9},{9,8},{10,11... | collective-permute-start | bytes 1376264 | tf_op jit(solution)/shard_map/ppermute | solution.py:323
  56.3 1.6 %collective-permute-done.8 = bf16[2,896,128]{2,1,0:T(8,128)(2,1)} collective-permute-done((bf16[2,896,128]{2,1,0:T(8,128)(2,1)S(1)}, bf16[2,896,128]{2,1,0:T(8,128)(2,1)}, u32[]{:S(2)}, u32[]{:S(2)}) %collective-permute-start.8) | collective-permute-done | bytes 458784 | tf_op jit(solution)/shard_map/ppermute | solution.py:323
  57.9 1.0 add_convert_fusion.4
  58.9 2.0 %collective-permute-start.9 = (bf16[1,896,128]{2,1,0:T(8,128)(2,1)S(1)}, bf16[1,896,128]{2,1,0:T(8,128)(2,1)S(1)}, u32[]{:S(2)}, u32[]{:S(2)}) collective-permute-start(bf16[1,896,128]{2,1,0:T(8,128)(2,1)S(1)} %add_convert_fusion.4), channel_id=1, source_target_pairs={{0,2},{1,3},{2,0},{3,1},{4,6},{5,7},{6,4},{7,5},{8,10},{9,11},{10,... | collective-permute-start | bytes 688136 | tf_op jit(solution)/shard_map/ppermute | solution.py:323
  60.9 5.9 %collective-permute-done.9 = bf16[1,896,128]{2,1,0:T(8,128)(2,1)S(1)} collective-permute-done((bf16[1,896,128]{2,1,0:T(8,128)(2,1)S(1)}, bf16[1,896,128]{2,1,0:T(8,128)(2,1)S(1)}, u32[]{:S(2)}, u32[]{:S(2)}) %collective-permute-start.9) | collective-permute-done | bytes 229408 | tf_op jit(solution)/shard_map/ppermute | solution.py:323
  66.8 1.1 add_convert_fusion.3
  67.9 5.0 %collective-permute-start.10 = (bf16[448,128]{1,0:T(8,128)(2,1)S(1)}, bf16[448,128]{1,0:T(8,128)(2,1)S(1)}, u32[]{:S(2)}, u32[]{:S(2)}) collective-permute-start(bf16[448,128]{1,0:T(8,128)(2,1)S(1)} %dynamic-slice_bitcast_fusion.1), channel_id=1, source_target_pairs={{0,4},{4,0},{8,12},{12,8},{16,20},{20,16},{24,28},{28,24},{1,5},{5... | collective-permute-start | bytes 344072 | tf_op jit(solution)/shard_map/ppermute | solution.py:323
  72.9 2.9 %collective-permute-done.10 = bf16[448,128]{1,0:T(8,128)(2,1)S(1)} collective-permute-done((bf16[448,128]{1,0:T(8,128)(2,1)S(1)}, bf16[448,128]{1,0:T(8,128)(2,1)S(1)}, u32[]{:S(2)}, u32[]{:S(2)}) %collective-permute-start.10) | collective-permute-done | bytes 114720 | tf_op jit(solution)/shard_map/ppermute | solution.py:323
  75.8 3.4 %collective-permute-start.11 = (bf16[224,128]{1,0:T(8,128)(2,1)S(1)}, bf16[224,128]{1,0:T(8,128)(2,1)S(1)}, u32[]{:S(2)}, u32[]{:S(2)}) collective-permute-start(bf16[224,128]{1,0:T(8,128)(2,1)S(1)} %constant_dynamic-slice_fusion.2), channel_id=1, source_target_pairs={{0,8},{4,12},{8,0},{12,4},{16,24},{20,28},{24,16},{28,20},{1,9},{5... | collective-permute-start | bytes 172040 | tf_op jit(solution)/shard_map/ppermute | solution.py:323
  79.3 2.2 %collective-permute-done.11 = bf16[224,128]{1,0:T(8,128)(2,1)S(1)} collective-permute-done((bf16[224,128]{1,0:T(8,128)(2,1)S(1)}, bf16[224,128]{1,0:T(8,128)(2,1)S(1)}, u32[]{:S(2)}, u32[]{:S(2)}) %collective-permute-start.11) | collective-permute-done | bytes 57376 | tf_op jit(solution)/shard_map/ppermute | solution.py:323
  81.5 3.3 %collective-permute-start.12 = (bf16[112,128]{1,0:T(8,128)(2,1)S(1)}, bf16[112,128]{1,0:T(8,128)(2,1)S(1)}, u32[]{:S(2)}, u32[]{:S(2)}) collective-permute-start(bf16[112,128]{1,0:T(8,128)(2,1)S(1)} %constant_dynamic-slice_fusion.1), channel_id=1, source_target_pairs={{0,16},{4,20},{8,24},{12,28},{16,0},{20,4},{24,8},{28,12},{1,17},{... | collective-permute-start | bytes 86024 | tf_op jit(solution)/shard_map/ppermute | solution.py:323
  84.8 2.1 %collective-permute-done.12 = bf16[112,128]{1,0:T(8,128)(2,1)S(1)} collective-permute-done((bf16[112,128]{1,0:T(8,128)(2,1)S(1)}, bf16[112,128]{1,0:T(8,128)(2,1)S(1)}, u32[]{:S(2)}, u32[]{:S(2)}) %collective-permute-start.12) | collective-permute-done | bytes 28704 | tf_op jit(solution)/shard_map/ppermute | solution.py:323
  86.9 2.8 %collective-permute-start.13 = (bf16[112,128]{1,0:T(8,128)(2,1)S(1)}, bf16[112,128]{1,0:T(8,128)(2,1)S(1)}, u32[]{:S(2)}, u32[]{:S(2)}) collective-permute-start(bf16[112,128]{1,0:T(8,128)(2,1)S(1)} %add_convert_fusion.9), channel_id=1, source_target_pairs={{0,16},{4,20},{8,24},{12,28},{16,0},{20,4},{24,8},{28,12},{1,17},{... | collective-permute-start | bytes 86024 | tf_op jit(solution)/shard_map/ppermute | solution.py:323
  89.7 1.1 add_convert_fusion.1
  90.9 1.8 %collective-permute-start.17 = (bf16[1,1792,128]{2,1,0:T(8,128)(2,1)S(1)}, bf16[1,1792,128]{2,1,0:T(8,128)(2,1)S(1)}, u32[]{:S(2)}, u32[]{:S(2)}) collective-permute-start(bf16[1,1792,128]{2,1,0:T(8,128)(2,1)S(1)} %add_convert_fusion.1), channel_id=1, source_target_pairs={{0,2},{1,3},{2,0},{3,1},{4,6},{5,7},{6,4},{7,5},{8,10},{9,11},{10,... | collective-permute-start | bytes 1376264 | tf_op jit(solution)/shard_map/ppermute | solution.py:323
  92.7 0.8 collective-permute-start.14
  93.4 1.8 %merge.1 = bf16[8,16,32,128]{3,2,1,0:T(8,128)(2,1)} custom-call(s32[3]{0:T(128)S(1)} %pad_add_fusion.par, bf16[8,16,32,128]{3,2,1,0:T(8,128)(2,1)S(1)} %get-tuple-element.31.hidden, bf16[4,8,16,256]{3,2,1,0:T(8,128)(2,1)S(1)} %get-tuple-element.37.coarse, bf16[256,128]{1,0:T(8,128)(2,1)S(1)} %copy-done.5), custom_call_target="tpu_custom_call" | custom-call | tf_op jit(solution)/shard_map/merge/pallas_call | solution.py:18
  95.3 1.6 %collective-permute-done.14 = bf16[224,128]{1,0:T(8,128)(2,1)S(1)} collective-permute-done((bf16[224,128]{1,0:T(8,128)(2,1)S(1)}, bf16[224,128]{1,0:T(8,128)(2,1)S(1)}, u32[]{:S(2)}, u32[]{:S(2)}) %collective-permute-start.14) | collective-permute-done | bytes 57376 | tf_op jit(solution)/shard_map/ppermute | solution.py:323
  97.0 1.2 collective-permute-start.15
  98.2 1.2 collective-permute-done.17
  99.4 1.3 add_convert_fusion
  100.7 1.2 collective-permute-start.18
  102.0 4.8 %collective-permute-done.18 = bf16[896,128]{1,0:T(8,128)(2,1)S(1)} collective-permute-done((bf16[896,128]{1,0:T(8,128)(2,1)S(1)}, bf16[896,128]{1,0:T(8,128)(2,1)S(1)}, u32[]{:S(2)}, u32[]{:S(2)}) %collective-permute-start.18) | collective-permute-done | bytes 229408 | tf_op jit(solution)/shard_map/ppermute | solution.py:323
  106.9 0.9 collective-permute-start.19
  107.8 3.9 %collective-permute-done.19 = bf16[448,128]{1,0:T(8,128)(2,1)S(1)} collective-permute-done((bf16[448,128]{1,0:T(8,128)(2,1)S(1)}, bf16[448,128]{1,0:T(8,128)(2,1)S(1)}, u32[]{:S(2)}, u32[]{:S(2)}) %collective-permute-start.19) | collective-permute-done | bytes 114720 | tf_op jit(solution)/shard_map/ppermute | solution.py:323
  111.8 0.7 collective-permute-start.20
  112.5 0.8 copy_bitcast_fusion.1
  113.3 3.7 %collective-permute-done.20 = bf16[224,128]{1,0:T(8,128)(2,1)S(1)} collective-permute-done((bf16[224,128]{1,0:T(8,128)(2,1)S(1)}, bf16[224,128]{1,0:T(8,128)(2,1)S(1)}, u32[]{:S(2)}, u32[]{:S(2)}) %collective-permute-start.20) | collective-permute-done | bytes 57376 | tf_op jit(solution)/shard_map/ppermute | solution.py:323
  117.1 1.2 collective-permute-start.21
  118.3 3.9 %collective-permute-done.21 = bf16[224,128]{1,0:T(8,128)(2,1)S(1)} collective-permute-done((bf16[224,128]{1,0:T(8,128)(2,1)S(1)}, bf16[224,128]{1,0:T(8,128)(2,1)S(1)}, u32[]{:S(2)}, u32[]{:S(2)}) %collective-permute-start.21) | collective-permute-done | bytes 57376 | tf_op jit(solution)/shard_map/ppermute | solution.py:323
  122.2 1.4 %collective-permute-start.22 = (bf16[448,128]{1,0:T(8,128)(2,1)S(1)}, bf16[448,128]{1,0:T(8,128)(2,1)S(1)}, u32[]{:S(2)}, u32[]{:S(2)}) collective-permute-start(bf16[448,128]{1,0:T(8,128)(2,1)S(1)} %pad_maximum_fusion.4), channel_id=1, source_target_pairs={{0,8},{4,12},{8,0},{12,4},{16,24},{20,28},{24,16},{28,20},{1,9},{5... | collective-permute-start | bytes 344072 | tf_op jit(solution)/shard_map/ppermute | solution.py:323
  123.7 0.1 fusion.5
  123.7 0.1 copy.19
  123.8 0.1 copy.20
  123.9 3.2 %collective-permute-done.22 = bf16[448,128]{1,0:T(8,128)(2,1)S(1)} collective-permute-done((bf16[448,128]{1,0:T(8,128)(2,1)S(1)}, bf16[448,128]{1,0:T(8,128)(2,1)S(1)}, u32[]{:S(2)}, u32[]{:S(2)}) %collective-permute-start.22) | collective-permute-done | bytes 114720 | tf_op jit(solution)/shard_map/ppermute | solution.py:323
  127.2 2.0 %collective-permute-start.23 = (bf16[896,128]{1,0:T(8,128)(2,1)S(1)}, bf16[896,128]{1,0:T(8,128)(2,1)S(1)}, u32[]{:S(2)}, u32[]{:S(2)}) collective-permute-start(bf16[896,128]{1,0:T(8,128)(2,1)S(1)} %pad_maximum_fusion.2), channel_id=1, source_target_pairs={{0,4},{4,0},{8,12},{12,8},{16,20},{20,16},{24,28},{28,24},{1,5},{5... | collective-permute-start | bytes 688136 | tf_op jit(solution)/shard_map/ppermute | solution.py:323
  129.2 0.6 maximum_convert_fusion
  129.8 0.1 copy.18
  129.9 0.5 bitcast_convert_fusion
  130.4 2.9 %collective-permute-done.23 = bf16[896,128]{1,0:T(8,128)(2,1)S(1)} collective-permute-done((bf16[896,128]{1,0:T(8,128)(2,1)S(1)}, bf16[896,128]{1,0:T(8,128)(2,1)S(1)}, u32[]{:S(2)}, u32[]{:S(2)}) %collective-permute-start.23) | collective-permute-done | bytes 229408 | tf_op jit(solution)/shard_map/ppermute | solution.py:323
  133.3 0.1 broadcast_select_fusion.1
  133.4 0.6 slice_convert_fusion
  134.0 1.0 copy_bitcast_fusion
  (50 shorter events, 0.7 us)
Async XLA Ops:
  0.6 15.1 %copy-start.7 = (f32[128]{0:T(128)S(1)}, f32[128]{0:T(128)}, u32[]{:S(2)}) copy-start(f32[128]{0:T(128)} %param.10) | copy-start | bytes 1540
  1.7 1.2 copy-start.1
  3.0 12.8 %copy-start.3 = (bf16[8,16,32,128]{3,2,1,0:T(8,128)(2,1)S(1)}, bf16[8,16,32,128]{3,2,1,0:T(8,128)(2,1)}, u32[]{:S(2)}) copy-start(bf16[8,16,32,128]{3,2,1,0:T(8,128)(2,1)} %field.1) | copy-start | bytes 3145732
  3.0 12.8 %copy-start.4 = (bf16[3,3,3,128,128]{4,3,2,1,0:T(8,128)(2,1)S(1)}, bf16[3,3,3,128,128]{4,3,2,1,0:T(8,128)(2,1)}, u32[]{:S(2)}) copy-start(bf16[3,3,3,128,128]{4,3,2,1,0:T(8,128)(2,1)} %w.3) | copy-start | bytes 2654212
  3.8 10.0 %collective-permute-start = (bf16[640,128]{1,0:T(8,128)(2,1)S(1)}, bf16[640,128]{1,0:T(8,128)(2,1)S(1)}, u32[]{:S(2)}, u32[]{:S(2)}) collective-permute-start(bf16[640,128]{1,0:T(8,128)(2,1)S(1)} %get-tuple-element.26), channel_id=1, source_target_pairs={{0,4},{4,0},{8,12},{12,8},{16,20},{20,16},{24,28},{28,24},{1,5},{5... | collective-permute-start | bytes 491528 | tf_op jit(solution)/shard_map/ppermute | solution.py:330
  6.8 28.2 %copy-start = (bf16[3,3,3,128,256]{4,3,2,1,0:T(8,128)(2,1)S(1)}, bf16[3,3,3,128,256]{4,3,2,1,0:T(8,128)(2,1)}, u32[]{:S(2)}) copy-start(bf16[3,3,3,128,256]{4,3,2,1,0:T(8,128)(2,1)} %w.5) | copy-start | bytes 5308420
  6.8 28.2 %copy-start.5 = (bf16[256,128]{1,0:T(8,128)(2,1)S(1)}, bf16[256,128]{1,0:T(8,128)(2,1)}, u32[]{:S(2)}) copy-start(bf16[256,128]{1,0:T(8,128)(2,1)} %wm.3) | copy-start | bytes 196612
  6.8 28.2 %copy-start.6 = (f32[256]{0:T(256)S(1)}, f32[256]{0:T(256)}, u32[]{:S(2)}) copy-start(f32[256]{0:T(256)} %param.12) | copy-start | bytes 3076
  6.8 7.0 %collective-permute-start.1 = (bf16[640,128]{1,0:T(8,128)(2,1)S(1)}, bf16[640,128]{1,0:T(8,128)(2,1)S(1)}, u32[]{:S(2)}, u32[]{:S(2)}) collective-permute-start(bf16[640,128]{1,0:T(8,128)(2,1)S(1)} %get-tuple-element.27), channel_id=1, source_target_pairs={{4,8},{8,4},{12,16},{16,12},{20,24},{24,20},{5,9},{9,5},{13,17},{1... | collective-permute-start | bytes 491528 | tf_op jit(solution)/shard_map/ppermute | solution.py:330
  14.4 1.4 %collective-permute-start.2 = (bf16[416,128]{1,0:T(8,128)(2,1)S(1)}, bf16[416,128]{1,0:T(8,128)(2,1)S(1)}, u32[]{:S(2)}, u32[]{:S(2)}) collective-permute-start(bf16[416,128]{1,0:T(8,128)(2,1)S(1)} %get-tuple-element.29), channel_id=1, source_target_pairs={{0,1},{1,0},{2,3},{3,2},{4,5},{5,4},{6,7},{7,6},{8,9},{9,8},{10,11... | collective-permute-start | bytes 319496 | tf_op jit(solution)/shard_map/ppermute | solution.py:330
  14.5 1.3 collective-permute-start.3
  24.4 16.6 %copy-start.2 = (bf16[8,16,32,128]{3,2,1,0:T(8,128)(2,1)S(1)}, bf16[8,16,32,128]{3,2,1,0:T(8,128)(2,1)}, u32[]{:S(2)}) copy-start(bf16[8,16,32,128]{3,2,1,0:T(8,128)(2,1)} %cot.3) | copy-start | bytes 3145732
  24.4 4.7 %collective-permute-start.4 = (bf16[256,128]{1,0:T(8,128)(2,1)S(1)}, bf16[256,128]{1,0:T(8,128)(2,1)S(1)}, u32[]{:S(2)}, u32[]{:S(2)}) collective-permute-start(bf16[256,128]{1,0:T(8,128)(2,1)S(1)} %get-tuple-element.33), channel_id=1, source_target_pairs={{0,4},{4,0},{8,12},{12,8},{16,20},{20,16},{24,28},{28,24},{1,5},{5... | collective-permute-start | bytes 196616 | tf_op jit(solution)/shard_map/ppermute | solution.py:330
  26.9 2.2 %collective-permute-start.5 = (bf16[256,128]{1,0:T(8,128)(2,1)S(1)}, bf16[256,128]{1,0:T(8,128)(2,1)S(1)}, u32[]{:S(2)}, u32[]{:S(2)}) collective-permute-start(bf16[256,128]{1,0:T(8,128)(2,1)S(1)} %get-tuple-element.34), channel_id=1, source_target_pairs={{4,8},{8,4},{12,16},{16,12},{20,24},{24,20},{5,9},{9,5},{13,17},{1... | collective-permute-start | bytes 196616 | tf_op jit(solution)/shard_map/ppermute | solution.py:330
  29.7 5.3 %collective-permute-start.6 = (bf16[256,128]{1,0:T(8,128)(2,1)S(1)}, bf16[256,128]{1,0:T(8,128)(2,1)S(1)}, u32[]{:S(2)}, u32[]{:S(2)}) collective-permute-start(bf16[256,128]{1,0:T(8,128)(2,1)S(1)} %get-tuple-element.35), channel_id=1, source_target_pairs={{0,1},{1,0},{2,3},{3,2},{4,5},{5,4},{6,7},{7,6},{8,9},{9,8},{10,11... | collective-permute-start | bytes 196616 | tf_op jit(solution)/shard_map/ppermute | solution.py:330
  34.1 0.9 collective-permute-start.7
  41.0 10.2 %copy-start.8 = (bf16[2,1792,128]{2,1,0:T(8,128)(2,1)}, bf16[2,1792,128]{2,1,0:T(8,128)(2,1)S(1)}, u32[]{:S(2)}) copy-start(bf16[2,1792,128]{2,1,0:T(8,128)(2,1)S(1)} %get-tuple-element.45) | copy-start | bytes 2752516
  51.2 6.7 %collective-permute-start.8 = (bf16[2,896,128]{2,1,0:T(8,128)(2,1)S(1)}, bf16[2,896,128]{2,1,0:T(8,128)(2,1)}, u32[]{:S(2)}, u32[]{:S(2)}) collective-permute-start(bf16[2,896,128]{2,1,0:T(8,128)(2,1)S(1)} %get-tuple-element.43), channel_id=1, source_target_pairs={{0,1},{1,0},{2,3},{3,2},{4,5},{5,4},{6,7},{7,6},{8,9},{9,8},{10,11... | collective-permute-start | bytes 1376264 | tf_op jit(solution)/shard_map/ppermute | solution.py:323
  58.9 7.9 %collective-permute-start.9 = (bf16[1,896,128]{2,1,0:T(8,128)(2,1)S(1)}, bf16[1,896,128]{2,1,0:T(8,128)(2,1)S(1)}, u32[]{:S(2)}, u32[]{:S(2)}) collective-permute-start(bf16[1,896,128]{2,1,0:T(8,128)(2,1)S(1)} %add_convert_fusion.4), channel_id=1, source_target_pairs={{0,2},{1,3},{2,0},{3,1},{4,6},{5,7},{6,4},{7,5},{8,10},{9,11},{10,... | collective-permute-start | bytes 688136 | tf_op jit(solution)/shard_map/ppermute | solution.py:323
  67.9 7.9 %collective-permute-start.10 = (bf16[448,128]{1,0:T(8,128)(2,1)S(1)}, bf16[448,128]{1,0:T(8,128)(2,1)S(1)}, u32[]{:S(2)}, u32[]{:S(2)}) collective-permute-start(bf16[448,128]{1,0:T(8,128)(2,1)S(1)} %dynamic-slice_bitcast_fusion.1), channel_id=1, source_target_pairs={{0,4},{4,0},{8,12},{12,8},{16,20},{20,16},{24,28},{28,24},{1,5},{5... | collective-permute-start | bytes 344072 | tf_op jit(solution)/shard_map/ppermute | solution.py:323
  72.9 16.8 %collective-permute-start.16 = (bf16[2,1792,128]{2,1,0:T(8,128)(2,1)}, bf16[2,1792,128]{2,1,0:T(8,128)(2,1)}, u32[]{:S(2)}, u32[]{:S(2)}) collective-permute-start(bf16[2,1792,128]{2,1,0:T(8,128)(2,1)} %copy-done.8), channel_id=1, source_target_pairs={{0,1},{1,0},{2,3},{3,2},{4,5},{5,4},{6,7},{7,6},{8,9},{9,8},{10,11... | collective-permute-start | bytes 2752520 | tf_op jit(solution)/shard_map/ppermute | solution.py:323
  75.8 5.6 %collective-permute-start.11 = (bf16[224,128]{1,0:T(8,128)(2,1)S(1)}, bf16[224,128]{1,0:T(8,128)(2,1)S(1)}, u32[]{:S(2)}, u32[]{:S(2)}) collective-permute-start(bf16[224,128]{1,0:T(8,128)(2,1)S(1)} %constant_dynamic-slice_fusion.2), channel_id=1, source_target_pairs={{0,8},{4,12},{8,0},{12,4},{16,24},{20,28},{24,16},{28,20},{1,9},{5... | collective-permute-start | bytes 172040 | tf_op jit(solution)/shard_map/ppermute | solution.py:323
  81.5 5.4 %collective-permute-start.12 = (bf16[112,128]{1,0:T(8,128)(2,1)S(1)}, bf16[112,128]{1,0:T(8,128)(2,1)S(1)}, u32[]{:S(2)}, u32[]{:S(2)}) collective-permute-start(bf16[112,128]{1,0:T(8,128)(2,1)S(1)} %constant_dynamic-slice_fusion.1), channel_id=1, source_target_pairs={{0,16},{4,20},{8,24},{12,28},{16,0},{20,4},{24,8},{28,12},{1,17},{... | collective-permute-start | bytes 86024 | tf_op jit(solution)/shard_map/ppermute | solution.py:323
  86.9 5.7 %collective-permute-start.13 = (bf16[112,128]{1,0:T(8,128)(2,1)S(1)}, bf16[112,128]{1,0:T(8,128)(2,1)S(1)}, u32[]{:S(2)}, u32[]{:S(2)}) collective-permute-start(bf16[112,128]{1,0:T(8,128)(2,1)S(1)} %add_convert_fusion.9), channel_id=1, source_target_pairs={{0,16},{4,20},{8,24},{12,28},{16,0},{20,4},{24,8},{28,12},{1,17},{... | collective-permute-start | bytes 86024 | tf_op jit(solution)/shard_map/ppermute | solution.py:323
  90.9 8.5 %collective-permute-start.17 = (bf16[1,1792,128]{2,1,0:T(8,128)(2,1)S(1)}, bf16[1,1792,128]{2,1,0:T(8,128)(2,1)S(1)}, u32[]{:S(2)}, u32[]{:S(2)}) collective-permute-start(bf16[1,1792,128]{2,1,0:T(8,128)(2,1)S(1)} %add_convert_fusion.1), channel_id=1, source_target_pairs={{0,2},{1,3},{2,0},{3,1},{4,6},{5,7},{6,4},{7,5},{8,10},{9,11},{10,... | collective-permute-start | bytes 1376264 | tf_op jit(solution)/shard_map/ppermute | solution.py:323
  92.7 4.2 %collective-permute-start.14 = (bf16[224,128]{1,0:T(8,128)(2,1)S(1)}, bf16[224,128]{1,0:T(8,128)(2,1)S(1)}, u32[]{:S(2)}, u32[]{:S(2)}) collective-permute-start(bf16[224,128]{1,0:T(8,128)(2,1)S(1)} %pad_maximum_fusion.5), channel_id=1, source_target_pairs={{0,8},{4,12},{8,0},{12,4},{16,24},{20,28},{24,16},{28,20},{1,9},{5... | collective-permute-start | bytes 172040 | tf_op jit(solution)/shard_map/ppermute | solution.py:323
  97.0 5.0 %collective-permute-start.15 = (bf16[448,128]{1,0:T(8,128)(2,1)S(1)}, bf16[448,128]{1,0:T(8,128)(2,1)S(1)}, u32[]{:S(2)}, u32[]{:S(2)}) collective-permute-start(bf16[448,128]{1,0:T(8,128)(2,1)S(1)} %pad_maximum_fusion.3), channel_id=1, source_target_pairs={{0,4},{4,0},{8,12},{12,8},{16,20},{20,16},{24,28},{28,24},{1,5},{5... | collective-permute-start | bytes 344072 | tf_op jit(solution)/shard_map/ppermute | solution.py:323
  100.7 6.1 %collective-permute-start.18 = (bf16[896,128]{1,0:T(8,128)(2,1)S(1)}, bf16[896,128]{1,0:T(8,128)(2,1)S(1)}, u32[]{:S(2)}, u32[]{:S(2)}) collective-permute-start(bf16[896,128]{1,0:T(8,128)(2,1)S(1)} %dynamic-slice_bitcast_fusion), channel_id=1, source_target_pairs={{0,4},{4,0},{8,12},{12,8},{16,20},{20,16},{24,28},{28,24},{1,5},{5... | collective-permute-start | bytes 688136 | tf_op jit(solution)/shard_map/ppermute | solution.py:323
  106.9 4.9 %collective-permute-start.19 = (bf16[448,128]{1,0:T(8,128)(2,1)S(1)}, bf16[448,128]{1,0:T(8,128)(2,1)S(1)}, u32[]{:S(2)}, u32[]{:S(2)}) collective-permute-start(bf16[448,128]{1,0:T(8,128)(2,1)S(1)} %constant_dynamic-slice_fusion), channel_id=1, source_target_pairs={{0,8},{4,12},{8,0},{12,4},{16,24},{20,28},{24,16},{28,20},{1,9},{5... | collective-permute-start | bytes 344072 | tf_op jit(solution)/shard_map/ppermute | solution.py:323
  111.8 5.2 %collective-permute-start.20 = (bf16[224,128]{1,0:T(8,128)(2,1)S(1)}, bf16[224,128]{1,0:T(8,128)(2,1)S(1)}, u32[]{:S(2)}, u32[]{:S(2)}) collective-permute-start(bf16[224,128]{1,0:T(8,128)(2,1)S(1)} %constant_dynamic-slice_fusion.3), channel_id=1, source_target_pairs={{0,16},{4,20},{8,24},{12,28},{16,0},{20,4},{24,8},{28,12},{1,17},{... | collective-permute-start | bytes 172040 | tf_op jit(solution)/shard_map/ppermute | solution.py:323
  117.1 5.1 %collective-permute-start.21 = (bf16[224,128]{1,0:T(8,128)(2,1)S(1)}, bf16[224,128]{1,0:T(8,128)(2,1)S(1)}, u32[]{:S(2)}, u32[]{:S(2)}) collective-permute-start(bf16[224,128]{1,0:T(8,128)(2,1)S(1)} %add_convert_fusion.7), channel_id=1, source_target_pairs={{0,16},{4,20},{8,24},{12,28},{16,0},{20,4},{24,8},{28,12},{1,17},{... | collective-permute-start | bytes 172040 | tf_op jit(solution)/shard_map/ppermute | solution.py:323
  122.2 4.9 %collective-permute-start.22 = (bf16[448,128]{1,0:T(8,128)(2,1)S(1)}, bf16[448,128]{1,0:T(8,128)(2,1)S(1)}, u32[]{:S(2)}, u32[]{:S(2)}) collective-permute-start(bf16[448,128]{1,0:T(8,128)(2,1)S(1)} %pad_maximum_fusion.4), channel_id=1, source_target_pairs={{0,8},{4,12},{8,0},{12,4},{16,24},{20,28},{24,16},{28,20},{1,9},{5... | collective-permute-start | bytes 344072 | tf_op jit(solution)/shard_map/ppermute | solution.py:323
  127.2 6.1 %collective-permute-start.23 = (bf16[896,128]{1,0:T(8,128)(2,1)S(1)}, bf16[896,128]{1,0:T(8,128)(2,1)S(1)}, u32[]{:S(2)}, u32[]{:S(2)}) collective-permute-start(bf16[896,128]{1,0:T(8,128)(2,1)S(1)} %pad_maximum_fusion.2), channel_id=1, source_target_pairs={{0,4},{4,0},{8,12},{12,8},{16,20},{20,16},{24,28},{28,24},{1,5},{5... | collective-permute-start | bytes 688136 | tf_op jit(solution)/shard_map/ppermute | solution.py:323
where the time goes:
time: 136 us; the launch traced here: 135 us
  waiting for transfers between devices  47.7 us (35%)
  starting transfers between devices  45.6 us (34%)
  Pallas kernels  28.6 us (21%)
  other arithmetic  8.61 us (6%)
  local copies, waits for them, and re-layouts  3.59 us (3%)
    ppermute x16, waiting for transfers between devices, swap(): return lax.ppermute(value, axis, [(i, i ^ 1 << bit) for i in range(n)])  39.9 us
    ppermute x16, starting transfers between devices, swap(): return lax.ppermute(value, axis, [(i, i ^ 1 << bit) for i in range(n)])  32.9 us
    pallas_call x7, Pallas kernels, call(): pl.pallas_call(body, name=name, out_shape=[jax.ShapeDtypeStruct(s, t) for...  28.6 us
    ppermute x8, starting transfers between devices, swap_faces(): return (lax.ppermute(first, axis, one), lax.ppermute(second, axis, two))  12.7 us
    ppermute x8, waiting for transfers between devices, swap_faces(): return (lax.ppermute(first, axis, one), lax.ppermute(second, axis, two))  7.76 us
    convert_element_type x10, other arithmetic, add(): return (a.astype(F32) + b.astype(F32)).astype(BF16)  4.64 us
  transfers between devices with their start and end apart: 24, of which 17 were waited for; matrix products, arithmetic and copies ran while one was open for 4% of the time, Pallas kernels for 1%

commit v1 on v0

--- a/solution.py
+++ b/solution.py
@@ -12,19 +12,29 @@
 VMEM_LIMIT = 48 * 1024 * 1024
 
 
-def call(body, name, args, outs, scratch=(), flops=0, nbytes=0):
+def call(body, name, args, outs, scratch=(), micros=1):
     specs = [pl.BlockSpec(memory_space=pltpu.SMEM)]
-    specs += [pl.BlockSpec(memory_space=pltpu.VMEM) for _ in args[1:]]
+    arrays = [args[0]]
+    for arg in args[1:]:
+        if isinstance(arg, tuple):
+            arrays.append(arg[0])
+            specs.append(pl.BlockSpec(arg[1], functools.partial(lambda at, _: at, arg[2])))
+        else:
+            arrays.append(arg)
+            specs.append(pl.BlockSpec(memory_space=pltpu.VMEM))
     return pl.pallas_call(
         body,
         name=name,
         out_shape=[jax.ShapeDtypeStruct(s, t) for s, t in outs],
+        grid=(1,) if any(isinstance(arg, tuple) for arg in args) else (),
         in_specs=specs,
         out_specs=[pl.BlockSpec(memory_space=pltpu.VMEM) for _ in outs],
         scratch_shapes=list(scratch),
         compiler_params=pltpu.CompilerParams(vmem_limit_bytes=VMEM_LIMIT),
-        cost_estimate=pl.CostEstimate(flops=flops, bytes_accessed=nbytes, transcendentals=0),
-    )(*args)
+        cost_estimate=pl.CostEstimate(
+            flops=int(micros * 1e9), bytes_accessed=0, transcendentals=0
+        ),
+    )(*arrays)
 
 
 def put_faces(odd, first, second, low, high):
@@ -247,7 +257,7 @@
     spread(par[2], keep, send, n, 28, piece)
 
 
-def back_body(n, par, slope, w, cot, ds, fpad, cbias, keep, send, up, st, rhs, acc, wt):
+def slope_body(par, slope, w, cot, ds, st, up):
     bx, by, bz, c = cot.shape
     cx, cy, cz = bx // 2, by // 2, bz // 2
     c2 = slope.shape[3]
@@ -278,7 +288,12 @@
         st[pl.ds(0, c), pl.ds(x * rows, rows)] = shift_rows(wide, -1, bz).astype(BF16).T
         st[pl.ds(c, c), pl.ds(x * rows, rows)] = fs.T
         st[pl.ds(2 * c, c), pl.ds(x * rows, rows)] = shift_rows(wide, 1, bz).astype(BF16).T
-    voxels = bx * rows
+
+
+def grad_body(n, par, st, fpad, cbias, keep, send, rhs, acc):
+    bx, by, bz, c = fpad.shape[0] - 2, fpad.shape[1] - 2, fpad.shape[2], fpad.shape[3]
+    voxels = bx * by * bz
+    c2 = cbias.shape[0]
     for t in range(0, 10, 2):
         for h in (0, 1):
             i, j = (t + h) // 3, (t + h) % 3
@@ -318,11 +333,6 @@
         out[x] = total.astype(BF16).reshape(by, bz, c)
 
 
-def swap(value, axis, bit):
-    n = lax.axis_size(axis)
-    return lax.ppermute(value, axis, [(i, i ^ (1 << bit)) for i in range(n)])
-
-
 def swap_faces(first, second, axis):
     n = lax.axis_size(axis)
     one = [p for i in range(0, n - 1, 2) for p in ((i, i + 1), (i + 1, i))]
@@ -330,37 +340,132 @@
     return lax.ppermute(first, axis, one), lax.ppermute(second, axis, two)
 
 
-def add(a, b):
-    return (a.astype(F32) + b.astype(F32)).astype(BF16)
-
-
-def half_of(value, which):
-    size = value.shape[0] // 2
-    return lax.dynamic_slice_in_dim(value, which * size, size, 0)
-
-
-def reduce_all(keep, send, sub, grp):
-    got = swap(send, "sub", 0)
-    for bit in range(1, lax.axis_size("sub").bit_length() - 1):
-        mine = (sub >> bit) & 1
-        send = add(half_of(keep, 1 - mine), half_of(got, 1 - mine))
-        keep = add(half_of(keep, mine), half_of(got, mine))
-        got = swap(send, "sub", bit)
-    total = add(keep, got)[0]
-    order = []
-    for bit in range(lax.axis_size("grp").bit_length() - 1):
-        mine = (grp >> bit) & 1
-        if total.shape[0] % 32:
-            total = add(total, swap(total, "grp", bit))
+def split4_body(par, keep, got, own, over_sub, over_grp, over_both):
+    g, s = par[0], par[1]
+
+    def part(a, b):
+        return (keep[a, :, b].astype(F32) + got[a, :, b].astype(F32)).astype(BF16)
+
+    over_both[...] = part(1 - s, 1 - g)
+    over_sub[...] = part(1 - s, g)
+    over_grp[...] = part(s, 1 - g)
+    own[...] = part(s, g)
+
+
+def split_body(count, par, *refs):
+    parts, keep, send = refs[:count], refs[count], refs[count + 1]
+
+    def part(at):
+        return sum(p[at].astype(F32) for p in parts).astype(BF16)
+
+    send[...] = part(1 - par[0])
+    keep[...] = part(par[0])
+
+
+def sum_body(count, par, *refs):
+    refs[count][...] = sum(p[...].astype(F32) for p in refs[:count]).astype(BF16)
+
+
+def partners(value, grp_mask, sub_mask):
+    n_grp, n_sub = lax.axis_size("grp"), lax.axis_size("sub")
+    pairs = [
+        (g * n_sub + s, (g ^ grp_mask) * n_sub + (s ^ sub_mask))
+        for g in range(n_grp)
+        for s in range(n_sub)
+    ]
+    return lax.ppermute(value, ("grp", "sub"), pairs)
+
+
+def split_sum(parts, bit, name):
+    rows, c = parts[0].shape
+    half = ((rows // 2, c), BF16)
+    shaped = [p.reshape(2, rows // 2, c) for p in parts]
+    return call(
+        functools.partial(split_body, len(parts)), name, (bit.reshape(1), *shaped), [half, half], (), 0.8
+    )
+
+
+def cores(send):
+    return partners(send, 0, 1)
+
+
+def spread_sum(keep, got, bits, name):
+    half, rows, c = keep.shape
+    rest = half // 2
+    shape = (2, rest, 2, rows // 2, c)
+    out = ((rest, rows // 2, c), BF16)
+    own, over_sub, over_grp, over_both = call(
+        split4_body, name, (bits, keep.reshape(shape), got.reshape(shape)), [out] * 4, (), 1
+    )
+    return own, over_sub, over_grp, over_both
+
+
+def cross(own, over_sub, over_grp, over_both):
+    return [own, partners(over_both, 1, 2), partners(over_sub, 0, 2), partners(over_grp, 1, 0)]
+
+
+def finish_sum(parts, sub, grp, name):
+    rest, rows, c = parts[0].shape
+    parts = [p.reshape(rest * rows, c) for p in parts]
+    for bit in range(2, lax.axis_size("sub").bit_length() - 1):
+        keep, send = split_sum(parts, (sub >> bit) & 1, name + f"_sub{bit}")
+        parts = [keep, partners(send, 0, 1 << bit)]
+    bits = [0]
+    last = lax.axis_size("grp").bit_length() - 2
+    for bit in range(1, last + 1):
+        mask = 1 << bit
+        if bit == 1 and bit < last and parts[0].shape[0] % 32 == 0:
+            keep, send = split_sum(parts, (grp >> bit) & 1, name + "_half")
+            parts = [keep, partners(send, mask, 0)]
+            bits.append(bit)
             continue
-        got = swap(half_of(total, 1 - mine), "grp", bit)
-        total = add(half_of(total, mine), got)
-        order.append((bit, mine))
-    for bit, mine in reversed(order):
-        got = swap(total, "grp", bit)
-        first, second = jnp.where(mine == 0, total, got), jnp.where(mine == 0, got, total)
-        total = jnp.concatenate([first, second], axis=0)
-    return total
+        out = [(parts[0].shape, BF16)]
+        (total,) = call(
+            functools.partial(sum_body, len(parts)), name + f"_sum{bit}", (sub.reshape(1), *parts), out, (), 0.5
+        )
+        parts = [total, partners(total, mask, 0)]
+    (total,) = call(
+        functools.partial(sum_body, len(parts)), name + "_total", (sub.reshape(1), *parts), [(parts[0].shape, BF16)], (), 0.5
+    )
+    pieces = [total]
+    for which in range(1, 2 ** len(bits)):
+        pieces.append(partners(total, sum(1 << bits[b] for b in range(len(bits)) if which >> b & 1), 0))
+    return pieces, bits
+
+
+def last_body(count, per, par, *refs):
+    pieces, rest, rows = refs[:count], refs[count:-1], refs[-1]
+    size = pieces[0].shape[0]
+    mine = par[0] if count == 2 else 2 * par[0] + par[1]
+    for which in range(count):
+        mask = which if count == 2 else 2 * (which & 1) + (which >> 1)
+        rows[mine ^ mask] = pieces[which][...]
+    kernel, extra = rest[0], rest[1]
+
+    def block(t):
+        at, off = t * per // size, t * per % size
+        if off + per <= size:
+            return rows[at, pl.ds(off, per)]
+        first = size - off
+        return jnp.concatenate([rows[at, pl.ds(off, first)], rows[at + 1, pl.ds(0, per - first)]], axis=0)
+
+    for t in range(27):
+        kernel[(t // 3) % 3, t % 3, t // 9] = block(t).astype(F32).T
+    extra[...] = block(27).astype(F32)
+
+
+def last(pieces, bits, grp, per, name):
+    count = len(pieces)
+    size, c = pieces[0].shape
+    order = jnp.stack([(grp >> b) & 1 for b in (bits + bits)[:2]]).astype(jnp.int32)
+    return call(
+        functools.partial(last_body, count, per),
+        name,
+        (order, *pieces),
+        [((3, 3, 3, c, per), F32), ((per, c), F32)],
+        [pltpu.VMEM((count, size, c), BF16)],
+        2,
+    )
 
 
 def per_device(field, cotangent, fine_kernel, fine_bias, coarse_kernel, coarse_bias, merge_weight):
@@ -369,12 +474,17 @@
     bx, by, bz, c = field.shape
     cx, cy, cz = bx // 2, by // 2, bz // 2
     c2 = merge_weight.shape[0]
-    par = jnp.stack([grp % 2, sub % 2, sub % 2]).astype(jnp.int32)
+    par = jnp.stack([grp & 1, sub & 1, sub & 1]).astype(jnp.int32)
+    cross_bits = jnp.stack([grp & 1, (sub >> 1) & 1]).astype(jnp.int32)
     face = by * bz + cy * cz
+    xlo = (field, (1, by, bz, c), (0, 0, 0, 0))
+    xhi = (field, (1, by, bz, c), (bx - 1, 0, 0, 0))
+    ylo = (field, (bx, 1, bz, c), (0, 0, 0, 0))
+    yhi = (field, (bx, 1, bz, c), (0, by - 1, 0, 0))
     pg, sa, sb = call(
         prep_body,
         "prep",
-        (par, field[:1], field[bx - 1 :], cotangent),
+        (par, xlo, xhi, cotangent),
         [((cx, cy, cz, c), BF16), ((face, c), BF16), ((face, c), BF16)],
         [pltpu.VMEM((cx * cy * bz, c), F32)],
     )
@@ -383,7 +493,7 @@
     ta, tb = call(
         turn_body,
         "turn",
-        (par, field[:, :1], field[:, by - 1 :], pg, xa, xb),
+        (par, ylo, yhi, pg, xa, xb),
         [((edge, c), BF16), ((edge, c), BF16)],
     )
     ya, yb = swap_faces(ta, tb, "sub")
@@ -401,6 +511,7 @@
             ((side, c), BF16),
         ],
         [pltpu.VMEM((9 * c, 3 * c), BF16), pltpu.VMEM((cy * bz, c), F32)],
+        8,
     )
     pxa, pxb = swap_faces(pa, pb, "grp")
     side = (cx + 4) * 2 * cz
@@ -433,46 +544,52 @@
             pltpu.VMEM((3 * c2, 10 * c), BF16),
             pltpu.VMEM((c2, c), BF16),
         ],
-    )
-    coarse_sum = reduce_all(ckeep, csend, sub, grp)
+        6,
+    )
+    cgot = cores(csend)
+    voxels = bx * by * bz
+    (st,) = call(
+        slope_body,
+        "slope",
+        (par, slope, coarse_kernel, cotangent, ds),
+        [((3 * c, voxels), BF16)],
+        [pltpu.VMEM((cx * cy * bz, c), F32)],
+        4,
+    )
+    st, cgot = lax.optimization_barrier((st, cgot))
+    csent = spread_sum(ckeep, cgot, cross_bits, "coarse_split")
+    st, csent = lax.optimization_barrier((st, csent))
+    cparts = cross(*csent)
     part = (n // 2, 28 * (c // n), c)
     fkeep, fsend = call(
-        functools.partial(back_body, n),
-        "back",
-        (par, slope, coarse_kernel, cotangent, ds, fpad, cbias),
+        functools.partial(grad_body, n),
+        "grad",
+        (par, st, fpad, cbias),
         [(part, BF16), (part, BF16)],
-        [
-            pltpu.VMEM((cx * cy * bz, c), F32),
-            pltpu.VMEM((3 * c, bx * by * bz), BF16),
-            pltpu.VMEM((bx * by * bz, 2 * c), BF16),
-            pltpu.VMEM((3 * c, 10 * c), BF16),
-            pltpu.VMEM((16, 128), BF16),
-        ],
-    )
-    fine_sum = reduce_all(fkeep, fsend, sub, grp)
+        [pltpu.VMEM((voxels, 2 * c), BF16), pltpu.VMEM((3 * c, 10 * c), BF16)],
+        6,
+    )
+    fgot = cores(fsend)
+    fparts = cross(*spread_sum(fkeep, fgot, cross_bits, "fine_split"))
+    coarse_sum = finish_sum(cparts, sub, grp, "coarse")
+    fine_sum = finish_sum(fparts, sub, grp, "fine")
     (output,) = call(
         merge_body,
         "merge",
         (par, hidden, coarse, merge_weight),
         [((bx, by, bz, c), BF16)],
         [pltpu.VMEM((cx * cy * bz, c), F32)],
-    )
-    per, cper = c // n, c2 // n
-    fine_sum = fine_sum.reshape(28, per, c)
-    coarse_sum = coarse_sum.reshape(28, cper, c)
-
-    def kernel_of(total, size):
-        shaped = total[:27].reshape(3, 3, 3, size, c)
-        return jnp.transpose(shaped, (1, 2, 0, 4, 3)).astype(F32)
-
-    grad_coarse_bias = jnp.concatenate([fine_sum[27, :, 1], fine_sum[27, :, 2]]).astype(F32)
+        2,
+    )
+    grad_coarse, grad_merge = last(*coarse_sum, grp, c2 // n, "coarse_last")
+    grad_fine, extra = last(*fine_sum, grp, c // n, "fine_last")
     return (
         output,
-        kernel_of(fine_sum, per),
-        fine_sum[27, :, 0].astype(F32),
-        kernel_of(coarse_sum, cper),
-        grad_coarse_bias,
-        coarse_sum[27].astype(F32),
+        grad_fine,
+        extra[:, 0],
+        grad_coarse,
+        jnp.concatenate([extra[:, 1], extra[:, 2]]),
+        grad_merge,
     )
 
 

time: 136 us -> 117 us (0.86)
  waiting for transfers between devices: 47.7 us -> 27.2 us
  local copies, waits for them, and re-layouts: 3.59 us -> 11.9 us
  other arithmetic: 8.61 us -> 0.81 us
  Pallas kernels: 28.6 us -> 34.4 us
  starting transfers between devices: 45.6 us -> 41.7 us
    ppermute x16 -> x18, waiting for transfers between devices: 39.9 us -> 18.4 us  [partners(): return lax.ppermute(value, ('grp', 'sub'), pairs)]
    unnamed x21 -> x38, local copies, waits for them, and re-layouts: 1.53 us -> 11.2 us
    convert_element_type x15 -> x0, other arithmetic: 8.18 us -> none  [the longest x10 4.64 us: add(): return (a.astype(F32) + b.astype(F32)).astype(BF16)]
    pallas_call x7 -> x18, Pallas kernels: 28.6 us -> 34.4 us  [call(): pl.pallas_call(body, name=name, out_shape=[jax.ShapeDtypeStruct(s, t) for...]
    ppermute x16 -> x18, starting transfers between devices: 32.9 us -> 29.1 us  [partners(): return lax.ppermute(value, ('grp', 'sub'), pairs)]
  transfers between devices with their start and end apart: 24 -> 26, of which waited for: 17 -> 11; matrix products, arithmetic and copies ran while one was open for 4% -> 1% of each run, Pallas kernels for 1% -> 7%
where the time goes in v1:
time: 117 us
  starting transfers between devices  41.7 us (36%)
  Pallas kernels  34.4 us (29%)
  waiting for transfers between devices  27.2 us (23%)
  local copies, waits for them, and re-layouts  11.9 us (10%)
    pallas_call x18, Pallas kernels, call(): pl.pallas_call(body, name=name, out_shape=[jax.ShapeDtypeStruct(s, t) for...  34.4 us
    ppermute x18, starting transfers between devices, partners(): return lax.ppermute(value, ('grp', 'sub'), pairs)  29.1 us
    ppermute x18, waiting for transfers between devices, partners(): return lax.ppermute(value, ('grp', 'sub'), pairs)  18.4 us
    ppermute x8, starting transfers between devices, swap_faces(): return (lax.ppermute(first, axis, one), lax.ppermute(second, axis, two))  12.6 us
    unnamed x38, local copies, waits for them, and re-layouts  11.2 us
    ppermute x8, waiting for transfers between devices, swap_faces(): return (lax.ppermute(first, axis, one), lax.ppermute(second, axis, two))  8.79 us
  transfers between devices with their start and end apart: 26, of which 11 were waited for; matrix products, arithmetic and copies ran while one was open for 1% of the time, Pallas kernels for 7%

profile of v1, /device:TPU:0, one launch (start us, length us, event | category | flops | bytes accessed | tf_op | source)
XLA Modules:
  0.0 116.9 jit_solution(6579376450726601944)
XLA Ops:
  0.6 0.1 pad_add_fusion.par
  0.7 1.2 %copy-done.1 = bf16[8,16,32,128]{3,2,1,0:T(8,128)(2,1)S(1)} copy-done((bf16[8,16,32,128]{3,2,1,0:T(8,128)(2,1)S(1)}, bf16[8,16,32,128]{3,2,1,0:T(8,128)(2,1)}, u32[]{:S(2)}) %copy-start.1) | copy-done | bytes 1048600
  1.9 1.2 %copy-done.2 = bf16[8,16,32,128]{3,2,1,0:T(8,128)(2,1)S(1)} copy-done((bf16[8,16,32,128]{3,2,1,0:T(8,128)(2,1)S(1)}, bf16[8,16,32,128]{3,2,1,0:T(8,128)(2,1)}, u32[]{:S(2)}) %copy-start.2) | copy-done | bytes 1048600
  3.2 0.8 prep.1
  4.0 3.0 %collective-permute-start = (bf16[640,128]{1,0:T(8,128)(2,1)S(1)}, bf16[640,128]{1,0:T(8,128)(2,1)S(1)}, u32[]{:S(2)}, u32[]{:S(2)}) collective-permute-start(bf16[640,128]{1,0:T(8,128)(2,1)S(1)} %get-tuple-element.49), channel_id=1, source_target_pairs={{0,4},{4,0},{8,12},{12,8},{16,20},{20,16},{24,28},{28,24},{1,5},{5... | collective-permute-start | bytes 491528 | tf_op jit(solution)/shard_map/ppermute | solution.py:340
  7.0 0.7 collective-permute-start.1
  7.7 6.3 %collective-permute-done.ra.fa = bf16[640,128]{1,0:T(8,128)(2,1)S(1)} collective-permute-done((bf16[640,128]{1,0:T(8,128)(2,1)S(1)}, bf16[640,128]{1,0:T(8,128)(2,1)S(1)}, u32[]{:S(2)}, u32[]{:S(2)}) %collective-permute-start) | collective-permute-done | bytes 163872 | tf_op jit(solution)/shard_map/ppermute | solution.py:340
  14.0 0.6 turn.1
  14.6 0.1 collective-permute-start.2
  14.7 0.7 collective-permute-start.3
  15.3 0.6 collective-permute-done.2.ua.ga
  16.0 8.7 %fine.1 = (bf16[10,18,32,128]{3,2,1,0:T(8,128)(2,1)S(1)}, bf16[8,16,32,128]{3,2,1,0:T(8,128)(2,1)S(1)}, f32[8,16,32,128]{3,2,1,0:T(8,128)}, bf16[4,8,16,128]{3,2...) custom-call(s32[3]{0:T(128)S(1)} %pad_add_fusion.par, ...), custom_call_target="tpu_custom_call" | custom-call | flops 8000000000 | tf_op jit(solution)/shard_map/fine/pallas_call | solution.py:25
  24.7 1.1 copy-done.16
  25.8 2.4 %collective-permute-start.4 = (bf16[256,128]{1,0:T(8,128)(2,1)S(1)}, bf16[256,128]{1,0:T(8,128)(2,1)S(1)}, u32[]{:S(2)}, u32[]{:S(2)}) collective-permute-start(bf16[256,128]{1,0:T(8,128)(2,1)S(1)} %get-tuple-element.56), channel_id=1, source_target_pairs={{0,4},{4,0},{8,12},{12,8},{16,20},{20,16},{24,28},{28,24},{1,5},{5... | collective-permute-start | bytes 196616 | tf_op jit(solution)/shard_map/ppermute | solution.py:340
  28.2 0.7 collective-permute-start.5
  28.9 1.6 %collective-permute-done.4.ra = bf16[256,128]{1,0:T(8,128)(2,1)S(1)} collective-permute-done((bf16[256,128]{1,0:T(8,128)(2,1)S(1)}, bf16[256,128]{1,0:T(8,128)(2,1)S(1)}, u32[]{:S(2)}, u32[]{:S(2)}) %collective-permute-start.4) | collective-permute-done | bytes 65568 | tf_op jit(solution)/shard_map/ppermute | solution.py:340
  30.5 0.6 turn2.1
  31.1 4.4 %collective-permute-start.6 = (bf16[256,128]{1,0:T(8,128)(2,1)S(1)}, bf16[256,128]{1,0:T(8,128)(2,1)S(1)}, u32[]{:S(2)}, u32[]{:S(2)}) collective-permute-start(bf16[256,128]{1,0:T(8,128)(2,1)S(1)} %get-tuple-element.58), channel_id=1, source_target_pairs={{0,1},{1,0},{2,3},{3,2},{4,5},{5,4},{6,7},{7,6},{8,9},{9,8},{10,11... | collective-permute-start | bytes 196616 | tf_op jit(solution)/shard_map/ppermute | solution.py:340
  35.5 0.7 collective-permute-start.7
  36.1 0.2 collective-permute-done.6.ua
  36.4 6.9 %coarse.1 = (bf16[6,10,16,256]{3,2,1,0:T(8,128)(2,1)S(1)}, bf16[4,8,16,256]{3,2,1,0:T(8,128)(2,1)S(1)}, bf16[2,1792,128]{2,1,0:T(8,128)(2,1)S(1)}, bf16[2,1792,128]{2,1,0:T(8,128)(2,1)}, bf16[256,128]{1,0:T(8,128)(2,1)S(1)}) custom-call(s32[3]{0:T(128)S(1)} %pad_add_fusion.par, bf16[4,8,16,128]{3,2,1,0:T(8,128)(2,1)S(1)} %get-tuple-element.55.pooled, ...), custom_call_target="tpu_custom_call" | custom-call | flops 6000000000 | tf_op jit(solution)/shard_map/coarse/pallas_call | solution.py:25
  43.3 0.9 copy-done.8
  44.2 0.8 copy-done.14
  45.0 5.0 %collective-permute-start.8 = (bf16[2,1792,128]{2,1,0:T(8,128)(2,1)}, bf16[2,1792,128]{2,1,0:T(8,128)(2,1)}, u32[]{:S(2)}, u32[]{:S(2)}) collective-permute-start(bf16[2,1792,128]{2,1,0:T(8,128)(2,1)} %get-tuple-element.63), channel_id=1, source_target_pairs={{0,1},{1,0},{2,3},{3,2},{4,5},{5,4},{6,7},{7,6},{8,9},{9,8},{10,11... | collective-permute-start | bytes 2752520 | tf_op jit(solution)/shard_map/ppermute | solution.py:376
  50.0 0.1 pad_add_fusion.2.par
  50.1 1.6 %copy-done.11 = f32[8,16,32,128]{3,2,1,0:T(8,128)S(1)} copy-done((f32[8,16,32,128]{3,2,1,0:T(8,128)S(1)}, f32[8,16,32,128]{3,2,1,0:T(8,128)}, u32[]{:S(2)}) %copy-start.11) | copy-done | bytes 2097176
  51.7 1.0 copy-done.15
  52.7 4.4 %slope.1.st = bf16[384,4096]{1,0:T(8,128)(2,1)} custom-call(s32[3]{0:T(128)S(1)} %pad_add_fusion.par, bf16[6,10,16,256]{3,2,1,0:T(8,128)(2,1)S(1)} %copy-done.15, bf16[3,3,3,128,256]{4,3,2,1,0:T(8,128)(2,1)S(1)} %copy-done, bf16[8,16,32,128]{3,2,1,0:T(8,128)(2,1)S(1)} %copy-done.3, f32[8,16,32,128]{3,2,1,0:T(8,128)S(1)} %copy-done.11), custom_call_target="tpu_custom_call" | custom-call | flops 4000000000 | tf_op jit(solution)/shard_map/slope/pallas_call | solution.py:25
  57.1 1.6 %coarse_split.1 = (bf16[1,896,128]{2,1,0:T(8,128)(2,1)S(1)}, bf16[1,896,128]{2,1,0:T(8,128)(2,1)S(1)}, bf16[1,896,128]{2,1,0:T(8,128)(2,1)S(1)}, bf16[1,896,128]{2,1,0:T(8,128)(2,1)S(1)}) custom-call(s32[2]{0:T(128)S(1)} %pad_add_fusion.2.par, bf16[2,1,2,896,128]{4,3,2,1,0:T(8,128)(2,1)S(1)} %bitcast.29, bf16[2,1,2,896,128]{4,3,2,1,0:T(8,128)(2,1)} %bitcast.9.got), custom_call_target="tpu_custom_call" | custom-call | flops 1000000000 | tf_op jit(solution)/shard_map/coarse_split/pallas_call | solution.py:25
  58.7 0.6 copy-done.10
  59.3 5.9 %grad.1 = (bf16[2,896,128]{2,1,0:T(8,128)(2,1)S(1)}, bf16[2,896,128]{2,1,0:T(8,128)(2,1)S(1)}) custom-call(s32[3]{0:T(128)S(1)} %pad_add_fusion.par, bf16[384,4096]{1,0:T(8,128)(2,1)S(1)} %copy-done.10, bf16[10,18,32,128]{3,2,1,0:T(8,128)(2,1)S(1)} %copy-done.17, bf16[256,128]{1,0:T(8,128)(2,1)S(1)} %get-tuple-element.73.cbias), custom_call_target="tpu_custom_call" | custom-call | flops 6000000000 | tf_op jit(solution)/shard_map/grad/pallas_call | solution.py:25
  65.2 0.1 collective-permute-start.9
  65.2 6.5 %collective-permute-start.18 = (bf16[1,896,128]{2,1,0:T(8,128)(2,1)S(1)}, bf16[1,896,128]{2,1,0:T(8,128)(2,1)S(1)}, u32[]{:S(2)}, u32[]{:S(2)}) collective-permute-start(bf16[1,896,128]{2,1,0:T(8,128)(2,1)S(1)} %get-tuple-element.85), channel_id=1, source_target_pairs={{0,6},{1,7},{2,4},{3,5},{4,2},{5,3},{6,0},{7,1},{8,14},{9,15},{10,... | collective-permute-start | bytes 688136 | tf_op jit(solution)/shard_map/ppermute | solution.py:376
  71.7 0.6 collective-permute-start.20
  72.3 5.9 %collective-permute-done.18 = bf16[1,896,128]{2,1,0:T(8,128)(2,1)S(1)} collective-permute-done((bf16[1,896,128]{2,1,0:T(8,128)(2,1)S(1)}, bf16[1,896,128]{2,1,0:T(8,128)(2,1)S(1)}, u32[]{:S(2)}, u32[]{:S(2)}) %collective-permute-start.18) | collective-permute-done | bytes 229408 | tf_op jit(solution)/shard_map/ppermute | solution.py:376
  78.1 4.3 %collective-permute-done.19 = bf16[1,896,128]{2,1,0:T(8,128)(2,1)S(1)} collective-permute-done((bf16[1,896,128]{2,1,0:T(8,128)(2,1)S(1)}, bf16[1,896,128]{2,1,0:T(8,128)(2,1)S(1)}, u32[]{:S(2)}, u32[]{:S(2)}) %collective-permute-start.19) | collective-permute-done | bytes 229408 | tf_op jit(solution)/shard_map/ppermute | solution.py:376
  82.5 0.1 coarse_half.1
  82.6 3.3 %collective-permute-start.21 = (bf16[448,128]{1,0:T(8,128)(2,1)S(1)}, bf16[448,128]{1,0:T(8,128)(2,1)S(1)}, u32[]{:S(2)}, u32[]{:S(2)}) collective-permute-start(bf16[448,128]{1,0:T(8,128)(2,1)S(1)} %get-tuple-element.89), channel_id=1, source_target_pairs={{0,8},{1,9},{2,10},{3,11},{4,12},{5,13},{6,14},{7,15},{8,0},{9,1},... | collective-permute-start | bytes 344072 | tf_op jit(solution)/shard_map/ppermute | solution.py:376
  85.9 0.7 fine_split.1
  86.5 1.6 %collective-permute-start.10 = (bf16[1,448,128]{2,1,0:T(8,128)(2,1)S(1)}, bf16[1,448,128]{2,1,0:T(8,128)(2,1)S(1)}, u32[]{:S(2)}, u32[]{:S(2)}) collective-permute-start(bf16[1,448,128]{2,1,0:T(8,128)(2,1)S(1)} %get-tuple-element.77), channel_id=1, source_target_pairs={{0,6},{1,7},{2,4},{3,5},{4,2},{5,3},{6,0},{7,1},{8,14},{9,15},{10,... | collective-permute-start | bytes 344072 | tf_op jit(solution)/shard_map/ppermute | solution.py:376
  88.1 1.0 collective-permute-start.11
  89.1 1.0 collective-permute-start.12
  90.1 1.7 %collective-permute-start.22 = (bf16[448,128]{1,0:T(8,128)(2,1)S(1)}, bf16[448,128]{1,0:T(8,128)(2,1)S(1)}, u32[]{:S(2)}, u32[]{:S(2)}) collective-permute-start(bf16[448,128]{1,0:T(8,128)(2,1)S(1)} %coarse_sum2.1.refs_0_), channel_id=1, source_target_pairs={{0,16},{1,17},{2,18},{3,19},{4,20},{5,21},{6,22},{7,23},{8,24},{9,... | collective-permute-start | bytes 344072 | tf_op jit(solution)/shard_map/ppermute | solution.py:376
  91.8 1.7 %collective-permute-done.10 = bf16[1,448,128]{2,1,0:T(8,128)(2,1)S(1)} collective-permute-done((bf16[1,448,128]{2,1,0:T(8,128)(2,1)S(1)}, bf16[1,448,128]{2,1,0:T(8,128)(2,1)S(1)}, u32[]{:S(2)}, u32[]{:S(2)}) %collective-permute-start.10) | collective-permute-done | bytes 114720 | tf_op jit(solution)/shard_map/ppermute | solution.py:376
  93.5 1.0 collective-permute-done.11
  94.6 0.4 collective-permute-start.13
  94.9 0.1 pad_add_fusion.1.par
  95.0 2.3 %collective-permute-done.22.refs_1_ = bf16[448,128]{1,0:T(8,128)(2,1)S(1)} collective-permute-done((bf16[448,128]{1,0:T(8,128)(2,1)S(1)}, bf16[448,128]{1,0:T(8,128)(2,1)S(1)}, u32[]{:S(2)}, u32[]{:S(2)}) %collective-permute-start.22) | collective-permute-done | bytes 114720 | tf_op jit(solution)/shard_map/ppermute | solution.py:376
  97.3 0.1 collective-permute-start.25
  97.4 2.4 %collective-permute-start.24 = (bf16[448,128]{1,0:T(8,128)(2,1)S(1)}, bf16[448,128]{1,0:T(8,128)(2,1)S(1)}, u32[]{:S(2)}, u32[]{:S(2)}) collective-permute-start(bf16[448,128]{1,0:T(8,128)(2,1)S(1)} %coarse_total.1.refs_0_), channel_id=1, source_target_pairs={{0,8},{1,9},{2,10},{3,11},{4,12},{5,13},{6,14},{7,15},{8,0},{9,1},... | collective-permute-start | bytes 344072 | tf_op jit(solution)/shard_map/ppermute | solution.py:376
  99.8 1.0 collective-permute-start.23
  100.9 1.1 collective-permute-start.14
  102.0 1.8 %merge.1 = bf16[8,16,32,128]{3,2,1,0:T(8,128)(2,1)} custom-call(s32[3]{0:T(128)S(1)} %pad_add_fusion.par, bf16[8,16,32,128]{3,2,1,0:T(8,128)(2,1)S(1)} %copy-done.13, bf16[4,8,16,256]{3,2,1,0:T(8,128)(2,1)S(1)} %get-tuple-element.60.coarse, bf16[256,128]{1,0:T(8,128)(2,1)S(1)} %copy-done.5), custom_call_target="tpu_custom_call" | custom-call | flops 2000000000 | tf_op jit(solution)/shard_map/merge/pallas_call | solution.py:25
  103.8 3.0 %collective-permute-done.14.refs_1_ = bf16[224,128]{1,0:T(8,128)(2,1)S(1)} collective-permute-done((bf16[224,128]{1,0:T(8,128)(2,1)S(1)}, bf16[224,128]{1,0:T(8,128)(2,1)S(1)}, u32[]{:S(2)}, u32[]{:S(2)}) %collective-permute-start.14) | collective-permute-done | bytes 57376 | tf_op jit(solution)/shard_map/ppermute | solution.py:376
  106.8 0.7 collective-permute-start.17
  107.5 1.8 %collective-permute-start.16 = (bf16[224,128]{1,0:T(8,128)(2,1)S(1)}, bf16[224,128]{1,0:T(8,128)(2,1)S(1)}, u32[]{:S(2)}, u32[]{:S(2)}) collective-permute-start(bf16[224,128]{1,0:T(8,128)(2,1)S(1)} %fine_total.1.refs_0_), channel_id=1, source_target_pairs={{0,8},{1,9},{2,10},{3,11},{4,12},{5,13},{6,14},{7,15},{8,0},{9,1},... | collective-permute-start | bytes 172040 | tf_op jit(solution)/shard_map/ppermute | solution.py:376
  109.3 1.0 collective-permute-start.15
  110.4 1.4 %coarse_last.1 = (f32[3,3,3,128,64]{4,3,2,1,0:T(8,128)S(1)}, f32[64,128]{1,0:T(8,128)}) custom-call(s32[2]{0:T(128)S(1)} %pad_add_fusion.1.par, bf16[448,128]{1,0:T(8,128)(2,1)S(1)} %coarse_total.1.refs_0_, bf16[448,128]{1,0:T(8,128)(2,1)S(1)} %collective-permute-done.23.refs_1_, bf16[448,128]{1,0:T(8,128)(2,1)S(1)} %collective-permute-done.24.refs_2_, ...), custom_call_target="tpu_custom_call" | custom-call | flops 2000000000 | tf_op jit(solution)/shard_map/coarse_last/pallas_call | solution.py:25
  111.8 1.4 %copy.16 = f32[3,3,3,128,64]{3,4,2,1,0:T(8,128)} copy(f32[3,3,3,128,64]{4,3,2,1,0:T(8,128)S(1)} %get-tuple-element.101) | data formatting | bytes 1769472
  113.2 0.3 collective-permute-done.15.refs_1_
  113.5 0.9 fine_last.1
  114.4 1.3 %copy.15 = f32[3,3,3,128,32]{3,4,2,1,0:T(8,128)} copy(f32[3,3,3,128,32]{4,3,2,1,0:T(8,128)S(1)} %get-tuple-element.99) | data formatting | bytes 884736
  115.6 0.6 slice_reduce_fusion.1
  116.3 0.6 pad_maximum_fusion
  (49 shorter events, 0.2 us)
Async XLA Ops:
  0.7 1.2 %copy-start.1 = (bf16[8,16,32,128]{3,2,1,0:T(8,128)(2,1)S(1)}, bf16[8,16,32,128]{3,2,1,0:T(8,128)(2,1)}, u32[]{:S(2)}) copy-start(bf16[8,16,32,128]{3,2,1,0:T(8,128)(2,1)} %field.1) | copy-start | bytes 3145732
  1.9 1.2 %copy-start.2 = (bf16[8,16,32,128]{3,2,1,0:T(8,128)(2,1)S(1)}, bf16[8,16,32,128]{3,2,1,0:T(8,128)(2,1)}, u32[]{:S(2)}) copy-start(bf16[8,16,32,128]{3,2,1,0:T(8,128)(2,1)} %cot.3) | copy-start | bytes 3145732
  4.0 10.0 %collective-permute-start = (bf16[640,128]{1,0:T(8,128)(2,1)S(1)}, bf16[640,128]{1,0:T(8,128)(2,1)S(1)}, u32[]{:S(2)}, u32[]{:S(2)}) collective-permute-start(bf16[640,128]{1,0:T(8,128)(2,1)S(1)} %get-tuple-element.49), channel_id=1, source_target_pairs={{0,4},{4,0},{8,12},{12,8},{16,20},{20,16},{24,28},{28,24},{1,5},{5... | collective-permute-start | bytes 491528 | tf_op jit(solution)/shard_map/ppermute | solution.py:340
  7.0 7.0 %collective-permute-start.1 = (bf16[640,128]{1,0:T(8,128)(2,1)S(1)}, bf16[640,128]{1,0:T(8,128)(2,1)S(1)}, u32[]{:S(2)}, u32[]{:S(2)}) collective-permute-start(bf16[640,128]{1,0:T(8,128)(2,1)S(1)} %get-tuple-element.50), channel_id=1, source_target_pairs={{4,8},{8,4},{12,16},{16,12},{20,24},{24,20},{5,9},{9,5},{13,17},{1... | collective-permute-start | bytes 491528 | tf_op jit(solution)/shard_map/ppermute | solution.py:340
  14.0 2.0 %copy-start.4 = (bf16[3,3,3,128,128]{4,3,2,1,0:T(8,128)(2,1)S(1)}, bf16[3,3,3,128,128]{4,3,2,1,0:T(8,128)(2,1)}, u32[]{:S(2)}) copy-start(bf16[3,3,3,128,128]{4,3,2,1,0:T(8,128)(2,1)} %w.3) | copy-start | bytes 2654212
  14.0 2.0 %copy-start.7 = (f32[128]{0:T(128)S(1)}, f32[128]{0:T(128)}, u32[]{:S(2)}) copy-start(f32[128]{0:T(128)} %param.10) | copy-start | bytes 1540
  14.6 1.4 %collective-permute-start.2 = (bf16[416,128]{1,0:T(8,128)(2,1)S(1)}, bf16[416,128]{1,0:T(8,128)(2,1)S(1)}, u32[]{:S(2)}, u32[]{:S(2)}) collective-permute-start(bf16[416,128]{1,0:T(8,128)(2,1)S(1)} %get-tuple-element.52), channel_id=1, source_target_pairs={{0,1},{1,0},{2,3},{3,2},{4,5},{5,4},{6,7},{7,6},{8,9},{9,8},{10,11... | collective-permute-start | bytes 319496 | tf_op jit(solution)/shard_map/ppermute | solution.py:340
  14.7 1.3 %collective-permute-start.3 = (bf16[416,128]{1,0:T(8,128)(2,1)S(1)}, bf16[416,128]{1,0:T(8,128)(2,1)S(1)}, u32[]{:S(2)}, u32[]{:S(2)}) collective-permute-start(bf16[416,128]{1,0:T(8,128)(2,1)S(1)} %get-tuple-element.53), channel_id=1, source_target_pairs={{1,2},{2,1},{5,6},{6,5},{9,10},{10,9},{13,14},{14,13},{17,18},{18,... | collective-permute-start | bytes 319496 | tf_op jit(solution)/shard_map/ppermute | solution.py:340
  24.7 1.1 copy-start.16
  25.8 5.3 %copy-start.12 = (bf16[8,16,32,128]{3,2,1,0:T(8,128)(2,1)}, bf16[8,16,32,128]{3,2,1,0:T(8,128)(2,1)S(1)}, u32[]{:S(2)}) copy-start(bf16[8,16,32,128]{3,2,1,0:T(8,128)(2,1)S(1)} %get-tuple-element.54.hidden) | copy-start | bytes 3145732
  25.8 4.7 %collective-permute-start.4 = (bf16[256,128]{1,0:T(8,128)(2,1)S(1)}, bf16[256,128]{1,0:T(8,128)(2,1)S(1)}, u32[]{:S(2)}, u32[]{:S(2)}) collective-permute-start(bf16[256,128]{1,0:T(8,128)(2,1)S(1)} %get-tuple-element.56), channel_id=1, source_target_pairs={{0,4},{4,0},{8,12},{12,8},{16,20},{20,16},{24,28},{28,24},{1,5},{5... | collective-permute-start | bytes 196616 | tf_op jit(solution)/shard_map/ppermute | solution.py:340
  28.2 2.2 %collective-permute-start.5 = (bf16[256,128]{1,0:T(8,128)(2,1)S(1)}, bf16[256,128]{1,0:T(8,128)(2,1)S(1)}, u32[]{:S(2)}, u32[]{:S(2)}) collective-permute-start(bf16[256,128]{1,0:T(8,128)(2,1)S(1)} %get-tuple-element.57), channel_id=1, source_target_pairs={{4,8},{8,4},{12,16},{16,12},{20,24},{24,20},{5,9},{9,5},{13,17},{1... | collective-permute-start | bytes 196616 | tf_op jit(solution)/shard_map/ppermute | solution.py:340
  30.5 5.9 %copy-start = (bf16[3,3,3,128,256]{4,3,2,1,0:T(8,128)(2,1)S(1)}, bf16[3,3,3,128,256]{4,3,2,1,0:T(8,128)(2,1)}, u32[]{:S(2)}) copy-start(bf16[3,3,3,128,256]{4,3,2,1,0:T(8,128)(2,1)} %w.5) | copy-start | bytes 5308420
  30.5 5.9 %copy-start.5 = (bf16[256,128]{1,0:T(8,128)(2,1)S(1)}, bf16[256,128]{1,0:T(8,128)(2,1)}, u32[]{:S(2)}) copy-start(bf16[256,128]{1,0:T(8,128)(2,1)} %wm.3) | copy-start | bytes 196612
  30.5 5.9 %copy-start.6 = (f32[256]{0:T(256)S(1)}, f32[256]{0:T(256)}, u32[]{:S(2)}) copy-start(f32[256]{0:T(256)} %param.12) | copy-start | bytes 3076
  31.1 5.3 %collective-permute-start.6 = (bf16[256,128]{1,0:T(8,128)(2,1)S(1)}, bf16[256,128]{1,0:T(8,128)(2,1)S(1)}, u32[]{:S(2)}, u32[]{:S(2)}) collective-permute-start(bf16[256,128]{1,0:T(8,128)(2,1)S(1)} %get-tuple-element.58), channel_id=1, source_target_pairs={{0,1},{1,0},{2,3},{3,2},{4,5},{5,4},{6,7},{7,6},{8,9},{9,8},{10,11... | collective-permute-start | bytes 196616 | tf_op jit(solution)/shard_map/ppermute | solution.py:340
  35.5 0.9 collective-permute-start.7
  36.4 13.7 %copy-start.3 = (bf16[8,16,32,128]{3,2,1,0:T(8,128)(2,1)S(1)}, bf16[8,16,32,128]{3,2,1,0:T(8,128)(2,1)}, u32[]{:S(2)}) copy-start(bf16[8,16,32,128]{3,2,1,0:T(8,128)(2,1)} %cot.3) | copy-start | bytes 3145732
  43.3 0.9 copy-start.8
  44.2 0.8 copy-start.14
  45.0 12.1 %collective-permute-start.8 = (bf16[2,1792,128]{2,1,0:T(8,128)(2,1)}, bf16[2,1792,128]{2,1,0:T(8,128)(2,1)}, u32[]{:S(2)}, u32[]{:S(2)}) collective-permute-start(bf16[2,1792,128]{2,1,0:T(8,128)(2,1)} %get-tuple-element.63), channel_id=1, source_target_pairs={{0,1},{1,0},{2,3},{3,2},{4,5},{5,4},{6,7},{7,6},{8,9},{9,8},{10,11... | collective-permute-start | bytes 2752520 | tf_op jit(solution)/shard_map/ppermute | solution.py:376
  50.1 1.6 %copy-start.11 = (f32[8,16,32,128]{3,2,1,0:T(8,128)S(1)}, f32[8,16,32,128]{3,2,1,0:T(8,128)}, u32[]{:S(2)}) copy-start(f32[8,16,32,128]{3,2,1,0:T(8,128)} %get-tuple-element.62.ds) | copy-start | bytes 6291460
  51.7 1.0 copy-start.15
  52.7 4.4 %copy-start.9 = (bf16[2,1792,128]{2,1,0:T(8,128)(2,1)S(1)}, bf16[2,1792,128]{2,1,0:T(8,128)(2,1)}, u32[]{:S(2)}) copy-start(bf16[2,1792,128]{2,1,0:T(8,128)(2,1)} %copy-done.8) | copy-start | bytes 2752516
  52.7 6.0 %copy-start.17 = (bf16[10,18,32,128]{3,2,1,0:T(8,128)(2,1)S(1)}, bf16[10,18,32,128]{3,2,1,0:T(8,128)(2,1)}, u32[]{:S(2)}) copy-start(bf16[10,18,32,128]{3,2,1,0:T(8,128)(2,1)} %copy-done.16) | copy-start | bytes 4423684
  57.1 2.2 %copy-start.10 = (bf16[384,4096]{1,0:T(8,128)(2,1)S(1)}, bf16[384,4096]{1,0:T(8,128)(2,1)}, u32[]{:S(2)}) copy-start(bf16[384,4096]{1,0:T(8,128)(2,1)} %slope.1.st) | copy-start | bytes 9437188
  65.2 20.7 %collective-permute-start.9 = (bf16[2,896,128]{2,1,0:T(8,128)(2,1)S(1)}, bf16[2,896,128]{2,1,0:T(8,128)(2,1)S(1)}, u32[]{:S(2)}, u32[]{:S(2)}) collective-permute-start(bf16[2,896,128]{2,1,0:T(8,128)(2,1)S(1)} %get-tuple-element.75), channel_id=1, source_target_pairs={{0,1},{1,0},{2,3},{3,2},{4,5},{5,4},{6,7},{7,6},{8,9},{9,8},{10,11... | collective-permute-start | bytes 1376264 | tf_op jit(solution)/shard_map/ppermute | solution.py:376
  65.2 12.9 %collective-permute-start.18 = (bf16[1,896,128]{2,1,0:T(8,128)(2,1)S(1)}, bf16[1,896,128]{2,1,0:T(8,128)(2,1)S(1)}, u32[]{:S(2)}, u32[]{:S(2)}) collective-permute-start(bf16[1,896,128]{2,1,0:T(8,128)(2,1)S(1)} %get-tuple-element.85), channel_id=1, source_target_pairs={{0,6},{1,7},{2,4},{3,5},{4,2},{5,3},{6,0},{7,1},{8,14},{9,15},{10,... | collective-permute-start | bytes 688136 | tf_op jit(solution)/shard_map/ppermute | solution.py:376
  71.7 10.8 %collective-permute-start.19 = (bf16[1,896,128]{2,1,0:T(8,128)(2,1)S(1)}, bf16[1,896,128]{2,1,0:T(8,128)(2,1)S(1)}, u32[]{:S(2)}, u32[]{:S(2)}) collective-permute-start(bf16[1,896,128]{2,1,0:T(8,128)(2,1)S(1)} %get-tuple-element.86), channel_id=1, source_target_pairs={{0,2},{1,3},{2,0},{3,1},{4,6},{5,7},{6,4},{7,5},{8,10},{9,11},{10,... | collective-permute-start | bytes 688136 | tf_op jit(solution)/shard_map/ppermute | solution.py:376
  71.7 10.8 %collective-permute-start.20 = (bf16[1,896,128]{2,1,0:T(8,128)(2,1)S(1)}, bf16[1,896,128]{2,1,0:T(8,128)(2,1)S(1)}, u32[]{:S(2)}, u32[]{:S(2)}) collective-permute-start(bf16[1,896,128]{2,1,0:T(8,128)(2,1)S(1)} %get-tuple-element.87), channel_id=1, source_target_pairs={{0,4},{1,5},{2,6},{3,7},{4,0},{5,1},{6,2},{7,3},{8,12},{9,13},{10,... | collective-permute-start | bytes 688136 | tf_op jit(solution)/shard_map/ppermute | solution.py:376
  82.6 7.5 %collective-permute-start.21 = (bf16[448,128]{1,0:T(8,128)(2,1)S(1)}, bf16[448,128]{1,0:T(8,128)(2,1)S(1)}, u32[]{:S(2)}, u32[]{:S(2)}) collective-permute-start(bf16[448,128]{1,0:T(8,128)(2,1)S(1)} %get-tuple-element.89), channel_id=1, source_target_pairs={{0,8},{1,9},{2,10},{3,11},{4,12},{5,13},{6,14},{7,15},{8,0},{9,1},... | collective-permute-start | bytes 344072 | tf_op jit(solution)/shard_map/ppermute | solution.py:376
  86.5 6.9 %collective-permute-start.10 = (bf16[1,448,128]{2,1,0:T(8,128)(2,1)S(1)}, bf16[1,448,128]{2,1,0:T(8,128)(2,1)S(1)}, u32[]{:S(2)}, u32[]{:S(2)}) collective-permute-start(bf16[1,448,128]{2,1,0:T(8,128)(2,1)S(1)} %get-tuple-element.77), channel_id=1, source_target_pairs={{0,6},{1,7},{2,4},{3,5},{4,2},{5,3},{6,0},{7,1},{8,14},{9,15},{10,... | collective-permute-start | bytes 344072 | tf_op jit(solution)/shard_map/ppermute | solution.py:376
  88.1 6.4 %collective-permute-start.11 = (bf16[1,448,128]{2,1,0:T(8,128)(2,1)S(1)}, bf16[1,448,128]{2,1,0:T(8,128)(2,1)S(1)}, u32[]{:S(2)}, u32[]{:S(2)}) collective-permute-start(bf16[1,448,128]{2,1,0:T(8,128)(2,1)S(1)} %get-tuple-element.78), channel_id=1, source_target_pairs={{0,2},{1,3},{2,0},{3,1},{4,6},{5,7},{6,4},{7,5},{8,10},{9,11},{10,... | collective-permute-start | bytes 344072 | tf_op jit(solution)/shard_map/ppermute | solution.py:376
  89.1 5.4 %collective-permute-start.12 = (bf16[1,448,128]{2,1,0:T(8,128)(2,1)S(1)}, bf16[1,448,128]{2,1,0:T(8,128)(2,1)S(1)}, u32[]{:S(2)}, u32[]{:S(2)}) collective-permute-start(bf16[1,448,128]{2,1,0:T(8,128)(2,1)S(1)} %get-tuple-element.79), channel_id=1, source_target_pairs={{0,4},{1,5},{2,6},{3,7},{4,0},{5,1},{6,2},{7,3},{8,12},{9,13},{10,... | collective-permute-start | bytes 344072 | tf_op jit(solution)/shard_map/ppermute | solution.py:376
  90.1 7.2 %collective-permute-start.22 = (bf16[448,128]{1,0:T(8,128)(2,1)S(1)}, bf16[448,128]{1,0:T(8,128)(2,1)S(1)}, u32[]{:S(2)}, u32[]{:S(2)}) collective-permute-start(bf16[448,128]{1,0:T(8,128)(2,1)S(1)} %coarse_sum2.1.refs_0_), channel_id=1, source_target_pairs={{0,16},{1,17},{2,18},{3,19},{4,20},{5,21},{6,22},{7,23},{8,24},{9,... | collective-permute-start | bytes 344072 | tf_op jit(solution)/shard_map/ppermute | solution.py:376
  94.6 6.3 %collective-permute-start.13 = (bf16[224,128]{1,0:T(8,128)(2,1)S(1)}, bf16[224,128]{1,0:T(8,128)(2,1)S(1)}, u32[]{:S(2)}, u32[]{:S(2)}) collective-permute-start(bf16[224,128]{1,0:T(8,128)(2,1)S(1)} %get-tuple-element.81), channel_id=1, source_target_pairs={{0,8},{1,9},{2,10},{3,11},{4,12},{5,13},{6,14},{7,15},{8,0},{9,1},... | collective-permute-start | bytes 172040 | tf_op jit(solution)/shard_map/ppermute | solution.py:376
  95.0 7.0 %copy-start.13 = (bf16[8,16,32,128]{3,2,1,0:T(8,128)(2,1)S(1)}, bf16[8,16,32,128]{3,2,1,0:T(8,128)(2,1)}, u32[]{:S(2)}) copy-start(bf16[8,16,32,128]{3,2,1,0:T(8,128)(2,1)} %copy-done.12) | copy-start | bytes 3145732
  97.3 12.0 %collective-permute-start.25 = (bf16[448,128]{1,0:T(8,128)(2,1)S(1)}, bf16[448,128]{1,0:T(8,128)(2,1)S(1)}, u32[]{:S(2)}, u32[]{:S(2)}) collective-permute-start(bf16[448,128]{1,0:T(8,128)(2,1)S(1)} %coarse_total.1.refs_0_), channel_id=1, source_target_pairs={{0,12},{1,13},{2,14},{3,15},{4,8},{5,9},{6,10},{7,11},{8,4},{9,5},... | collective-permute-start | bytes 344072 | tf_op jit(solution)/shard_map/ppermute | solution.py:376
  97.4 12.9 %collective-permute-start.24 = (bf16[448,128]{1,0:T(8,128)(2,1)S(1)}, bf16[448,128]{1,0:T(8,128)(2,1)S(1)}, u32[]{:S(2)}, u32[]{:S(2)}) collective-permute-start(bf16[448,128]{1,0:T(8,128)(2,1)S(1)} %coarse_total.1.refs_0_), channel_id=1, source_target_pairs={{0,8},{1,9},{2,10},{3,11},{4,12},{5,13},{6,14},{7,15},{8,0},{9,1},... | collective-permute-start | bytes 344072 | tf_op jit(solution)/shard_map/ppermute | solution.py:376
  99.8 10.5 %collective-permute-start.23 = (bf16[448,128]{1,0:T(8,128)(2,1)S(1)}, bf16[448,128]{1,0:T(8,128)(2,1)S(1)}, u32[]{:S(2)}, u32[]{:S(2)}) collective-permute-start(bf16[448,128]{1,0:T(8,128)(2,1)S(1)} %coarse_total.1.refs_0_), channel_id=1, source_target_pairs={{0,4},{1,5},{2,6},{3,7},{4,0},{5,1},{6,2},{7,3},{8,12},{9,13},{10,... | collective-permute-start | bytes 344072 | tf_op jit(solution)/shard_map/ppermute | solution.py:376
  100.9 5.9 %collective-permute-start.14 = (bf16[224,128]{1,0:T(8,128)(2,1)S(1)}, bf16[224,128]{1,0:T(8,128)(2,1)S(1)}, u32[]{:S(2)}, u32[]{:S(2)}) collective-permute-start(bf16[224,128]{1,0:T(8,128)(2,1)S(1)} %fine_sum2.1.refs_0_), channel_id=1, source_target_pairs={{0,16},{1,17},{2,18},{3,19},{4,20},{5,21},{6,22},{7,23},{8,24},{9,... | collective-permute-start | bytes 172040 | tf_op jit(solution)/shard_map/ppermute | solution.py:376
  106.8 6.4 %collective-permute-start.17 = (bf16[224,128]{1,0:T(8,128)(2,1)S(1)}, bf16[224,128]{1,0:T(8,128)(2,1)S(1)}, u32[]{:S(2)}, u32[]{:S(2)}) collective-permute-start(bf16[224,128]{1,0:T(8,128)(2,1)S(1)} %fine_total.1.refs_0_), channel_id=1, source_target_pairs={{0,12},{1,13},{2,14},{3,15},{4,8},{5,9},{6,10},{7,11},{8,4},{9,5},... | collective-permute-start | bytes 172040 | tf_op jit(solution)/shard_map/ppermute | solution.py:376
  107.5 5.7 %collective-permute-start.16 = (bf16[224,128]{1,0:T(8,128)(2,1)S(1)}, bf16[224,128]{1,0:T(8,128)(2,1)S(1)}, u32[]{:S(2)}, u32[]{:S(2)}) collective-permute-start(bf16[224,128]{1,0:T(8,128)(2,1)S(1)} %fine_total.1.refs_0_), channel_id=1, source_target_pairs={{0,8},{1,9},{2,10},{3,11},{4,12},{5,13},{6,14},{7,15},{8,0},{9,1},... | collective-permute-start | bytes 172040 | tf_op jit(solution)/shard_map/ppermute | solution.py:376
  109.3 4.2 %collective-permute-start.15 = (bf16[224,128]{1,0:T(8,128)(2,1)S(1)}, bf16[224,128]{1,0:T(8,128)(2,1)S(1)}, u32[]{:S(2)}, u32[]{:S(2)}) collective-permute-start(bf16[224,128]{1,0:T(8,128)(2,1)S(1)} %fine_total.1.refs_0_), channel_id=1, source_target_pairs={{0,4},{1,5},{2,6},{3,7},{4,0},{5,1},{6,2},{7,3},{8,12},{9,13},{10,... | collective-permute-start | bytes 172040 | tf_op jit(solution)/shard_map/ppermute | solution.py:376

commit v2 on v1

--- a/solution.py
+++ b/solution.py
@@ -9,14 +9,17 @@
 
 F32 = jnp.float32
 BF16 = jnp.bfloat16
-VMEM_LIMIT = 48 * 1024 * 1024
+VMEM_LIMIT = 32 * 1024 * 1024
 
 
 def call(body, name, args, outs, scratch=(), micros=1):
     specs = [pl.BlockSpec(memory_space=pltpu.SMEM)]
     arrays = [args[0]]
     for arg in args[1:]:
-        if isinstance(arg, tuple):
+        if isinstance(arg, tuple) and arg[1] is None:
+            arrays.append(arg[0])
+            specs.append(pl.BlockSpec(memory_space=pltpu.HBM))
+        elif isinstance(arg, tuple):
             arrays.append(arg[0])
             specs.append(pl.BlockSpec(arg[1], functools.partial(lambda at, _: at, arg[2])))
         else:
@@ -26,7 +29,7 @@
         body,
         name=name,
         out_shape=[jax.ShapeDtypeStruct(s, t) for s, t in outs],
-        grid=(1,) if any(isinstance(arg, tuple) for arg in args) else (),
+        grid=(1,) if any(isinstance(arg, tuple) and arg[1] for arg in args) else (),
         in_specs=specs,
         out_specs=[pl.BlockSpec(memory_space=pltpu.VMEM) for _ in outs],
         scratch_shapes=list(scratch),
@@ -65,53 +68,37 @@
     return 1.0 / (1.0 + jnp.exp(-value))
 
 
-def prep_body(par, lo, hi, cot, pg, out_a, out_b, tmp):
-    bx, by, bz, c = cot.shape
-    cx, cy, cz = bx // 2, by // 2, bz // 2
-    total = jnp.sum(cot[...].astype(F32).reshape(cx, 2, cy, 2, bz, c), axis=(1, 3))
-    grad = sum_cube(cx * cy * bz, total.reshape(cx * cy * bz, c), tmp).astype(BF16)
-    pg[...] = grad.reshape(cx, cy, cz, c)
-    face = cy * cz
-    low = jnp.concatenate([lo[0].reshape(by * bz, c), grad[:face]], axis=0)
-    high = jnp.concatenate([hi[0].reshape(by * bz, c), grad[-face:]], axis=0)
-    put_faces(par[0] == 1, out_a, out_b, low, high)
-
-
-def turn_body(par, lo, hi, pg, ra, rb, out_a, out_b):
+def prep_body(par, field, out_a, out_b, sems):
+    odd, end = par[0], field.shape[0] - 1
+    one = pltpu.make_async_copy(field.at[(1 - odd) * end], out_a, sems.at[0])
+    two = pltpu.make_async_copy(field.at[odd * end], out_b, sems.at[1])
+    one.start()
+    two.start()
+    one.wait()
+    two.wait()
+
+
+def turn_body(par, lo, hi, ra, rb, out_a, out_b):
     bx, _, bz, c = lo.shape
-    cx, cy, cz, _ = pg.shape
     xlo, xhi = get_faces(par[0] == 1, ra, rb)
-    fine = 2 * cy * bz
-
-    def side(face, row, coarse, crow):
-        return jnp.concatenate(
-            [
-                xlo[row : row + bz],
-                face[...].reshape(bx * bz, c),
-                xhi[row : row + bz],
-                xlo[fine + crow : fine + crow + cz],
-                coarse.reshape(cx * cz, c),
-                xhi[fine + crow : fine + crow + cz],
-            ],
-            axis=0,
-        )
-
-    low = side(lo, 0, pg[:, 0], 0)
-    high = side(hi, fine - bz, pg[:, cy - 1], (cy - 1) * cz)
-    put_faces(par[1] == 1, out_a, out_b, low, high)
-
-
-def fine_body(par, field, ra, rb, ua, ub, w, bias, fpad, hidden, ds, pooled, out_a, out_b, wb, tmp):
+
+    def side(face, y):
+        return jnp.concatenate([xlo[y : y + 1], face[:, 0], xhi[y : y + 1]], axis=0)
+
+    put_faces(par[1] == 1, out_a, out_b, side(lo, 0), side(hi, xlo.shape[0] - 1))
+
+
+def fine_body(par, field, ra, rb, ua, ub, w, bias, pg, fpad, hidden, ds, pooled, out_a, out_b, wb, tmp):
     bx, by, bz, c = field.shape
     cx, cy, cz = bx // 2, by // 2, bz // 2
     rows = by * bz
     xlo, xhi = get_faces(par[0] == 1, ra, rb)
     ylo, yhi = get_faces(par[1] == 1, ua, ub)
     fpad[1 : bx + 1, 1 : by + 1] = field[...]
-    fpad[0, 1 : by + 1] = xlo[:rows].reshape(by, bz, c)
-    fpad[bx + 1, 1 : by + 1] = xhi[:rows].reshape(by, bz, c)
-    fpad[:, 0] = ylo[: (bx + 2) * bz].reshape(bx + 2, bz, c)
-    fpad[:, by + 1] = yhi[: (bx + 2) * bz].reshape(bx + 2, bz, c)
+    fpad[0, 1 : by + 1] = xlo
+    fpad[bx + 1, 1 : by + 1] = xhi
+    fpad[:, 0] = ylo
+    fpad[:, by + 1] = yhi
     for i in range(3):
         for j in range(3):
             for k in range(3):
@@ -139,21 +126,29 @@
         return carry
 
     lax.fori_loop(0, cx, pair, 0)
-    low = pooled[0:2].reshape(2 * cy * cz, c)
-    high = pooled[cx - 2 : cx].reshape(2 * cy * cz, c)
+    low = jnp.concatenate([pooled[0:2], pg[0:1]], axis=0)
+    high = jnp.concatenate([pooled[cx - 2 : cx], pg[cx - 1 : cx]], axis=0)
     put_faces(par[0] == 1, out_a, out_b, low, high)
 
 
-def turn2_body(par, pooled, ra, rb, out_a, out_b):
-    cx, cy, cz, c = pooled.shape
+def cubes_body(par, cot, pg, tmp):
+    bx, by, bz, c = cot.shape
+    cx, cy, cz = bx // 2, by // 2, bz // 2
+    total = jnp.sum(cot[...].astype(F32).reshape(cx, 2, cy, 2, bz, c), axis=(1, 3))
+    grad = sum_cube(cx * cy * bz, total.reshape(cx * cy * bz, c), tmp).astype(BF16)
+    pg[...] = grad.reshape(cx, cy, cz, c)
+
+
+def turn2_body(par, pooled, pg, ra, rb, out_a, out_b):
+    cy = pooled.shape[1]
     xlo, xhi = get_faces(par[0] == 1, ra, rb)
-    xlo, xhi = xlo.reshape(2, cy, cz, c), xhi.reshape(2, cy, cz, c)
-
-    def side(y):
-        parts = [xlo[:, y : y + 2], pooled[:, y : y + 2], xhi[:, y : y + 2]]
-        return jnp.concatenate([p.reshape(-1, c) for p in parts], axis=0)
-
-    put_faces(par[1] == 1, out_a, out_b, side(0), side(cy - 2))
+
+    def side(y, last):
+        two = [jnp.concatenate([xlo[0:2, at], pooled[:, at], xhi[0:2, at]], axis=0) for at in (y, y + 1)]
+        one = jnp.concatenate([xlo[2:3, last], pg[:, last], xhi[2:3, last]], axis=0)
+        return jnp.concatenate([*two, one], axis=0)
+
+    put_faces(par[1] == 1, out_a, out_b, side(0, 0), side(cy - 2, cy - 1))
 
 
 def reverse_bits(value, count):
@@ -179,7 +174,7 @@
 
 
 def coarse_body(
-    n, par, pooled, ra, rb, ua, ub, pg, fa, fb, ga, gb, w, bias, wm,
+    n, par, pooled, ra, rb, ua, ub, pg, w, bias, wm,
     slope, coarse, keep, send, cbias, qpad, gpad, wb, st, rhs, acc, ct,
 ):
     cx, cy, cz, c = pooled.shape
@@ -187,19 +182,17 @@
     xlo, xhi = get_faces(par[0] == 1, ra, rb)
     ylo, yhi = get_faces(par[1] == 1, ua, ub)
     qpad[2 : cx + 2, 2 : cy + 2] = pooled[...]
-    qpad[0:2, 2 : cy + 2] = xlo.reshape(2, cy, cz, c)
-    qpad[cx + 2 : cx + 4, 2 : cy + 2] = xhi.reshape(2, cy, cz, c)
-    qpad[:, 0:2] = ylo.reshape(cx + 4, 2, cz, c)
-    qpad[:, cy + 2 : cy + 4] = yhi.reshape(cx + 4, 2, cz, c)
-    face = cy * cz
-    glo, ghi = get_faces(par[0] == 1, fa, fb)
-    hlo, hhi = get_faces(par[1] == 1, ga, gb)
+    qpad[0:2, 2 : cy + 2] = xlo[0:2]
+    qpad[cx + 2 : cx + 4, 2 : cy + 2] = xhi[0:2]
+    wide = cx + 4
+    for t in (0, 1):
+        qpad[:, t] = ylo[t * wide : (t + 1) * wide]
+        qpad[:, cy + 2 + t] = yhi[t * wide : (t + 1) * wide]
     gpad[1 : cx + 1, 1 : cy + 1] = pg[...]
-    gpad[0, 1 : cy + 1] = glo[-face:].reshape(cy, cz, c)
-    gpad[cx + 1, 1 : cy + 1] = ghi[-face:].reshape(cy, cz, c)
-    edge = (cx + 2) * cz
-    gpad[:, 0] = hlo[-edge:].reshape(cx + 2, cz, c)
-    gpad[:, cy + 1] = hhi[-edge:].reshape(cx + 2, cz, c)
+    gpad[0, 1 : cy + 1] = xlo[2]
+    gpad[cx + 1, 1 : cy + 1] = xhi[2]
+    gpad[:, 0] = ylo[2 * wide :]
+    gpad[:, cy + 1] = yhi[2 * wide :]
     for i in range(3):
         for j in range(3):
             for k in range(3):
@@ -257,7 +250,7 @@
     spread(par[2], keep, send, n, 28, piece)
 
 
-def slope_body(par, slope, w, cot, ds, st, up):
+def back_body(n, par, slope, w, cot, ds, fpad, cbias, keep, send, up, st, rhs, acc):
     bx, by, bz, c = cot.shape
     cx, cy, cz = bx // 2, by // 2, bz // 2
     c2 = slope.shape[3]
@@ -288,12 +281,7 @@
         st[pl.ds(0, c), pl.ds(x * rows, rows)] = shift_rows(wide, -1, bz).astype(BF16).T
         st[pl.ds(c, c), pl.ds(x * rows, rows)] = fs.T
         st[pl.ds(2 * c, c), pl.ds(x * rows, rows)] = shift_rows(wide, 1, bz).astype(BF16).T
-
-
-def grad_body(n, par, st, fpad, cbias, keep, send, rhs, acc):
-    bx, by, bz, c = fpad.shape[0] - 2, fpad.shape[1] - 2, fpad.shape[2], fpad.shape[3]
-    voxels = bx * by * bz
-    c2 = cbias.shape[0]
+    voxels = bx * rows
     for t in range(0, 10, 2):
         for h in (0, 1):
             i, j = (t + h) // 3, (t + h) % 3
@@ -337,7 +325,8 @@
     n = lax.axis_size(axis)
     one = [p for i in range(0, n - 1, 2) for p in ((i, i + 1), (i + 1, i))]
     two = [p for i in range(1, n - 1, 2) for p in ((i, i + 1), (i + 1, i))]
-    return lax.ppermute(first, axis, one), lax.ppermute(second, axis, two)
+    got = lax.ppermute(second, axis, two)
+    return lax.ppermute(first, axis, one), got
 
 
 def split4_body(par, keep, got, own, over_sub, over_grp, over_both):
@@ -433,39 +422,46 @@
     return pieces, bits
 
 
-def last_body(count, per, par, *refs):
-    pieces, rest, rows = refs[:count], refs[count:-1], refs[-1]
+def last_body(count, par, *refs):
+    pieces, kernel, extra, rows = refs[:count], refs[count], refs[count + 1], refs[-1]
     size = pieces[0].shape[0]
+    per = extra.shape[0] if len(refs) == count + 3 else kernel.shape[3]
     mine = par[0] if count == 2 else 2 * par[0] + par[1]
     for which in range(count):
         mask = which if count == 2 else 2 * (which & 1) + (which >> 1)
         rows[mine ^ mask] = pieces[which][...]
-    kernel, extra = rest[0], rest[1]
 
     def block(t):
         at, off = t * per // size, t * per % size
         if off + per <= size:
-            return rows[at, pl.ds(off, per)]
+            return rows[at, pl.ds(off, per)].astype(F32)
         first = size - off
-        return jnp.concatenate([rows[at, pl.ds(off, first)], rows[at + 1, pl.ds(0, per - first)]], axis=0)
+        return jnp.concatenate([rows[at, pl.ds(off, first)], rows[at + 1, pl.ds(0, per - first)]], axis=0).astype(F32)
 
     for t in range(27):
-        kernel[(t // 3) % 3, t % 3, t // 9] = block(t).astype(F32).T
-    extra[...] = block(27).astype(F32)
-
-
-def last(pieces, bits, grp, per, name):
+        kernel[(t // 3) % 3, t % 3, t // 9] = block(t)
+    if len(refs) == count + 3:
+        extra[...] = block(27)
+    else:
+        turned = block(27).T
+        extra[...] = turned[0:1]
+        refs[count + 2][:, pl.ds(0, per)] = turned[1:2]
+        refs[count + 2][:, pl.ds(per, per)] = turned[2:3]
+
+
+def last(pieces, bits, grp, per, outs, name):
     count = len(pieces)
     size, c = pieces[0].shape
     order = jnp.stack([(grp >> b) & 1 for b in (bits + bits)[:2]]).astype(jnp.int32)
-    return call(
-        functools.partial(last_body, count, per),
+    kernel, *rest = call(
+        functools.partial(last_body, count),
         name,
         (order, *pieces),
-        [((3, 3, 3, c, per), F32), ((per, c), F32)],
+        [((3, 3, 3, per, c), F32), *outs],
         [pltpu.VMEM((count, size, c), BF16)],
-        2,
-    )
+        1,
+    )
+    return jnp.swapaxes(kernel, 3, 4), *rest
 
 
 def per_device(field, cotangent, fine_kernel, fine_bias, coarse_kernel, coarse_bias, merge_weight):
@@ -476,58 +472,45 @@
     c2 = merge_weight.shape[0]
     par = jnp.stack([grp & 1, sub & 1, sub & 1]).astype(jnp.int32)
     cross_bits = jnp.stack([grp & 1, (sub >> 1) & 1]).astype(jnp.int32)
-    face = by * bz + cy * cz
-    xlo = (field, (1, by, bz, c), (0, 0, 0, 0))
-    xhi = (field, (1, by, bz, c), (bx - 1, 0, 0, 0))
     ylo = (field, (bx, 1, bz, c), (0, 0, 0, 0))
     yhi = (field, (bx, 1, bz, c), (0, by - 1, 0, 0))
-    pg, sa, sb = call(
-        prep_body,
-        "prep",
-        (par, xlo, xhi, cotangent),
-        [((cx, cy, cz, c), BF16), ((face, c), BF16), ((face, c), BF16)],
-        [pltpu.VMEM((cx * cy * bz, c), F32)],
+    face = ((by, bz, c), BF16)
+    sa, sb = call(
+        prep_body, "prep", (par, (field, None, None)), [face, face], [pltpu.SemaphoreType.DMA((2,))]
     )
     xa, xb = swap_faces(sa, sb, "grp")
-    edge = (bx + 2) * bz + (cx + 2) * cz
-    ta, tb = call(
-        turn_body,
-        "turn",
-        (par, ylo, yhi, pg, xa, xb),
-        [((edge, c), BF16), ((edge, c), BF16)],
-    )
+    (pg,) = call(
+        cubes_body, "cubes", (par, cotangent), [((cx, cy, cz, c), BF16)], [pltpu.VMEM((cx * cy * bz, c), F32)]
+    )
+    face = ((bx + 2, bz, c), BF16)
+    ta, tb = call(turn_body, "turn", (par, ylo, yhi, xa, xb), [face, face])
     ya, yb = swap_faces(ta, tb, "sub")
-    side = 2 * cy * cz
+    face = ((3, cy, cz, c), BF16)
     fpad, hidden, ds, pooled, pa, pb = call(
         fine_body,
         "fine",
-        (par, field, xa, xb, ya, yb, fine_kernel, fine_bias.reshape(1, c)),
+        (par, field, xa, xb, ya, yb, fine_kernel, fine_bias.reshape(1, c), pg),
         [
             ((bx + 2, by + 2, bz, c), BF16),
             ((bx, by, bz, c), BF16),
             ((bx, by, bz, c), F32),
             ((cx, cy, cz, c), BF16),
-            ((side, c), BF16),
-            ((side, c), BF16),
+            face,
+            face,
         ],
         [pltpu.VMEM((9 * c, 3 * c), BF16), pltpu.VMEM((cy * bz, c), F32)],
         8,
     )
     pxa, pxb = swap_faces(pa, pb, "grp")
-    side = (cx + 4) * 2 * cz
-    qa, qb = call(
-        turn2_body,
-        "turn2",
-        (par, pooled, pxa, pxb),
-        [((side, c), BF16), ((side, c), BF16)],
-    )
+    face = ((2 * (cx + 4) + cx + 2, cz, c), BF16)
+    qa, qb = call(turn2_body, "turn2", (par, pooled, pg, pxa, pxb), [face, face])
     pya, pyb = swap_faces(qa, qb, "sub")
     cells = cx * cy * cz
     part = (n // 2, 28 * (c2 // n), c)
     slope, coarse, ckeep, csend, cbias = call(
         functools.partial(coarse_body, n),
         "coarse",
-        (par, pooled, pxa, pxb, pya, pyb, pg, xa, xb, ya, yb, coarse_kernel, coarse_bias.reshape(1, c2), merge_weight),
+        (par, pooled, pxa, pxb, pya, pyb, pg, coarse_kernel, coarse_bias.reshape(1, c2), merge_weight),
         [
             ((cx + 2, cy + 2, cz, c2), BF16),
             ((cx, cy, cz, c2), BF16),
@@ -547,32 +530,6 @@
         6,
     )
     cgot = cores(csend)
-    voxels = bx * by * bz
-    (st,) = call(
-        slope_body,
-        "slope",
-        (par, slope, coarse_kernel, cotangent, ds),
-        [((3 * c, voxels), BF16)],
-        [pltpu.VMEM((cx * cy * bz, c), F32)],
-        4,
-    )
-    st, cgot = lax.optimization_barrier((st, cgot))
-    csent = spread_sum(ckeep, cgot, cross_bits, "coarse_split")
-    st, csent = lax.optimization_barrier((st, csent))
-    cparts = cross(*csent)
-    part = (n // 2, 28 * (c // n), c)
-    fkeep, fsend = call(
-        functools.partial(grad_body, n),
-        "grad",
-        (par, st, fpad, cbias),
-        [(part, BF16), (part, BF16)],
-        [pltpu.VMEM((voxels, 2 * c), BF16), pltpu.VMEM((3 * c, 10 * c), BF16)],
-        6,
-    )
-    fgot = cores(fsend)
-    fparts = cross(*spread_sum(fkeep, fgot, cross_bits, "fine_split"))
-    coarse_sum = finish_sum(cparts, sub, grp, "coarse")
-    fine_sum = finish_sum(fparts, sub, grp, "fine")
     (output,) = call(
         merge_body,
         "merge",
@@ -581,16 +538,35 @@
         [pltpu.VMEM((cx * cy * bz, c), F32)],
         2,
     )
-    grad_coarse, grad_merge = last(*coarse_sum, grp, c2 // n, "coarse_last")
-    grad_fine, extra = last(*fine_sum, grp, c // n, "fine_last")
-    return (
-        output,
-        grad_fine,
-        extra[:, 0],
-        grad_coarse,
-        jnp.concatenate([extra[:, 1], extra[:, 2]]),
-        grad_merge,
-    )
+    output, cgot = lax.optimization_barrier((output, cgot))
+    csent = spread_sum(ckeep, cgot, cross_bits, "coarse_split")
+    slope, csent = lax.optimization_barrier((slope, csent))
+    cparts = cross(*csent)
+    voxels = bx * by * bz
+    part = (n // 2, 28 * (c // n), c)
+    fkeep, fsend = call(
+        functools.partial(back_body, n),
+        "back",
+        (par, slope, coarse_kernel, cotangent, ds, fpad, cbias),
+        [(part, BF16), (part, BF16)],
+        [
+            pltpu.VMEM((cx * cy * bz, c), F32),
+            pltpu.VMEM((3 * c, voxels), BF16),
+            pltpu.VMEM((voxels, 2 * c), BF16),
+            pltpu.VMEM((3 * c, 10 * c), BF16),
+        ],
+        10,
+    )
+    fsend, cparts = lax.optimization_barrier((fsend, cparts))
+    fgot = cores(fsend)
+    fparts = cross(*spread_sum(fkeep, fgot, cross_bits, "fine_split"))
+    coarse_sum = finish_sum(cparts, sub, grp, "coarse")
+    fine_sum = finish_sum(fparts, sub, grp, "fine")
+    per, cper = c // n, c2 // n
+    grad_coarse, grad_merge = last(*coarse_sum, grp, cper, [((cper, c), F32)], "coarse_last")
+    biases = [((1, per), F32), ((1, cper), F32)]
+    grad_fine, bias, coarse_sums = last(*fine_sum, grp, per, biases, "fine_last")
+    return (output, grad_fine, bias[0], grad_coarse, coarse_sums[0], grad_merge)
 
 
 def solution(mesh):

time: 117 us -> 108 us (0.923)
  waiting for transfers between devices: 27.2 us -> 16.2 us
  starting transfers between devices: 41.7 us -> 45.8 us
  Pallas kernels: 34.4 us -> 33.2 us
    ppermute x18, waiting for transfers between devices: 18.4 us -> 11.3 us  [partners(): return lax.ppermute(value, ('grp', 'sub'), pairs)]
    ppermute x8, waiting for transfers between devices: 8.79 us -> 4.91 us  [the longest x4 4.9 us: swap_faces(): return (lax.ppermute(first, axis, one), got)]
    ppermute x8, starting transfers between devices: 12.6 us -> 14.7 us  [the longest x4 11.8 us: swap_faces(): return (lax.ppermute(first, axis, one), got)]
    ppermute x18, starting transfers between devices: 29.1 us -> 31.1 us  [partners(): return lax.ppermute(value, ('grp', 'sub'), pairs)]
    pallas_call x18, Pallas kernels: 34.4 us -> 33.2 us  [call(): pl.pallas_call(body, name=name, out_shape=[jax.ShapeDtypeStruct(s, t) for...]
    unnamed x38 -> x56, local copies, waits for them, and re-layouts: 11.2 us -> 11.6 us
  transfers between devices with their start and end apart: 26 -> 26, of which waited for: 11 -> 11; matrix products, arithmetic and copies ran while one was open for 1% -> 0% of each run, Pallas kernels for 7% -> 13%
where the time goes in v2:
time: 108 us
  starting transfers between devices  45.8 us (42%)
  Pallas kernels  33.2 us (31%)
  waiting for transfers between devices  16.2 us (15%)
  local copies, waits for them, and re-layouts  11.6 us (11%)
    pallas_call x18, Pallas kernels, call(): pl.pallas_call(body, name=name, out_shape=[jax.ShapeDtypeStruct(s, t) for...  33.2 us
    ppermute x18, starting transfers between devices, partners(): return lax.ppermute(value, ('grp', 'sub'), pairs)  31.1 us
    ppermute x4, starting transfers between devices, swap_faces(): return (lax.ppermute(first, axis, one), got)  11.8 us
    unnamed x56, local copies, waits for them, and re-layouts  11.6 us
    ppermute x18, waiting for transfers between devices, partners(): return lax.ppermute(value, ('grp', 'sub'), pairs)  11.3 us
    ppermute x4, waiting for transfers between devices, swap_faces(): return (lax.ppermute(first, axis, one), got)  4.9 us
    ppermute x4, starting transfers between devices, swap_faces(): got = lax.ppermute(second, axis, two)  2.89 us
  transfers between devices with their start and end apart: 26, of which 11 were waited for; matrix products, arithmetic and copies ran while one was open for 0% of the time, Pallas kernels for 13%

profile of v2, /device:TPU:0, one launch (start us, length us, event | category | flops | bytes accessed | tf_op | source)
XLA Modules:
  0.0 108.0 jit_solution(14574662826656567686)
XLA Ops:
  0.6 0.1 pad_add_fusion.par
  0.7 1.2 %copy-done.1 = bf16[8,16,32,128]{3,2,1,0:T(8,128)(2,1)S(1)} copy-done((bf16[8,16,32,128]{3,2,1,0:T(8,128)(2,1)S(1)}, bf16[8,16,32,128]{3,2,1,0:T(8,128)(2,1)}, u32[]{:S(2)}) %copy-start.1) | copy-done | bytes 1048600
  1.9 0.9 prep.1
  2.9 3.0 %collective-permute-start = (bf16[16,32,128]{2,1,0:T(8,128)(2,1)S(1)}, bf16[16,32,128]{2,1,0:T(8,128)(2,1)S(1)}, u32[]{:S(2)}, u32[]{:S(2)}) collective-permute-start(bf16[16,32,128]{2,1,0:T(8,128)(2,1)S(1)} %get-tuple-element.54), channel_id=1, source_target_pairs={{0,4},{4,0},{8,12},{12,8},{16,20},{20,16},{24,28},{28,24},{1,5},{5... | collective-permute-start | bytes 393224 | tf_op jit(solution)/shard_map/ppermute | solution.py:329
  5.9 0.8 collective-permute-start.1
  6.7 2.7 %collective-permute-done.ra = bf16[16,32,128]{2,1,0:T(8,128)(2,1)S(1)} collective-permute-done((bf16[16,32,128]{2,1,0:T(8,128)(2,1)S(1)}, bf16[16,32,128]{2,1,0:T(8,128)(2,1)S(1)}, u32[]{:S(2)}, u32[]{:S(2)}) %collective-permute-start) | collective-permute-done | bytes 131104 | tf_op jit(solution)/shard_map/ppermute | solution.py:329
  9.4 0.6 turn.1
  9.9 0.1 collective-permute-start.2
  10.1 0.8 collective-permute-start.3
  10.9 0.8 cubes.1.pg
  11.7 7.4 %fine.1 = (bf16[10,18,32,128]{3,2,1,0:T(8,128)(2,1)S(1)}, bf16[8,16,32,128]{3,2,1,0:T(8,128)(2,1)S(1)}, f32[8,16,32,128]{3,2,1,0:T(8,128)S(1)}, bf16[4,8,16,128]...) custom-call(s32[3]{0:T(128)S(1)} %pad_add_fusion.par, ...), custom_call_target="tpu_custom_call" | custom-call | flops 8000000000 | tf_op jit(solution)/shard_map/fine/pallas_call | solution.py:28
  19.1 1.1 %copy-done.22 = bf16[10,18,32,128]{3,2,1,0:T(8,128)(2,1)} copy-done((bf16[10,18,32,128]{3,2,1,0:T(8,128)(2,1)}, bf16[10,18,32,128]{3,2,1,0:T(8,128)(2,1)S(1)}, u32[]{:S(2)}) %copy-start.22) | copy-done | bytes 1474584
  20.2 4.8 %collective-permute-start.4 = (bf16[3,8,16,128]{3,2,1,0:T(8,128)(2,1)S(1)}, bf16[3,8,16,128]{3,2,1,0:T(8,128)(2,1)S(1)}, u32[]{:S(2)}, u32[]{:S(2)}) collective-permute-start(bf16[3,8,16,128]{3,2,1,0:T(8,128)(2,1)S(1)} %get-tuple-element.60), channel_id=1, source_target_pairs={{0,4},{4,0},{8,12},{12,8},{16,20},{20,16},{24,28},{28,24},{1,5},{5... | collective-permute-start | bytes 294920 | tf_op jit(solution)/shard_map/ppermute | solution.py:329
  25.0 0.7 collective-permute-start.5
  25.6 1.9 %collective-permute-done.4.ra = bf16[3,8,16,128]{3,2,1,0:T(8,128)(2,1)S(1)} collective-permute-done((bf16[3,8,16,128]{3,2,1,0:T(8,128)(2,1)S(1)}, bf16[3,8,16,128]{3,2,1,0:T(8,128)(2,1)S(1)}, u32[]{:S(2)}, u32[]{:S(2)}) %collective-permute-start.4) | collective-permute-done | bytes 98336 | tf_op jit(solution)/shard_map/ppermute | solution.py:329
  27.6 0.6 turn2.1
  28.2 3.9 %collective-permute-start.6 = (bf16[22,16,128]{2,1,0:T(8,128)(2,1)S(1)}, bf16[22,16,128]{2,1,0:T(8,128)(2,1)S(1)}, u32[]{:S(2)}, u32[]{:S(2)}) collective-permute-start(bf16[22,16,128]{2,1,0:T(8,128)(2,1)S(1)} %get-tuple-element.62), channel_id=1, source_target_pairs={{0,1},{1,0},{2,3},{3,2},{4,5},{5,4},{6,7},{7,6},{8,9},{9,8},{10,11... | collective-permute-start | bytes 270344 | tf_op jit(solution)/shard_map/ppermute | solution.py:329
  32.1 0.7 collective-permute-start.7
  32.8 0.3 collective-permute-done.6.ua
  33.1 6.8 %coarse.1 = (bf16[6,10,16,256]{3,2,1,0:T(8,128)(2,1)S(1)}, bf16[4,8,16,256]{3,2,1,0:T(8,128)(2,1)S(1)}, bf16[2,1792,128]{2,1,0:T(8,128)(2,1)S(1)}, bf16[2,1792,128]{2,1,0:T(8,128)(2,1)}, bf16[256,128]{1,0:T(8,128)(2,1)S(1)}) custom-call(s32[3]{0:T(128)S(1)} %pad_add_fusion.par, bf16[4,8,16,128]{3,2,1,0:T(8,128)(2,1)S(1)} %get-tuple-element.59.pooled, ...), custom_call_target="tpu_custom_call" | custom-call | flops 6000000000 | tf_op jit(solution)/shard_map/coarse/pallas_call | solution.py:28
  39.9 0.9 copy-done.12
  40.8 0.8 copy-done.24
  41.6 0.6 copy-done.26
  42.2 5.4 %collective-permute-start.8 = (bf16[2,1792,128]{2,1,0:T(8,128)(2,1)}, bf16[2,1792,128]{2,1,0:T(8,128)(2,1)}, u32[]{:S(2)}, u32[]{:S(2)}) collective-permute-start(bf16[2,1792,128]{2,1,0:T(8,128)(2,1)} %get-tuple-element.65), channel_id=1, source_target_pairs={{0,1},{1,0},{2,3},{3,2},{4,5},{5,4},{6,7},{7,6},{8,9},{9,8},{10,11... | collective-permute-start | bytes 2752520 | tf_op jit(solution)/shard_map/ppermute | solution.py:365
  47.6 0.1 pad_add_fusion.2.par
  47.7 1.2 %copy-done.19 = bf16[8,16,32,128]{3,2,1,0:T(8,128)(2,1)S(1)} copy-done((bf16[8,16,32,128]{3,2,1,0:T(8,128)(2,1)S(1)}, bf16[8,16,32,128]{3,2,1,0:T(8,128)(2,1)}, u32[]{:S(2)}) %copy-start.19) | copy-done | bytes 1048600
  48.9 1.8 %merge.1 = bf16[8,16,32,128]{3,2,1,0:T(8,128)(2,1)} custom-call(s32[3]{0:T(128)S(1)} %pad_add_fusion.par, bf16[8,16,32,128]{3,2,1,0:T(8,128)(2,1)S(1)} %copy-done.19, bf16[4,8,16,256]{3,2,1,0:T(8,128)(2,1)S(1)} %get-tuple-element.64.coarse, bf16[256,128]{1,0:T(8,128)(2,1)S(1)} %copy-done.9), custom_call_target="tpu_custom_call" | custom-call | flops 2000000000 | tf_op jit(solution)/shard_map/merge/pallas_call | solution.py:28
  50.8 1.6 %coarse_split.1 = (bf16[1,896,128]{2,1,0:T(8,128)(2,1)S(1)}, bf16[1,896,128]{2,1,0:T(8,128)(2,1)S(1)}, bf16[1,896,128]{2,1,0:T(8,128)(2,1)S(1)}, bf16[1,896,128]{2,1,0:T(8,128)(2,1)S(1)}) custom-call(s32[2]{0:T(128)S(1)} %pad_add_fusion.2.par, bf16[2,1,2,896,128]{4,3,2,1,0:T(8,128)(2,1)S(1)} %bitcast.33, bf16[2,1,2,896,128]{4,3,2,1,0:T(8,128)(2,1)} %bitcast.9.got), custom_call_target="tpu_custom_call" | custom-call | flops 1000000000 | tf_op jit(solution)/shard_map/coarse_split/pallas_call | solution.py:28
  52.4 0.7 copy-done.16
  53.1 1.6 %collective-permute-start.10 = (bf16[1,896,128]{2,1,0:T(8,128)(2,1)S(1)}, bf16[1,896,128]{2,1,0:T(8,128)(2,1)S(1)}, u32[]{:S(2)}, u32[]{:S(2)}) collective-permute-start(bf16[1,896,128]{2,1,0:T(8,128)(2,1)S(1)} %get-tuple-element.82), channel_id=1, source_target_pairs={{0,2},{1,3},{2,0},{3,1},{4,6},{5,7},{6,4},{7,5},{8,10},{9,11},{10,... | collective-permute-start | bytes 688136 | tf_op jit(solution)/shard_map/ppermute | solution.py:365
  54.7 4.9 %collective-permute-start.11 = (bf16[1,896,128]{2,1,0:T(8,128)(2,1)S(1)}, bf16[1,896,128]{2,1,0:T(8,128)(2,1)S(1)}, u32[]{:S(2)}, u32[]{:S(2)}) collective-permute-start(bf16[1,896,128]{2,1,0:T(8,128)(2,1)S(1)} %get-tuple-element.83), channel_id=1, source_target_pairs={{0,4},{1,5},{2,6},{3,7},{4,0},{5,1},{6,2},{7,3},{8,12},{9,13},{10,... | collective-permute-start | bytes 688136 | tf_op jit(solution)/shard_map/ppermute | solution.py:365
  59.6 8.9 %back.1 = (bf16[2,896,128]{2,1,0:T(8,128)(2,1)S(1)}, bf16[2,896,128]{2,1,0:T(8,128)(2,1)S(1)}) custom-call(s32[3]{0:T(128)S(1)} %pad_add_fusion.par, bf16[6,10,16,256]{3,2,1,0:T(8,128)(2,1)S(1)} %copy-done.25, bf16[3,3,3,128,256]{4,3,2,1,0:T(8,128)(2,1)S(1)} %copy-done, bf16[8,16,32,128]{3,2,1,0:T(8,128)(2,1)S(1)} %copy-done.3, ...), custom_call_target="tpu_custom_call" | custom-call | flops 10000000000 | tf_op jit(solution)/shard_map/back/pallas_call | solution.py:28
  68.5 0.8 copy-done.14
  69.3 0.7 copy-done.5
  70.0 0.3 collective-permute-done.9
  70.2 0.7 copy-done.7
  70.9 0.9 copy-done.6
  71.9 0.9 copy-done.8
  72.8 0.9 copy-done.17
  73.7 0.1 coarse_half.1
  73.9 3.3 %collective-permute-start.21 = (bf16[448,128]{1,0:T(8,128)(2,1)S(1)}, bf16[448,128]{1,0:T(8,128)(2,1)S(1)}, u32[]{:S(2)}, u32[]{:S(2)}) collective-permute-start(bf16[448,128]{1,0:T(8,128)(2,1)S(1)} %get-tuple-element.98), channel_id=1, source_target_pairs={{0,8},{1,9},{2,10},{3,11},{4,12},{5,13},{6,14},{7,15},{8,0},{9,1},... | collective-permute-start | bytes 344072 | tf_op jit(solution)/shard_map/ppermute | solution.py:365
  77.1 0.7 fine_split.1
  77.8 2.7 %collective-permute-start.13 = (bf16[1,448,128]{2,1,0:T(8,128)(2,1)S(1)}, bf16[1,448,128]{2,1,0:T(8,128)(2,1)S(1)}, u32[]{:S(2)}, u32[]{:S(2)}) collective-permute-start(bf16[1,448,128]{2,1,0:T(8,128)(2,1)S(1)} %get-tuple-element.86), channel_id=1, source_target_pairs={{0,6},{1,7},{2,4},{3,5},{4,2},{5,3},{6,0},{7,1},{8,14},{9,15},{10,... | collective-permute-start | bytes 344072 | tf_op jit(solution)/shard_map/ppermute | solution.py:365
  80.5 0.3 collective-permute-start.14
  80.8 0.5 collective-permute-start.15
  81.4 2.4 %collective-permute-start.22 = (bf16[448,128]{1,0:T(8,128)(2,1)S(1)}, bf16[448,128]{1,0:T(8,128)(2,1)S(1)}, u32[]{:S(2)}, u32[]{:S(2)}) collective-permute-start(bf16[448,128]{1,0:T(8,128)(2,1)S(1)} %coarse_sum2.1.refs_0_), channel_id=1, source_target_pairs={{0,16},{1,17},{2,18},{3,19},{4,20},{5,21},{6,22},{7,23},{8,24},{9,... | collective-permute-start | bytes 344072 | tf_op jit(solution)/shard_map/ppermute | solution.py:365
  83.8 0.4 collective-permute-done.13
  84.2 2.4 %collective-permute-done.14 = bf16[1,448,128]{2,1,0:T(8,128)(2,1)S(1)} collective-permute-done((bf16[1,448,128]{2,1,0:T(8,128)(2,1)S(1)}, bf16[1,448,128]{2,1,0:T(8,128)(2,1)S(1)}, u32[]{:S(2)}, u32[]{:S(2)}) %collective-permute-start.14) | collective-permute-done | bytes 114720 | tf_op jit(solution)/shard_map/ppermute | solution.py:365
  86.5 0.3 collective-permute-done.15
  86.8 0.1 fine_half.1
  86.8 1.2 %collective-permute-start.16 = (bf16[224,128]{1,0:T(8,128)(2,1)S(1)}, bf16[224,128]{1,0:T(8,128)(2,1)S(1)}, u32[]{:S(2)}, u32[]{:S(2)}) collective-permute-start(bf16[224,128]{1,0:T(8,128)(2,1)S(1)} %get-tuple-element.90), channel_id=1, source_target_pairs={{0,8},{1,9},{2,10},{3,11},{4,12},{5,13},{6,14},{7,15},{8,0},{9,1},... | collective-permute-start | bytes 172040 | tf_op jit(solution)/shard_map/ppermute | solution.py:365
  88.0 1.3 %collective-permute-done.22.refs_1_ = bf16[448,128]{1,0:T(8,128)(2,1)S(1)} collective-permute-done((bf16[448,128]{1,0:T(8,128)(2,1)S(1)}, bf16[448,128]{1,0:T(8,128)(2,1)S(1)}, u32[]{:S(2)}, u32[]{:S(2)}) %collective-permute-start.22) | collective-permute-done | bytes 114720 | tf_op jit(solution)/shard_map/ppermute | solution.py:365
  89.4 1.6 %collective-permute-start.23 = (bf16[448,128]{1,0:T(8,128)(2,1)S(1)}, bf16[448,128]{1,0:T(8,128)(2,1)S(1)}, u32[]{:S(2)}, u32[]{:S(2)}) collective-permute-start(bf16[448,128]{1,0:T(8,128)(2,1)S(1)} %coarse_total.1.refs_0_), channel_id=1, source_target_pairs={{0,4},{1,5},{2,6},{3,7},{4,0},{5,1},{6,2},{7,3},{8,12},{9,13},{10,... | collective-permute-start | bytes 344072 | tf_op jit(solution)/shard_map/ppermute | solution.py:365
  91.0 2.0 %collective-permute-start.25 = (bf16[448,128]{1,0:T(8,128)(2,1)S(1)}, bf16[448,128]{1,0:T(8,128)(2,1)S(1)}, u32[]{:S(2)}, u32[]{:S(2)}) collective-permute-start(bf16[448,128]{1,0:T(8,128)(2,1)S(1)} %coarse_total.1.refs_0_), channel_id=1, source_target_pairs={{0,12},{1,13},{2,14},{3,15},{4,8},{5,9},{6,10},{7,11},{8,4},{9,5},... | collective-permute-start | bytes 344072 | tf_op jit(solution)/shard_map/ppermute | solution.py:365
  93.0 1.7 %collective-permute-start.17 = (bf16[224,128]{1,0:T(8,128)(2,1)S(1)}, bf16[224,128]{1,0:T(8,128)(2,1)S(1)}, u32[]{:S(2)}, u32[]{:S(2)}) collective-permute-start(bf16[224,128]{1,0:T(8,128)(2,1)S(1)} %fine_sum2.1.refs_0_), channel_id=1, source_target_pairs={{0,16},{1,17},{2,18},{3,19},{4,20},{5,21},{6,22},{7,23},{8,24},{9,... | collective-permute-start | bytes 172040 | tf_op jit(solution)/shard_map/ppermute | solution.py:365
  94.7 0.1 pad_add_fusion.1.par
  94.8 3.9 %collective-permute-done.17.refs_1_ = bf16[224,128]{1,0:T(8,128)(2,1)S(1)} collective-permute-done((bf16[224,128]{1,0:T(8,128)(2,1)S(1)}, bf16[224,128]{1,0:T(8,128)(2,1)S(1)}, u32[]{:S(2)}, u32[]{:S(2)}) %collective-permute-start.17) | collective-permute-done | bytes 57376 | tf_op jit(solution)/shard_map/ppermute | solution.py:365
  98.7 1.2 %collective-permute-start.18 = (bf16[224,128]{1,0:T(8,128)(2,1)S(1)}, bf16[224,128]{1,0:T(8,128)(2,1)S(1)}, u32[]{:S(2)}, u32[]{:S(2)}) collective-permute-start(bf16[224,128]{1,0:T(8,128)(2,1)S(1)} %fine_total.1.refs_0_), channel_id=1, source_target_pairs={{0,4},{1,5},{2,6},{3,7},{4,0},{5,1},{6,2},{7,3},{8,12},{9,13},{10,... | collective-permute-start | bytes 172040 | tf_op jit(solution)/shard_map/ppermute | solution.py:365
  99.9 1.6 %collective-permute-start.19 = (bf16[224,128]{1,0:T(8,128)(2,1)S(1)}, bf16[224,128]{1,0:T(8,128)(2,1)S(1)}, u32[]{:S(2)}, u32[]{:S(2)}) collective-permute-start(bf16[224,128]{1,0:T(8,128)(2,1)S(1)} %fine_total.1.refs_0_), channel_id=1, source_target_pairs={{0,8},{1,9},{2,10},{3,11},{4,12},{5,13},{6,14},{7,15},{8,0},{9,1},... | collective-permute-start | bytes 172040 | tf_op jit(solution)/shard_map/ppermute | solution.py:365
  101.5 0.8 collective-permute-start.20
  102.3 1.5 %coarse_last.1 = (f32[3,3,3,64,128]{4,3,2,1,0:T(8,128)}, f32[64,128]{1,0:T(8,128)}) custom-call(s32[2]{0:T(128)S(1)} %pad_add_fusion.1.par, bf16[448,128]{1,0:T(8,128)(2,1)S(1)} %coarse_total.1.refs_0_, bf16[448,128]{1,0:T(8,128)(2,1)S(1)} %collective-permute-done.23.refs_1_, bf16[448,128]{1,0:T(8,128)(2,1)S(1)} %collective-permute-done.24.refs_2_, ...), custom_call_target="tpu_custom_call" | custom-call | flops 1000000000 | tf_op jit(solution)/shard_map/coarse_last/pallas_call | solution.py:28
  103.8 0.3 collective-permute-done.19.refs_2_
  104.1 2.5 %collective-permute-done.20.refs_3_ = bf16[224,128]{1,0:T(8,128)(2,1)S(1)} collective-permute-done((bf16[224,128]{1,0:T(8,128)(2,1)S(1)}, bf16[224,128]{1,0:T(8,128)(2,1)S(1)}, u32[]{:S(2)}, u32[]{:S(2)}) %collective-permute-start.20) | collective-permute-done | bytes 57376 | tf_op jit(solution)/shard_map/ppermute | solution.py:365
  106.6 1.4 %fine_last.1 = (f32[3,3,3,32,128]{4,3,2,1,0:T(8,128)}, f32[1,32]{1,0:T(1,128)}, f32[1,64]{1,0:T(1,128)}) custom-call(s32[2]{0:T(128)S(1)} %pad_add_fusion.1.par, bf16[224,128]{1,0:T(8,128)(2,1)S(1)} %fine_total.1.refs_0_, bf16[224,128]{1,0:T(8,128)(2,1)S(1)} %collective-permute-done.18.refs_1_, bf16[224,128]{1,0:T(8,128)(2,1)S(1)} %collective-permute-done.19.refs_2_, ...), custom_call_target="tpu_custom_call" | custom-call | flops 1000000000 | tf_op jit(solution)/shard_map/fine_last/pallas_call | solution.py:28
  (65 shorter events, 0.2 us)
Async XLA Ops:
  0.7 1.2 %copy-start.1 = (bf16[8,16,32,128]{3,2,1,0:T(8,128)(2,1)S(1)}, bf16[8,16,32,128]{3,2,1,0:T(8,128)(2,1)}, u32[]{:S(2)}) copy-start(bf16[8,16,32,128]{3,2,1,0:T(8,128)(2,1)} %field.3) | copy-start | bytes 3145732
  2.9 6.5 %collective-permute-start = (bf16[16,32,128]{2,1,0:T(8,128)(2,1)S(1)}, bf16[16,32,128]{2,1,0:T(8,128)(2,1)S(1)}, u32[]{:S(2)}, u32[]{:S(2)}) collective-permute-start(bf16[16,32,128]{2,1,0:T(8,128)(2,1)S(1)} %get-tuple-element.54), channel_id=1, source_target_pairs={{0,4},{4,0},{8,12},{12,8},{16,20},{20,16},{24,28},{28,24},{1,5},{5... | collective-permute-start | bytes 393224 | tf_op jit(solution)/shard_map/ppermute | solution.py:329
  5.9 5.0 %copy-start.3 = (bf16[8,16,32,128]{3,2,1,0:T(8,128)(2,1)S(1)}, bf16[8,16,32,128]{3,2,1,0:T(8,128)(2,1)}, u32[]{:S(2)}) copy-start(bf16[8,16,32,128]{3,2,1,0:T(8,128)(2,1)} %cot.3) | copy-start | bytes 3145732
  5.9 3.5 %collective-permute-start.1 = (bf16[16,32,128]{2,1,0:T(8,128)(2,1)S(1)}, bf16[16,32,128]{2,1,0:T(8,128)(2,1)S(1)}, u32[]{:S(2)}, u32[]{:S(2)}) collective-permute-start(bf16[16,32,128]{2,1,0:T(8,128)(2,1)S(1)} %get-tuple-element.55), channel_id=1, source_target_pairs={{4,8},{8,4},{12,16},{16,12},{20,24},{24,20},{5,9},{9,5},{13,17},{1... | collective-permute-start | bytes 393224 | tf_op jit(solution)/shard_map/ppermute | solution.py:328
  9.9 1.7 %collective-permute-start.2 = (bf16[10,32,128]{2,1,0:T(8,128)(2,1)S(1)}, bf16[10,32,128]{2,1,0:T(8,128)(2,1)S(1)}, u32[]{:S(2)}, u32[]{:S(2)}) collective-permute-start(bf16[10,32,128]{2,1,0:T(8,128)(2,1)S(1)} %get-tuple-element.56), channel_id=1, source_target_pairs={{0,1},{1,0},{2,3},{3,2},{4,5},{5,4},{6,7},{7,6},{8,9},{9,8},{10,11... | collective-permute-start | bytes 245768 | tf_op jit(solution)/shard_map/ppermute | solution.py:329
  10.0 1.6 %copy-start.2 = (bf16[8,16,32,128]{3,2,1,0:T(8,128)(2,1)S(1)}, bf16[8,16,32,128]{3,2,1,0:T(8,128)(2,1)}, u32[]{:S(2)}) copy-start(bf16[8,16,32,128]{3,2,1,0:T(8,128)(2,1)} %field.3) | copy-start | bytes 3145732
  10.0 1.6 %copy-start.4 = (bf16[3,3,3,128,128]{4,3,2,1,0:T(8,128)(2,1)S(1)}, bf16[3,3,3,128,128]{4,3,2,1,0:T(8,128)(2,1)}, u32[]{:S(2)}) copy-start(bf16[3,3,3,128,128]{4,3,2,1,0:T(8,128)(2,1)} %w.3) | copy-start | bytes 2654212
  10.0 1.6 %copy-start.11 = (f32[128]{0:T(128)S(1)}, f32[128]{0:T(128)}, u32[]{:S(2)}) copy-start(f32[128]{0:T(128)} %param.10) | copy-start | bytes 1540
  10.1 1.6 %collective-permute-start.3 = (bf16[10,32,128]{2,1,0:T(8,128)(2,1)S(1)}, bf16[10,32,128]{2,1,0:T(8,128)(2,1)S(1)}, u32[]{:S(2)}, u32[]{:S(2)}) collective-permute-start(bf16[10,32,128]{2,1,0:T(8,128)(2,1)S(1)} %get-tuple-element.57), channel_id=1, source_target_pairs={{1,2},{2,1},{5,6},{6,5},{9,10},{10,9},{13,14},{14,13},{17,18},{18,... | collective-permute-start | bytes 245768 | tf_op jit(solution)/shard_map/ppermute | solution.py:328
  19.1 1.1 %copy-start.22 = (bf16[10,18,32,128]{3,2,1,0:T(8,128)(2,1)}, bf16[10,18,32,128]{3,2,1,0:T(8,128)(2,1)S(1)}, u32[]{:S(2)}) copy-start(bf16[10,18,32,128]{3,2,1,0:T(8,128)(2,1)S(1)} %get-tuple-element.76.fpad) | copy-start | bytes 4423684
  20.2 8.0 %copy-start.18 = (bf16[8,16,32,128]{3,2,1,0:T(8,128)(2,1)}, bf16[8,16,32,128]{3,2,1,0:T(8,128)(2,1)S(1)}, u32[]{:S(2)}) copy-start(bf16[8,16,32,128]{3,2,1,0:T(8,128)(2,1)S(1)} %get-tuple-element.58.hidden) | copy-start | bytes 3145732
  20.2 8.0 %copy-start.20 = (f32[8,16,32,128]{3,2,1,0:T(8,128)}, f32[8,16,32,128]{3,2,1,0:T(8,128)S(1)}, u32[]{:S(2)}) copy-start(f32[8,16,32,128]{3,2,1,0:T(8,128)S(1)} %get-tuple-element.75.ds) | copy-start | bytes 6291460
  20.2 7.4 %collective-permute-start.4 = (bf16[3,8,16,128]{3,2,1,0:T(8,128)(2,1)S(1)}, bf16[3,8,16,128]{3,2,1,0:T(8,128)(2,1)S(1)}, u32[]{:S(2)}, u32[]{:S(2)}) collective-permute-start(bf16[3,8,16,128]{3,2,1,0:T(8,128)(2,1)S(1)} %get-tuple-element.60), channel_id=1, source_target_pairs={{0,4},{4,0},{8,12},{12,8},{16,20},{20,16},{24,28},{28,24},{1,5},{5... | collective-permute-start | bytes 294920 | tf_op jit(solution)/shard_map/ppermute | solution.py:329
  25.0 2.6 %collective-permute-start.5 = (bf16[3,8,16,128]{3,2,1,0:T(8,128)(2,1)S(1)}, bf16[3,8,16,128]{3,2,1,0:T(8,128)(2,1)S(1)}, u32[]{:S(2)}, u32[]{:S(2)}) collective-permute-start(bf16[3,8,16,128]{3,2,1,0:T(8,128)(2,1)S(1)} %get-tuple-element.61), channel_id=1, source_target_pairs={{4,8},{8,4},{12,16},{16,12},{20,24},{24,20},{5,9},{9,5},{13,17},{1... | collective-permute-start | bytes 294920 | tf_op jit(solution)/shard_map/ppermute | solution.py:328
  27.6 5.5 %copy-start = (bf16[3,3,3,128,256]{4,3,2,1,0:T(8,128)(2,1)S(1)}, bf16[3,3,3,128,256]{4,3,2,1,0:T(8,128)(2,1)}, u32[]{:S(2)}) copy-start(bf16[3,3,3,128,256]{4,3,2,1,0:T(8,128)(2,1)} %w.5) | copy-start | bytes 5308420
  27.6 5.5 %copy-start.9 = (bf16[256,128]{1,0:T(8,128)(2,1)S(1)}, bf16[256,128]{1,0:T(8,128)(2,1)}, u32[]{:S(2)}) copy-start(bf16[256,128]{1,0:T(8,128)(2,1)} %wm.3) | copy-start | bytes 196612
  27.6 5.5 %copy-start.10 = (f32[256]{0:T(256)S(1)}, f32[256]{0:T(256)}, u32[]{:S(2)}) copy-start(f32[256]{0:T(256)} %param.12) | copy-start | bytes 3076
  28.2 4.9 %collective-permute-start.6 = (bf16[22,16,128]{2,1,0:T(8,128)(2,1)S(1)}, bf16[22,16,128]{2,1,0:T(8,128)(2,1)S(1)}, u32[]{:S(2)}, u32[]{:S(2)}) collective-permute-start(bf16[22,16,128]{2,1,0:T(8,128)(2,1)S(1)} %get-tuple-element.62), channel_id=1, source_target_pairs={{0,1},{1,0},{2,3},{3,2},{4,5},{5,4},{6,7},{7,6},{8,9},{9,8},{10,11... | collective-permute-start | bytes 270344 | tf_op jit(solution)/shard_map/ppermute | solution.py:329
  32.1 0.9 collective-permute-start.7
  39.9 0.9 copy-start.12
  40.8 0.8 copy-start.24
  41.6 0.6 copy-start.26
  42.2 8.5 %collective-permute-start.8 = (bf16[2,1792,128]{2,1,0:T(8,128)(2,1)}, bf16[2,1792,128]{2,1,0:T(8,128)(2,1)}, u32[]{:S(2)}, u32[]{:S(2)}) collective-permute-start(bf16[2,1792,128]{2,1,0:T(8,128)(2,1)} %get-tuple-element.65), channel_id=1, source_target_pairs={{0,1},{1,0},{2,3},{3,2},{4,5},{5,4},{6,7},{7,6},{8,9},{9,8},{10,11... | collective-permute-start | bytes 2752520 | tf_op jit(solution)/shard_map/ppermute | solution.py:365
  47.7 1.2 %copy-start.19 = (bf16[8,16,32,128]{3,2,1,0:T(8,128)(2,1)S(1)}, bf16[8,16,32,128]{3,2,1,0:T(8,128)(2,1)}, u32[]{:S(2)}) copy-start(bf16[8,16,32,128]{3,2,1,0:T(8,128)(2,1)} %copy-done.18) | copy-start | bytes 3145732
  48.9 1.8 %copy-start.13 = (bf16[2,1792,128]{2,1,0:T(8,128)(2,1)S(1)}, bf16[2,1792,128]{2,1,0:T(8,128)(2,1)}, u32[]{:S(2)}) copy-start(bf16[2,1792,128]{2,1,0:T(8,128)(2,1)} %copy-done.12) | copy-start | bytes 2752516
  48.9 10.7 %copy-start.25 = (bf16[6,10,16,256]{3,2,1,0:T(8,128)(2,1)S(1)}, bf16[6,10,16,256]{3,2,1,0:T(8,128)(2,1)}, u32[]{:S(2)}) copy-start(bf16[6,10,16,256]{3,2,1,0:T(8,128)(2,1)} %copy-done.24) | copy-start | bytes 1474564
  50.8 8.8 %copy-start.21 = (f32[8,16,32,128]{3,2,1,0:T(8,128)S(1)}, f32[8,16,32,128]{3,2,1,0:T(8,128)}, u32[]{:S(2)}) copy-start(f32[8,16,32,128]{3,2,1,0:T(8,128)} %copy-done.20) | copy-start | bytes 6291460
  50.8 8.8 %copy-start.23 = (bf16[10,18,32,128]{3,2,1,0:T(8,128)(2,1)S(1)}, bf16[10,18,32,128]{3,2,1,0:T(8,128)(2,1)}, u32[]{:S(2)}) copy-start(bf16[10,18,32,128]{3,2,1,0:T(8,128)(2,1)} %copy-done.22) | copy-start | bytes 4423684
  50.8 8.8 %copy-start.27 = (bf16[256,128]{1,0:T(8,128)(2,1)S(1)}, bf16[256,128]{1,0:T(8,128)(2,1)}, u32[]{:S(2)}) copy-start(bf16[256,128]{1,0:T(8,128)(2,1)} %copy-done.26) | copy-start | bytes 196612
  52.4 0.7 copy-start.16
  53.1 16.2 %collective-permute-start.10 = (bf16[1,896,128]{2,1,0:T(8,128)(2,1)S(1)}, bf16[1,896,128]{2,1,0:T(8,128)(2,1)S(1)}, u32[]{:S(2)}, u32[]{:S(2)}) collective-permute-start(bf16[1,896,128]{2,1,0:T(8,128)(2,1)S(1)} %get-tuple-element.82), channel_id=1, source_target_pairs={{0,2},{1,3},{2,0},{3,1},{4,6},{5,7},{6,4},{7,5},{8,10},{9,11},{10,... | collective-permute-start | bytes 688136 | tf_op jit(solution)/shard_map/ppermute | solution.py:365
  54.7 14.6 %collective-permute-start.11 = (bf16[1,896,128]{2,1,0:T(8,128)(2,1)S(1)}, bf16[1,896,128]{2,1,0:T(8,128)(2,1)S(1)}, u32[]{:S(2)}, u32[]{:S(2)}) collective-permute-start(bf16[1,896,128]{2,1,0:T(8,128)(2,1)S(1)} %get-tuple-element.83), channel_id=1, source_target_pairs={{0,4},{1,5},{2,6},{3,7},{4,0},{5,1},{6,2},{7,3},{8,12},{9,13},{10,... | collective-permute-start | bytes 688136 | tf_op jit(solution)/shard_map/ppermute | solution.py:365
  59.6 10.6 %collective-permute-start.9 = (bf16[1,896,128]{2,1,0:T(8,128)(2,1)S(1)}, bf16[1,896,128]{2,1,0:T(8,128)(2,1)S(1)}, u32[]{:S(2)}, u32[]{:S(2)}) collective-permute-start(bf16[1,896,128]{2,1,0:T(8,128)(2,1)S(1)} %get-tuple-element.81), channel_id=1, source_target_pairs={{0,6},{1,7},{2,4},{3,5},{4,2},{5,3},{6,0},{7,1},{8,14},{9,15},{10,... | collective-permute-start | bytes 688136 | tf_op jit(solution)/shard_map/ppermute | solution.py:365
  68.5 0.8 copy-start.14
  69.3 0.7 copy-start.5
  70.2 0.7 copy-start.7
  70.9 6.2 %collective-permute-start.12 = (bf16[2,896,128]{2,1,0:T(8,128)(2,1)S(1)}, bf16[2,896,128]{2,1,0:T(8,128)(2,1)S(1)}, u32[]{:S(2)}, u32[]{:S(2)}) collective-permute-start(bf16[2,896,128]{2,1,0:T(8,128)(2,1)S(1)} %get-tuple-element.84), channel_id=1, source_target_pairs={{0,1},{1,0},{2,3},{3,2},{4,5},{5,4},{6,7},{7,6},{8,9},{9,8},{10,11... | collective-permute-start | bytes 1376264 | tf_op jit(solution)/shard_map/ppermute | solution.py:365
  70.9 0.9 copy-start.6
  71.9 0.9 copy-start.8
  72.8 0.9 copy-start.17
  73.7 3.4 %copy-start.15 = (bf16[2,896,128]{2,1,0:T(8,128)(2,1)S(1)}, bf16[2,896,128]{2,1,0:T(8,128)(2,1)}, u32[]{:S(2)}) copy-start(bf16[2,896,128]{2,1,0:T(8,128)(2,1)} %copy-done.14) | copy-start | bytes 1376260
  73.9 7.5 %collective-permute-start.21 = (bf16[448,128]{1,0:T(8,128)(2,1)S(1)}, bf16[448,128]{1,0:T(8,128)(2,1)S(1)}, u32[]{:S(2)}, u32[]{:S(2)}) collective-permute-start(bf16[448,128]{1,0:T(8,128)(2,1)S(1)} %get-tuple-element.98), channel_id=1, source_target_pairs={{0,8},{1,9},{2,10},{3,11},{4,12},{5,13},{6,14},{7,15},{8,0},{9,1},... | collective-permute-start | bytes 344072 | tf_op jit(solution)/shard_map/ppermute | solution.py:365
  77.8 6.4 %collective-permute-start.13 = (bf16[1,448,128]{2,1,0:T(8,128)(2,1)S(1)}, bf16[1,448,128]{2,1,0:T(8,128)(2,1)S(1)}, u32[]{:S(2)}, u32[]{:S(2)}) collective-permute-start(bf16[1,448,128]{2,1,0:T(8,128)(2,1)S(1)} %get-tuple-element.86), channel_id=1, source_target_pairs={{0,6},{1,7},{2,4},{3,5},{4,2},{5,3},{6,0},{7,1},{8,14},{9,15},{10,... | collective-permute-start | bytes 344072 | tf_op jit(solution)/shard_map/ppermute | solution.py:365
  80.5 6.0 %collective-permute-start.14 = (bf16[1,448,128]{2,1,0:T(8,128)(2,1)S(1)}, bf16[1,448,128]{2,1,0:T(8,128)(2,1)S(1)}, u32[]{:S(2)}, u32[]{:S(2)}) collective-permute-start(bf16[1,448,128]{2,1,0:T(8,128)(2,1)S(1)} %get-tuple-element.87), channel_id=1, source_target_pairs={{0,2},{1,3},{2,0},{3,1},{4,6},{5,7},{6,4},{7,5},{8,10},{9,11},{10,... | collective-permute-start | bytes 344072 | tf_op jit(solution)/shard_map/ppermute | solution.py:365
  80.8 6.0 %collective-permute-start.15 = (bf16[1,448,128]{2,1,0:T(8,128)(2,1)S(1)}, bf16[1,448,128]{2,1,0:T(8,128)(2,1)S(1)}, u32[]{:S(2)}, u32[]{:S(2)}) collective-permute-start(bf16[1,448,128]{2,1,0:T(8,128)(2,1)S(1)} %get-tuple-element.88), channel_id=1, source_target_pairs={{0,4},{1,5},{2,6},{3,7},{4,0},{5,1},{6,2},{7,3},{8,12},{9,13},{10,... | collective-permute-start | bytes 344072 | tf_op jit(solution)/shard_map/ppermute | solution.py:365
  81.4 8.0 %collective-permute-start.22 = (bf16[448,128]{1,0:T(8,128)(2,1)S(1)}, bf16[448,128]{1,0:T(8,128)(2,1)S(1)}, u32[]{:S(2)}, u32[]{:S(2)}) collective-permute-start(bf16[448,128]{1,0:T(8,128)(2,1)S(1)} %coarse_sum2.1.refs_0_), channel_id=1, source_target_pairs={{0,16},{1,17},{2,18},{3,19},{4,20},{5,21},{6,22},{7,23},{8,24},{9,... | collective-permute-start | bytes 344072 | tf_op jit(solution)/shard_map/ppermute | solution.py:365
  86.8 6.1 %collective-permute-start.16 = (bf16[224,128]{1,0:T(8,128)(2,1)S(1)}, bf16[224,128]{1,0:T(8,128)(2,1)S(1)}, u32[]{:S(2)}, u32[]{:S(2)}) collective-permute-start(bf16[224,128]{1,0:T(8,128)(2,1)S(1)} %get-tuple-element.90), channel_id=1, source_target_pairs={{0,8},{1,9},{2,10},{3,11},{4,12},{5,13},{6,14},{7,15},{8,0},{9,1},... | collective-permute-start | bytes 172040 | tf_op jit(solution)/shard_map/ppermute | solution.py:365
  89.4 12.1 %collective-permute-start.23 = (bf16[448,128]{1,0:T(8,128)(2,1)S(1)}, bf16[448,128]{1,0:T(8,128)(2,1)S(1)}, u32[]{:S(2)}, u32[]{:S(2)}) collective-permute-start(bf16[448,128]{1,0:T(8,128)(2,1)S(1)} %coarse_total.1.refs_0_), channel_id=1, source_target_pairs={{0,4},{1,5},{2,6},{3,7},{4,0},{5,1},{6,2},{7,3},{8,12},{9,13},{10,... | collective-permute-start | bytes 344072 | tf_op jit(solution)/shard_map/ppermute | solution.py:365
  91.0 11.3 %collective-permute-start.24 = (bf16[448,128]{1,0:T(8,128)(2,1)S(1)}, bf16[448,128]{1,0:T(8,128)(2,1)S(1)}, u32[]{:S(2)}, u32[]{:S(2)}) collective-permute-start(bf16[448,128]{1,0:T(8,128)(2,1)S(1)} %coarse_total.1.refs_0_), channel_id=1, source_target_pairs={{0,8},{1,9},{2,10},{3,11},{4,12},{5,13},{6,14},{7,15},{8,0},{9,1},... | collective-permute-start | bytes 344072 | tf_op jit(solution)/shard_map/ppermute | solution.py:365
  91.0 11.3 %collective-permute-start.25 = (bf16[448,128]{1,0:T(8,128)(2,1)S(1)}, bf16[448,128]{1,0:T(8,128)(2,1)S(1)}, u32[]{:S(2)}, u32[]{:S(2)}) collective-permute-start(bf16[448,128]{1,0:T(8,128)(2,1)S(1)} %coarse_total.1.refs_0_), channel_id=1, source_target_pairs={{0,12},{1,13},{2,14},{3,15},{4,8},{5,9},{6,10},{7,11},{8,4},{9,5},... | collective-permute-start | bytes 344072 | tf_op jit(solution)/shard_map/ppermute | solution.py:365
  93.0 5.7 %collective-permute-start.17 = (bf16[224,128]{1,0:T(8,128)(2,1)S(1)}, bf16[224,128]{1,0:T(8,128)(2,1)S(1)}, u32[]{:S(2)}, u32[]{:S(2)}) collective-permute-start(bf16[224,128]{1,0:T(8,128)(2,1)S(1)} %fine_sum2.1.refs_0_), channel_id=1, source_target_pairs={{0,16},{1,17},{2,18},{3,19},{4,20},{5,21},{6,22},{7,23},{8,24},{9,... | collective-permute-start | bytes 172040 | tf_op jit(solution)/shard_map/ppermute | solution.py:365
  98.7 5.1 %collective-permute-start.18 = (bf16[224,128]{1,0:T(8,128)(2,1)S(1)}, bf16[224,128]{1,0:T(8,128)(2,1)S(1)}, u32[]{:S(2)}, u32[]{:S(2)}) collective-permute-start(bf16[224,128]{1,0:T(8,128)(2,1)S(1)} %fine_total.1.refs_0_), channel_id=1, source_target_pairs={{0,4},{1,5},{2,6},{3,7},{4,0},{5,1},{6,2},{7,3},{8,12},{9,13},{10,... | collective-permute-start | bytes 172040 | tf_op jit(solution)/shard_map/ppermute | solution.py:365
  99.9 4.2 %collective-permute-start.19 = (bf16[224,128]{1,0:T(8,128)(2,1)S(1)}, bf16[224,128]{1,0:T(8,128)(2,1)S(1)}, u32[]{:S(2)}, u32[]{:S(2)}) collective-permute-start(bf16[224,128]{1,0:T(8,128)(2,1)S(1)} %fine_total.1.refs_0_), channel_id=1, source_target_pairs={{0,8},{1,9},{2,10},{3,11},{4,12},{5,13},{6,14},{7,15},{8,0},{9,1},... | collective-permute-start | bytes 172040 | tf_op jit(solution)/shard_map/ppermute | solution.py:365
  101.5 5.1 %collective-permute-start.20 = (bf16[224,128]{1,0:T(8,128)(2,1)S(1)}, bf16[224,128]{1,0:T(8,128)(2,1)S(1)}, u32[]{:S(2)}, u32[]{:S(2)}) collective-permute-start(bf16[224,128]{1,0:T(8,128)(2,1)S(1)} %fine_total.1.refs_0_), channel_id=1, source_target_pairs={{0,12},{1,13},{2,14},{3,15},{4,8},{5,9},{6,10},{7,11},{8,4},{9,5},... | collective-permute-start | bytes 172040 | tf_op jit(solution)/shard_map/ppermute | solution.py:365

commit v3 on v2

--- a/solution.py
+++ b/solution.py
@@ -12,7 +12,7 @@
 VMEM_LIMIT = 32 * 1024 * 1024
 
 
-def call(body, name, args, outs, scratch=(), micros=1):
+def call(body, name, args, outs, scratch=(), micros=1, limit=VMEM_LIMIT):
     specs = [pl.BlockSpec(memory_space=pltpu.SMEM)]
     arrays = [args[0]]
     for arg in args[1:]:
@@ -33,7 +33,7 @@
         in_specs=specs,
         out_specs=[pl.BlockSpec(memory_space=pltpu.VMEM) for _ in outs],
         scratch_shapes=list(scratch),
-        compiler_params=pltpu.CompilerParams(vmem_limit_bytes=VMEM_LIMIT),
+        compiler_params=pltpu.CompilerParams(vmem_limit_bytes=limit),
         cost_estimate=pl.CostEstimate(
             flops=int(micros * 1e9), bytes_accessed=0, transcendentals=0
         ),
@@ -68,64 +68,76 @@
     return 1.0 / (1.0 + jnp.exp(-value))
 
 
-def prep_body(par, field, out_a, out_b, sems):
-    odd, end = par[0], field.shape[0] - 1
-    one = pltpu.make_async_copy(field.at[(1 - odd) * end], out_a, sems.at[0])
-    two = pltpu.make_async_copy(field.at[odd * end], out_b, sems.at[1])
+def prep_body(sub, par, field, out_a, out_b, sems):
+    odd, end = par[sub], field.shape[1] - 1
+    one = pltpu.make_async_copy(field.at[:, (1 - odd) * end], out_a, sems.at[0])
+    two = pltpu.make_async_copy(field.at[:, odd * end], out_b, sems.at[1])
     one.start()
     two.start()
     one.wait()
     two.wait()
 
 
-def turn_body(par, lo, hi, ra, rb, out_a, out_b):
-    bx, _, bz, c = lo.shape
-    xlo, xhi = get_faces(par[0] == 1, ra, rb)
-
-    def side(face, y):
-        return jnp.concatenate([xlo[y : y + 1], face[:, 0], xhi[y : y + 1]], axis=0)
-
-    put_faces(par[1] == 1, out_a, out_b, side(lo, 0), side(hi, xlo.shape[0] - 1))
-
-
-def fine_body(par, field, ra, rb, ua, ub, w, bias, pg, fpad, hidden, ds, pooled, out_a, out_b, wb, tmp):
-    bx, by, bz, c = field.shape
-    cx, cy, cz = bx // 2, by // 2, bz // 2
+def turn_body(sub, par, field, ya, yb, own, out_a, out_b):
+    bx, by = field.shape[0], field.shape[1]
+    ylo, yhi = get_faces(par[sub] == 1, ya, yb)
+    own[:, 1 : by + 1] = field[...]
+    own[:, 0] = ylo
+    own[:, by + 1] = yhi
+    put_faces(par[0] == 1, out_a, out_b, own[0], own[bx - 1])
+
+
+def fine_plane(three, wb, bias, by):
+    _, bz, c = three[0].shape
     rows = by * bz
-    xlo, xhi = get_faces(par[0] == 1, ra, rb)
-    ylo, yhi = get_faces(par[1] == 1, ua, ub)
-    fpad[1 : bx + 1, 1 : by + 1] = field[...]
-    fpad[0, 1 : by + 1] = xlo
-    fpad[bx + 1, 1 : by + 1] = xhi
-    fpad[:, 0] = ylo
-    fpad[:, by + 1] = yhi
+    taps = [plane[j : j + by].reshape(rows, c) for plane in three for j in range(3)]
+    part = jnp.dot(jnp.concatenate(taps, axis=1), wb[...], preferred_element_type=F32)
+    pre = (
+        part[:, c : 2 * c]
+        + shift_rows(part[:, :c], 1, bz)
+        + shift_rows(part[:, 2 * c :], -1, bz)
+        + bias[...]
+    )
+    sig = sigmoid(pre)
+    hid = (pre * sig).astype(BF16).reshape(by, bz, c)
+    return hid, (sig * (1.0 + pre * (1.0 - sig))).reshape(by, bz, c)
+
+
+def pool(one, two, tmp):
+    by, bz, c = one.shape
+    cy = by // 2
+    both = jnp.sum((one.astype(F32) + two.astype(F32)).reshape(cy, 2, bz, c), axis=1)
+    total = sum_cube(cy * bz, both.reshape(cy * bz, c), tmp)
+    return (total / 8.0).astype(BF16).reshape(cy, bz // 2, c)
+
+
+def inner_body(par, own, w, bias, hidden, ds, pooled, wb, tmp):
+    by, c = own.shape[1] - 2, own.shape[3]
     for i in range(3):
         for j in range(3):
             for k in range(3):
                 wb[pl.ds((3 * i + j) * c, c), pl.ds(k * c, c)] = w[i, j, k]
 
-    def plane(x):
-        taps = [fpad[x + i, j : j + by].reshape(rows, c) for i in range(3) for j in range(3)]
-        part = jnp.dot(jnp.concatenate(taps, axis=1), wb[...], preferred_element_type=F32)
-        pre = (
-            part[:, c : 2 * c]
-            + shift_rows(part[:, :c], 1, bz)
-            + shift_rows(part[:, 2 * c :], -1, bz)
-            + bias[...]
-        )
-        sig = sigmoid(pre)
-        hid = (pre * sig).astype(BF16)
-        hidden[x] = hid.reshape(by, bz, c)
-        ds[x] = (sig * (1.0 + pre * (1.0 - sig))).reshape(by, bz, c)
-        return hid.astype(F32)
-
-    def pair(q, carry):
-        both = plane(2 * q) + plane(2 * q + 1)
-        both = jnp.sum(both.reshape(cy, 2, bz, c), axis=1).reshape(cy * bz, c)
-        pooled[q] = (sum_cube(cy * bz, both, tmp) / 8.0).astype(BF16).reshape(cy, cz, c)
+    def plane(x, carry):
+        hid, slope = fine_plane([own[x], own[x + 1], own[x + 2]], wb, bias, by)
+        hidden[x], ds[x] = hid, slope
         return carry
 
-    lax.fori_loop(0, cx, pair, 0)
+    lax.fori_loop(0, hidden.shape[0], plane, 0)
+    for q in range(pooled.shape[0]):
+        pooled[q] = pool(hidden[2 * q + 1], hidden[2 * q + 2], tmp)
+
+
+def outer_body(par, own, ra, rb, wb, bias, hid_in, pool_in, pg, hidden, ds, halo, pooled, out_a, out_b, tmp):
+    bx, by = own.shape[0], own.shape[1] - 2
+    cx = bx // 2
+    xlo, xhi = get_faces(par[0] == 1, ra, rb)
+    halo[0], halo[1] = xlo, xhi
+    for at, three in ((0, [halo[0], own[0], own[1]]), (1, [own[bx - 2], own[bx - 1], halo[1]])):
+        hidden[at], ds[at] = fine_plane(three, wb, bias, by)
+    pooled[0] = pool(hidden[0], hid_in[0], tmp)
+    pooled[1 : cx - 1] = pool_in[...]
+    pooled[cx - 1] = pool(hid_in[bx - 3], hidden[1], tmp)
     low = jnp.concatenate([pooled[0:2], pg[0:1]], axis=0)
     high = jnp.concatenate([pooled[cx - 2 : cx], pg[cx - 1 : cx]], axis=0)
     put_faces(par[0] == 1, out_a, out_b, low, high)
@@ -139,7 +151,7 @@
     pg[...] = grad.reshape(cx, cy, cz, c)
 
 
-def turn2_body(par, pooled, pg, ra, rb, out_a, out_b):
+def turn2_body(sub, par, pooled, pg, ra, rb, out_a, out_b):
     cy = pooled.shape[1]
     xlo, xhi = get_faces(par[0] == 1, ra, rb)
 
@@ -148,7 +160,7 @@
         one = jnp.concatenate([xlo[2:3, last], pg[:, last], xhi[2:3, last]], axis=0)
         return jnp.concatenate([*two, one], axis=0)
 
-    put_faces(par[1] == 1, out_a, out_b, side(0, 0), side(cy - 2, cy - 1))
+    put_faces(par[sub] == 1, out_a, out_b, side(0, 0), side(cy - 2, cy - 1))
 
 
 def reverse_bits(value, count):
@@ -174,13 +186,13 @@
 
 
 def coarse_body(
-    n, par, pooled, ra, rb, ua, ub, pg, w, bias, wm,
+    n, sub, par, pooled, ra, rb, ua, ub, pg, w, bias, wm,
     slope, coarse, keep, send, cbias, qpad, gpad, wb, st, rhs, acc, ct,
 ):
     cx, cy, cz, c = pooled.shape
     c2 = wm.shape[0]
     xlo, xhi = get_faces(par[0] == 1, ra, rb)
-    ylo, yhi = get_faces(par[1] == 1, ua, ub)
+    ylo, yhi = get_faces(par[sub] == 1, ua, ub)
     qpad[2 : cx + 2, 2 : cy + 2] = pooled[...]
     qpad[0:2, 2 : cy + 2] = xlo[0:2]
     qpad[cx + 2 : cx + 4, 2 : cy + 2] = xhi[0:2]
@@ -247,10 +259,10 @@
         k, tap = t // 9, t % 9
         return acc[pl.ds(k * c2 + s * per, per), pl.ds(tap * c, c)]
 
-    spread(par[2], keep, send, n, 28, piece)
-
-
-def back_body(n, par, slope, w, cot, ds, fpad, cbias, keep, send, up, st, rhs, acc):
+    spread(par[sub], keep, send, n, 28, piece)
+
+
+def back_body(n, sub, par, slope, w, cot, ds, ds_edge, own, halo, cbias, keep, send, up, st, rhs, acc):
     bx, by, bz, c = cot.shape
     cx, cy, cz = bx // 2, by // 2, bz // 2
     c2 = slope.shape[3]
@@ -276,7 +288,8 @@
     for x in range(bx):
         base = up[pl.ds((x // 2) * cy * bz, cy * bz), :].reshape(cy, 1, bz, c)
         fine = cot[x].astype(F32).reshape(cy, 2, bz, c) + base
-        fs = (fine.reshape(rows, c) * ds[x].reshape(rows, c)).astype(BF16)
+        gain = ds[x - 1] if 0 < x < bx - 1 else ds_edge[x // (bx - 1)]
+        fs = (fine.reshape(rows, c) * gain.reshape(rows, c)).astype(BF16)
         wide = fs.astype(F32)
         st[pl.ds(0, c), pl.ds(x * rows, rows)] = shift_rows(wide, -1, bz).astype(BF16).T
         st[pl.ds(c, c), pl.ds(x * rows, rows)] = fs.T
@@ -288,7 +301,13 @@
             if t + h == 9:
                 rhs[:, pl.ds(h * c, c)] = jnp.ones((voxels, c), BF16)
             else:
-                rhs[:, pl.ds(h * c, c)] = fpad[i : i + bx, j : j + by].reshape(voxels, c)
+                first, past = max(i - 1, 0), min(i - 1 + bx, bx)
+                at = (first - i + 1) * rows
+                size = (past - first) * rows
+                rhs[pl.ds(at, size), pl.ds(h * c, c)] = own[first:past, j : j + by].reshape(size, c)
+                if i != 1:
+                    edge = halo[i // 2, j : j + by].reshape(rows, c)
+                    rhs[pl.ds(0 if i == 0 else size, rows), pl.ds(h * c, c)] = edge
         acc[:, pl.ds(t * c, 2 * c)] = jnp.dot(
             st[...], rhs[...], preferred_element_type=F32
         ).astype(BF16)
@@ -304,11 +323,11 @@
         k, tap = t // 9, t % 9
         return acc[pl.ds(k * c + s * per, per), pl.ds(tap * c, c)]
 
-    spread(par[2], keep, send, n, 28, piece)
-
-
-def merge_body(par, hidden, coarse, wm, out, tmp):
-    bx, by, bz, c = hidden.shape
+    spread(par[sub], keep, send, n, 28, piece)
+
+
+def merge_body(par, hidden, hid_edge, coarse, wm, out, tmp):
+    bx, by, bz, c = out.shape
     cx, cy, cz = bx // 2, by // 2, bz // 2
     c2 = coarse.shape[3]
     cells = cx * cy * cz
@@ -317,7 +336,8 @@
     tmp[pl.ds(1, cells, stride=2), :] = proj
     for x in range(bx):
         base = tmp[pl.ds((x // 2) * cy * bz, cy * bz), :].reshape(cy, 1, bz, c)
-        total = hidden[x].astype(F32).reshape(cy, 2, bz, c) + base
+        hid = hidden[x - 1] if 0 < x < bx - 1 else hid_edge[x // (bx - 1)]
+        total = hid.astype(F32).reshape(cy, 2, bz, c) + base
         out[x] = total.astype(BF16).reshape(by, bz, c)
 
 
@@ -329,8 +349,8 @@
     return lax.ppermute(first, axis, one), got
 
 
-def split4_body(par, keep, got, own, over_sub, over_grp, over_both):
-    g, s = par[0], par[1]
+def split4_body(at_grp, at_sub, par, keep, got, own, over_sub, over_grp, over_both):
+    g, s = par[at_grp], par[at_sub]
 
     def part(a, b):
         return (keep[a, :, b].astype(F32) + got[a, :, b].astype(F32)).astype(BF16)
@@ -341,14 +361,14 @@
     own[...] = part(s, g)
 
 
-def split_body(count, par, *refs):
+def split_body(count, bit, par, *refs):
     parts, keep, send = refs[:count], refs[count], refs[count + 1]
 
     def part(at):
         return sum(p[at].astype(F32) for p in parts).astype(BF16)
 
-    send[...] = part(1 - par[0])
-    keep[...] = part(par[0])
+    send[...] = part(1 - par[bit])
+    keep[...] = part(par[bit])
 
 
 def sum_body(count, par, *refs):
@@ -365,13 +385,17 @@
     return lax.ppermute(value, ("grp", "sub"), pairs)
 
 
-def split_sum(parts, bit, name):
+def split_sum(parts, bits, bit, name):
     rows, c = parts[0].shape
     half = ((rows // 2, c), BF16)
     shaped = [p.reshape(2, rows // 2, c) for p in parts]
     return call(
-        functools.partial(split_body, len(parts)), name, (bit.reshape(1), *shaped), [half, half], (), 0.8
-    )
+        functools.partial(split_body, len(parts), bit), name, (bits, *shaped), [half, half], (), 0.8
+    )
+
+
+def grp_bits():
+    return lax.axis_size("grp").bit_length() - 1
 
 
 def cores(send):
@@ -384,7 +408,7 @@
     shape = (2, rest, 2, rows // 2, c)
     out = ((rest, rows // 2, c), BF16)
     own, over_sub, over_grp, over_both = call(
-        split4_body, name, (bits, keep.reshape(shape), got.reshape(shape)), [out] * 4, (), 1
+        functools.partial(split4_body, 0, grp_bits() + 1), name, (bits, keep.reshape(shape), got.reshape(shape)), [out] * 4, (), 1
     )
     return own, over_sub, over_grp, over_both
 
@@ -393,28 +417,28 @@
     return [own, partners(over_both, 1, 2), partners(over_sub, 0, 2), partners(over_grp, 1, 0)]
 
 
-def finish_sum(parts, sub, grp, name):
+def finish_sum(parts, places, name):
     rest, rows, c = parts[0].shape
     parts = [p.reshape(rest * rows, c) for p in parts]
     for bit in range(2, lax.axis_size("sub").bit_length() - 1):
-        keep, send = split_sum(parts, (sub >> bit) & 1, name + f"_sub{bit}")
+        keep, send = split_sum(parts, places, grp_bits() + bit, name + f"_sub{bit}")
         parts = [keep, partners(send, 0, 1 << bit)]
     bits = [0]
-    last = lax.axis_size("grp").bit_length() - 2
+    last = grp_bits() - 1
     for bit in range(1, last + 1):
         mask = 1 << bit
         if bit == 1 and bit < last and parts[0].shape[0] % 32 == 0:
-            keep, send = split_sum(parts, (grp >> bit) & 1, name + "_half")
+            keep, send = split_sum(parts, places, bit, name + "_half")
             parts = [keep, partners(send, mask, 0)]
             bits.append(bit)
             continue
         out = [(parts[0].shape, BF16)]
         (total,) = call(
-            functools.partial(sum_body, len(parts)), name + f"_sum{bit}", (sub.reshape(1), *parts), out, (), 0.5
+            functools.partial(sum_body, len(parts)), name + f"_sum{bit}", (places, *parts), out, (), 0.5
         )
         parts = [total, partners(total, mask, 0)]
     (total,) = call(
-        functools.partial(sum_body, len(parts)), name + "_total", (sub.reshape(1), *parts), [(parts[0].shape, BF16)], (), 0.5
+        functools.partial(sum_body, len(parts)), name + "_total", (places, *parts), [(parts[0].shape, BF16)], (), 0.5
     )
     pieces = [total]
     for which in range(1, 2 ** len(bits)):
@@ -449,14 +473,13 @@
         refs[count + 2][:, pl.ds(per, per)] = turned[2:3]
 
 
-def last(pieces, bits, grp, per, outs, name):
+def last(pieces, bits, places, per, outs, name):
     count = len(pieces)
     size, c = pieces[0].shape
-    order = jnp.stack([(grp >> b) & 1 for b in (bits + bits)[:2]]).astype(jnp.int32)
     kernel, *rest = call(
         functools.partial(last_body, count),
         name,
-        (order, *pieces),
+        (places, *pieces),
         [((3, 3, 3, per, c), F32), *outs],
         [pltpu.VMEM((count, size, c), BF16)],
         1,
@@ -470,45 +493,68 @@
     bx, by, bz, c = field.shape
     cx, cy, cz = bx // 2, by // 2, bz // 2
     c2 = merge_weight.shape[0]
-    par = jnp.stack([grp & 1, sub & 1, sub & 1]).astype(jnp.int32)
-    cross_bits = jnp.stack([grp & 1, (sub >> 1) & 1]).astype(jnp.int32)
-    ylo = (field, (bx, 1, bz, c), (0, 0, 0, 0))
-    yhi = (field, (bx, 1, bz, c), (0, by - 1, 0, 0))
-    face = ((by, bz, c), BF16)
+    count = grp_bits()
+    order = jnp.arange(count + n.bit_length() - 1, dtype=jnp.int32)
+    par = jnp.where(order < count, grp >> order, sub >> (order - count)).astype(jnp.int32) & 1
+    face = ((bx, bz, c), BF16)
     sa, sb = call(
-        prep_body, "prep", (par, (field, None, None)), [face, face], [pltpu.SemaphoreType.DMA((2,))]
-    )
-    xa, xb = swap_faces(sa, sb, "grp")
+        functools.partial(prep_body, count),
+        "prep",
+        (par, (field, None, None)),
+        [face, face],
+        [pltpu.SemaphoreType.DMA((2,))],
+        limit=127 * 512 * 1024,
+    )
+    ya, yb = swap_faces(sa, sb, "sub")
     (pg,) = call(
         cubes_body, "cubes", (par, cotangent), [((cx, cy, cz, c), BF16)], [pltpu.VMEM((cx * cy * bz, c), F32)]
     )
-    face = ((bx + 2, bz, c), BF16)
-    ta, tb = call(turn_body, "turn", (par, ylo, yhi, xa, xb), [face, face])
-    ya, yb = swap_faces(ta, tb, "sub")
+    face = ((by + 2, bz, c), BF16)
+    own, ta, tb = call(
+        functools.partial(turn_body, count),
+        "turn",
+        (par, field, ya, yb),
+        [((bx, by + 2, bz, c), BF16), face, face],
+    )
+    xa, xb = swap_faces(ta, tb, "grp")
+    bias = fine_bias.reshape(1, c)
+    hidden, ds, pooled, wb = call(
+        inner_body,
+        "inner",
+        (par, own, fine_kernel, bias),
+        [
+            ((bx - 2, by, bz, c), BF16),
+            ((bx - 2, by, bz, c), F32),
+            ((cx - 2, cy, cz, c), BF16),
+            ((9 * c, 3 * c), BF16),
+        ],
+        [pltpu.VMEM((cy * bz, c), F32)],
+        6,
+    )
     face = ((3, cy, cz, c), BF16)
-    fpad, hidden, ds, pooled, pa, pb = call(
-        fine_body,
-        "fine",
-        (par, field, xa, xb, ya, yb, fine_kernel, fine_bias.reshape(1, c), pg),
+    hid_edge, ds_edge, halo, pooled, pa, pb = call(
+        outer_body,
+        "outer",
+        (par, own, xa, xb, wb, bias, hidden, pooled, pg),
         [
-            ((bx + 2, by + 2, bz, c), BF16),
-            ((bx, by, bz, c), BF16),
-            ((bx, by, bz, c), F32),
+            ((2, by, bz, c), BF16),
+            ((2, by, bz, c), F32),
+            ((2, by + 2, bz, c), BF16),
             ((cx, cy, cz, c), BF16),
             face,
             face,
         ],
-        [pltpu.VMEM((9 * c, 3 * c), BF16), pltpu.VMEM((cy * bz, c), F32)],
-        8,
+        [pltpu.VMEM((cy * bz, c), F32)],
+        2,
     )
     pxa, pxb = swap_faces(pa, pb, "grp")
     face = ((2 * (cx + 4) + cx + 2, cz, c), BF16)
-    qa, qb = call(turn2_body, "turn2", (par, pooled, pg, pxa, pxb), [face, face])
+    qa, qb = call(functools.partial(turn2_body, count), "turn2", (par, pooled, pg, pxa, pxb), [face, face])
     pya, pyb = swap_faces(qa, qb, "sub")
     cells = cx * cy * cz
     part = (n // 2, 28 * (c2 // n), c)
     slope, coarse, ckeep, csend, cbias = call(
-        functools.partial(coarse_body, n),
+        functools.partial(coarse_body, n, count),
         "coarse",
         (par, pooled, pxa, pxb, pya, pyb, pg, coarse_kernel, coarse_bias.reshape(1, c2), merge_weight),
         [
@@ -533,21 +579,21 @@
     (output,) = call(
         merge_body,
         "merge",
-        (par, hidden, coarse, merge_weight),
+        (par, hidden, hid_edge, coarse, merge_weight),
         [((bx, by, bz, c), BF16)],
         [pltpu.VMEM((cx * cy * bz, c), F32)],
         2,
     )
     output, cgot = lax.optimization_barrier((output, cgot))
-    csent = spread_sum(ckeep, cgot, cross_bits, "coarse_split")
+    csent = spread_sum(ckeep, cgot, par, "coarse_split")
     slope, csent = lax.optimization_barrier((slope, csent))
     cparts = cross(*csent)
     voxels = bx * by * bz
     part = (n // 2, 28 * (c // n), c)
     fkeep, fsend = call(
-        functools.partial(back_body, n),
+        functools.partial(back_body, n, count),
         "back",
-        (par, slope, coarse_kernel, cotangent, ds, fpad, cbias),
+        (par, slope, coarse_kernel, cotangent, ds, ds_edge, own, halo, cbias),
         [(part, BF16), (part, BF16)],
         [
             pltpu.VMEM((cx * cy * bz, c), F32),
@@ -559,13 +605,13 @@
     )
     fsend, cparts = lax.optimization_barrier((fsend, cparts))
     fgot = cores(fsend)
-    fparts = cross(*spread_sum(fkeep, fgot, cross_bits, "fine_split"))
-    coarse_sum = finish_sum(cparts, sub, grp, "coarse")
-    fine_sum = finish_sum(fparts, sub, grp, "fine")
+    fparts = cross(*spread_sum(fkeep, fgot, par, "fine_split"))
+    coarse_sum = finish_sum(cparts, par, "coarse")
+    fine_sum = finish_sum(fparts, par, "fine")
     per, cper = c // n, c2 // n
-    grad_coarse, grad_merge = last(*coarse_sum, grp, cper, [((cper, c), F32)], "coarse_last")
+    grad_coarse, grad_merge = last(*coarse_sum, par, cper, [((cper, c), F32)], "coarse_last")
     biases = [((1, per), F32), ((1, cper), F32)]
-    grad_fine, bias, coarse_sums = last(*fine_sum, grp, per, biases, "fine_last")
+    grad_fine, bias, coarse_sums = last(*fine_sum, par, per, biases, "fine_last")
     return (output, grad_fine, bias[0], grad_coarse, coarse_sums[0], grad_merge)
 
 

time: 108 us -> 97.2 us (0.900)
  local copies, waits for them, and re-layouts: 11.6 us -> 1.25 us
  Pallas kernels: 33.2 us -> 37.4 us
  waiting for transfers between devices: 16.2 us -> 13.1 us
  starting transfers between devices: 45.8 us -> 43.8 us
    unnamed x56 -> x18, local copies, waits for them, and re-layouts: 11.6 us -> 1.25 us
    pallas_call x18 -> x19, Pallas kernels: 33.2 us -> 37.4 us  [call(): pl.pallas_call(body, name=name, out_shape=[jax.ShapeDtypeStruct(s, t) for...]
    ppermute x4, waiting for transfers between devices: 4.9 us -> 2.21 us  [swap_faces(): return (lax.ppermute(first, axis, one), got)]
    ppermute x4, starting transfers between devices: 11.8 us -> 9.63 us  [swap_faces(): return (lax.ppermute(first, axis, one), got)]
  transfers between devices with their start and end apart: 26 -> 26, of which waited for: 11 -> 9; matrix products, arithmetic and copies ran while one was open for 0% -> 0% of each run, Pallas kernels for 13% -> 24%
where the time goes in v3:
time: 97.2 us; the launch traced here: 97 us
  starting transfers between devices  43.8 us (45%)
  Pallas kernels  37.4 us (38%)
  waiting for transfers between devices  13.1 us (13%)
  local copies, waits for them, and re-layouts  1.25 us (1%)
    pallas_call x19, Pallas kernels, call(): pl.pallas_call(body, name=name, out_shape=[jax.ShapeDtypeStruct(s, t) for...  37.4 us
    ppermute x18, starting transfers between devices, partners(): return lax.ppermute(value, ('grp', 'sub'), pairs)  31.4 us
    ppermute x18, waiting for transfers between devices, partners(): return lax.ppermute(value, ('grp', 'sub'), pairs)  10.9 us
    ppermute x4, starting transfers between devices, swap_faces(): return (lax.ppermute(first, axis, one), got)  9.63 us
    ppermute x4, starting transfers between devices, swap_faces(): got = lax.ppermute(second, axis, two)  2.75 us
    ppermute x4, waiting for transfers between devices, swap_faces(): return (lax.ppermute(first, axis, one), got)  2.21 us
  transfers between devices with their start and end apart: 26, of which 9 were waited for; matrix products, arithmetic and copies ran while one was open for 0% of the time, Pallas kernels for 24%

profile of v3, /device:TPU:0, one launch (start us, length us, event | category | flops | bytes accessed | tf_op | source)
XLA Modules:
  0.0 97.0 jit_solution(2106773733681724565)
XLA Ops:
  0.6 0.5 fusion.par
  1.2 2.3 %prep.1 = (bf16[8,32,128]{2,1,0:T(8,128)(2,1)}, bf16[8,32,128]{2,1,0:T(8,128)(2,1)}) custom-call(s32[5]{0:T(128)} %fusion.par, bf16[8,16,32,128]{3,2,1,0:T(8,128)(2,1)} %field.3), custom_call_target="tpu_custom_call" | custom-call | flops 1000000000 | tf_op jit(solution)/shard_map/prep/pallas_call | solution.py:28
  3.5 0.5 collective-permute-start
  4.0 0.8 collective-permute-start.1
  4.8 0.0 copy-start.2
  4.8 1.2 %copy-done.2 = bf16[8,16,32,128]{3,2,1,0:T(8,128)(2,1)S(1)} copy-done((bf16[8,16,32,128]{3,2,1,0:T(8,128)(2,1)S(1)}, bf16[8,16,32,128]{3,2,1,0:T(8,128)(2,1)}, u32[]{:S(2)}) %copy-start.2) | copy-done | bytes 1048600
  6.0 0.7 cubes.1.pg
  6.8 0.0 copy-start.4
  6.8 0.0 copy-start.7
  6.8 0.0 collective-permute-done.ya
  6.8 0.0 collective-permute-done.1.yb
  6.9 0.7 turn.1
  7.6 2.6 %collective-permute-start.2 = (bf16[18,32,128]{2,1,0:T(8,128)(2,1)S(1)}, bf16[18,32,128]{2,1,0:T(8,128)(2,1)S(1)}, u32[]{:S(2)}, u32[]{:S(2)}) collective-permute-start(bf16[18,32,128]{2,1,0:T(8,128)(2,1)S(1)} %get-tuple-element.63), channel_id=1, source_target_pairs={{0,4},{4,0},{8,12},{12,8},{16,20},{20,16},{24,28},{28,24},{1,5},{5... | collective-permute-start | bytes 442376 | tf_op jit(solution)/shard_map/ppermute | solution.py:349
  10.2 0.7 collective-permute-start.3
  10.8 6.3 %inner.1 = (bf16[6,16,32,128]{3,2,1,0:T(8,128)(2,1)S(1)}, f32[6,16,32,128]{3,2,1,0:T(8,128)S(1)}, bf16[2,8,16,128]{3,2,1,0:T(8,128)(2,1)S(1)}, bf16[1152,384]{1,0:T(8,128)(2,1)S(1)}) custom-call(s32[5]{0:T(128)S(1)} %copy-done.8, bf16[8,18,32,128]{3,2,1,0:T(8,128)(2,1)S(1)} %get-tuple-element.61.own, bf16[3,3,3,128,128]{4,3,2,1,0:T(8,128)(2,1)S(1)} %copy-done.4, ...), custom_call_target="tpu_custom_call" | custom-call | flops 6000000000 | tf_op jit(solution)/shard_map/inner/pallas_call | solution.py:28
  17.1 0.0 collective-permute-done.2.ra
  17.1 2.2 %outer.1 = (bf16[2,16,32,128]{3,2,1,0:T(8,128)(2,1)S(1)}, f32[2,16,32,128]{3,2,1,0:T(8,128)S(1)}, bf16[2,18,32,128]{3,2,1,0:T(8,128)(2,1)S(1)}, bf16[4,8,16,128]...) custom-call(s32[5]{0:T(128)S(1)} %copy-done.8, ...), custom_call_target="tpu_custom_call" | custom-call | flops 2000000000 | tf_op jit(solution)/shard_map/outer/pallas_call | solution.py:28
  19.4 4.3 %collective-permute-start.4 = (bf16[3,8,16,128]{3,2,1,0:T(8,128)(2,1)S(1)}, bf16[3,8,16,128]{3,2,1,0:T(8,128)(2,1)S(1)}, u32[]{:S(2)}, u32[]{:S(2)}) collective-permute-start(bf16[3,8,16,128]{3,2,1,0:T(8,128)(2,1)S(1)} %get-tuple-element.69), channel_id=1, source_target_pairs={{0,4},{4,0},{8,12},{12,8},{16,20},{20,16},{24,28},{28,24},{1,5},{5... | collective-permute-start | bytes 294920 | tf_op jit(solution)/shard_map/ppermute | solution.py:349
  23.7 0.7 collective-permute-start.5
  24.4 1.9 %collective-permute-done.4.ra = bf16[3,8,16,128]{3,2,1,0:T(8,128)(2,1)S(1)} collective-permute-done((bf16[3,8,16,128]{3,2,1,0:T(8,128)(2,1)S(1)}, bf16[3,8,16,128]{3,2,1,0:T(8,128)(2,1)S(1)}, u32[]{:S(2)}, u32[]{:S(2)}) %collective-permute-start.4) | collective-permute-done | bytes 98336 | tf_op jit(solution)/shard_map/ppermute | solution.py:349
  26.3 0.0 collective-permute-done.5.rb
  26.3 0.6 turn2.1
  26.9 2.2 %collective-permute-start.6 = (bf16[22,16,128]{2,1,0:T(8,128)(2,1)S(1)}, bf16[22,16,128]{2,1,0:T(8,128)(2,1)S(1)}, u32[]{:S(2)}, u32[]{:S(2)}) collective-permute-start(bf16[22,16,128]{2,1,0:T(8,128)(2,1)S(1)} %get-tuple-element.71), channel_id=1, source_target_pairs={{0,1},{1,0},{2,3},{3,2},{4,5},{5,4},{6,7},{7,6},{8,9},{9,8},{10,11... | collective-permute-start | bytes 270344 | tf_op jit(solution)/shard_map/ppermute | solution.py:349
  29.1 0.7 collective-permute-start.7
  29.8 0.3 collective-permute-done.6.ua
  30.1 5.9 %coarse.1 = (bf16[6,10,16,256]{3,2,1,0:T(8,128)(2,1)S(1)}, bf16[4,8,16,256]{3,2,1,0:T(8,128)(2,1)S(1)}, bf16[2,1792,128]{2,1,0:T(8,128)(2,1)S(1)}, bf16[2,1792,128]{2,1,0:T(8,128)(2,1)S(1)}, bf16[256,128]{1,0:T(8,128)(2,1)S(1)}) custom-call(s32[5]{0:T(128)S(1)} %copy-done.8, bf16[4,8,16,128]{3,2,1,0:T(8,128)(2,1)S(1)} %get-tuple-element.68.pooled, ...), custom_call_target="tpu_custom_call" | custom-call | flops 6000000000 | tf_op jit(solution)/shard_map/coarse/pallas_call | solution.py:28
  36.0 5.9 %collective-permute-start.8 = (bf16[2,1792,128]{2,1,0:T(8,128)(2,1)S(1)}, bf16[2,1792,128]{2,1,0:T(8,128)(2,1)S(1)}, u32[]{:S(2)}, u32[]{:S(2)}) collective-permute-start(bf16[2,1792,128]{2,1,0:T(8,128)(2,1)S(1)} %get-tuple-element.74), channel_id=1, source_target_pairs={{0,1},{1,0},{2,3},{3,2},{4,5},{5,4},{6,7},{7,6},{8,9},{9,8},{10,11... | collective-permute-start | bytes 2752520 | tf_op jit(solution)/shard_map/ppermute | solution.py:385
  41.8 1.8 %merge.1 = bf16[8,16,32,128]{3,2,1,0:T(8,128)(2,1)} custom-call(s32[5]{0:T(128)S(1)} %copy-done.8, bf16[6,16,32,128]{3,2,1,0:T(8,128)(2,1)S(1)} %get-tuple-element.62.hid_in.hidden, bf16[2,16,32,128]{3,2,1,0:T(8,128)(2,1)S(1)} %get-tuple-element.67.hid_edge, bf16[4,8,16,256]{3,2,1,0:T(8,128)(2,1)S(1)} %get-tuple-element.73.coarse, bf16[256,128]{1,0:T(8,128)(2,1)S(1)} %copy-done.5), custom_call_target="tpu_custom_call" | custom-call | flops 2000000000 | tf_op jit(solution)/shard_map/merge/pallas_call | solution.py:28
  43.7 0.3 collective-permute-done.8
  43.9 0.8 coarse_split.1
  44.7 6.4 %collective-permute-start.9 = (bf16[1,896,128]{2,1,0:T(8,128)(2,1)S(1)}, bf16[1,896,128]{2,1,0:T(8,128)(2,1)S(1)}, u32[]{:S(2)}, u32[]{:S(2)}) collective-permute-start(bf16[1,896,128]{2,1,0:T(8,128)(2,1)S(1)} %get-tuple-element.91), channel_id=1, source_target_pairs={{0,6},{1,7},{2,4},{3,5},{4,2},{5,3},{6,0},{7,1},{8,14},{9,15},{10,... | collective-permute-start | bytes 688136 | tf_op jit(solution)/shard_map/ppermute | solution.py:385
  51.1 0.1 collective-permute-start.10
  51.2 0.6 collective-permute-start.11
  51.7 8.9 %back.1 = (bf16[2,896,128]{2,1,0:T(8,128)(2,1)S(1)}, bf16[2,896,128]{2,1,0:T(8,128)(2,1)S(1)}) custom-call(s32[5]{0:T(128)S(1)} %copy-done.8, bf16[6,10,16,256]{3,2,1,0:T(8,128)(2,1)S(1)} %get-tuple-element.83.slope, bf16[3,3,3,128,256]{4,3,2,1,0:T(8,128)(2,1)S(1)} %copy-done, bf16[8,16,32,128]{3,2,1,0:T(8,128)(2,1)S(1)} %copy-done.3, ...), custom_call_target="tpu_custom_call" | custom-call | flops 10000000000 | tf_op jit(solution)/shard_map/back/pallas_call | solution.py:28
  60.6 1.3 %collective-permute-done.10 = bf16[1,896,128]{2,1,0:T(8,128)(2,1)S(1)} collective-permute-done((bf16[1,896,128]{2,1,0:T(8,128)(2,1)S(1)}, bf16[1,896,128]{2,1,0:T(8,128)(2,1)S(1)}, u32[]{:S(2)}, u32[]{:S(2)}) %collective-permute-start.10) | collective-permute-done | bytes 229408 | tf_op jit(solution)/shard_map/ppermute | solution.py:385
  61.9 0.0 collective-permute-start.12
  61.9 0.7 coarse_half.1
  62.6 3.3 %collective-permute-start.21 = (bf16[448,128]{1,0:T(8,128)(2,1)S(1)}, bf16[448,128]{1,0:T(8,128)(2,1)S(1)}, u32[]{:S(2)}, u32[]{:S(2)}) collective-permute-start(bf16[448,128]{1,0:T(8,128)(2,1)S(1)} %get-tuple-element.108), channel_id=1, source_target_pairs={{0,8},{1,9},{2,10},{3,11},{4,12},{5,13},{6,14},{7,15},{8,0},{9,1},... | collective-permute-start | bytes 344072 | tf_op jit(solution)/shard_map/ppermute | solution.py:385
  65.9 0.7 fine_split.1
  66.5 1.1 %collective-permute-start.13 = (bf16[1,448,128]{2,1,0:T(8,128)(2,1)S(1)}, bf16[1,448,128]{2,1,0:T(8,128)(2,1)S(1)}, u32[]{:S(2)}, u32[]{:S(2)}) collective-permute-start(bf16[1,448,128]{2,1,0:T(8,128)(2,1)S(1)} %get-tuple-element.96), channel_id=1, source_target_pairs={{0,6},{1,7},{2,4},{3,5},{4,2},{5,3},{6,0},{7,1},{8,14},{9,15},{10,... | collective-permute-start | bytes 344072 | tf_op jit(solution)/shard_map/ppermute | solution.py:385
  67.6 0.7 collective-permute-start.14
  68.3 1.8 %collective-permute-start.15 = (bf16[1,448,128]{2,1,0:T(8,128)(2,1)S(1)}, bf16[1,448,128]{2,1,0:T(8,128)(2,1)S(1)}, u32[]{:S(2)}, u32[]{:S(2)}) collective-permute-start(bf16[1,448,128]{2,1,0:T(8,128)(2,1)S(1)} %get-tuple-element.98), channel_id=1, source_target_pairs={{0,4},{1,5},{2,6},{3,7},{4,0},{5,1},{6,2},{7,3},{8,12},{9,13},{10,... | collective-permute-start | bytes 344072 | tf_op jit(solution)/shard_map/ppermute | solution.py:385
  70.1 0.6 coarse_sum2.1.refs_0_
  70.7 2.4 %collective-permute-start.22 = (bf16[448,128]{1,0:T(8,128)(2,1)S(1)}, bf16[448,128]{1,0:T(8,128)(2,1)S(1)}, u32[]{:S(2)}, u32[]{:S(2)}) collective-permute-start(bf16[448,128]{1,0:T(8,128)(2,1)S(1)} %coarse_sum2.1.refs_0_), channel_id=1, source_target_pairs={{0,16},{1,17},{2,18},{3,19},{4,20},{5,21},{6,22},{7,23},{8,24},{9,... | collective-permute-start | bytes 344072 | tf_op jit(solution)/shard_map/ppermute | solution.py:385
  73.1 0.4 collective-permute-done.13
  73.5 1.5 %collective-permute-done.14 = bf16[1,448,128]{2,1,0:T(8,128)(2,1)S(1)} collective-permute-done((bf16[1,448,128]{2,1,0:T(8,128)(2,1)S(1)}, bf16[1,448,128]{2,1,0:T(8,128)(2,1)S(1)}, u32[]{:S(2)}, u32[]{:S(2)}) %collective-permute-start.14) | collective-permute-done | bytes 114720 | tf_op jit(solution)/shard_map/ppermute | solution.py:385
  75.1 0.6 fine_half.1
  75.7 1.1 %collective-permute-start.16 = (bf16[224,128]{1,0:T(8,128)(2,1)S(1)}, bf16[224,128]{1,0:T(8,128)(2,1)S(1)}, u32[]{:S(2)}, u32[]{:S(2)}) collective-permute-start(bf16[224,128]{1,0:T(8,128)(2,1)S(1)} %get-tuple-element.100), channel_id=1, source_target_pairs={{0,8},{1,9},{2,10},{3,11},{4,12},{5,13},{6,14},{7,15},{8,0},{9,1},... | collective-permute-start | bytes 172040 | tf_op jit(solution)/shard_map/ppermute | solution.py:385
  76.7 2.0 %collective-permute-done.22.refs_1_ = bf16[448,128]{1,0:T(8,128)(2,1)S(1)} collective-permute-done((bf16[448,128]{1,0:T(8,128)(2,1)S(1)}, bf16[448,128]{1,0:T(8,128)(2,1)S(1)}, u32[]{:S(2)}, u32[]{:S(2)}) %collective-permute-start.22) | collective-permute-done | bytes 114720 | tf_op jit(solution)/shard_map/ppermute | solution.py:385
  78.7 0.6 coarse_total.1.refs_0_
  79.3 0.1 collective-permute-start.25
  79.4 1.5 %collective-permute-start.24 = (bf16[448,128]{1,0:T(8,128)(2,1)S(1)}, bf16[448,128]{1,0:T(8,128)(2,1)S(1)}, u32[]{:S(2)}, u32[]{:S(2)}) collective-permute-start(bf16[448,128]{1,0:T(8,128)(2,1)S(1)} %coarse_total.1.refs_0_), channel_id=1, source_target_pairs={{0,8},{1,9},{2,10},{3,11},{4,12},{5,13},{6,14},{7,15},{8,0},{9,1},... | collective-permute-start | bytes 344072 | tf_op jit(solution)/shard_map/ppermute | solution.py:385
  80.9 1.9 %collective-permute-start.23 = (bf16[448,128]{1,0:T(8,128)(2,1)S(1)}, bf16[448,128]{1,0:T(8,128)(2,1)S(1)}, u32[]{:S(2)}, u32[]{:S(2)}) collective-permute-start(bf16[448,128]{1,0:T(8,128)(2,1)S(1)} %coarse_total.1.refs_0_), channel_id=1, source_target_pairs={{0,4},{1,5},{2,6},{3,7},{4,0},{5,1},{6,2},{7,3},{8,12},{9,13},{10,... | collective-permute-start | bytes 344072 | tf_op jit(solution)/shard_map/ppermute | solution.py:385
  82.9 0.6 fine_sum2.1.refs_0_
  83.4 1.1 %collective-permute-start.17 = (bf16[224,128]{1,0:T(8,128)(2,1)S(1)}, bf16[224,128]{1,0:T(8,128)(2,1)S(1)}, u32[]{:S(2)}, u32[]{:S(2)}) collective-permute-start(bf16[224,128]{1,0:T(8,128)(2,1)S(1)} %fine_sum2.1.refs_0_), channel_id=1, source_target_pairs={{0,16},{1,17},{2,18},{3,19},{4,20},{5,21},{6,22},{7,23},{8,24},{9,... | collective-permute-start | bytes 172040 | tf_op jit(solution)/shard_map/ppermute | solution.py:385
  84.5 4.3 %collective-permute-done.17.refs_1_ = bf16[224,128]{1,0:T(8,128)(2,1)S(1)} collective-permute-done((bf16[224,128]{1,0:T(8,128)(2,1)S(1)}, bf16[224,128]{1,0:T(8,128)(2,1)S(1)}, u32[]{:S(2)}, u32[]{:S(2)}) %collective-permute-start.17) | collective-permute-done | bytes 57376 | tf_op jit(solution)/shard_map/ppermute | solution.py:385
  88.8 0.6 fine_total.1.refs_0_
  89.4 0.3 collective-permute-start.20
  89.6 1.7 %collective-permute-start.19 = (bf16[224,128]{1,0:T(8,128)(2,1)S(1)}, bf16[224,128]{1,0:T(8,128)(2,1)S(1)}, u32[]{:S(2)}, u32[]{:S(2)}) collective-permute-start(bf16[224,128]{1,0:T(8,128)(2,1)S(1)} %fine_total.1.refs_0_), channel_id=1, source_target_pairs={{0,8},{1,9},{2,10},{3,11},{4,12},{5,13},{6,14},{7,15},{8,0},{9,1},... | collective-permute-start | bytes 172040 | tf_op jit(solution)/shard_map/ppermute | solution.py:385
  91.4 1.5 %collective-permute-start.18 = (bf16[224,128]{1,0:T(8,128)(2,1)S(1)}, bf16[224,128]{1,0:T(8,128)(2,1)S(1)}, u32[]{:S(2)}, u32[]{:S(2)}) collective-permute-start(bf16[224,128]{1,0:T(8,128)(2,1)S(1)} %fine_total.1.refs_0_), channel_id=1, source_target_pairs={{0,4},{1,5},{2,6},{3,7},{4,0},{5,1},{6,2},{7,3},{8,12},{9,13},{10,... | collective-permute-start | bytes 172040 | tf_op jit(solution)/shard_map/ppermute | solution.py:385
  92.9 1.5 %coarse_last.1 = (f32[3,3,3,64,128]{4,3,2,1,0:T(8,128)}, f32[64,128]{1,0:T(8,128)}) custom-call(s32[5]{0:T(128)S(1)} %copy-done.8, bf16[448,128]{1,0:T(8,128)(2,1)S(1)} %coarse_total.1.refs_0_, bf16[448,128]{1,0:T(8,128)(2,1)S(1)} %collective-permute-done.23.refs_1_, bf16[448,128]{1,0:T(8,128)(2,1)S(1)} %collective-permute-done.24.refs_2_, ...), custom_call_target="tpu_custom_call" | custom-call | flops 1000000000 | tf_op jit(solution)/shard_map/coarse_last/pallas_call | solution.py:28
  94.5 0.0 collective-permute-done.20.refs_3_
  94.5 1.1 %collective-permute-done.18.refs_1_ = bf16[224,128]{1,0:T(8,128)(2,1)S(1)} collective-permute-done((bf16[224,128]{1,0:T(8,128)(2,1)S(1)}, bf16[224,128]{1,0:T(8,128)(2,1)S(1)}, u32[]{:S(2)}, u32[]{:S(2)}) %collective-permute-start.18) | collective-permute-done | bytes 57376 | tf_op jit(solution)/shard_map/ppermute | solution.py:385
  95.6 1.4 %fine_last.1 = (f32[3,3,3,32,128]{4,3,2,1,0:T(8,128)}, f32[1,32]{1,0:T(1,128)}, f32[1,64]{1,0:T(1,128)}) custom-call(s32[5]{0:T(128)S(1)} %copy-done.8, bf16[224,128]{1,0:T(8,128)(2,1)S(1)} %fine_total.1.refs_0_, bf16[224,128]{1,0:T(8,128)(2,1)S(1)} %collective-permute-done.18.refs_1_, bf16[224,128]{1,0:T(8,128)(2,1)S(1)} %collective-permute-done.19.refs_2_, ...), custom_call_target="tpu_custom_call" | custom-call | flops 1000000000 | tf_op jit(solution)/shard_map/fine_last/pallas_call | solution.py:28
  (26 shorter events, 0.1 us)
Async XLA Ops:
  1.2 3.7 %copy-start.8 = (s32[5]{0:T(128)S(1)}, s32[5]{0:T(128)}, u32[]{:S(2)}) copy-start(s32[5]{0:T(128)} %fusion.par) | copy-start | bytes 64
  3.5 3.3 %collective-permute-start = (bf16[8,32,128]{2,1,0:T(8,128)(2,1)}, bf16[8,32,128]{2,1,0:T(8,128)(2,1)S(1)}, u32[]{:S(2)}, u32[]{:S(2)}) collective-permute-start(bf16[8,32,128]{2,1,0:T(8,128)(2,1)} %get-tuple-element.59), channel_id=1, source_target_pairs={{0,1},{1,0},{2,3},{3,2},{4,5},{5,4},{6,7},{7,6},{8,9},{9,8},{10,11... | collective-permute-start | bytes 196616 | tf_op jit(solution)/shard_map/ppermute | solution.py:349
  4.0 2.8 %copy-start.1 = (bf16[8,16,32,128]{3,2,1,0:T(8,128)(2,1)S(1)}, bf16[8,16,32,128]{3,2,1,0:T(8,128)(2,1)}, u32[]{:S(2)}) copy-start(bf16[8,16,32,128]{3,2,1,0:T(8,128)(2,1)} %field.3) | copy-start | bytes 3145732
  4.0 2.8 %collective-permute-start.1 = (bf16[8,32,128]{2,1,0:T(8,128)(2,1)}, bf16[8,32,128]{2,1,0:T(8,128)(2,1)S(1)}, u32[]{:S(2)}, u32[]{:S(2)}) collective-permute-start(bf16[8,32,128]{2,1,0:T(8,128)(2,1)} %get-tuple-element.60), channel_id=1, source_target_pairs={{1,2},{2,1},{5,6},{6,5},{9,10},{10,9},{13,14},{14,13},{17,18},{18,... | collective-permute-start | bytes 196616 | tf_op jit(solution)/shard_map/ppermute | solution.py:348
  4.8 1.2 %copy-start.2 = (bf16[8,16,32,128]{3,2,1,0:T(8,128)(2,1)S(1)}, bf16[8,16,32,128]{3,2,1,0:T(8,128)(2,1)}, u32[]{:S(2)}) copy-start(bf16[8,16,32,128]{3,2,1,0:T(8,128)(2,1)} %cot.3) | copy-start | bytes 3145732
  6.8 4.0 %copy-start.4 = (bf16[3,3,3,128,128]{4,3,2,1,0:T(8,128)(2,1)S(1)}, bf16[3,3,3,128,128]{4,3,2,1,0:T(8,128)(2,1)}, u32[]{:S(2)}) copy-start(bf16[3,3,3,128,128]{4,3,2,1,0:T(8,128)(2,1)} %w.3) | copy-start | bytes 2654212
  6.8 4.0 %copy-start.7 = (f32[128]{0:T(128)S(1)}, f32[128]{0:T(128)}, u32[]{:S(2)}) copy-start(f32[128]{0:T(128)} %param.10) | copy-start | bytes 1540
  7.6 9.6 %collective-permute-start.2 = (bf16[18,32,128]{2,1,0:T(8,128)(2,1)S(1)}, bf16[18,32,128]{2,1,0:T(8,128)(2,1)S(1)}, u32[]{:S(2)}, u32[]{:S(2)}) collective-permute-start(bf16[18,32,128]{2,1,0:T(8,128)(2,1)S(1)} %get-tuple-element.63), channel_id=1, source_target_pairs={{0,4},{4,0},{8,12},{12,8},{16,20},{20,16},{24,28},{28,24},{1,5},{5... | collective-permute-start | bytes 442376 | tf_op jit(solution)/shard_map/ppermute | solution.py:349
  10.2 7.0 %collective-permute-start.3 = (bf16[18,32,128]{2,1,0:T(8,128)(2,1)S(1)}, bf16[18,32,128]{2,1,0:T(8,128)(2,1)S(1)}, u32[]{:S(2)}, u32[]{:S(2)}) collective-permute-start(bf16[18,32,128]{2,1,0:T(8,128)(2,1)S(1)} %get-tuple-element.64), channel_id=1, source_target_pairs={{4,8},{8,4},{12,16},{16,12},{20,24},{24,20},{5,9},{9,5},{13,17},{1... | collective-permute-start | bytes 442376 | tf_op jit(solution)/shard_map/ppermute | solution.py:348
  19.4 6.9 %collective-permute-start.4 = (bf16[3,8,16,128]{3,2,1,0:T(8,128)(2,1)S(1)}, bf16[3,8,16,128]{3,2,1,0:T(8,128)(2,1)S(1)}, u32[]{:S(2)}, u32[]{:S(2)}) collective-permute-start(bf16[3,8,16,128]{3,2,1,0:T(8,128)(2,1)S(1)} %get-tuple-element.69), channel_id=1, source_target_pairs={{0,4},{4,0},{8,12},{12,8},{16,20},{20,16},{24,28},{28,24},{1,5},{5... | collective-permute-start | bytes 294920 | tf_op jit(solution)/shard_map/ppermute | solution.py:349
  23.7 2.6 %collective-permute-start.5 = (bf16[3,8,16,128]{3,2,1,0:T(8,128)(2,1)S(1)}, bf16[3,8,16,128]{3,2,1,0:T(8,128)(2,1)S(1)}, u32[]{:S(2)}, u32[]{:S(2)}) collective-permute-start(bf16[3,8,16,128]{3,2,1,0:T(8,128)(2,1)S(1)} %get-tuple-element.70), channel_id=1, source_target_pairs={{4,8},{8,4},{12,16},{16,12},{20,24},{24,20},{5,9},{9,5},{13,17},{1... | collective-permute-start | bytes 294920 | tf_op jit(solution)/shard_map/ppermute | solution.py:348
  26.3 3.7 %copy-start = (bf16[3,3,3,128,256]{4,3,2,1,0:T(8,128)(2,1)S(1)}, bf16[3,3,3,128,256]{4,3,2,1,0:T(8,128)(2,1)}, u32[]{:S(2)}) copy-start(bf16[3,3,3,128,256]{4,3,2,1,0:T(8,128)(2,1)} %w.5) | copy-start | bytes 5308420
  26.3 3.7 %copy-start.5 = (bf16[256,128]{1,0:T(8,128)(2,1)S(1)}, bf16[256,128]{1,0:T(8,128)(2,1)}, u32[]{:S(2)}) copy-start(bf16[256,128]{1,0:T(8,128)(2,1)} %wm.3) | copy-start | bytes 196612
  26.3 3.7 %copy-start.6 = (f32[256]{0:T(256)S(1)}, f32[256]{0:T(256)}, u32[]{:S(2)}) copy-start(f32[256]{0:T(256)} %param.12) | copy-start | bytes 3076
  26.9 3.1 %collective-permute-start.6 = (bf16[22,16,128]{2,1,0:T(8,128)(2,1)S(1)}, bf16[22,16,128]{2,1,0:T(8,128)(2,1)S(1)}, u32[]{:S(2)}, u32[]{:S(2)}) collective-permute-start(bf16[22,16,128]{2,1,0:T(8,128)(2,1)S(1)} %get-tuple-element.71), channel_id=1, source_target_pairs={{0,1},{1,0},{2,3},{3,2},{4,5},{5,4},{6,7},{7,6},{8,9},{9,8},{10,11... | collective-permute-start | bytes 270344 | tf_op jit(solution)/shard_map/ppermute | solution.py:349
  29.1 0.9 collective-permute-start.7
  36.0 8.0 %collective-permute-start.8 = (bf16[2,1792,128]{2,1,0:T(8,128)(2,1)S(1)}, bf16[2,1792,128]{2,1,0:T(8,128)(2,1)S(1)}, u32[]{:S(2)}, u32[]{:S(2)}) collective-permute-start(bf16[2,1792,128]{2,1,0:T(8,128)(2,1)S(1)} %get-tuple-element.74), channel_id=1, source_target_pairs={{0,1},{1,0},{2,3},{3,2},{4,5},{5,4},{6,7},{7,6},{8,9},{9,8},{10,11... | collective-permute-start | bytes 2752520 | tf_op jit(solution)/shard_map/ppermute | solution.py:385
  43.9 7.8 %copy-start.3 = (bf16[8,16,32,128]{3,2,1,0:T(8,128)(2,1)S(1)}, bf16[8,16,32,128]{3,2,1,0:T(8,128)(2,1)}, u32[]{:S(2)}) copy-start(bf16[8,16,32,128]{3,2,1,0:T(8,128)(2,1)} %cot.3) | copy-start | bytes 3145732
  44.7 15.9 %collective-permute-start.9 = (bf16[1,896,128]{2,1,0:T(8,128)(2,1)S(1)}, bf16[1,896,128]{2,1,0:T(8,128)(2,1)S(1)}, u32[]{:S(2)}, u32[]{:S(2)}) collective-permute-start(bf16[1,896,128]{2,1,0:T(8,128)(2,1)S(1)} %get-tuple-element.91), channel_id=1, source_target_pairs={{0,6},{1,7},{2,4},{3,5},{4,2},{5,3},{6,0},{7,1},{8,14},{9,15},{10,... | collective-permute-start | bytes 688136 | tf_op jit(solution)/shard_map/ppermute | solution.py:385
  51.1 10.8 %collective-permute-start.10 = (bf16[1,896,128]{2,1,0:T(8,128)(2,1)S(1)}, bf16[1,896,128]{2,1,0:T(8,128)(2,1)S(1)}, u32[]{:S(2)}, u32[]{:S(2)}) collective-permute-start(bf16[1,896,128]{2,1,0:T(8,128)(2,1)S(1)} %get-tuple-element.92), channel_id=1, source_target_pairs={{0,2},{1,3},{2,0},{3,1},{4,6},{5,7},{6,4},{7,5},{8,10},{9,11},{10,... | collective-permute-start | bytes 688136 | tf_op jit(solution)/shard_map/ppermute | solution.py:385
  51.2 10.8 %collective-permute-start.11 = (bf16[1,896,128]{2,1,0:T(8,128)(2,1)S(1)}, bf16[1,896,128]{2,1,0:T(8,128)(2,1)S(1)}, u32[]{:S(2)}, u32[]{:S(2)}) collective-permute-start(bf16[1,896,128]{2,1,0:T(8,128)(2,1)S(1)} %get-tuple-element.93), channel_id=1, source_target_pairs={{0,4},{1,5},{2,6},{3,7},{4,0},{5,1},{6,2},{7,3},{8,12},{9,13},{10,... | collective-permute-start | bytes 688136 | tf_op jit(solution)/shard_map/ppermute | solution.py:385
  61.9 4.0 %collective-permute-start.12 = (bf16[2,896,128]{2,1,0:T(8,128)(2,1)S(1)}, bf16[2,896,128]{2,1,0:T(8,128)(2,1)S(1)}, u32[]{:S(2)}, u32[]{:S(2)}) collective-permute-start(bf16[2,896,128]{2,1,0:T(8,128)(2,1)S(1)} %get-tuple-element.94), channel_id=1, source_target_pairs={{0,1},{1,0},{2,3},{3,2},{4,5},{5,4},{6,7},{7,6},{8,9},{9,8},{10,11... | collective-permute-start | bytes 1376264 | tf_op jit(solution)/shard_map/ppermute | solution.py:385
  62.6 7.5 %collective-permute-start.21 = (bf16[448,128]{1,0:T(8,128)(2,1)S(1)}, bf16[448,128]{1,0:T(8,128)(2,1)S(1)}, u32[]{:S(2)}, u32[]{:S(2)}) collective-permute-start(bf16[448,128]{1,0:T(8,128)(2,1)S(1)} %get-tuple-element.108), channel_id=1, source_target_pairs={{0,8},{1,9},{2,10},{3,11},{4,12},{5,13},{6,14},{7,15},{8,0},{9,1},... | collective-permute-start | bytes 344072 | tf_op jit(solution)/shard_map/ppermute | solution.py:385
  66.5 7.0 %collective-permute-start.13 = (bf16[1,448,128]{2,1,0:T(8,128)(2,1)S(1)}, bf16[1,448,128]{2,1,0:T(8,128)(2,1)S(1)}, u32[]{:S(2)}, u32[]{:S(2)}) collective-permute-start(bf16[1,448,128]{2,1,0:T(8,128)(2,1)S(1)} %get-tuple-element.96), channel_id=1, source_target_pairs={{0,6},{1,7},{2,4},{3,5},{4,2},{5,3},{6,0},{7,1},{8,14},{9,15},{10,... | collective-permute-start | bytes 344072 | tf_op jit(solution)/shard_map/ppermute | solution.py:385
  67.6 7.4 %collective-permute-start.14 = (bf16[1,448,128]{2,1,0:T(8,128)(2,1)S(1)}, bf16[1,448,128]{2,1,0:T(8,128)(2,1)S(1)}, u32[]{:S(2)}, u32[]{:S(2)}) collective-permute-start(bf16[1,448,128]{2,1,0:T(8,128)(2,1)S(1)} %get-tuple-element.97), channel_id=1, source_target_pairs={{0,2},{1,3},{2,0},{3,1},{4,6},{5,7},{6,4},{7,5},{8,10},{9,11},{10,... | collective-permute-start | bytes 344072 | tf_op jit(solution)/shard_map/ppermute | solution.py:385
  68.3 6.7 %collective-permute-start.15 = (bf16[1,448,128]{2,1,0:T(8,128)(2,1)S(1)}, bf16[1,448,128]{2,1,0:T(8,128)(2,1)S(1)}, u32[]{:S(2)}, u32[]{:S(2)}) collective-permute-start(bf16[1,448,128]{2,1,0:T(8,128)(2,1)S(1)} %get-tuple-element.98), channel_id=1, source_target_pairs={{0,4},{1,5},{2,6},{3,7},{4,0},{5,1},{6,2},{7,3},{8,12},{9,13},{10,... | collective-permute-start | bytes 344072 | tf_op jit(solution)/shard_map/ppermute | solution.py:385
  70.7 8.1 %collective-permute-start.22 = (bf16[448,128]{1,0:T(8,128)(2,1)S(1)}, bf16[448,128]{1,0:T(8,128)(2,1)S(1)}, u32[]{:S(2)}, u32[]{:S(2)}) collective-permute-start(bf16[448,128]{1,0:T(8,128)(2,1)S(1)} %coarse_sum2.1.refs_0_), channel_id=1, source_target_pairs={{0,16},{1,17},{2,18},{3,19},{4,20},{5,21},{6,22},{7,23},{8,24},{9,... | collective-permute-start | bytes 344072 | tf_op jit(solution)/shard_map/ppermute | solution.py:385
  75.7 7.2 %collective-permute-start.16 = (bf16[224,128]{1,0:T(8,128)(2,1)S(1)}, bf16[224,128]{1,0:T(8,128)(2,1)S(1)}, u32[]{:S(2)}, u32[]{:S(2)}) collective-permute-start(bf16[224,128]{1,0:T(8,128)(2,1)S(1)} %get-tuple-element.100), channel_id=1, source_target_pairs={{0,8},{1,9},{2,10},{3,11},{4,12},{5,13},{6,14},{7,15},{8,0},{9,1},... | collective-permute-start | bytes 172040 | tf_op jit(solution)/shard_map/ppermute | solution.py:385
  79.3 12.1 %collective-permute-start.25 = (bf16[448,128]{1,0:T(8,128)(2,1)S(1)}, bf16[448,128]{1,0:T(8,128)(2,1)S(1)}, u32[]{:S(2)}, u32[]{:S(2)}) collective-permute-start(bf16[448,128]{1,0:T(8,128)(2,1)S(1)} %coarse_total.1.refs_0_), channel_id=1, source_target_pairs={{0,12},{1,13},{2,14},{3,15},{4,8},{5,9},{6,10},{7,11},{8,4},{9,5},... | collective-permute-start | bytes 344072 | tf_op jit(solution)/shard_map/ppermute | solution.py:385
  79.4 13.5 %collective-permute-start.24 = (bf16[448,128]{1,0:T(8,128)(2,1)S(1)}, bf16[448,128]{1,0:T(8,128)(2,1)S(1)}, u32[]{:S(2)}, u32[]{:S(2)}) collective-permute-start(bf16[448,128]{1,0:T(8,128)(2,1)S(1)} %coarse_total.1.refs_0_), channel_id=1, source_target_pairs={{0,8},{1,9},{2,10},{3,11},{4,12},{5,13},{6,14},{7,15},{8,0},{9,1},... | collective-permute-start | bytes 344072 | tf_op jit(solution)/shard_map/ppermute | solution.py:385
  80.9 12.0 %collective-permute-start.23 = (bf16[448,128]{1,0:T(8,128)(2,1)S(1)}, bf16[448,128]{1,0:T(8,128)(2,1)S(1)}, u32[]{:S(2)}, u32[]{:S(2)}) collective-permute-start(bf16[448,128]{1,0:T(8,128)(2,1)S(1)} %coarse_total.1.refs_0_), channel_id=1, source_target_pairs={{0,4},{1,5},{2,6},{3,7},{4,0},{5,1},{6,2},{7,3},{8,12},{9,13},{10,... | collective-permute-start | bytes 344072 | tf_op jit(solution)/shard_map/ppermute | solution.py:385
  83.4 5.4 %collective-permute-start.17 = (bf16[224,128]{1,0:T(8,128)(2,1)S(1)}, bf16[224,128]{1,0:T(8,128)(2,1)S(1)}, u32[]{:S(2)}, u32[]{:S(2)}) collective-permute-start(bf16[224,128]{1,0:T(8,128)(2,1)S(1)} %fine_sum2.1.refs_0_), channel_id=1, source_target_pairs={{0,16},{1,17},{2,18},{3,19},{4,20},{5,21},{6,22},{7,23},{8,24},{9,... | collective-permute-start | bytes 172040 | tf_op jit(solution)/shard_map/ppermute | solution.py:385
  89.4 5.1 %collective-permute-start.20 = (bf16[224,128]{1,0:T(8,128)(2,1)S(1)}, bf16[224,128]{1,0:T(8,128)(2,1)S(1)}, u32[]{:S(2)}, u32[]{:S(2)}) collective-permute-start(bf16[224,128]{1,0:T(8,128)(2,1)S(1)} %fine_total.1.refs_0_), channel_id=1, source_target_pairs={{0,12},{1,13},{2,14},{3,15},{4,8},{5,9},{6,10},{7,11},{8,4},{9,5},... | collective-permute-start | bytes 172040 | tf_op jit(solution)/shard_map/ppermute | solution.py:385
  89.6 4.9 %collective-permute-start.19 = (bf16[224,128]{1,0:T(8,128)(2,1)S(1)}, bf16[224,128]{1,0:T(8,128)(2,1)S(1)}, u32[]{:S(2)}, u32[]{:S(2)}) collective-permute-start(bf16[224,128]{1,0:T(8,128)(2,1)S(1)} %fine_total.1.refs_0_), channel_id=1, source_target_pairs={{0,8},{1,9},{2,10},{3,11},{4,12},{5,13},{6,14},{7,15},{8,0},{9,1},... | collective-permute-start | bytes 172040 | tf_op jit(solution)/shard_map/ppermute | solution.py:385
  91.4 4.2 %collective-permute-start.18 = (bf16[224,128]{1,0:T(8,128)(2,1)S(1)}, bf16[224,128]{1,0:T(8,128)(2,1)S(1)}, u32[]{:S(2)}, u32[]{:S(2)}) collective-permute-start(bf16[224,128]{1,0:T(8,128)(2,1)S(1)} %fine_total.1.refs_0_), channel_id=1, source_target_pairs={{0,4},{1,5},{2,6},{3,7},{4,0},{5,1},{6,2},{7,3},{8,12},{9,13},{10,... | collective-permute-start | bytes 172040 | tf_op jit(solution)/shard_map/ppermute | solution.py:385

commit v4 on v3

--- a/solution.py
+++ b/solution.py
@@ -10,34 +10,26 @@
 F32 = jnp.float32
 BF16 = jnp.bfloat16
 VMEM_LIMIT = 32 * 1024 * 1024
-
-
-def call(body, name, args, outs, scratch=(), micros=1, limit=VMEM_LIMIT):
-    specs = [pl.BlockSpec(memory_space=pltpu.SMEM)]
-    arrays = [args[0]]
-    for arg in args[1:]:
-        if isinstance(arg, tuple) and arg[1] is None:
-            arrays.append(arg[0])
-            specs.append(pl.BlockSpec(memory_space=pltpu.HBM))
-        elif isinstance(arg, tuple):
-            arrays.append(arg[0])
-            specs.append(pl.BlockSpec(arg[1], functools.partial(lambda at, _: at, arg[2])))
-        else:
-            arrays.append(arg)
-            specs.append(pl.BlockSpec(memory_space=pltpu.VMEM))
+PREP_LIMIT = 127 * 512 * 1024
+
+
+def bit_of(axis, bit=0):
+    return (lax.axis_index(axis) >> bit) & 1
+
+
+def call(body, name, args, outs, scratch=(), micros=1, space=pltpu.VMEM):
     return pl.pallas_call(
         body,
         name=name,
         out_shape=[jax.ShapeDtypeStruct(s, t) for s, t in outs],
-        grid=(1,) if any(isinstance(arg, tuple) and arg[1] for arg in args) else (),
-        in_specs=specs,
-        out_specs=[pl.BlockSpec(memory_space=pltpu.VMEM) for _ in outs],
+        in_specs=[pl.BlockSpec(memory_space=space) for _ in args],
+        out_specs=[pl.BlockSpec(memory_space=space) for _ in outs],
         scratch_shapes=list(scratch),
-        compiler_params=pltpu.CompilerParams(vmem_limit_bytes=limit),
+        compiler_params=pltpu.CompilerParams(vmem_limit_bytes=VMEM_LIMIT if space == pltpu.VMEM else PREP_LIMIT),
         cost_estimate=pl.CostEstimate(
             flops=int(micros * 1e9), bytes_accessed=0, transcendentals=0
         ),
-    )(*arrays)
+    )(*args)
 
 
 def put_faces(odd, first, second, low, high):
@@ -68,8 +60,8 @@
     return 1.0 / (1.0 + jnp.exp(-value))
 
 
-def prep_body(sub, par, field, out_a, out_b, sems):
-    odd, end = par[sub], field.shape[1] - 1
+def prep_body(field, out_a, out_b, sems):
+    odd, end = bit_of("sub"), field.shape[1] - 1
     one = pltpu.make_async_copy(field.at[:, (1 - odd) * end], out_a, sems.at[0])
     two = pltpu.make_async_copy(field.at[:, odd * end], out_b, sems.at[1])
     one.start()
@@ -78,13 +70,13 @@
     two.wait()
 
 
-def turn_body(sub, par, field, ya, yb, own, out_a, out_b):
+def turn_body(field, ya, yb, own, out_a, out_b):
     bx, by = field.shape[0], field.shape[1]
-    ylo, yhi = get_faces(par[sub] == 1, ya, yb)
+    ylo, yhi = get_faces(bit_of("sub") == 1, ya, yb)
     own[:, 1 : by + 1] = field[...]
     own[:, 0] = ylo
     own[:, by + 1] = yhi
-    put_faces(par[0] == 1, out_a, out_b, own[0], own[bx - 1])
+    put_faces(bit_of("grp") == 1, out_a, out_b, own[0], own[bx - 1])
 
 
 def fine_plane(three, wb, bias, by):
@@ -111,7 +103,7 @@
     return (total / 8.0).astype(BF16).reshape(cy, bz // 2, c)
 
 
-def inner_body(par, own, w, bias, hidden, ds, pooled, wb, tmp):
+def inner_body(own, w, bias, hidden, ds, pooled, wb, tmp):
     by, c = own.shape[1] - 2, own.shape[3]
     for i in range(3):
         for j in range(3):
@@ -128,10 +120,10 @@
         pooled[q] = pool(hidden[2 * q + 1], hidden[2 * q + 2], tmp)
 
 
-def outer_body(par, own, ra, rb, wb, bias, hid_in, pool_in, pg, hidden, ds, halo, pooled, out_a, out_b, tmp):
+def outer_body(own, ra, rb, wb, bias, hid_in, pool_in, pg, hidden, ds, halo, pooled, out_a, out_b, tmp):
     bx, by = own.shape[0], own.shape[1] - 2
     cx = bx // 2
-    xlo, xhi = get_faces(par[0] == 1, ra, rb)
+    xlo, xhi = get_faces(bit_of("grp") == 1, ra, rb)
     halo[0], halo[1] = xlo, xhi
     for at, three in ((0, [halo[0], own[0], own[1]]), (1, [own[bx - 2], own[bx - 1], halo[1]])):
         hidden[at], ds[at] = fine_plane(three, wb, bias, by)
@@ -140,27 +132,31 @@
     pooled[cx - 1] = pool(hid_in[bx - 3], hidden[1], tmp)
     low = jnp.concatenate([pooled[0:2], pg[0:1]], axis=0)
     high = jnp.concatenate([pooled[cx - 2 : cx], pg[cx - 1 : cx]], axis=0)
-    put_faces(par[0] == 1, out_a, out_b, low, high)
-
-
-def cubes_body(par, cot, pg, tmp):
+    put_faces(bit_of("grp") == 1, out_a, out_b, low, high)
+
+
+def cubes_body(cot, pg, bits, tmp):
     bx, by, bz, c = cot.shape
     cx, cy, cz = bx // 2, by // 2, bz // 2
     total = jnp.sum(cot[...].astype(F32).reshape(cx, 2, cy, 2, bz, c), axis=(1, 3))
     grad = sum_cube(cx * cy * bz, total.reshape(cx * cy * bz, c), tmp).astype(BF16)
     pg[...] = grad.reshape(cx, cy, cz, c)
-
-
-def turn2_body(sub, par, pooled, pg, ra, rb, out_a, out_b):
+    first = grp_bits()
+    for k in range(bits.shape[0]):
+        value = bit_of("grp", k) if k < first else bit_of("sub", k - first)
+        bits[k] = jnp.full(bits.shape[1:], value, jnp.int32)
+
+
+def turn2_body(pooled, pg, ra, rb, out_a, out_b):
     cy = pooled.shape[1]
-    xlo, xhi = get_faces(par[0] == 1, ra, rb)
+    xlo, xhi = get_faces(bit_of("grp") == 1, ra, rb)
 
     def side(y, last):
         two = [jnp.concatenate([xlo[0:2, at], pooled[:, at], xhi[0:2, at]], axis=0) for at in (y, y + 1)]
         one = jnp.concatenate([xlo[2:3, last], pg[:, last], xhi[2:3, last]], axis=0)
         return jnp.concatenate([*two, one], axis=0)
 
-    put_faces(par[sub] == 1, out_a, out_b, side(0, 0), side(cy - 2, cy - 1))
+    put_faces(bit_of("sub") == 1, out_a, out_b, side(0, 0), side(cy - 2, cy - 1))
 
 
 def reverse_bits(value, count):
@@ -170,12 +166,12 @@
     return out
 
 
-def spread(par, keep, send, n, blocks, piece):
+def spread(keep, send, n, blocks, piece):
     bits = n.bit_length() - 1
     half = n // 2
     for b in (0, 1):
 
-        @pl.when(par == b)
+        @pl.when(bit_of("sub") == b)
         def _():
             for s in range(n):
                 target = keep if s % 2 == b else send
@@ -186,13 +182,13 @@
 
 
 def coarse_body(
-    n, sub, par, pooled, ra, rb, ua, ub, pg, w, bias, wm,
+    n, pooled, ra, rb, ua, ub, pg, w, bias, wm,
     slope, coarse, keep, send, cbias, qpad, gpad, wb, st, rhs, acc, ct,
 ):
     cx, cy, cz, c = pooled.shape
     c2 = wm.shape[0]
-    xlo, xhi = get_faces(par[0] == 1, ra, rb)
-    ylo, yhi = get_faces(par[sub] == 1, ua, ub)
+    xlo, xhi = get_faces(bit_of("grp") == 1, ra, rb)
+    ylo, yhi = get_faces(bit_of("sub") == 1, ua, ub)
     qpad[2 : cx + 2, 2 : cy + 2] = pooled[...]
     qpad[0:2, 2 : cy + 2] = xlo[0:2]
     qpad[cx + 2 : cx + 4, 2 : cy + 2] = xhi[0:2]
@@ -259,10 +255,10 @@
         k, tap = t // 9, t % 9
         return acc[pl.ds(k * c2 + s * per, per), pl.ds(tap * c, c)]
 
-    spread(par[sub], keep, send, n, 28, piece)
-
-
-def back_body(n, sub, par, slope, w, cot, ds, ds_edge, own, halo, cbias, keep, send, up, st, rhs, acc):
+    spread(keep, send, n, 28, piece)
+
+
+def back_body(n, slope, w, cot, ds, ds_edge, own, halo, cbias, keep, send, up, st, rhs, acc):
     bx, by, bz, c = cot.shape
     cx, cy, cz = bx // 2, by // 2, bz // 2
     c2 = slope.shape[3]
@@ -323,10 +319,10 @@
         k, tap = t // 9, t % 9
         return acc[pl.ds(k * c + s * per, per), pl.ds(tap * c, c)]
 
-    spread(par[sub], keep, send, n, 28, piece)
-
-
-def merge_body(par, hidden, hid_edge, coarse, wm, out, tmp):
+    spread(keep, send, n, 28, piece)
+
+
+def merge_body(hidden, hid_edge, coarse, wm, out, tmp):
     bx, by, bz, c = out.shape
     cx, cy, cz = bx // 2, by // 2, bz // 2
     c2 = coarse.shape[3]
@@ -349,8 +345,8 @@
     return lax.ppermute(first, axis, one), got
 
 
-def split4_body(at_grp, at_sub, par, keep, got, own, over_sub, over_grp, over_both):
-    g, s = par[at_grp], par[at_sub]
+def split4_body(keep, got, own, over_sub, over_grp, over_both):
+    g, s = bit_of("grp"), bit_of("sub", 1)
 
     def part(a, b):
         return (keep[a, :, b].astype(F32) + got[a, :, b].astype(F32)).astype(BF16)
@@ -361,18 +357,12 @@
     own[...] = part(s, g)
 
 
-def split_body(count, bit, par, *refs):
-    parts, keep, send = refs[:count], refs[count], refs[count + 1]
-
-    def part(at):
-        return sum(p[at].astype(F32) for p in parts).astype(BF16)
-
-    send[...] = part(1 - par[bit])
-    keep[...] = part(par[bit])
-
-
-def sum_body(count, par, *refs):
-    refs[count][...] = sum(p[...].astype(F32) for p in refs[:count]).astype(BF16)
+def total_of(parts):
+    return sum(p.astype(F32) for p in parts).astype(BF16)
+
+
+def halves(pair, bit):
+    return jnp.where(bit == 1, pair[1], pair[0]), jnp.where(bit == 1, pair[0], pair[1])
 
 
 def partners(value, grp_mask, sub_mask):
@@ -385,13 +375,9 @@
     return lax.ppermute(value, ("grp", "sub"), pairs)
 
 
-def split_sum(parts, bits, bit, name):
+def split_sum(parts, bit):
     rows, c = parts[0].shape
-    half = ((rows // 2, c), BF16)
-    shaped = [p.reshape(2, rows // 2, c) for p in parts]
-    return call(
-        functools.partial(split_body, len(parts), bit), name, (bits, *shaped), [half, half], (), 0.8
-    )
+    return halves(total_of([p.reshape(2, rows // 2, c) for p in parts]), bit)
 
 
 def grp_bits():
@@ -402,14 +388,21 @@
     return partners(send, 0, 1)
 
 
-def spread_sum(keep, got, bits, name):
+def spread_sum(keep, got):
     half, rows, c = keep.shape
     rest = half // 2
     shape = (2, rest, 2, rows // 2, c)
     out = ((rest, rows // 2, c), BF16)
-    own, over_sub, over_grp, over_both = call(
-        functools.partial(split4_body, 0, grp_bits() + 1), name, (bits, keep.reshape(shape), got.reshape(shape)), [out] * 4, (), 1
-    )
+    return call(split4_body, "split", (keep.reshape(shape), got.reshape(shape)), [out] * 4, (), 1)
+
+
+def spread_sum_plain(keep, got, places):
+    half, rows, c = keep.shape
+    rest = half // 2
+    total = total_of([keep, got]).reshape(2, rest, 2, rows // 2, c)
+    near, far = halves(total, places[grp_bits() + 1])
+    own, over_grp = halves((near[:, 0], near[:, 1]), places[0])
+    over_sub, over_both = halves((far[:, 0], far[:, 1]), places[0])
     return own, over_sub, over_grp, over_both
 
 
@@ -417,40 +410,35 @@
     return [own, partners(over_both, 1, 2), partners(over_sub, 0, 2), partners(over_grp, 1, 0)]
 
 
-def finish_sum(parts, places, name):
+def finish_sum(parts, places):
     rest, rows, c = parts[0].shape
     parts = [p.reshape(rest * rows, c) for p in parts]
     for bit in range(2, lax.axis_size("sub").bit_length() - 1):
-        keep, send = split_sum(parts, places, grp_bits() + bit, name + f"_sub{bit}")
+        keep, send = split_sum(parts, places[grp_bits() + bit])
         parts = [keep, partners(send, 0, 1 << bit)]
     bits = [0]
     last = grp_bits() - 1
     for bit in range(1, last + 1):
         mask = 1 << bit
         if bit == 1 and bit < last and parts[0].shape[0] % 32 == 0:
-            keep, send = split_sum(parts, places, bit, name + "_half")
+            keep, send = split_sum(parts, places[bit])
             parts = [keep, partners(send, mask, 0)]
             bits.append(bit)
-            continue
-        out = [(parts[0].shape, BF16)]
-        (total,) = call(
-            functools.partial(sum_body, len(parts)), name + f"_sum{bit}", (places, *parts), out, (), 0.5
-        )
-        parts = [total, partners(total, mask, 0)]
-    (total,) = call(
-        functools.partial(sum_body, len(parts)), name + "_total", (places, *parts), [(parts[0].shape, BF16)], (), 0.5
-    )
+        else:
+            total = total_of(parts)
+            parts = [total, partners(total, mask, 0)]
+    total = total_of(parts)
     pieces = [total]
     for which in range(1, 2 ** len(bits)):
         pieces.append(partners(total, sum(1 << bits[b] for b in range(len(bits)) if which >> b & 1), 0))
-    return pieces, bits
-
-
-def last_body(count, par, *refs):
+    return pieces
+
+
+def last_body(count, *refs):
     pieces, kernel, extra, rows = refs[:count], refs[count], refs[count + 1], refs[-1]
     size = pieces[0].shape[0]
     per = extra.shape[0] if len(refs) == count + 3 else kernel.shape[3]
-    mine = par[0] if count == 2 else 2 * par[0] + par[1]
+    mine = bit_of("grp") if count == 2 else 2 * bit_of("grp") + bit_of("grp", 1)
     for which in range(count):
         mask = which if count == 2 else 2 * (which & 1) + (which >> 1)
         rows[mine ^ mask] = pieces[which][...]
@@ -473,13 +461,13 @@
         refs[count + 2][:, pl.ds(per, per)] = turned[2:3]
 
 
-def last(pieces, bits, places, per, outs, name):
+def last(pieces, per, outs, name):
     count = len(pieces)
     size, c = pieces[0].shape
     kernel, *rest = call(
         functools.partial(last_body, count),
         name,
-        (places, *pieces),
+        tuple(pieces),
         [((3, 3, 3, per, c), F32), *outs],
         [pltpu.VMEM((count, size, c), BF16)],
         1,
@@ -488,32 +476,28 @@
 
 
 def per_device(field, cotangent, fine_kernel, fine_bias, coarse_kernel, coarse_bias, merge_weight):
-    grp, sub = lax.axis_index("grp"), lax.axis_index("sub")
     n = lax.axis_size("sub")
     bx, by, bz, c = field.shape
     cx, cy, cz = bx // 2, by // 2, bz // 2
     c2 = merge_weight.shape[0]
-    count = grp_bits()
-    order = jnp.arange(count + n.bit_length() - 1, dtype=jnp.int32)
-    par = jnp.where(order < count, grp >> order, sub >> (order - count)).astype(jnp.int32) & 1
     face = ((bx, bz, c), BF16)
     sa, sb = call(
-        functools.partial(prep_body, count),
-        "prep",
-        (par, (field, None, None)),
-        [face, face],
-        [pltpu.SemaphoreType.DMA((2,))],
-        limit=127 * 512 * 1024,
+        prep_body, "prep", (field,), [face, face], [pltpu.SemaphoreType.DMA((2,))], space=pltpu.HBM
     )
     ya, yb = swap_faces(sa, sb, "sub")
-    (pg,) = call(
-        cubes_body, "cubes", (par, cotangent), [((cx, cy, cz, c), BF16)], [pltpu.VMEM((cx * cy * bz, c), F32)]
+    count = grp_bits() + n.bit_length() - 1
+    pg, places = call(
+        cubes_body,
+        "cubes",
+        (cotangent,),
+        [((cx, cy, cz, c), BF16), ((count, 1, c), jnp.int32)],
+        [pltpu.VMEM((cx * cy * bz, c), F32)],
     )
     face = ((by + 2, bz, c), BF16)
     own, ta, tb = call(
-        functools.partial(turn_body, count),
+        turn_body,
         "turn",
-        (par, field, ya, yb),
+        (field, ya, yb),
         [((bx, by + 2, bz, c), BF16), face, face],
     )
     xa, xb = swap_faces(ta, tb, "grp")
@@ -521,7 +505,7 @@
     hidden, ds, pooled, wb = call(
         inner_body,
         "inner",
-        (par, own, fine_kernel, bias),
+        (own, fine_kernel, bias),
         [
             ((bx - 2, by, bz, c), BF16),
             ((bx - 2, by, bz, c), F32),
@@ -535,7 +519,7 @@
     hid_edge, ds_edge, halo, pooled, pa, pb = call(
         outer_body,
         "outer",
-        (par, own, xa, xb, wb, bias, hidden, pooled, pg),
+        (own, xa, xb, wb, bias, hidden, pooled, pg),
         [
             ((2, by, bz, c), BF16),
             ((2, by, bz, c), F32),
@@ -549,14 +533,14 @@
     )
     pxa, pxb = swap_faces(pa, pb, "grp")
     face = ((2 * (cx + 4) + cx + 2, cz, c), BF16)
-    qa, qb = call(functools.partial(turn2_body, count), "turn2", (par, pooled, pg, pxa, pxb), [face, face])
+    qa, qb = call(turn2_body, "turn2", (pooled, pg, pxa, pxb), [face, face])
     pya, pyb = swap_faces(qa, qb, "sub")
     cells = cx * cy * cz
     part = (n // 2, 28 * (c2 // n), c)
     slope, coarse, ckeep, csend, cbias = call(
-        functools.partial(coarse_body, n, count),
+        functools.partial(coarse_body, n),
         "coarse",
-        (par, pooled, pxa, pxb, pya, pyb, pg, coarse_kernel, coarse_bias.reshape(1, c2), merge_weight),
+        (pooled, pxa, pxb, pya, pyb, pg, coarse_kernel, coarse_bias.reshape(1, c2), merge_weight),
         [
             ((cx + 2, cy + 2, cz, c2), BF16),
             ((cx, cy, cz, c2), BF16),
@@ -579,21 +563,21 @@
     (output,) = call(
         merge_body,
         "merge",
-        (par, hidden, hid_edge, coarse, merge_weight),
+        (hidden, hid_edge, coarse, merge_weight),
         [((bx, by, bz, c), BF16)],
         [pltpu.VMEM((cx * cy * bz, c), F32)],
         2,
     )
     output, cgot = lax.optimization_barrier((output, cgot))
-    csent = spread_sum(ckeep, cgot, par, "coarse_split")
+    csent = spread_sum(ckeep, cgot)
     slope, csent = lax.optimization_barrier((slope, csent))
     cparts = cross(*csent)
     voxels = bx * by * bz
     part = (n // 2, 28 * (c // n), c)
     fkeep, fsend = call(
-        functools.partial(back_body, n, count),
+        functools.partial(back_body, n),
         "back",
-        (par, slope, coarse_kernel, cotangent, ds, ds_edge, own, halo, cbias),
+        (slope, coarse_kernel, cotangent, ds, ds_edge, own, halo, cbias),
         [(part, BF16), (part, BF16)],
         [
             pltpu.VMEM((cx * cy * bz, c), F32),
@@ -605,13 +589,13 @@
     )
     fsend, cparts = lax.optimization_barrier((fsend, cparts))
     fgot = cores(fsend)
-    fparts = cross(*spread_sum(fkeep, fgot, par, "fine_split"))
-    coarse_sum = finish_sum(cparts, par, "coarse")
-    fine_sum = finish_sum(fparts, par, "fine")
+    fparts = cross(*spread_sum_plain(fkeep, fgot, places))
+    coarse_sum = finish_sum(cparts, places)
+    fine_sum = finish_sum(fparts, places)
     per, cper = c // n, c2 // n
-    grad_coarse, grad_merge = last(*coarse_sum, par, cper, [((cper, c), F32)], "coarse_last")
+    grad_coarse, grad_merge = last(coarse_sum, cper, [((cper, c), F32)], "coarse_last")
     biases = [((1, per), F32), ((1, cper), F32)]
-    grad_fine, bias, coarse_sums = last(*fine_sum, par, per, biases, "fine_last")
+    grad_fine, bias, coarse_sums = last(fine_sum, per, biases, "fine_last")
     return (output, grad_fine, bias[0], grad_coarse, coarse_sums[0], grad_merge)
 
 

time: 97.2 us -> 96.9 us (level)
  Pallas kernels: 37.4 us -> 29.9 us
  waiting for transfers between devices: 13.1 us -> 18.1 us
  starting transfers between devices: 43.8 us -> 45.8 us
    pallas_call x19 -> x12, Pallas kernels: 37.4 us -> 29.9 us  [call(): pl.pallas_call(body, name=name, out_shape=[jax.ShapeDtypeStruct(s, t) for...]
    ppermute x18, waiting for transfers between devices: 10.9 us -> 15.9 us  [partners(): return lax.ppermute(value, ('grp', 'sub'), pairs)]
    ppermute x4, starting transfers between devices: 9.63 us -> 11.1 us  [swap_faces(): return (lax.ppermute(first, axis, one), got)]
  transfers between devices with their start and end apart: 26 -> 26, of which waited for: 9 -> 11; matrix products, arithmetic and copies ran while one was open for 0% -> 1% of each run, Pallas kernels for 24% -> 17%
where the time goes in v4:
time: 96.9 us; the launch traced here: 96.6 us
  starting transfers between devices  45.8 us (47%)
  Pallas kernels  29.9 us (31%)
  waiting for transfers between devices  18.1 us (19%)
  local copies, waits for them, and re-layouts  1.3 us (1%)
    ppermute x18, starting transfers between devices, partners(): return lax.ppermute(value, ('grp', 'sub'), pairs)  32 us
    pallas_call x12, Pallas kernels, call(): pl.pallas_call(body, name=name, out_shape=[jax.ShapeDtypeStruct(s, t) for...  29.9 us
    ppermute x18, waiting for transfers between devices, partners(): return lax.ppermute(value, ('grp', 'sub'), pairs)  15.9 us
    ppermute x4, starting transfers between devices, swap_faces(): return (lax.ppermute(first, axis, one), got)  11.1 us
    ppermute x4, starting transfers between devices, swap_faces(): got = lax.ppermute(second, axis, two)  2.75 us
    ppermute x4, waiting for transfers between devices, swap_faces(): return (lax.ppermute(first, axis, one), got)  2.21 us
  transfers between devices with their start and end apart: 26, of which 11 were waited for; matrix products, arithmetic and copies ran while one was open for 1% of the time, Pallas kernels for 17%

profile of v4, /device:TPU:0, one launch (start us, length us, event | category | flops | bytes accessed | tf_op | source)
XLA Modules:
  0.0 96.6 jit_solution(298929580736784088)
XLA Ops:
  0.6 5.1 %prep.1 = (bf16[8,32,128]{2,1,0:T(8,128)(2,1)}, bf16[8,32,128]{2,1,0:T(8,128)(2,1)}) custom-call(bf16[8,16,32,128]{3,2,1,0:T(8,128)(2,1)} %field.3), custom_call_target="tpu_custom_call" | custom-call | flops 1000000000 | tf_op jit(solution)/shard_map/prep/pallas_call | solution.py:21
  5.7 0.5 collective-permute-start
  6.3 0.8 collective-permute-start.1
  7.0 0.0 copy-start.2
  7.1 1.2 %copy-done.2 = bf16[8,16,32,128]{3,2,1,0:T(8,128)(2,1)S(1)} copy-done((bf16[8,16,32,128]{3,2,1,0:T(8,128)(2,1)S(1)}, bf16[8,16,32,128]{3,2,1,0:T(8,128)(2,1)}, u32[]{:S(2)}) %copy-start.2) | copy-done | bytes 1048600
  8.3 0.2 cubes.1
  8.5 0.0 copy-start.4
  8.5 0.0 copy-start.7
  8.5 0.0 collective-permute-done.ya
  8.5 0.0 collective-permute-done.1.yb
  8.5 0.2 turn.1
  8.7 2.6 %collective-permute-start.2 = (bf16[18,32,128]{2,1,0:T(8,128)(2,1)S(1)}, bf16[18,32,128]{2,1,0:T(8,128)(2,1)S(1)}, u32[]{:S(2)}, u32[]{:S(2)}) collective-permute-start(bf16[18,32,128]{2,1,0:T(8,128)(2,1)S(1)} %get-tuple-element.57), channel_id=1, source_target_pairs={{0,4},{4,0},{8,12},{12,8},{16,20},{20,16},{24,28},{28,24},{1,5},{5... | collective-permute-start | bytes 442376 | tf_op jit(solution)/shard_map/ppermute | solution.py:345
  11.3 0.7 collective-permute-start.3
  12.0 5.7 %inner.1 = (bf16[6,16,32,128]{3,2,1,0:T(8,128)(2,1)S(1)}, f32[6,16,32,128]{3,2,1,0:T(8,128)S(1)}, bf16[2,8,16,128]{3,2,1,0:T(8,128)(2,1)S(1)}, bf16[1152,384]{1,0:T(8,128)(2,1)S(1)}) custom-call(bf16[8,18,32,128]{3,2,1,0:T(8,128)(2,1)S(1)} %get-tuple-element.55.own, bf16[3,3,3,128,128]{4,3,2,1,0:T(8,128)(2,1)S(1)} %copy-done.4, f32[1,128]{1,0:T(1,128)S(1)} %bitcast.66), custom_call_target="tpu_custom_call" | custom-call | flops 6000000000 | tf_op jit(solution)/shard_map/inner/pallas_call | solution.py:21
  17.7 0.0 collective-permute-done.2.ra
  17.7 0.0 collective-permute-done.3.rb
  17.7 1.7 %outer.1 = (bf16[2,16,32,128]{3,2,1,0:T(8,128)(2,1)S(1)}, f32[2,16,32,128]{3,2,1,0:T(8,128)S(1)}, bf16[2,18,32,128]{3,2,1,0:T(8,128)(2,1)S(1)}, bf16[4,8,16,128]...) custom-call(bf16[8,18,32,128]{3,2,1,0:T(8,128)(2,1)S(1)} %get-tuple-element.55.own, ...), custom_call_target="tpu_custom_call" | custom-call | flops 2000000000 | tf_op jit(solution)/shard_map/outer/pallas_call | solution.py:21
  19.4 4.3 %collective-permute-start.4 = (bf16[3,8,16,128]{3,2,1,0:T(8,128)(2,1)S(1)}, bf16[3,8,16,128]{3,2,1,0:T(8,128)(2,1)S(1)}, u32[]{:S(2)}, u32[]{:S(2)}) collective-permute-start(bf16[3,8,16,128]{3,2,1,0:T(8,128)(2,1)S(1)} %get-tuple-element.64), channel_id=1, source_target_pairs={{0,4},{4,0},{8,12},{12,8},{16,20},{20,16},{24,28},{28,24},{1,5},{5... | collective-permute-start | bytes 294920 | tf_op jit(solution)/shard_map/ppermute | solution.py:345
  23.7 0.7 collective-permute-start.5
  24.4 1.9 %collective-permute-done.4.ra = bf16[3,8,16,128]{3,2,1,0:T(8,128)(2,1)S(1)} collective-permute-done((bf16[3,8,16,128]{3,2,1,0:T(8,128)(2,1)S(1)}, bf16[3,8,16,128]{3,2,1,0:T(8,128)(2,1)S(1)}, u32[]{:S(2)}, u32[]{:S(2)}) %collective-permute-start.4) | collective-permute-done | bytes 98336 | tf_op jit(solution)/shard_map/ppermute | solution.py:345
  26.3 0.0 collective-permute-done.5.rb
  26.4 3.6 %collective-permute-start.6 = (bf16[22,16,128]{2,1,0:T(8,128)(2,1)S(1)}, bf16[22,16,128]{2,1,0:T(8,128)(2,1)S(1)}, u32[]{:S(2)}, u32[]{:S(2)}) collective-permute-start(bf16[22,16,128]{2,1,0:T(8,128)(2,1)S(1)} %get-tuple-element.66), channel_id=1, source_target_pairs={{0,1},{1,0},{2,3},{3,2},{4,5},{5,4},{6,7},{7,6},{8,9},{9,8},{10,11... | collective-permute-start | bytes 270344 | tf_op jit(solution)/shard_map/ppermute | solution.py:345
  30.0 0.7 collective-permute-start.7
  30.7 0.3 collective-permute-done.6.ua
  31.0 0.0 collective-permute-done.7.ub
  31.0 5.5 %coarse.1 = (bf16[6,10,16,256]{3,2,1,0:T(8,128)(2,1)S(1)}, bf16[4,8,16,256]{3,2,1,0:T(8,128)(2,1)S(1)}, bf16[2,1792,128]{2,1,0:T(8,128)(2,1)S(1)}, bf16[2,1792,128]{2,1,0:T(8,128)(2,1)S(1)}, bf16[256,128]{1,0:T(8,128)(2,1)S(1)}) custom-call(bf16[4,8,16,128]{3,2,1,0:T(8,128)(2,1)S(1)} %get-tuple-element.63.pooled, ...), custom_call_target="tpu_custom_call" | custom-call | flops 6000000000 | tf_op jit(solution)/shard_map/coarse/pallas_call | solution.py:21
  36.5 5.1 %collective-permute-start.8 = (bf16[2,1792,128]{2,1,0:T(8,128)(2,1)S(1)}, bf16[2,1792,128]{2,1,0:T(8,128)(2,1)S(1)}, u32[]{:S(2)}, u32[]{:S(2)}) collective-permute-start(bf16[2,1792,128]{2,1,0:T(8,128)(2,1)S(1)} %get-tuple-element.69), channel_id=1, source_target_pairs={{0,1},{1,0},{2,3},{3,2},{4,5},{5,4},{6,7},{7,6},{8,9},{9,8},{10,11... | collective-permute-start | bytes 2752520 | tf_op jit(solution)/shard_map/ppermute | solution.py:375
  41.6 1.3 %merge.1 = bf16[8,16,32,128]{3,2,1,0:T(8,128)(2,1)} custom-call(bf16[6,16,32,128]{3,2,1,0:T(8,128)(2,1)S(1)} %get-tuple-element.56.hid_in.hidden, bf16[2,16,32,128]{3,2,1,0:T(8,128)(2,1)S(1)} %get-tuple-element.62.hid_edge, bf16[4,8,16,256]{3,2,1,0:T(8,128)(2,1)S(1)} %get-tuple-element.68.coarse, bf16[256,128]{1,0:T(8,128)(2,1)S(1)} %copy-done.5), custom_call_target="tpu_custom_call" | custom-call | flops 2000000000 | tf_op jit(solution)/shard_map/merge/pallas_call | solution.py:21
  43.0 0.8 collective-permute-done.8
  43.7 0.2 split.1
  44.0 6.4 %collective-permute-start.9 = (bf16[1,896,128]{2,1,0:T(8,128)(2,1)S(1)}, bf16[1,896,128]{2,1,0:T(8,128)(2,1)S(1)}, u32[]{:S(2)}, u32[]{:S(2)}) collective-permute-start(bf16[1,896,128]{2,1,0:T(8,128)(2,1)S(1)} %get-tuple-element.87), channel_id=1, source_target_pairs={{0,6},{1,7},{2,4},{3,5},{4,2},{5,3},{6,0},{7,1},{8,14},{9,15},{10,... | collective-permute-start | bytes 688136 | tf_op jit(solution)/shard_map/ppermute | solution.py:375
  50.3 0.1 collective-permute-start.10
  50.4 0.6 collective-permute-start.11
  51.0 8.1 %back.1 = (bf16[2,896,128]{2,1,0:T(8,128)(2,1)S(1)}, bf16[2,896,128]{2,1,0:T(8,128)(2,1)S(1)}) custom-call(bf16[6,10,16,256]{3,2,1,0:T(8,128)(2,1)S(1)} %get-tuple-element.79.slope, bf16[3,3,3,128,256]{4,3,2,1,0:T(8,128)(2,1)S(1)} %copy-done, bf16[8,16,32,128]{3,2,1,0:T(8,128)(2,1)S(1)} %copy-done.3, f32[6,16,32,128]{3,2,1,0:T(8,128)S(1)} %get-tuple-element.80.ds, ...), custom_call_target="tpu_custom_call" | custom-call | flops 10000000000 | tf_op jit(solution)/shard_map/back/pallas_call | solution.py:21
  59.1 0.0 collective-permute-done.9
  59.1 2.1 %collective-permute-done.10 = bf16[1,896,128]{2,1,0:T(8,128)(2,1)S(1)} collective-permute-done((bf16[1,896,128]{2,1,0:T(8,128)(2,1)S(1)}, bf16[1,896,128]{2,1,0:T(8,128)(2,1)S(1)}, u32[]{:S(2)}, u32[]{:S(2)}) %collective-permute-start.10) | collective-permute-done | bytes 229408 | tf_op jit(solution)/shard_map/ppermute | solution.py:375
  61.1 0.0 collective-permute-start.12
  61.2 0.1 add_convert_fusion.1
  61.3 3.3 %collective-permute-start.21 = (bf16[448,128]{1,0:T(8,128)(2,1)S(1)}, bf16[448,128]{1,0:T(8,128)(2,1)S(1)}, u32[]{:S(2)}, u32[]{:S(2)}) collective-permute-start(bf16[448,128]{1,0:T(8,128)(2,1)S(1)} %broadcast_select_fusion.2), channel_id=1, source_target_pairs={{0,8},{1,9},{2,10},{3,11},{4,12},{5,13},{6,14},{7,15},{8,0},{9,1},... | collective-permute-start | bytes 344072 | tf_op jit(solution)/shard_map/ppermute | solution.py:375
  64.6 0.1 add_convert_fusion
  64.8 1.1 %collective-permute-start.13 = (bf16[1,448,128]{2,1,0:T(8,128)(2,1)S(1)}, bf16[1,448,128]{2,1,0:T(8,128)(2,1)S(1)}, u32[]{:S(2)}, u32[]{:S(2)}) collective-permute-start(bf16[1,448,128]{2,1,0:T(8,128)(2,1)S(1)} %get-tuple-element.104), channel_id=1, source_target_pairs={{0,6},{1,7},{2,4},{3,5},{4,2},{5,3},{6,0},{7,1},{8,14},{9,15},{10,... | collective-permute-start | bytes 344072 | tf_op jit(solution)/shard_map/ppermute | solution.py:375
  65.9 0.7 collective-permute-start.14
  66.6 1.8 %collective-permute-start.15 = (bf16[1,448,128]{2,1,0:T(8,128)(2,1)S(1)}, bf16[1,448,128]{2,1,0:T(8,128)(2,1)S(1)}, u32[]{:S(2)}, u32[]{:S(2)}) collective-permute-start(bf16[1,448,128]{2,1,0:T(8,128)(2,1)S(1)} %get-tuple-element.111), channel_id=1, source_target_pairs={{0,4},{1,5},{2,6},{3,7},{4,0},{5,1},{6,2},{7,3},{8,12},{9,13},{10,... | collective-permute-start | bytes 344072 | tf_op jit(solution)/shard_map/ppermute | solution.py:375
  68.4 3.4 %collective-permute-done.13 = bf16[1,448,128]{2,1,0:T(8,128)(2,1)S(1)} collective-permute-done((bf16[1,448,128]{2,1,0:T(8,128)(2,1)S(1)}, bf16[1,448,128]{2,1,0:T(8,128)(2,1)S(1)}, u32[]{:S(2)}, u32[]{:S(2)}) %collective-permute-start.13) | collective-permute-done | bytes 114720 | tf_op jit(solution)/shard_map/ppermute | solution.py:375
  71.8 1.5 %collective-permute-done.14 = bf16[1,448,128]{2,1,0:T(8,128)(2,1)S(1)} collective-permute-done((bf16[1,448,128]{2,1,0:T(8,128)(2,1)S(1)}, bf16[1,448,128]{2,1,0:T(8,128)(2,1)S(1)}, u32[]{:S(2)}, u32[]{:S(2)}) %collective-permute-start.14) | collective-permute-done | bytes 114720 | tf_op jit(solution)/shard_map/ppermute | solution.py:375
  73.3 0.0 collective-permute-done.15
  73.4 0.1 fusion
  73.5 1.6 %collective-permute-start.16 = (bf16[224,128]{1,0:T(8,128)(2,1)S(1)}, bf16[224,128]{1,0:T(8,128)(2,1)S(1)}, u32[]{:S(2)}, u32[]{:S(2)}) collective-permute-start(bf16[224,128]{1,0:T(8,128)(2,1)S(1)} %broadcast_select_fusion.5), channel_id=1, source_target_pairs={{0,8},{1,9},{2,10},{3,11},{4,12},{5,13},{6,14},{7,15},{8,0},{9,1},... | collective-permute-start | bytes 172040 | tf_op jit(solution)/shard_map/ppermute | solution.py:375
  75.0 0.0 collective-permute-done.21
  75.1 1.5 %collective-permute-start.22 = (bf16[448,128]{1,0:T(8,128)(2,1)S(1)}, bf16[448,128]{1,0:T(8,128)(2,1)S(1)}, u32[]{:S(2)}, u32[]{:S(2)}) collective-permute-start(bf16[448,128]{1,0:T(8,128)(2,1)S(1)} %add_convert_fusion.3), channel_id=1, source_target_pairs={{0,16},{1,17},{2,18},{3,19},{4,20},{5,21},{6,22},{7,23},{8,24},{9,... | collective-permute-start | bytes 344072 | tf_op jit(solution)/shard_map/ppermute | solution.py:375
  76.6 1.1 %collective-permute-done.16 = bf16[224,128]{1,0:T(8,128)(2,1)S(1)} collective-permute-done((bf16[224,128]{1,0:T(8,128)(2,1)S(1)}, bf16[224,128]{1,0:T(8,128)(2,1)S(1)}, u32[]{:S(2)}, u32[]{:S(2)}) %collective-permute-start.16) | collective-permute-done | bytes 57376 | tf_op jit(solution)/shard_map/ppermute | solution.py:375
  77.7 3.1 %collective-permute-start.17 = (bf16[224,128]{1,0:T(8,128)(2,1)S(1)}, bf16[224,128]{1,0:T(8,128)(2,1)S(1)}, u32[]{:S(2)}, u32[]{:S(2)}) collective-permute-start(bf16[224,128]{1,0:T(8,128)(2,1)S(1)} %add_convert_fusion.5), channel_id=1, source_target_pairs={{0,16},{1,17},{2,18},{3,19},{4,20},{5,21},{6,22},{7,23},{8,24},{9,... | collective-permute-start | bytes 172040 | tf_op jit(solution)/shard_map/ppermute | solution.py:375
  80.8 4.0 %collective-permute-done.22 = bf16[448,128]{1,0:T(8,128)(2,1)S(1)} collective-permute-done((bf16[448,128]{1,0:T(8,128)(2,1)S(1)}, bf16[448,128]{1,0:T(8,128)(2,1)S(1)}, u32[]{:S(2)}, u32[]{:S(2)}) %collective-permute-start.22) | collective-permute-done | bytes 114720 | tf_op jit(solution)/shard_map/ppermute | solution.py:375
  84.8 0.1 collective-permute-start.25
  84.9 2.2 %collective-permute-start.24 = (bf16[448,128]{1,0:T(8,128)(2,1)S(1)}, bf16[448,128]{1,0:T(8,128)(2,1)S(1)}, u32[]{:S(2)}, u32[]{:S(2)}) collective-permute-start(bf16[448,128]{1,0:T(8,128)(2,1)S(1)} %add_convert_fusion.2.refs_0_), channel_id=1, source_target_pairs={{0,8},{1,9},{2,10},{3,11},{4,12},{5,13},{6,14},{7,15},{8,0},{9,1},... | collective-permute-start | bytes 344072 | tf_op jit(solution)/shard_map/ppermute | solution.py:375
  87.1 1.3 %collective-permute-start.23 = (bf16[448,128]{1,0:T(8,128)(2,1)S(1)}, bf16[448,128]{1,0:T(8,128)(2,1)S(1)}, u32[]{:S(2)}, u32[]{:S(2)}) collective-permute-start(bf16[448,128]{1,0:T(8,128)(2,1)S(1)} %add_convert_fusion.2.refs_0_), channel_id=1, source_target_pairs={{0,4},{1,5},{2,6},{3,7},{4,0},{5,1},{6,2},{7,3},{8,12},{9,13},{10,... | collective-permute-start | bytes 344072 | tf_op jit(solution)/shard_map/ppermute | solution.py:375
  88.4 0.3 collective-permute-start.20
  88.7 2.0 %collective-permute-start.19 = (bf16[224,128]{1,0:T(8,128)(2,1)S(1)}, bf16[224,128]{1,0:T(8,128)(2,1)S(1)}, u32[]{:S(2)}, u32[]{:S(2)}) collective-permute-start(bf16[224,128]{1,0:T(8,128)(2,1)S(1)} %add_convert_fusion.4.refs_0_), channel_id=1, source_target_pairs={{0,8},{1,9},{2,10},{3,11},{4,12},{5,13},{6,14},{7,15},{8,0},{9,1},... | collective-permute-start | bytes 172040 | tf_op jit(solution)/shard_map/ppermute | solution.py:375
  90.7 0.9 collective-permute-done.25.refs_3_
  91.6 1.0 %collective-permute-start.18 = (bf16[224,128]{1,0:T(8,128)(2,1)S(1)}, bf16[224,128]{1,0:T(8,128)(2,1)S(1)}, u32[]{:S(2)}, u32[]{:S(2)}) collective-permute-start(bf16[224,128]{1,0:T(8,128)(2,1)S(1)} %add_convert_fusion.4.refs_0_), channel_id=1, source_target_pairs={{0,4},{1,5},{2,6},{3,7},{4,0},{5,1},{6,2},{7,3},{8,12},{9,13},{10,... | collective-permute-start | bytes 172040 | tf_op jit(solution)/shard_map/ppermute | solution.py:375
  92.6 0.5 collective-permute-done.23.refs_1_
  93.1 1.0 %coarse_last.1 = (f32[3,3,3,64,128]{4,3,2,1,0:T(8,128)}, f32[64,128]{1,0:T(8,128)}) custom-call(bf16[448,128]{1,0:T(8,128)(2,1)S(1)} %add_convert_fusion.2.refs_0_, bf16[448,128]{1,0:T(8,128)(2,1)S(1)} %collective-permute-done.23.refs_1_, bf16[448,128]{1,0:T(8,128)(2,1)S(1)} %collective-permute-done.24.refs_2_, ...), custom_call_target="tpu_custom_call" | custom-call | flops 1000000000 | tf_op jit(solution)/shard_map/coarse_last/pallas_call | solution.py:21
  94.1 1.6 %collective-permute-done.18.refs_1_ = bf16[224,128]{1,0:T(8,128)(2,1)S(1)} collective-permute-done((bf16[224,128]{1,0:T(8,128)(2,1)S(1)}, bf16[224,128]{1,0:T(8,128)(2,1)S(1)}, u32[]{:S(2)}, u32[]{:S(2)}) %collective-permute-start.18) | collective-permute-done | bytes 57376 | tf_op jit(solution)/shard_map/ppermute | solution.py:375
  95.8 0.9 fine_last.1
  (30 shorter events, 0.4 us)
Async XLA Ops:
  5.7 2.8 %collective-permute-start = (bf16[8,32,128]{2,1,0:T(8,128)(2,1)}, bf16[8,32,128]{2,1,0:T(8,128)(2,1)S(1)}, u32[]{:S(2)}, u32[]{:S(2)}) collective-permute-start(bf16[8,32,128]{2,1,0:T(8,128)(2,1)} %get-tuple-element.53), channel_id=1, source_target_pairs={{0,1},{1,0},{2,3},{3,2},{4,5},{5,4},{6,7},{7,6},{8,9},{9,8},{10,11... | collective-permute-start | bytes 196616 | tf_op jit(solution)/shard_map/ppermute | solution.py:345
  6.3 2.3 %copy-start.1 = (bf16[8,16,32,128]{3,2,1,0:T(8,128)(2,1)S(1)}, bf16[8,16,32,128]{3,2,1,0:T(8,128)(2,1)}, u32[]{:S(2)}) copy-start(bf16[8,16,32,128]{3,2,1,0:T(8,128)(2,1)} %field.3) | copy-start | bytes 3145732
  6.3 2.3 %collective-permute-start.1 = (bf16[8,32,128]{2,1,0:T(8,128)(2,1)}, bf16[8,32,128]{2,1,0:T(8,128)(2,1)S(1)}, u32[]{:S(2)}, u32[]{:S(2)}) collective-permute-start(bf16[8,32,128]{2,1,0:T(8,128)(2,1)} %get-tuple-element.54), channel_id=1, source_target_pairs={{1,2},{2,1},{5,6},{6,5},{9,10},{10,9},{13,14},{14,13},{17,18},{18,... | collective-permute-start | bytes 196616 | tf_op jit(solution)/shard_map/ppermute | solution.py:344
  7.0 1.2 %copy-start.2 = (bf16[8,16,32,128]{3,2,1,0:T(8,128)(2,1)S(1)}, bf16[8,16,32,128]{3,2,1,0:T(8,128)(2,1)}, u32[]{:S(2)}) copy-start(bf16[8,16,32,128]{3,2,1,0:T(8,128)(2,1)} %cot.3) | copy-start | bytes 3145732
  8.5 3.5 %copy-start.4 = (bf16[3,3,3,128,128]{4,3,2,1,0:T(8,128)(2,1)S(1)}, bf16[3,3,3,128,128]{4,3,2,1,0:T(8,128)(2,1)}, u32[]{:S(2)}) copy-start(bf16[3,3,3,128,128]{4,3,2,1,0:T(8,128)(2,1)} %w.3) | copy-start | bytes 2654212
  8.5 3.5 %copy-start.7 = (f32[128]{0:T(128)S(1)}, f32[128]{0:T(128)}, u32[]{:S(2)}) copy-start(f32[128]{0:T(128)} %param.10) | copy-start | bytes 1540
  8.7 9.0 %collective-permute-start.2 = (bf16[18,32,128]{2,1,0:T(8,128)(2,1)S(1)}, bf16[18,32,128]{2,1,0:T(8,128)(2,1)S(1)}, u32[]{:S(2)}, u32[]{:S(2)}) collective-permute-start(bf16[18,32,128]{2,1,0:T(8,128)(2,1)S(1)} %get-tuple-element.57), channel_id=1, source_target_pairs={{0,4},{4,0},{8,12},{12,8},{16,20},{20,16},{24,28},{28,24},{1,5},{5... | collective-permute-start | bytes 442376 | tf_op jit(solution)/shard_map/ppermute | solution.py:345
  11.3 6.4 %collective-permute-start.3 = (bf16[18,32,128]{2,1,0:T(8,128)(2,1)S(1)}, bf16[18,32,128]{2,1,0:T(8,128)(2,1)S(1)}, u32[]{:S(2)}, u32[]{:S(2)}) collective-permute-start(bf16[18,32,128]{2,1,0:T(8,128)(2,1)S(1)} %get-tuple-element.58), channel_id=1, source_target_pairs={{4,8},{8,4},{12,16},{16,12},{20,24},{24,20},{5,9},{9,5},{13,17},{1... | collective-permute-start | bytes 442376 | tf_op jit(solution)/shard_map/ppermute | solution.py:344
  19.4 6.9 %collective-permute-start.4 = (bf16[3,8,16,128]{3,2,1,0:T(8,128)(2,1)S(1)}, bf16[3,8,16,128]{3,2,1,0:T(8,128)(2,1)S(1)}, u32[]{:S(2)}, u32[]{:S(2)}) collective-permute-start(bf16[3,8,16,128]{3,2,1,0:T(8,128)(2,1)S(1)} %get-tuple-element.64), channel_id=1, source_target_pairs={{0,4},{4,0},{8,12},{12,8},{16,20},{20,16},{24,28},{28,24},{1,5},{5... | collective-permute-start | bytes 294920 | tf_op jit(solution)/shard_map/ppermute | solution.py:345
  23.7 2.6 %collective-permute-start.5 = (bf16[3,8,16,128]{3,2,1,0:T(8,128)(2,1)S(1)}, bf16[3,8,16,128]{3,2,1,0:T(8,128)(2,1)S(1)}, u32[]{:S(2)}, u32[]{:S(2)}) collective-permute-start(bf16[3,8,16,128]{3,2,1,0:T(8,128)(2,1)S(1)} %get-tuple-element.65), channel_id=1, source_target_pairs={{4,8},{8,4},{12,16},{16,12},{20,24},{24,20},{5,9},{9,5},{13,17},{1... | collective-permute-start | bytes 294920 | tf_op jit(solution)/shard_map/ppermute | solution.py:344
  26.3 4.6 %copy-start = (bf16[3,3,3,128,256]{4,3,2,1,0:T(8,128)(2,1)S(1)}, bf16[3,3,3,128,256]{4,3,2,1,0:T(8,128)(2,1)}, u32[]{:S(2)}) copy-start(bf16[3,3,3,128,256]{4,3,2,1,0:T(8,128)(2,1)} %w.5) | copy-start | bytes 5308420
  26.3 4.6 %copy-start.5 = (bf16[256,128]{1,0:T(8,128)(2,1)S(1)}, bf16[256,128]{1,0:T(8,128)(2,1)}, u32[]{:S(2)}) copy-start(bf16[256,128]{1,0:T(8,128)(2,1)} %wm.3) | copy-start | bytes 196612
  26.3 4.6 %copy-start.6 = (f32[256]{0:T(256)S(1)}, f32[256]{0:T(256)}, u32[]{:S(2)}) copy-start(f32[256]{0:T(256)} %param.12) | copy-start | bytes 3076
  26.4 4.6 %collective-permute-start.6 = (bf16[22,16,128]{2,1,0:T(8,128)(2,1)S(1)}, bf16[22,16,128]{2,1,0:T(8,128)(2,1)S(1)}, u32[]{:S(2)}, u32[]{:S(2)}) collective-permute-start(bf16[22,16,128]{2,1,0:T(8,128)(2,1)S(1)} %get-tuple-element.66), channel_id=1, source_target_pairs={{0,1},{1,0},{2,3},{3,2},{4,5},{5,4},{6,7},{7,6},{8,9},{9,8},{10,11... | collective-permute-start | bytes 270344 | tf_op jit(solution)/shard_map/ppermute | solution.py:345
  30.0 0.9 collective-permute-start.7
  36.5 7.2 %collective-permute-start.8 = (bf16[2,1792,128]{2,1,0:T(8,128)(2,1)S(1)}, bf16[2,1792,128]{2,1,0:T(8,128)(2,1)S(1)}, u32[]{:S(2)}, u32[]{:S(2)}) collective-permute-start(bf16[2,1792,128]{2,1,0:T(8,128)(2,1)S(1)} %get-tuple-element.69), channel_id=1, source_target_pairs={{0,1},{1,0},{2,3},{3,2},{4,5},{5,4},{6,7},{7,6},{8,9},{9,8},{10,11... | collective-permute-start | bytes 2752520 | tf_op jit(solution)/shard_map/ppermute | solution.py:375
  43.7 7.2 %copy-start.3 = (bf16[8,16,32,128]{3,2,1,0:T(8,128)(2,1)S(1)}, bf16[8,16,32,128]{3,2,1,0:T(8,128)(2,1)}, u32[]{:S(2)}) copy-start(bf16[8,16,32,128]{3,2,1,0:T(8,128)(2,1)} %cot.3) | copy-start | bytes 3145732
  44.0 15.1 %collective-permute-start.9 = (bf16[1,896,128]{2,1,0:T(8,128)(2,1)S(1)}, bf16[1,896,128]{2,1,0:T(8,128)(2,1)S(1)}, u32[]{:S(2)}, u32[]{:S(2)}) collective-permute-start(bf16[1,896,128]{2,1,0:T(8,128)(2,1)S(1)} %get-tuple-element.87), channel_id=1, source_target_pairs={{0,6},{1,7},{2,4},{3,5},{4,2},{5,3},{6,0},{7,1},{8,14},{9,15},{10,... | collective-permute-start | bytes 688136 | tf_op jit(solution)/shard_map/ppermute | solution.py:375
  50.3 10.8 %collective-permute-start.10 = (bf16[1,896,128]{2,1,0:T(8,128)(2,1)S(1)}, bf16[1,896,128]{2,1,0:T(8,128)(2,1)S(1)}, u32[]{:S(2)}, u32[]{:S(2)}) collective-permute-start(bf16[1,896,128]{2,1,0:T(8,128)(2,1)S(1)} %get-tuple-element.88), channel_id=1, source_target_pairs={{0,2},{1,3},{2,0},{3,1},{4,6},{5,7},{6,4},{7,5},{8,10},{9,11},{10,... | collective-permute-start | bytes 688136 | tf_op jit(solution)/shard_map/ppermute | solution.py:375
  50.4 10.8 %collective-permute-start.11 = (bf16[1,896,128]{2,1,0:T(8,128)(2,1)S(1)}, bf16[1,896,128]{2,1,0:T(8,128)(2,1)S(1)}, u32[]{:S(2)}, u32[]{:S(2)}) collective-permute-start(bf16[1,896,128]{2,1,0:T(8,128)(2,1)S(1)} %get-tuple-element.89), channel_id=1, source_target_pairs={{0,4},{1,5},{2,6},{3,7},{4,0},{5,1},{6,2},{7,3},{8,12},{9,13},{10,... | collective-permute-start | bytes 688136 | tf_op jit(solution)/shard_map/ppermute | solution.py:375
  61.1 3.5 %collective-permute-start.12 = (bf16[2,896,128]{2,1,0:T(8,128)(2,1)S(1)}, bf16[2,896,128]{2,1,0:T(8,128)(2,1)S(1)}, u32[]{:S(2)}, u32[]{:S(2)}) collective-permute-start(bf16[2,896,128]{2,1,0:T(8,128)(2,1)S(1)} %get-tuple-element.90), channel_id=1, source_target_pairs={{0,1},{1,0},{2,3},{3,2},{4,5},{5,4},{6,7},{7,6},{8,9},{9,8},{10,11... | collective-permute-start | bytes 1376264 | tf_op jit(solution)/shard_map/ppermute | solution.py:375
  61.3 13.7 %collective-permute-start.21 = (bf16[448,128]{1,0:T(8,128)(2,1)S(1)}, bf16[448,128]{1,0:T(8,128)(2,1)S(1)}, u32[]{:S(2)}, u32[]{:S(2)}) collective-permute-start(bf16[448,128]{1,0:T(8,128)(2,1)S(1)} %broadcast_select_fusion.2), channel_id=1, source_target_pairs={{0,8},{1,9},{2,10},{3,11},{4,12},{5,13},{6,14},{7,15},{8,0},{9,1},... | collective-permute-start | bytes 344072 | tf_op jit(solution)/shard_map/ppermute | solution.py:375
  64.8 7.0 %collective-permute-start.13 = (bf16[1,448,128]{2,1,0:T(8,128)(2,1)S(1)}, bf16[1,448,128]{2,1,0:T(8,128)(2,1)S(1)}, u32[]{:S(2)}, u32[]{:S(2)}) collective-permute-start(bf16[1,448,128]{2,1,0:T(8,128)(2,1)S(1)} %get-tuple-element.104), channel_id=1, source_target_pairs={{0,6},{1,7},{2,4},{3,5},{4,2},{5,3},{6,0},{7,1},{8,14},{9,15},{10,... | collective-permute-start | bytes 344072 | tf_op jit(solution)/shard_map/ppermute | solution.py:375
  65.9 7.4 %collective-permute-start.14 = (bf16[1,448,128]{2,1,0:T(8,128)(2,1)S(1)}, bf16[1,448,128]{2,1,0:T(8,128)(2,1)S(1)}, u32[]{:S(2)}, u32[]{:S(2)}) collective-permute-start(bf16[1,448,128]{2,1,0:T(8,128)(2,1)S(1)} %get-tuple-element.105), channel_id=1, source_target_pairs={{0,2},{1,3},{2,0},{3,1},{4,6},{5,7},{6,4},{7,5},{8,10},{9,11},{10,... | collective-permute-start | bytes 344072 | tf_op jit(solution)/shard_map/ppermute | solution.py:375
  66.6 6.7 %collective-permute-start.15 = (bf16[1,448,128]{2,1,0:T(8,128)(2,1)S(1)}, bf16[1,448,128]{2,1,0:T(8,128)(2,1)S(1)}, u32[]{:S(2)}, u32[]{:S(2)}) collective-permute-start(bf16[1,448,128]{2,1,0:T(8,128)(2,1)S(1)} %get-tuple-element.111), channel_id=1, source_target_pairs={{0,4},{1,5},{2,6},{3,7},{4,0},{5,1},{6,2},{7,3},{8,12},{9,13},{10,... | collective-permute-start | bytes 344072 | tf_op jit(solution)/shard_map/ppermute | solution.py:375
  73.5 4.2 %collective-permute-start.16 = (bf16[224,128]{1,0:T(8,128)(2,1)S(1)}, bf16[224,128]{1,0:T(8,128)(2,1)S(1)}, u32[]{:S(2)}, u32[]{:S(2)}) collective-permute-start(bf16[224,128]{1,0:T(8,128)(2,1)S(1)} %broadcast_select_fusion.5), channel_id=1, source_target_pairs={{0,8},{1,9},{2,10},{3,11},{4,12},{5,13},{6,14},{7,15},{8,0},{9,1},... | collective-permute-start | bytes 172040 | tf_op jit(solution)/shard_map/ppermute | solution.py:375
  75.1 9.7 %collective-permute-start.22 = (bf16[448,128]{1,0:T(8,128)(2,1)S(1)}, bf16[448,128]{1,0:T(8,128)(2,1)S(1)}, u32[]{:S(2)}, u32[]{:S(2)}) collective-permute-start(bf16[448,128]{1,0:T(8,128)(2,1)S(1)} %add_convert_fusion.3), channel_id=1, source_target_pairs={{0,16},{1,17},{2,18},{3,19},{4,20},{5,21},{6,22},{7,23},{8,24},{9,... | collective-permute-start | bytes 344072 | tf_op jit(solution)/shard_map/ppermute | solution.py:375
  77.7 10.7 %collective-permute-start.17 = (bf16[224,128]{1,0:T(8,128)(2,1)S(1)}, bf16[224,128]{1,0:T(8,128)(2,1)S(1)}, u32[]{:S(2)}, u32[]{:S(2)}) collective-permute-start(bf16[224,128]{1,0:T(8,128)(2,1)S(1)} %add_convert_fusion.5), channel_id=1, source_target_pairs={{0,16},{1,17},{2,18},{3,19},{4,20},{5,21},{6,22},{7,23},{8,24},{9,... | collective-permute-start | bytes 172040 | tf_op jit(solution)/shard_map/ppermute | solution.py:375
  84.8 6.7 %collective-permute-start.25 = (bf16[448,128]{1,0:T(8,128)(2,1)S(1)}, bf16[448,128]{1,0:T(8,128)(2,1)S(1)}, u32[]{:S(2)}, u32[]{:S(2)}) collective-permute-start(bf16[448,128]{1,0:T(8,128)(2,1)S(1)} %add_convert_fusion.2.refs_0_), channel_id=1, source_target_pairs={{0,12},{1,13},{2,14},{3,15},{4,8},{5,9},{6,10},{7,11},{8,4},{9,5},... | collective-permute-start | bytes 344072 | tf_op jit(solution)/shard_map/ppermute | solution.py:375
  84.9 7.7 %collective-permute-start.24 = (bf16[448,128]{1,0:T(8,128)(2,1)S(1)}, bf16[448,128]{1,0:T(8,128)(2,1)S(1)}, u32[]{:S(2)}, u32[]{:S(2)}) collective-permute-start(bf16[448,128]{1,0:T(8,128)(2,1)S(1)} %add_convert_fusion.2.refs_0_), channel_id=1, source_target_pairs={{0,8},{1,9},{2,10},{3,11},{4,12},{5,13},{6,14},{7,15},{8,0},{9,1},... | collective-permute-start | bytes 344072 | tf_op jit(solution)/shard_map/ppermute | solution.py:375
  87.1 6.0 %collective-permute-start.23 = (bf16[448,128]{1,0:T(8,128)(2,1)S(1)}, bf16[448,128]{1,0:T(8,128)(2,1)S(1)}, u32[]{:S(2)}, u32[]{:S(2)}) collective-permute-start(bf16[448,128]{1,0:T(8,128)(2,1)S(1)} %add_convert_fusion.2.refs_0_), channel_id=1, source_target_pairs={{0,4},{1,5},{2,6},{3,7},{4,0},{5,1},{6,2},{7,3},{8,12},{9,13},{10,... | collective-permute-start | bytes 344072 | tf_op jit(solution)/shard_map/ppermute | solution.py:375
  88.4 5.7 %collective-permute-start.20 = (bf16[224,128]{1,0:T(8,128)(2,1)S(1)}, bf16[224,128]{1,0:T(8,128)(2,1)S(1)}, u32[]{:S(2)}, u32[]{:S(2)}) collective-permute-start(bf16[224,128]{1,0:T(8,128)(2,1)S(1)} %add_convert_fusion.4.refs_0_), channel_id=1, source_target_pairs={{0,12},{1,13},{2,14},{3,15},{4,8},{5,9},{6,10},{7,11},{8,4},{9,5},... | collective-permute-start | bytes 172040 | tf_op jit(solution)/shard_map/ppermute | solution.py:375
  88.7 5.4 %collective-permute-start.19 = (bf16[224,128]{1,0:T(8,128)(2,1)S(1)}, bf16[224,128]{1,0:T(8,128)(2,1)S(1)}, u32[]{:S(2)}, u32[]{:S(2)}) collective-permute-start(bf16[224,128]{1,0:T(8,128)(2,1)S(1)} %add_convert_fusion.4.refs_0_), channel_id=1, source_target_pairs={{0,8},{1,9},{2,10},{3,11},{4,12},{5,13},{6,14},{7,15},{8,0},{9,1},... | collective-permute-start | bytes 172040 | tf_op jit(solution)/shard_map/ppermute | solution.py:375
  91.6 4.2 %collective-permute-start.18 = (bf16[224,128]{1,0:T(8,128)(2,1)S(1)}, bf16[224,128]{1,0:T(8,128)(2,1)S(1)}, u32[]{:S(2)}, u32[]{:S(2)}) collective-permute-start(bf16[224,128]{1,0:T(8,128)(2,1)S(1)} %add_convert_fusion.4.refs_0_), channel_id=1, source_target_pairs={{0,4},{1,5},{2,6},{3,7},{4,0},{5,1},{6,2},{7,3},{8,12},{9,13},{10,... | collective-permute-start | bytes 172040 | tf_op jit(solution)/shard_map/ppermute | solution.py:375

commit v5 on v4

--- a/solution.py
+++ b/solution.py
@@ -10,22 +10,21 @@
 F32 = jnp.float32
 BF16 = jnp.bfloat16
 VMEM_LIMIT = 32 * 1024 * 1024
-PREP_LIMIT = 127 * 512 * 1024
 
 
 def bit_of(axis, bit=0):
     return (lax.axis_index(axis) >> bit) & 1
 
 
-def call(body, name, args, outs, scratch=(), micros=1, space=pltpu.VMEM):
+def call(body, name, args, outs, scratch=(), micros=1):
     return pl.pallas_call(
         body,
         name=name,
         out_shape=[jax.ShapeDtypeStruct(s, t) for s, t in outs],
-        in_specs=[pl.BlockSpec(memory_space=space) for _ in args],
-        out_specs=[pl.BlockSpec(memory_space=space) for _ in outs],
+        in_specs=[pl.BlockSpec(memory_space=pltpu.VMEM) for _ in args],
+        out_specs=[pl.BlockSpec(memory_space=pltpu.VMEM) for _ in outs],
         scratch_shapes=list(scratch),
-        compiler_params=pltpu.CompilerParams(vmem_limit_bytes=VMEM_LIMIT if space == pltpu.VMEM else PREP_LIMIT),
+        compiler_params=pltpu.CompilerParams(vmem_limit_bytes=VMEM_LIMIT),
         cost_estimate=pl.CostEstimate(
             flops=int(micros * 1e9), bytes_accessed=0, transcendentals=0
         ),
@@ -58,16 +57,6 @@
 
 def sigmoid(value):
     return 1.0 / (1.0 + jnp.exp(-value))
-
-
-def prep_body(field, out_a, out_b, sems):
-    odd, end = bit_of("sub"), field.shape[1] - 1
-    one = pltpu.make_async_copy(field.at[:, (1 - odd) * end], out_a, sems.at[0])
-    two = pltpu.make_async_copy(field.at[:, odd * end], out_b, sems.at[1])
-    one.start()
-    two.start()
-    one.wait()
-    two.wait()
 
 
 def turn_body(field, ya, yb, own, out_a, out_b):
@@ -396,21 +385,37 @@
     return call(split4_body, "split", (keep.reshape(shape), got.reshape(shape)), [out] * 4, (), 1)
 
 
-def spread_sum_plain(keep, got, places):
-    half, rows, c = keep.shape
-    rest = half // 2
-    total = total_of([keep, got]).reshape(2, rest, 2, rows // 2, c)
-    near, far = halves(total, places[grp_bits() + 1])
-    own, over_grp = halves((near[:, 0], near[:, 1]), places[0])
-    over_sub, over_both = halves((far[:, 0], far[:, 1]), places[0])
-    return own, over_sub, over_grp, over_both
-
-
 def cross(own, over_sub, over_grp, over_both):
     return [own, partners(over_both, 1, 2), partners(over_sub, 0, 2), partners(over_grp, 1, 0)]
 
 
-def finish_sum(parts, places):
+def split_body(count, axis, bit, *refs):
+    mine = bit_of(axis, bit)
+
+    def part(at):
+        return sum(p[at].astype(F32) for p in refs[:count]).astype(BF16)
+
+    refs[count + 1][...] = part(1 - mine)
+    refs[count][...] = part(mine)
+
+
+def sum_body(count, *refs):
+    refs[count][...] = sum(p[...].astype(F32) for p in refs[:count]).astype(BF16)
+
+
+def split_sum_kernel(parts, axis, bit, name):
+    rows, c = parts[0].shape
+    half = ((rows // 2, c), BF16)
+    shaped = [p.reshape(2, rows // 2, c) for p in parts]
+    return call(functools.partial(split_body, len(parts), axis, bit), name, shaped, [half, half], (), 0.8)
+
+
+def sum_kernel(parts, name):
+    out = [(parts[0].shape, BF16)]
+    return call(functools.partial(sum_body, len(parts)), name, parts, out, (), 0.5)[0]
+
+
+def finish_sum(parts, places, name, kernels):
     rest, rows, c = parts[0].shape
     parts = [p.reshape(rest * rows, c) for p in parts]
     for bit in range(2, lax.axis_size("sub").bit_length() - 1):
@@ -421,13 +426,16 @@
     for bit in range(1, last + 1):
         mask = 1 << bit
         if bit == 1 and bit < last and parts[0].shape[0] % 32 == 0:
-            keep, send = split_sum(parts, places[bit])
+            if "half" in kernels:
+                keep, send = split_sum_kernel(parts, "grp", bit, name + "_half")
+            else:
+                keep, send = split_sum(parts, places[bit])
             parts = [keep, partners(send, mask, 0)]
             bits.append(bit)
         else:
-            total = total_of(parts)
+            total = sum_kernel(parts, name + "_sum") if "sum" in kernels else total_of(parts)
             parts = [total, partners(total, mask, 0)]
-    total = total_of(parts)
+    total = sum_kernel(parts, name + "_total") if "total" in kernels else total_of(parts)
     pieces = [total]
     for which in range(1, 2 ** len(bits)):
         pieces.append(partners(total, sum(1 << bits[b] for b in range(len(bits)) if which >> b & 1), 0))
@@ -480,10 +488,9 @@
     bx, by, bz, c = field.shape
     cx, cy, cz = bx // 2, by // 2, bz // 2
     c2 = merge_weight.shape[0]
-    face = ((bx, bz, c), BF16)
-    sa, sb = call(
-        prep_body, "prep", (field,), [face, face], [pltpu.SemaphoreType.DMA((2,))], space=pltpu.HBM
-    )
+    odd = bit_of("sub") == 1
+    sa = jnp.where(odd, field[:, 0], field[:, by - 1])
+    sb = jnp.where(odd, field[:, by - 1], field[:, 0])
     ya, yb = swap_faces(sa, sb, "sub")
     count = grp_bits() + n.bit_length() - 1
     pg, places = call(
@@ -589,9 +596,9 @@
     )
     fsend, cparts = lax.optimization_barrier((fsend, cparts))
     fgot = cores(fsend)
-    fparts = cross(*spread_sum_plain(fkeep, fgot, places))
-    coarse_sum = finish_sum(cparts, places)
-    fine_sum = finish_sum(fparts, places)
+    fparts = cross(*spread_sum(fkeep, fgot))
+    coarse_sum = finish_sum(cparts, places, "coarse", ('half', 'sum'))
+    fine_sum = finish_sum(fparts, places, "fine", ('half', 'sum'))
     per, cper = c // n, c2 // n
     grad_coarse, grad_merge = last(coarse_sum, cper, [((cper, c), F32)], "coarse_last")
     biases = [((1, per), F32), ((1, cper), F32)]

time: 96.9 us -> 87.5 us (0.903)
  Pallas kernels: 29.9 us -> 25.7 us
  waiting for transfers between devices: 18.1 us -> 14 us
  starting transfers between devices: 45.8 us -> 44.4 us
    ppermute x18, waiting for transfers between devices: 15.9 us -> 11.6 us  [partners(): return lax.ppermute(value, ('grp', 'sub'), pairs)]
    pallas_call x12 -> x16, Pallas kernels: 29.9 us -> 25.7 us  [call(): pl.pallas_call(body, name=name, out_shape=[jax.ShapeDtypeStruct(s, t) for...]
  transfers between devices with their start and end apart: 26 -> 26, of which waited for: 11 -> 13; matrix products, arithmetic and copies ran while one was open for 1% -> 0% of each run, Pallas kernels for 17% -> 20%
where the time goes in v5:
time: 87.5 us; the launch traced here: 87.2 us
  starting transfers between devices  44.4 us (51%)
  Pallas kernels  25.7 us (29%)
  waiting for transfers between devices  14 us (16%)
  local copies, waits for them, and re-layouts  1.31 us (1%)
  other arithmetic  0.95 us (1%)
    ppermute x18, starting transfers between devices, partners(): return lax.ppermute(value, ('grp', 'sub'), pairs)  31.3 us
    pallas_call x16, Pallas kernels, call(): pl.pallas_call(body, name=name, out_shape=[jax.ShapeDtypeStruct(s, t) for...  25.7 us
    ppermute x18, waiting for transfers between devices, partners(): return lax.ppermute(value, ('grp', 'sub'), pairs)  11.6 us
    ppermute x4, starting transfers between devices, swap_faces(): return (lax.ppermute(first, axis, one), got)  10.4 us
    ppermute x4, starting transfers between devices, swap_faces(): got = lax.ppermute(second, axis, two)  2.78 us
    ppermute x4, waiting for transfers between devices, swap_faces(): return (lax.ppermute(first, axis, one), got)  2.41 us
  transfers between devices with their start and end apart: 26, of which 13 were waited for; matrix products, arithmetic and copies ran while one was open for 0% of the time, Pallas kernels for 20%

profile of v5, /device:TPU:0, one launch (start us, length us, event | category | flops | bytes accessed | tf_op | source)
XLA Modules:
  0.0 87.2 jit_solution(5282230208387722881)
XLA Ops:
  0.6 0.9 %fusion.1 = (bf16[8,32,128]{2,1,0:T(8,128)(2,1)S(1)}, bf16[8,32,128]{2,1,0:T(8,128)(2,1)S(1)}) fusion(pred[]{:T(512)S(6)} %eq.3, bf16[8,16,32,128]{3,2,1,0:T(8,128)(2,1)} %field.1), kind=kLoop, calls=%fused_computation.5 | loop fusion | flops 65536 | bytes 262145 | tf_op jit(solution)/shard_map/jit(_where)/select_n | solution.py:493
  1.5 0.7 collective-permute-start.1
  2.2 0.0 copy-start
  2.2 4.4 %collective-permute-start = (bf16[8,32,128]{2,1,0:T(8,128)(2,1)S(1)}, bf16[8,32,128]{2,1,0:T(8,128)(2,1)S(1)}, u32[]{:S(2)}, u32[]{:S(2)}) collective-permute-start(bf16[8,32,128]{2,1,0:T(8,128)(2,1)S(1)} %get-tuple-element.111), channel_id=1, source_target_pairs={{0,1},{1,0},{2,3},{3,2},{4,5},{5,4},{6,7},{7,6},{8,9},{9,8},{10,11... | collective-permute-start | bytes 196616 | tf_op jit(solution)/shard_map/ppermute | solution.py:334
  6.6 1.2 %copy-done.2 = bf16[8,16,32,128]{3,2,1,0:T(8,128)(2,1)S(1)} copy-done((bf16[8,16,32,128]{3,2,1,0:T(8,128)(2,1)S(1)}, bf16[8,16,32,128]{3,2,1,0:T(8,128)(2,1)}, u32[]{:S(2)}) %copy-start.2) | copy-done | bytes 1048600
  7.8 0.8 cubes.1
  8.6 0.0 collective-permute-done.ya
  8.6 0.2 turn.1
  8.8 1.6 %collective-permute-start.2 = (bf16[18,32,128]{2,1,0:T(8,128)(2,1)S(1)}, bf16[18,32,128]{2,1,0:T(8,128)(2,1)S(1)}, u32[]{:S(2)}, u32[]{:S(2)}) collective-permute-start(bf16[18,32,128]{2,1,0:T(8,128)(2,1)S(1)} %get-tuple-element.60), channel_id=1, source_target_pairs={{0,4},{4,0},{8,12},{12,8},{16,20},{20,16},{24,28},{28,24},{1,5},{5... | collective-permute-start | bytes 442376 | tf_op jit(solution)/shard_map/ppermute | solution.py:334
  10.4 0.7 collective-permute-start.3
  11.1 5.7 %inner.1 = (bf16[6,16,32,128]{3,2,1,0:T(8,128)(2,1)S(1)}, f32[6,16,32,128]{3,2,1,0:T(8,128)S(1)}, bf16[2,8,16,128]{3,2,1,0:T(8,128)(2,1)S(1)}, bf16[1152,384]{1,0:T(8,128)(2,1)S(1)}) custom-call(bf16[8,18,32,128]{3,2,1,0:T(8,128)(2,1)S(1)} %get-tuple-element.58.own, bf16[3,3,3,128,128]{4,3,2,1,0:T(8,128)(2,1)S(1)} %copy-done.4, f32[1,128]{1,0:T(1,128)S(1)} %bitcast.41), custom_call_target="tpu_custom_call" | custom-call | flops 6000000000 | tf_op jit(solution)/shard_map/inner/pallas_call | solution.py:20
  16.8 0.0 collective-permute-done.3.rb
  16.8 1.7 %outer.1 = (bf16[2,16,32,128]{3,2,1,0:T(8,128)(2,1)S(1)}, f32[2,16,32,128]{3,2,1,0:T(8,128)S(1)}, bf16[2,18,32,128]{3,2,1,0:T(8,128)(2,1)S(1)}, bf16[4,8,16,128]...) custom-call(bf16[8,18,32,128]{3,2,1,0:T(8,128)(2,1)S(1)} %get-tuple-element.58.own, ...), custom_call_target="tpu_custom_call" | custom-call | flops 2000000000 | tf_op jit(solution)/shard_map/outer/pallas_call | solution.py:20
  18.4 4.3 %collective-permute-start.4 = (bf16[3,8,16,128]{3,2,1,0:T(8,128)(2,1)S(1)}, bf16[3,8,16,128]{3,2,1,0:T(8,128)(2,1)S(1)}, u32[]{:S(2)}, u32[]{:S(2)}) collective-permute-start(bf16[3,8,16,128]{3,2,1,0:T(8,128)(2,1)S(1)} %get-tuple-element.67), channel_id=1, source_target_pairs={{0,4},{4,0},{8,12},{12,8},{16,20},{20,16},{24,28},{28,24},{1,5},{5... | collective-permute-start | bytes 294920 | tf_op jit(solution)/shard_map/ppermute | solution.py:334
  22.8 0.7 collective-permute-start.5
  23.5 1.9 %collective-permute-done.4.ra = bf16[3,8,16,128]{3,2,1,0:T(8,128)(2,1)S(1)} collective-permute-done((bf16[3,8,16,128]{3,2,1,0:T(8,128)(2,1)S(1)}, bf16[3,8,16,128]{3,2,1,0:T(8,128)(2,1)S(1)}, u32[]{:S(2)}, u32[]{:S(2)}) %collective-permute-start.4) | collective-permute-done | bytes 98336 | tf_op jit(solution)/shard_map/ppermute | solution.py:334
  25.5 0.1 collective-permute-start.6
  25.5 0.8 collective-permute-start.7
  26.3 0.5 collective-permute-done.6.ua
  26.8 0.0 collective-permute-done.7.ub
  26.8 0.1 copy-done.1
  26.9 5.5 %coarse.1 = (bf16[6,10,16,256]{3,2,1,0:T(8,128)(2,1)S(1)}, bf16[4,8,16,256]{3,2,1,0:T(8,128)(2,1)S(1)}, bf16[2,1792,128]{2,1,0:T(8,128)(2,1)S(1)}, bf16[2,1792,128]{2,1,0:T(8,128)(2,1)S(1)}, bf16[256,128]{1,0:T(8,128)(2,1)S(1)}) custom-call(bf16[4,8,16,128]{3,2,1,0:T(8,128)(2,1)S(1)} %get-tuple-element.66.pooled, ...), custom_call_target="tpu_custom_call" | custom-call | flops 6000000000 | tf_op jit(solution)/shard_map/coarse/pallas_call | solution.py:20
  32.4 5.2 %collective-permute-start.8 = (bf16[2,1792,128]{2,1,0:T(8,128)(2,1)S(1)}, bf16[2,1792,128]{2,1,0:T(8,128)(2,1)S(1)}, u32[]{:S(2)}, u32[]{:S(2)}) collective-permute-start(bf16[2,1792,128]{2,1,0:T(8,128)(2,1)S(1)} %get-tuple-element.72), channel_id=1, source_target_pairs={{0,1},{1,0},{2,3},{3,2},{4,5},{5,4},{6,7},{7,6},{8,9},{9,8},{10,11... | collective-permute-start | bytes 2752520 | tf_op jit(solution)/shard_map/ppermute | solution.py:364
  37.6 1.3 %merge.1 = bf16[8,16,32,128]{3,2,1,0:T(8,128)(2,1)} custom-call(bf16[6,16,32,128]{3,2,1,0:T(8,128)(2,1)S(1)} %get-tuple-element.59.hid_in.hidden, bf16[2,16,32,128]{3,2,1,0:T(8,128)(2,1)S(1)} %get-tuple-element.65.hid_edge, bf16[4,8,16,256]{3,2,1,0:T(8,128)(2,1)S(1)} %get-tuple-element.71.coarse, bf16[256,128]{1,0:T(8,128)(2,1)S(1)} %copy-done.5), custom_call_target="tpu_custom_call" | custom-call | flops 2000000000 | tf_op jit(solution)/shard_map/merge/pallas_call | solution.py:20
  38.9 0.8 collective-permute-done.8
  39.7 0.2 split.2
  39.9 5.8 %collective-permute-start.9 = (bf16[1,896,128]{2,1,0:T(8,128)(2,1)S(1)}, bf16[1,896,128]{2,1,0:T(8,128)(2,1)S(1)}, u32[]{:S(2)}, u32[]{:S(2)}) collective-permute-start(bf16[1,896,128]{2,1,0:T(8,128)(2,1)S(1)} %get-tuple-element.89), channel_id=1, source_target_pairs={{0,6},{1,7},{2,4},{3,5},{4,2},{5,3},{6,0},{7,1},{8,14},{9,15},{10,... | collective-permute-start | bytes 688136 | tf_op jit(solution)/shard_map/ppermute | solution.py:364
  45.7 0.6 collective-permute-start.10
  46.3 0.1 collective-permute-start.11
  46.3 8.1 %back.1 = (bf16[2,896,128]{2,1,0:T(8,128)(2,1)S(1)}, bf16[2,896,128]{2,1,0:T(8,128)(2,1)S(1)}) custom-call(bf16[6,10,16,256]{3,2,1,0:T(8,128)(2,1)S(1)} %get-tuple-element.81.slope, bf16[3,3,3,128,256]{4,3,2,1,0:T(8,128)(2,1)S(1)} %copy-done.1, bf16[8,16,32,128]{3,2,1,0:T(8,128)(2,1)S(1)} %copy-done.3, f32[6,16,32,128]{3,2,1,0:T(8,128)S(1)} %get-tuple-element.82.ds, ...), custom_call_target="tpu_custom_call" | custom-call | flops 10000000000 | tf_op jit(solution)/shard_map/back/pallas_call | solution.py:20
  54.4 0.0 collective-permute-done.9
  54.4 2.1 %collective-permute-done.10 = bf16[1,896,128]{2,1,0:T(8,128)(2,1)S(1)} collective-permute-done((bf16[1,896,128]{2,1,0:T(8,128)(2,1)S(1)}, bf16[1,896,128]{2,1,0:T(8,128)(2,1)S(1)}, u32[]{:S(2)}, u32[]{:S(2)}) %collective-permute-start.10) | collective-permute-done | bytes 229408 | tf_op jit(solution)/shard_map/ppermute | solution.py:364
  56.5 0.0 collective-permute-done.11
  56.5 0.0 collective-permute-start.12
  56.5 0.1 coarse_half.1
  56.6 3.3 %collective-permute-start.21 = (bf16[448,128]{1,0:T(8,128)(2,1)S(1)}, bf16[448,128]{1,0:T(8,128)(2,1)S(1)}, u32[]{:S(2)}, u32[]{:S(2)}) collective-permute-start(bf16[448,128]{1,0:T(8,128)(2,1)S(1)} %get-tuple-element.106), channel_id=1, source_target_pairs={{0,8},{1,9},{2,10},{3,11},{4,12},{5,13},{6,14},{7,15},{8,0},{9,1},... | collective-permute-start | bytes 344072 | tf_op jit(solution)/shard_map/ppermute | solution.py:364
  59.9 0.1 split.3
  60.0 1.1 %collective-permute-start.13 = (bf16[1,448,128]{2,1,0:T(8,128)(2,1)S(1)}, bf16[1,448,128]{2,1,0:T(8,128)(2,1)S(1)}, u32[]{:S(2)}, u32[]{:S(2)}) collective-permute-start(bf16[1,448,128]{2,1,0:T(8,128)(2,1)S(1)} %get-tuple-element.94), channel_id=1, source_target_pairs={{0,6},{1,7},{2,4},{3,5},{4,2},{5,3},{6,0},{7,1},{8,14},{9,15},{10,... | collective-permute-start | bytes 344072 | tf_op jit(solution)/shard_map/ppermute | solution.py:364
  61.1 0.8 collective-permute-start.14
  61.9 1.7 %collective-permute-start.15 = (bf16[1,448,128]{2,1,0:T(8,128)(2,1)S(1)}, bf16[1,448,128]{2,1,0:T(8,128)(2,1)S(1)}, u32[]{:S(2)}, u32[]{:S(2)}) collective-permute-start(bf16[1,448,128]{2,1,0:T(8,128)(2,1)S(1)} %get-tuple-element.96), channel_id=1, source_target_pairs={{0,4},{1,5},{2,6},{3,7},{4,0},{5,1},{6,2},{7,3},{8,12},{9,13},{10,... | collective-permute-start | bytes 344072 | tf_op jit(solution)/shard_map/ppermute | solution.py:364
  63.6 0.1 collective-permute-done.21.refs_1_
  63.8 2.8 %collective-permute-start.22 = (bf16[448,128]{1,0:T(8,128)(2,1)S(1)}, bf16[448,128]{1,0:T(8,128)(2,1)S(1)}, u32[]{:S(2)}, u32[]{:S(2)}) collective-permute-start(bf16[448,128]{1,0:T(8,128)(2,1)S(1)} %coarse_sum.1), channel_id=1, source_target_pairs={{0,16},{1,17},{2,18},{3,19},{4,20},{5,21},{6,22},{7,23},{8,24},{9,... | collective-permute-start | bytes 344072 | tf_op jit(solution)/shard_map/ppermute | solution.py:364
  66.6 0.4 collective-permute-done.13
  67.0 1.5 %collective-permute-done.14 = bf16[1,448,128]{2,1,0:T(8,128)(2,1)S(1)} collective-permute-done((bf16[1,448,128]{2,1,0:T(8,128)(2,1)S(1)}, bf16[1,448,128]{2,1,0:T(8,128)(2,1)S(1)}, u32[]{:S(2)}, u32[]{:S(2)}) %collective-permute-start.14) | collective-permute-done | bytes 114720 | tf_op jit(solution)/shard_map/ppermute | solution.py:364
  68.5 0.0 collective-permute-done.15
  68.5 0.1 fine_half.1
  68.6 1.6 %collective-permute-start.16 = (bf16[224,128]{1,0:T(8,128)(2,1)S(1)}, bf16[224,128]{1,0:T(8,128)(2,1)S(1)}, u32[]{:S(2)}, u32[]{:S(2)}) collective-permute-start(bf16[224,128]{1,0:T(8,128)(2,1)S(1)} %get-tuple-element.98), channel_id=1, source_target_pairs={{0,8},{1,9},{2,10},{3,11},{4,12},{5,13},{6,14},{7,15},{8,0},{9,1},... | collective-permute-start | bytes 172040 | tf_op jit(solution)/shard_map/ppermute | solution.py:364
  70.2 3.2 %collective-permute-done.16.refs_1_ = bf16[224,128]{1,0:T(8,128)(2,1)S(1)} collective-permute-done((bf16[224,128]{1,0:T(8,128)(2,1)S(1)}, bf16[224,128]{1,0:T(8,128)(2,1)S(1)}, u32[]{:S(2)}, u32[]{:S(2)}) %collective-permute-start.16) | collective-permute-done | bytes 57376 | tf_op jit(solution)/shard_map/ppermute | solution.py:364
  73.4 2.0 %collective-permute-start.17 = (bf16[224,128]{1,0:T(8,128)(2,1)S(1)}, bf16[224,128]{1,0:T(8,128)(2,1)S(1)}, u32[]{:S(2)}, u32[]{:S(2)}) collective-permute-start(bf16[224,128]{1,0:T(8,128)(2,1)S(1)} %fine_sum.1), channel_id=1, source_target_pairs={{0,16},{1,17},{2,18},{3,19},{4,20},{5,21},{6,22},{7,23},{8,24},{9,... | collective-permute-start | bytes 172040 | tf_op jit(solution)/shard_map/ppermute | solution.py:364
  75.4 0.0 collective-permute-done.22
  75.4 0.9 %collective-permute-start.25 = (bf16[448,128]{1,0:T(8,128)(2,1)S(1)}, bf16[448,128]{1,0:T(8,128)(2,1)S(1)}, u32[]{:S(2)}, u32[]{:S(2)}) collective-permute-start(bf16[448,128]{1,0:T(8,128)(2,1)S(1)} %add_convert_fusion.refs_0_), channel_id=1, source_target_pairs={{0,12},{1,13},{2,14},{3,15},{4,8},{5,9},{6,10},{7,11},{8,4},{9,5},... | collective-permute-start | bytes 344072 | tf_op jit(solution)/shard_map/ppermute | solution.py:364
  76.3 1.2 %collective-permute-start.24 = (bf16[448,128]{1,0:T(8,128)(2,1)S(1)}, bf16[448,128]{1,0:T(8,128)(2,1)S(1)}, u32[]{:S(2)}, u32[]{:S(2)}) collective-permute-start(bf16[448,128]{1,0:T(8,128)(2,1)S(1)} %add_convert_fusion.refs_0_), channel_id=1, source_target_pairs={{0,8},{1,9},{2,10},{3,11},{4,12},{5,13},{6,14},{7,15},{8,0},{9,1},... | collective-permute-start | bytes 344072 | tf_op jit(solution)/shard_map/ppermute | solution.py:364
  77.5 1.5 %collective-permute-start.23 = (bf16[448,128]{1,0:T(8,128)(2,1)S(1)}, bf16[448,128]{1,0:T(8,128)(2,1)S(1)}, u32[]{:S(2)}, u32[]{:S(2)}) collective-permute-start(bf16[448,128]{1,0:T(8,128)(2,1)S(1)} %add_convert_fusion.refs_0_), channel_id=1, source_target_pairs={{0,4},{1,5},{2,6},{3,7},{4,0},{5,1},{6,2},{7,3},{8,12},{9,13},{10,... | collective-permute-start | bytes 344072 | tf_op jit(solution)/shard_map/ppermute | solution.py:364
  79.0 0.0 collective-permute-done.17
  79.0 0.9 collective-permute-start.20
  79.9 1.2 %collective-permute-start.19 = (bf16[224,128]{1,0:T(8,128)(2,1)S(1)}, bf16[224,128]{1,0:T(8,128)(2,1)S(1)}, u32[]{:S(2)}, u32[]{:S(2)}) collective-permute-start(bf16[224,128]{1,0:T(8,128)(2,1)S(1)} %add_convert_fusion.1.refs_0_), channel_id=1, source_target_pairs={{0,8},{1,9},{2,10},{3,11},{4,12},{5,13},{6,14},{7,15},{8,0},{9,1},... | collective-permute-start | bytes 172040 | tf_op jit(solution)/shard_map/ppermute | solution.py:364
  81.1 1.1 %collective-permute-done.25.refs_3_ = bf16[448,128]{1,0:T(8,128)(2,1)S(1)} collective-permute-done((bf16[448,128]{1,0:T(8,128)(2,1)S(1)}, bf16[448,128]{1,0:T(8,128)(2,1)S(1)}, u32[]{:S(2)}, u32[]{:S(2)}) %collective-permute-start.25) | collective-permute-done | bytes 114720 | tf_op jit(solution)/shard_map/ppermute | solution.py:364
  82.2 0.9 %collective-permute-start.18 = (bf16[224,128]{1,0:T(8,128)(2,1)S(1)}, bf16[224,128]{1,0:T(8,128)(2,1)S(1)}, u32[]{:S(2)}, u32[]{:S(2)}) collective-permute-start(bf16[224,128]{1,0:T(8,128)(2,1)S(1)} %add_convert_fusion.1.refs_0_), channel_id=1, source_target_pairs={{0,4},{1,5},{2,6},{3,7},{4,0},{5,1},{6,2},{7,3},{8,12},{9,13},{10,... | collective-permute-start | bytes 172040 | tf_op jit(solution)/shard_map/ppermute | solution.py:364
  83.1 1.0 %collective-permute-done.24.refs_2_ = bf16[448,128]{1,0:T(8,128)(2,1)S(1)} collective-permute-done((bf16[448,128]{1,0:T(8,128)(2,1)S(1)}, bf16[448,128]{1,0:T(8,128)(2,1)S(1)}, u32[]{:S(2)}, u32[]{:S(2)}) %collective-permute-start.24) | collective-permute-done | bytes 114720 | tf_op jit(solution)/shard_map/ppermute | solution.py:364
  84.0 0.2 collective-permute-done.23.refs_1_
  84.3 1.0 %coarse_last.1 = (f32[3,3,3,64,128]{4,3,2,1,0:T(8,128)}, f32[64,128]{1,0:T(8,128)}) custom-call(bf16[448,128]{1,0:T(8,128)(2,1)S(1)} %add_convert_fusion.refs_0_, bf16[448,128]{1,0:T(8,128)(2,1)S(1)} %collective-permute-done.23.refs_1_, bf16[448,128]{1,0:T(8,128)(2,1)S(1)} %collective-permute-done.24.refs_2_, ...), custom_call_target="tpu_custom_call" | custom-call | flops 1000000000 | tf_op jit(solution)/shard_map/coarse_last/pallas_call | solution.py:20
  85.3 0.5 collective-permute-done.19.refs_2_
  85.8 0.5 collective-permute-done.18.refs_1_
  86.4 0.9 fine_last.1
  (23 shorter events, 0.2 us)
Async XLA Ops:
  1.5 7.1 %collective-permute-start.1 = (bf16[8,32,128]{2,1,0:T(8,128)(2,1)S(1)}, bf16[8,32,128]{2,1,0:T(8,128)(2,1)S(1)}, u32[]{:S(2)}, u32[]{:S(2)}) collective-permute-start(bf16[8,32,128]{2,1,0:T(8,128)(2,1)S(1)} %get-tuple-element.110), channel_id=1, source_target_pairs={{1,2},{2,1},{5,6},{6,5},{9,10},{10,9},{13,14},{14,13},{17,18},{18,... | collective-permute-start | bytes 196616 | tf_op jit(solution)/shard_map/ppermute | solution.py:333
  2.2 6.4 %copy-start = (bf16[8,16,32,128]{3,2,1,0:T(8,128)(2,1)S(1)}, bf16[8,16,32,128]{3,2,1,0:T(8,128)(2,1)}, u32[]{:S(2)}) copy-start(bf16[8,16,32,128]{3,2,1,0:T(8,128)(2,1)} %field.1) | copy-start | bytes 3145732
  2.2 6.4 %collective-permute-start = (bf16[8,32,128]{2,1,0:T(8,128)(2,1)S(1)}, bf16[8,32,128]{2,1,0:T(8,128)(2,1)S(1)}, u32[]{:S(2)}, u32[]{:S(2)}) collective-permute-start(bf16[8,32,128]{2,1,0:T(8,128)(2,1)S(1)} %get-tuple-element.111), channel_id=1, source_target_pairs={{0,1},{1,0},{2,3},{3,2},{4,5},{5,4},{6,7},{7,6},{8,9},{9,8},{10,11... | collective-permute-start | bytes 196616 | tf_op jit(solution)/shard_map/ppermute | solution.py:334
  6.6 1.2 %copy-start.2 = (bf16[8,16,32,128]{3,2,1,0:T(8,128)(2,1)S(1)}, bf16[8,16,32,128]{3,2,1,0:T(8,128)(2,1)}, u32[]{:S(2)}) copy-start(bf16[8,16,32,128]{3,2,1,0:T(8,128)(2,1)} %cot.3) | copy-start | bytes 3145732
  8.6 2.4 %copy-start.4 = (bf16[3,3,3,128,128]{4,3,2,1,0:T(8,128)(2,1)S(1)}, bf16[3,3,3,128,128]{4,3,2,1,0:T(8,128)(2,1)}, u32[]{:S(2)}) copy-start(bf16[3,3,3,128,128]{4,3,2,1,0:T(8,128)(2,1)} %w.3) | copy-start | bytes 2654212
  8.6 2.4 %copy-start.7 = (f32[128]{0:T(128)S(1)}, f32[128]{0:T(128)}, u32[]{:S(2)}) copy-start(f32[128]{0:T(128)} %param.10) | copy-start | bytes 1540
  8.8 7.9 %collective-permute-start.2 = (bf16[18,32,128]{2,1,0:T(8,128)(2,1)S(1)}, bf16[18,32,128]{2,1,0:T(8,128)(2,1)S(1)}, u32[]{:S(2)}, u32[]{:S(2)}) collective-permute-start(bf16[18,32,128]{2,1,0:T(8,128)(2,1)S(1)} %get-tuple-element.60), channel_id=1, source_target_pairs={{0,4},{4,0},{8,12},{12,8},{16,20},{20,16},{24,28},{28,24},{1,5},{5... | collective-permute-start | bytes 442376 | tf_op jit(solution)/shard_map/ppermute | solution.py:334
  10.4 6.4 %collective-permute-start.3 = (bf16[18,32,128]{2,1,0:T(8,128)(2,1)S(1)}, bf16[18,32,128]{2,1,0:T(8,128)(2,1)S(1)}, u32[]{:S(2)}, u32[]{:S(2)}) collective-permute-start(bf16[18,32,128]{2,1,0:T(8,128)(2,1)S(1)} %get-tuple-element.61), channel_id=1, source_target_pairs={{4,8},{8,4},{12,16},{16,12},{20,24},{24,20},{5,9},{9,5},{13,17},{1... | collective-permute-start | bytes 442376 | tf_op jit(solution)/shard_map/ppermute | solution.py:333
  18.4 6.9 %collective-permute-start.4 = (bf16[3,8,16,128]{3,2,1,0:T(8,128)(2,1)S(1)}, bf16[3,8,16,128]{3,2,1,0:T(8,128)(2,1)S(1)}, u32[]{:S(2)}, u32[]{:S(2)}) collective-permute-start(bf16[3,8,16,128]{3,2,1,0:T(8,128)(2,1)S(1)} %get-tuple-element.67), channel_id=1, source_target_pairs={{0,4},{4,0},{8,12},{12,8},{16,20},{20,16},{24,28},{28,24},{1,5},{5... | collective-permute-start | bytes 294920 | tf_op jit(solution)/shard_map/ppermute | solution.py:334
  22.8 2.6 %collective-permute-start.5 = (bf16[3,8,16,128]{3,2,1,0:T(8,128)(2,1)S(1)}, bf16[3,8,16,128]{3,2,1,0:T(8,128)(2,1)S(1)}, u32[]{:S(2)}, u32[]{:S(2)}) collective-permute-start(bf16[3,8,16,128]{3,2,1,0:T(8,128)(2,1)S(1)} %get-tuple-element.68), channel_id=1, source_target_pairs={{4,8},{8,4},{12,16},{16,12},{20,24},{24,20},{5,9},{9,5},{13,17},{1... | collective-permute-start | bytes 294920 | tf_op jit(solution)/shard_map/ppermute | solution.py:333
  25.4 1.5 %copy-start.1 = (bf16[3,3,3,128,256]{4,3,2,1,0:T(8,128)(2,1)S(1)}, bf16[3,3,3,128,256]{4,3,2,1,0:T(8,128)(2,1)}, u32[]{:S(2)}) copy-start(bf16[3,3,3,128,256]{4,3,2,1,0:T(8,128)(2,1)} %w.5) | copy-start | bytes 5308420
  25.4 1.5 %copy-start.5 = (bf16[256,128]{1,0:T(8,128)(2,1)S(1)}, bf16[256,128]{1,0:T(8,128)(2,1)}, u32[]{:S(2)}) copy-start(bf16[256,128]{1,0:T(8,128)(2,1)} %wm.3) | copy-start | bytes 196612
  25.4 1.5 %copy-start.6 = (f32[256]{0:T(256)S(1)}, f32[256]{0:T(256)}, u32[]{:S(2)}) copy-start(f32[256]{0:T(256)} %param.12) | copy-start | bytes 3076
  25.5 1.4 %collective-permute-start.6 = (bf16[22,16,128]{2,1,0:T(8,128)(2,1)S(1)}, bf16[22,16,128]{2,1,0:T(8,128)(2,1)S(1)}, u32[]{:S(2)}, u32[]{:S(2)}) collective-permute-start(bf16[22,16,128]{2,1,0:T(8,128)(2,1)S(1)} %get-tuple-element.69), channel_id=1, source_target_pairs={{0,1},{1,0},{2,3},{3,2},{4,5},{5,4},{6,7},{7,6},{8,9},{9,8},{10,11... | collective-permute-start | bytes 270344 | tf_op jit(solution)/shard_map/ppermute | solution.py:334
  25.5 1.3 %collective-permute-start.7 = (bf16[22,16,128]{2,1,0:T(8,128)(2,1)S(1)}, bf16[22,16,128]{2,1,0:T(8,128)(2,1)S(1)}, u32[]{:S(2)}, u32[]{:S(2)}) collective-permute-start(bf16[22,16,128]{2,1,0:T(8,128)(2,1)S(1)} %get-tuple-element.70), channel_id=1, source_target_pairs={{1,2},{2,1},{5,6},{6,5},{9,10},{10,9},{13,14},{14,13},{17,18},{18,... | collective-permute-start | bytes 270344 | tf_op jit(solution)/shard_map/ppermute | solution.py:333
  32.4 7.3 %collective-permute-start.8 = (bf16[2,1792,128]{2,1,0:T(8,128)(2,1)S(1)}, bf16[2,1792,128]{2,1,0:T(8,128)(2,1)S(1)}, u32[]{:S(2)}, u32[]{:S(2)}) collective-permute-start(bf16[2,1792,128]{2,1,0:T(8,128)(2,1)S(1)} %get-tuple-element.72), channel_id=1, source_target_pairs={{0,1},{1,0},{2,3},{3,2},{4,5},{5,4},{6,7},{7,6},{8,9},{9,8},{10,11... | collective-permute-start | bytes 2752520 | tf_op jit(solution)/shard_map/ppermute | solution.py:364
  39.7 6.6 %copy-start.3 = (bf16[8,16,32,128]{3,2,1,0:T(8,128)(2,1)S(1)}, bf16[8,16,32,128]{3,2,1,0:T(8,128)(2,1)}, u32[]{:S(2)}) copy-start(bf16[8,16,32,128]{3,2,1,0:T(8,128)(2,1)} %cot.3) | copy-start | bytes 3145732
  39.9 14.5 %collective-permute-start.9 = (bf16[1,896,128]{2,1,0:T(8,128)(2,1)S(1)}, bf16[1,896,128]{2,1,0:T(8,128)(2,1)S(1)}, u32[]{:S(2)}, u32[]{:S(2)}) collective-permute-start(bf16[1,896,128]{2,1,0:T(8,128)(2,1)S(1)} %get-tuple-element.89), channel_id=1, source_target_pairs={{0,6},{1,7},{2,4},{3,5},{4,2},{5,3},{6,0},{7,1},{8,14},{9,15},{10,... | collective-permute-start | bytes 688136 | tf_op jit(solution)/shard_map/ppermute | solution.py:364
  45.7 10.8 %collective-permute-start.10 = (bf16[1,896,128]{2,1,0:T(8,128)(2,1)S(1)}, bf16[1,896,128]{2,1,0:T(8,128)(2,1)S(1)}, u32[]{:S(2)}, u32[]{:S(2)}) collective-permute-start(bf16[1,896,128]{2,1,0:T(8,128)(2,1)S(1)} %get-tuple-element.90), channel_id=1, source_target_pairs={{0,2},{1,3},{2,0},{3,1},{4,6},{5,7},{6,4},{7,5},{8,10},{9,11},{10,... | collective-permute-start | bytes 688136 | tf_op jit(solution)/shard_map/ppermute | solution.py:364
  46.3 10.2 %collective-permute-start.11 = (bf16[1,896,128]{2,1,0:T(8,128)(2,1)S(1)}, bf16[1,896,128]{2,1,0:T(8,128)(2,1)S(1)}, u32[]{:S(2)}, u32[]{:S(2)}) collective-permute-start(bf16[1,896,128]{2,1,0:T(8,128)(2,1)S(1)} %get-tuple-element.91), channel_id=1, source_target_pairs={{0,4},{1,5},{2,6},{3,7},{4,0},{5,1},{6,2},{7,3},{8,12},{9,13},{10,... | collective-permute-start | bytes 688136 | tf_op jit(solution)/shard_map/ppermute | solution.py:364
  56.5 3.4 %collective-permute-start.12 = (bf16[2,896,128]{2,1,0:T(8,128)(2,1)S(1)}, bf16[2,896,128]{2,1,0:T(8,128)(2,1)S(1)}, u32[]{:S(2)}, u32[]{:S(2)}) collective-permute-start(bf16[2,896,128]{2,1,0:T(8,128)(2,1)S(1)} %get-tuple-element.92), channel_id=1, source_target_pairs={{0,1},{1,0},{2,3},{3,2},{4,5},{5,4},{6,7},{7,6},{8,9},{9,8},{10,11... | collective-permute-start | bytes 1376264 | tf_op jit(solution)/shard_map/ppermute | solution.py:364
  56.6 7.1 %collective-permute-start.21 = (bf16[448,128]{1,0:T(8,128)(2,1)S(1)}, bf16[448,128]{1,0:T(8,128)(2,1)S(1)}, u32[]{:S(2)}, u32[]{:S(2)}) collective-permute-start(bf16[448,128]{1,0:T(8,128)(2,1)S(1)} %get-tuple-element.106), channel_id=1, source_target_pairs={{0,8},{1,9},{2,10},{3,11},{4,12},{5,13},{6,14},{7,15},{8,0},{9,1},... | collective-permute-start | bytes 344072 | tf_op jit(solution)/shard_map/ppermute | solution.py:364
  60.0 7.0 %collective-permute-start.13 = (bf16[1,448,128]{2,1,0:T(8,128)(2,1)S(1)}, bf16[1,448,128]{2,1,0:T(8,128)(2,1)S(1)}, u32[]{:S(2)}, u32[]{:S(2)}) collective-permute-start(bf16[1,448,128]{2,1,0:T(8,128)(2,1)S(1)} %get-tuple-element.94), channel_id=1, source_target_pairs={{0,6},{1,7},{2,4},{3,5},{4,2},{5,3},{6,0},{7,1},{8,14},{9,15},{10,... | collective-permute-start | bytes 344072 | tf_op jit(solution)/shard_map/ppermute | solution.py:364
  61.1 7.4 %collective-permute-start.14 = (bf16[1,448,128]{2,1,0:T(8,128)(2,1)S(1)}, bf16[1,448,128]{2,1,0:T(8,128)(2,1)S(1)}, u32[]{:S(2)}, u32[]{:S(2)}) collective-permute-start(bf16[1,448,128]{2,1,0:T(8,128)(2,1)S(1)} %get-tuple-element.95), channel_id=1, source_target_pairs={{0,2},{1,3},{2,0},{3,1},{4,6},{5,7},{6,4},{7,5},{8,10},{9,11},{10,... | collective-permute-start | bytes 344072 | tf_op jit(solution)/shard_map/ppermute | solution.py:364
  61.9 6.6 %collective-permute-start.15 = (bf16[1,448,128]{2,1,0:T(8,128)(2,1)S(1)}, bf16[1,448,128]{2,1,0:T(8,128)(2,1)S(1)}, u32[]{:S(2)}, u32[]{:S(2)}) collective-permute-start(bf16[1,448,128]{2,1,0:T(8,128)(2,1)S(1)} %get-tuple-element.96), channel_id=1, source_target_pairs={{0,4},{1,5},{2,6},{3,7},{4,0},{5,1},{6,2},{7,3},{8,12},{9,13},{10,... | collective-permute-start | bytes 344072 | tf_op jit(solution)/shard_map/ppermute | solution.py:364
  63.8 11.6 %collective-permute-start.22 = (bf16[448,128]{1,0:T(8,128)(2,1)S(1)}, bf16[448,128]{1,0:T(8,128)(2,1)S(1)}, u32[]{:S(2)}, u32[]{:S(2)}) collective-permute-start(bf16[448,128]{1,0:T(8,128)(2,1)S(1)} %coarse_sum.1), channel_id=1, source_target_pairs={{0,16},{1,17},{2,18},{3,19},{4,20},{5,21},{6,22},{7,23},{8,24},{9,... | collective-permute-start | bytes 344072 | tf_op jit(solution)/shard_map/ppermute | solution.py:364
  68.6 4.8 %collective-permute-start.16 = (bf16[224,128]{1,0:T(8,128)(2,1)S(1)}, bf16[224,128]{1,0:T(8,128)(2,1)S(1)}, u32[]{:S(2)}, u32[]{:S(2)}) collective-permute-start(bf16[224,128]{1,0:T(8,128)(2,1)S(1)} %get-tuple-element.98), channel_id=1, source_target_pairs={{0,8},{1,9},{2,10},{3,11},{4,12},{5,13},{6,14},{7,15},{8,0},{9,1},... | collective-permute-start | bytes 172040 | tf_op jit(solution)/shard_map/ppermute | solution.py:364
  73.4 5.6 %collective-permute-start.17 = (bf16[224,128]{1,0:T(8,128)(2,1)S(1)}, bf16[224,128]{1,0:T(8,128)(2,1)S(1)}, u32[]{:S(2)}, u32[]{:S(2)}) collective-permute-start(bf16[224,128]{1,0:T(8,128)(2,1)S(1)} %fine_sum.1), channel_id=1, source_target_pairs={{0,16},{1,17},{2,18},{3,19},{4,20},{5,21},{6,22},{7,23},{8,24},{9,... | collective-permute-start | bytes 172040 | tf_op jit(solution)/shard_map/ppermute | solution.py:364
  75.4 6.8 %collective-permute-start.25 = (bf16[448,128]{1,0:T(8,128)(2,1)S(1)}, bf16[448,128]{1,0:T(8,128)(2,1)S(1)}, u32[]{:S(2)}, u32[]{:S(2)}) collective-permute-start(bf16[448,128]{1,0:T(8,128)(2,1)S(1)} %add_convert_fusion.refs_0_), channel_id=1, source_target_pairs={{0,12},{1,13},{2,14},{3,15},{4,8},{5,9},{6,10},{7,11},{8,4},{9,5},... | collective-permute-start | bytes 344072 | tf_op jit(solution)/shard_map/ppermute | solution.py:364
  76.3 7.7 %collective-permute-start.24 = (bf16[448,128]{1,0:T(8,128)(2,1)S(1)}, bf16[448,128]{1,0:T(8,128)(2,1)S(1)}, u32[]{:S(2)}, u32[]{:S(2)}) collective-permute-start(bf16[448,128]{1,0:T(8,128)(2,1)S(1)} %add_convert_fusion.refs_0_), channel_id=1, source_target_pairs={{0,8},{1,9},{2,10},{3,11},{4,12},{5,13},{6,14},{7,15},{8,0},{9,1},... | collective-permute-start | bytes 344072 | tf_op jit(solution)/shard_map/ppermute | solution.py:364
  77.5 6.8 %collective-permute-start.23 = (bf16[448,128]{1,0:T(8,128)(2,1)S(1)}, bf16[448,128]{1,0:T(8,128)(2,1)S(1)}, u32[]{:S(2)}, u32[]{:S(2)}) collective-permute-start(bf16[448,128]{1,0:T(8,128)(2,1)S(1)} %add_convert_fusion.refs_0_), channel_id=1, source_target_pairs={{0,4},{1,5},{2,6},{3,7},{4,0},{5,1},{6,2},{7,3},{8,12},{9,13},{10,... | collective-permute-start | bytes 344072 | tf_op jit(solution)/shard_map/ppermute | solution.py:364
  79.0 6.3 %collective-permute-start.20 = (bf16[224,128]{1,0:T(8,128)(2,1)S(1)}, bf16[224,128]{1,0:T(8,128)(2,1)S(1)}, u32[]{:S(2)}, u32[]{:S(2)}) collective-permute-start(bf16[224,128]{1,0:T(8,128)(2,1)S(1)} %add_convert_fusion.1.refs_0_), channel_id=1, source_target_pairs={{0,12},{1,13},{2,14},{3,15},{4,8},{5,9},{6,10},{7,11},{8,4},{9,5},... | collective-permute-start | bytes 172040 | tf_op jit(solution)/shard_map/ppermute | solution.py:364
  79.9 6.0 %collective-permute-start.19 = (bf16[224,128]{1,0:T(8,128)(2,1)S(1)}, bf16[224,128]{1,0:T(8,128)(2,1)S(1)}, u32[]{:S(2)}, u32[]{:S(2)}) collective-permute-start(bf16[224,128]{1,0:T(8,128)(2,1)S(1)} %add_convert_fusion.1.refs_0_), channel_id=1, source_target_pairs={{0,8},{1,9},{2,10},{3,11},{4,12},{5,13},{6,14},{7,15},{8,0},{9,1},... | collective-permute-start | bytes 172040 | tf_op jit(solution)/shard_map/ppermute | solution.py:364
  82.2 4.2 %collective-permute-start.18 = (bf16[224,128]{1,0:T(8,128)(2,1)S(1)}, bf16[224,128]{1,0:T(8,128)(2,1)S(1)}, u32[]{:S(2)}, u32[]{:S(2)}) collective-permute-start(bf16[224,128]{1,0:T(8,128)(2,1)S(1)} %add_convert_fusion.1.refs_0_), channel_id=1, source_target_pairs={{0,4},{1,5},{2,6},{3,7},{4,0},{5,1},{6,2},{7,3},{8,12},{9,13},{10,... | collective-permute-start | bytes 172040 | tf_op jit(solution)/shard_map/ppermute | solution.py:364

commit v6 on v5

--- a/solution.py
+++ b/solution.py
@@ -59,19 +59,39 @@
     return 1.0 / (1.0 + jnp.exp(-value))
 
 
-def turn_body(field, ya, yb, own, out_a, out_b):
-    bx, by = field.shape[0], field.shape[1]
+def turn_body(field, ya, yb, pg, own, out_a, out_b):
+    bx, by, bz, c = field.shape
+    cx, cy, cz, _ = pg.shape
     ylo, yhi = get_faces(bit_of("sub") == 1, ya, yb)
     own[:, 1 : by + 1] = field[...]
     own[:, 0] = ylo
     own[:, by + 1] = yhi
-    put_faces(bit_of("grp") == 1, out_a, out_b, own[0], own[bx - 1])
+
+    def side(x, at):
+        return jnp.concatenate([own[x].reshape((by + 2) * bz, c), pg[at].reshape(cy * cz, c)], axis=0)
+
+    put_faces(bit_of("grp") == 1, out_a, out_b, side(0, 0), side(bx - 1, cx - 1))
+
+
+def x_faces(xa, xb, fine, coarse):
+    by, bz, c = fine
+    cy, cz, _ = coarse
+    lo, hi = get_faces(bit_of("grp") == 1, xa, xb)
+    rows = by * bz
+    return (
+        (lo[:rows].reshape(by, bz, c), hi[:rows].reshape(by, bz, c)),
+        (lo[rows:].reshape(cy, cz, c), hi[rows:].reshape(cy, cz, c)),
+    )
 
 
 def fine_plane(three, wb, bias, by):
     _, bz, c = three[0].shape
-    rows = by * bz
-    taps = [plane[j : j + by].reshape(rows, c) for plane in three for j in range(3)]
+    rows = by * bz * (len(three) - 2)
+    taps = [
+        jnp.concatenate([plane[j : j + by].reshape(by * bz, c) for plane in three[i : len(three) - 2 + i]], axis=0)
+        for i in range(3)
+        for j in range(3)
+    ]
     part = jnp.dot(jnp.concatenate(taps, axis=1), wb[...], preferred_element_type=F32)
     pre = (
         part[:, c : 2 * c]
@@ -80,8 +100,8 @@
         + bias[...]
     )
     sig = sigmoid(pre)
-    hid = (pre * sig).astype(BF16).reshape(by, bz, c)
-    return hid, (sig * (1.0 + pre * (1.0 - sig))).reshape(by, bz, c)
+    hid = (pre * sig).astype(BF16).reshape(-1, by, bz, c)
+    return hid, (sig * (1.0 + pre * (1.0 - sig))).reshape(-1, by, bz, c)
 
 
 def pool(one, two, tmp):
@@ -100,28 +120,35 @@
                 wb[pl.ds((3 * i + j) * c, c), pl.ds(k * c, c)] = w[i, j, k]
 
     def plane(x, carry):
-        hid, slope = fine_plane([own[x], own[x + 1], own[x + 2]], wb, bias, by)
-        hidden[x], ds[x] = hid, slope
+        hid, slope = fine_plane([own[3 * x + k] for k in range(5)], wb, bias, by)
+        hidden[pl.ds(3 * x, 3)], ds[pl.ds(3 * x, 3)] = hid, slope
         return carry
 
-    lax.fori_loop(0, hidden.shape[0], plane, 0)
+    lax.fori_loop(0, hidden.shape[0] // 3, plane, 0)
     for q in range(pooled.shape[0]):
         pooled[q] = pool(hidden[2 * q + 1], hidden[2 * q + 2], tmp)
 
 
-def outer_body(own, ra, rb, wb, bias, hid_in, pool_in, pg, hidden, ds, halo, pooled, out_a, out_b, tmp):
-    bx, by = own.shape[0], own.shape[1] - 2
+def edge_body(second, own, face, wb, bias, hid_in, pool_in, hidden, ds, pooled, out, tmp):
+    bx, by, bz, c = own.shape
     cx = bx // 2
-    xlo, xhi = get_faces(bit_of("grp") == 1, ra, rb)
-    halo[0], halo[1] = xlo, xhi
-    for at, three in ((0, [halo[0], own[0], own[1]]), (1, [own[bx - 2], own[bx - 1], halo[1]])):
-        hidden[at], ds[at] = fine_plane(three, wb, bias, by)
-    pooled[0] = pool(hidden[0], hid_in[0], tmp)
-    pooled[1 : cx - 1] = pool_in[...]
-    pooled[cx - 1] = pool(hid_in[bx - 3], hidden[1], tmp)
-    low = jnp.concatenate([pooled[0:2], pg[0:1]], axis=0)
-    high = jnp.concatenate([pooled[cx - 2 : cx], pg[cx - 1 : cx]], axis=0)
-    put_faces(bit_of("grp") == 1, out_a, out_b, low, high)
+    low = bit_of("grp") == (0 if second else 1)
+    halo = face[pl.ds(0, by * bz), :].reshape(by, bz, c)
+    near, inside = own[jnp.where(low, 0, bx - 1)], own[jnp.where(low, 1, bx - 2)]
+    three = [jnp.where(low, halo, inside), near, jnp.where(low, inside, halo)]
+    hid, slope = fine_plane(three, wb, bias, by - 2)
+    hidden[...], ds[...] = hid[0], slope[0]
+    pooled[...] = pool(hidden[...], hid_in[jnp.where(low, 0, bx - 3)], tmp)
+    out[0] = jnp.where(low, pooled[...], pool_in[cx - 3])
+    out[1] = jnp.where(low, pool_in[0], pooled[...])
+
+
+def taps_body(w, wb):
+    c, c2 = w.shape[3], w.shape[4]
+    for i in range(3):
+        for j in range(3):
+            for k in range(3):
+                wb[pl.ds((3 * i + j) * c, c), pl.ds(k * c2, c2)] = w[i, j, k]
 
 
 def cubes_body(cot, pg, bits, tmp):
@@ -136,13 +163,20 @@
         bits[k] = jnp.full(bits.shape[1:], value, jnp.int32)
 
 
-def turn2_body(pooled, pg, ra, rb, out_a, out_b):
-    cy = pooled.shape[1]
+def pooled_of(pool_in, pool_a, pool_b):
+    lo, hi = get_faces(bit_of("grp") == 1, pool_a, pool_b)
+    return jnp.concatenate([lo[None], pool_in[...], hi[None]], axis=0)
+
+
+def turn2_body(pool_in, pool_a, pool_b, pg, ra, rb, xa, xb, out_a, out_b):
+    cy, cz, c = pool_a.shape
+    pooled = pooled_of(pool_in, pool_a, pool_b)
     xlo, xhi = get_faces(bit_of("grp") == 1, ra, rb)
+    _, (glo, ghi) = x_faces(xa, xb, (2 * cy + 2, 2 * cz, c), (cy, cz, c))
 
     def side(y, last):
-        two = [jnp.concatenate([xlo[0:2, at], pooled[:, at], xhi[0:2, at]], axis=0) for at in (y, y + 1)]
-        one = jnp.concatenate([xlo[2:3, last], pg[:, last], xhi[2:3, last]], axis=0)
+        two = [jnp.concatenate([xlo[:, at], pooled[:, at], xhi[:, at]], axis=0) for at in (y, y + 1)]
+        one = jnp.concatenate([glo[None, last], pg[:, last], ghi[None, last]], axis=0)
         return jnp.concatenate([*two, one], axis=0)
 
     put_faces(bit_of("sub") == 1, out_a, out_b, side(0, 0), side(cy - 2, cy - 1))
@@ -170,55 +204,80 @@
                     target[reverse_bits(s, bits) % half, pl.ds(t * size, size)] = value
 
 
+def coarse_part(taps, grads, wb, bias, wm, cz):
+    c2 = wm.shape[0]
+    part = jnp.dot(jnp.concatenate(taps, axis=1), wb[...], preferred_element_type=F32)
+    pre = (
+        part[:, c2 : 2 * c2]
+        + shift_rows(part[:, :c2], 1, cz)
+        + shift_rows(part[:, 2 * c2 :], -1, cz)
+        + bias[...]
+    )
+    sig = sigmoid(pre)
+    back = lax.dot_general(grads, wm[...], (((1,), (1,)), ((), ())), preferred_element_type=F32)
+    return (back * (sig * (1.0 + pre * (1.0 - sig)))).astype(BF16), (pre * sig).astype(BF16)
+
+
+def mid_body(pool_in, pool_a, pool_b, ra, rb, xa, xb, pg, wb, bias, wm, slope, coarse, qx, gx):
+    cx, cy, cz, c = pg.shape
+    c2 = wm.shape[0]
+    qx[0:2], qx[cx + 2 : cx + 4] = get_faces(bit_of("grp") == 1, ra, rb)
+    qx[2 : cx + 2] = pooled_of(pool_in, pool_a, pool_b)
+    _, (gx[0], gx[cx + 1]) = x_faces(xa, xb, (2 * cy + 2, 2 * cz, c), (cy, cz, c))
+    gx[1 : cx + 1] = pg[...]
+    for first in range(0, cx + 2, 3):
+        planes = range(first, first + 3)
+        taps = [
+            jnp.concatenate([qx[x + i, j : j + cy - 2].reshape(-1, c) for x in planes], axis=0)
+            for i in range(3)
+            for j in range(3)
+        ]
+        grads = jnp.concatenate([gx[x, 1 : cy - 1].reshape(-1, c) for x in planes], axis=0)
+        out, act = coarse_part(taps, grads, wb, bias, wm, cz)
+        slope[first : first + 3] = out.reshape(3, cy - 2, cz, c2)
+        act = act.reshape(3, cy - 2, cz, c2)
+        for h, x in enumerate(planes):
+            if 1 <= x <= cx:
+                coarse[x - 1] = act[h]
+
+
 def coarse_body(
-    n, pooled, ra, rb, ua, ub, pg, w, bias, wm,
-    slope, coarse, keep, send, cbias, qpad, gpad, wb, st, rhs, acc, ct,
+    n, pool_in, pool_a, pool_b, ra, rb, ua, ub, xa, xb, pg, wb, bias, wm, slope_mid, coarse_mid,
+    slope, coarse, keep, send, cbias, qpad, gpad, st, rhs, acc, ct,
 ):
-    cx, cy, cz, c = pooled.shape
+    cx, cy, cz, c = pg.shape
     c2 = wm.shape[0]
     xlo, xhi = get_faces(bit_of("grp") == 1, ra, rb)
     ylo, yhi = get_faces(bit_of("sub") == 1, ua, ub)
-    qpad[2 : cx + 2, 2 : cy + 2] = pooled[...]
-    qpad[0:2, 2 : cy + 2] = xlo[0:2]
-    qpad[cx + 2 : cx + 4, 2 : cy + 2] = xhi[0:2]
+    qpad[2 : cx + 2, 2 : cy + 2] = pooled_of(pool_in, pool_a, pool_b)
+    qpad[0:2, 2 : cy + 2] = xlo
+    qpad[cx + 2 : cx + 4, 2 : cy + 2] = xhi
     wide = cx + 4
     for t in (0, 1):
         qpad[:, t] = ylo[t * wide : (t + 1) * wide]
         qpad[:, cy + 2 + t] = yhi[t * wide : (t + 1) * wide]
     gpad[1 : cx + 1, 1 : cy + 1] = pg[...]
-    gpad[0, 1 : cy + 1] = xlo[2]
-    gpad[cx + 1, 1 : cy + 1] = xhi[2]
+    _, (glo, ghi) = x_faces(xa, xb, (2 * cy + 2, 2 * cz, c), (cy, cz, c))
+    gpad[0, 1 : cy + 1] = glo
+    gpad[cx + 1, 1 : cy + 1] = ghi
     gpad[:, 0] = ylo[2 * wide :]
     gpad[:, cy + 1] = yhi[2 * wide :]
-    for i in range(3):
-        for j in range(3):
-            for k in range(3):
-                wb[pl.ds((3 * i + j) * c, c), pl.ds(k * c2, c2)] = w[i, j, k]
-    wide = cy + 2
-    rows = wide * cz
-
-    def plane(x, carry):
-        taps = [qpad[x + i, j : j + wide].reshape(rows, c) for i in range(3) for j in range(3)]
-        part = jnp.dot(jnp.concatenate(taps, axis=1), wb[...], preferred_element_type=F32)
-        pre = (
-            part[:, c2 : 2 * c2]
-            + shift_rows(part[:, :c2], 1, cz)
-            + shift_rows(part[:, 2 * c2 :], -1, cz)
-            + bias[...]
-        )
-        sig = sigmoid(pre)
-        back = lax.dot_general(
-            gpad[x].reshape(rows, c), wm[...], (((1,), (1,)), ((), ())), preferred_element_type=F32
-        )
-        slope[x] = (back * (sig * (1.0 + pre * (1.0 - sig)))).astype(BF16).reshape(wide, cz, c2)
-
-        @pl.when((x >= 1) & (x <= cx))
-        def _():
-            coarse[x - 1] = (pre * sig).astype(BF16).reshape(wide, cz, c2)[1 : cy + 1]
-
-        return carry
-
-    lax.fori_loop(0, cx + 2, plane, 0)
+    def both(ref, x, j):
+        return jnp.concatenate([ref[x, j : j + 2], ref[x, cy + j : cy + 2 + j]], axis=0).reshape(4 * cz, -1)
+
+    planes = range(cx + 2)
+    taps = [
+        jnp.concatenate([both(qpad, x + i, j) for x in planes], axis=0) for i in range(3) for j in range(3)
+    ]
+    grads = jnp.concatenate([both(gpad, x, 0) for x in planes], axis=0)
+    out, act = coarse_part(taps, grads, wb, bias, wm, cz)
+    out, act = (v.reshape(cx + 2, 4, cz, c2) for v in (out, act))
+    slope[:, 0:2] = out[:, 0:2]
+    slope[:, cy : cy + 2] = out[:, 2:4]
+    slope[:, 2:cy] = slope_mid[...]
+    coarse[:, 0] = act[1 : cx + 1, 1]
+    coarse[:, cy - 1] = act[1 : cx + 1, 2]
+    coarse[:, 1 : cy - 1] = coarse_mid[...]
     cells = cx * cy * cz
     mid = slope[1 : cx + 1, 1 : cy + 1].reshape(cells, c2)
     wide_mid = mid.astype(F32)
@@ -247,7 +306,7 @@
     spread(keep, send, n, 28, piece)
 
 
-def back_body(n, slope, w, cot, ds, ds_edge, own, halo, cbias, keep, send, up, st, rhs, acc):
+def back_body(n, slope, w, cot, ds, ds_a, ds_b, own, xa, xb, cbias, keep, send, up, st, rhs, acc):
     bx, by, bz, c = cot.shape
     cx, cy, cz = bx // 2, by // 2, bz // 2
     c2 = slope.shape[3]
@@ -270,10 +329,12 @@
     up[pl.ds(0, cells, stride=2), :] = pooled
     up[pl.ds(1, cells, stride=2), :] = pooled
     rows = by * bz
+    edges = get_faces(bit_of("grp") == 1, ds_a, ds_b)
+    halo, _ = x_faces(xa, xb, (by + 2, bz, c), (cy, cz, c))
     for x in range(bx):
         base = up[pl.ds((x // 2) * cy * bz, cy * bz), :].reshape(cy, 1, bz, c)
         fine = cot[x].astype(F32).reshape(cy, 2, bz, c) + base
-        gain = ds[x - 1] if 0 < x < bx - 1 else ds_edge[x // (bx - 1)]
+        gain = ds[x - 1] if 0 < x < bx - 1 else edges[x // (bx - 1)]
         fs = (fine.reshape(rows, c) * gain.reshape(rows, c)).astype(BF16)
         wide = fs.astype(F32)
         st[pl.ds(0, c), pl.ds(x * rows, rows)] = shift_rows(wide, -1, bz).astype(BF16).T
@@ -291,7 +352,7 @@
                 size = (past - first) * rows
                 rhs[pl.ds(at, size), pl.ds(h * c, c)] = own[first:past, j : j + by].reshape(size, c)
                 if i != 1:
-                    edge = halo[i // 2, j : j + by].reshape(rows, c)
+                    edge = halo[i // 2][j : j + by].reshape(rows, c)
                     rhs[pl.ds(0 if i == 0 else size, rows), pl.ds(h * c, c)] = edge
         acc[:, pl.ds(t * c, 2 * c)] = jnp.dot(
             st[...], rhs[...], preferred_element_type=F32
@@ -311,7 +372,7 @@
     spread(keep, send, n, 28, piece)
 
 
-def merge_body(hidden, hid_edge, coarse, wm, out, tmp):
+def merge_body(hidden, hid_a, hid_b, coarse, wm, out, tmp):
     bx, by, bz, c = out.shape
     cx, cy, cz = bx // 2, by // 2, bz // 2
     c2 = coarse.shape[3]
@@ -319,9 +380,10 @@
     proj = jnp.dot(coarse[...].reshape(cells, c2), wm[...], preferred_element_type=F32)
     tmp[pl.ds(0, cells, stride=2), :] = proj
     tmp[pl.ds(1, cells, stride=2), :] = proj
+    edges = get_faces(bit_of("grp") == 1, hid_a, hid_b)
     for x in range(bx):
         base = tmp[pl.ds((x // 2) * cy * bz, cy * bz), :].reshape(cy, 1, bz, c)
-        hid = hidden[x - 1] if 0 < x < bx - 1 else hid_edge[x // (bx - 1)]
+        hid = hidden[x - 1] if 0 < x < bx - 1 else edges[x // (bx - 1)]
         total = hid.astype(F32).reshape(cy, 2, bz, c) + base
         out[x] = total.astype(BF16).reshape(by, bz, c)
 
@@ -421,6 +483,7 @@
     for bit in range(2, lax.axis_size("sub").bit_length() - 1):
         keep, send = split_sum(parts, places[grp_bits() + bit])
         parts = [keep, partners(send, 0, 1 << bit)]
+    parts = yield parts
     bits = [0]
     last = grp_bits() - 1
     for bit in range(1, last + 1):
@@ -430,16 +493,44 @@
                 keep, send = split_sum_kernel(parts, "grp", bit, name + "_half")
             else:
                 keep, send = split_sum(parts, places[bit])
-            parts = [keep, partners(send, mask, 0)]
+            keep, send = yield keep, send
+            parts = yield keep, partners(send, mask, 0)
             bits.append(bit)
         else:
             total = sum_kernel(parts, name + "_sum") if "sum" in kernels else total_of(parts)
-            parts = [total, partners(total, mask, 0)]
+            total = yield total
+            parts = yield total, partners(total, mask, 0)
     total = sum_kernel(parts, name + "_total") if "total" in kernels else total_of(parts)
     pieces = [total]
     for which in range(1, 2 ** len(bits)):
         pieces.append(partners(total, sum(1 << bits[b] for b in range(len(bits)) if which >> b & 1), 0))
     return pieces
+
+
+def step(run, value):
+    try:
+        return run.send(value), None
+    except StopIteration as done:
+        return None, done.value
+
+
+def side_by_side(ahead, behind, arrived):
+    first, first_done = step(ahead, step(ahead, None)[0])
+    first, arrived = lax.optimization_barrier((first, arrived))
+    first, first_done = step(ahead, first)
+    behind = behind(arrived)
+    second, second_done = step(behind, None)
+    while second_done is None:
+        if first_done is None:
+            first, first_done = step(ahead, first)
+        if first_done is None:
+            first, first_done = step(ahead, first)
+        second, second_done = step(behind, second)
+        if second_done is None:
+            second, second_done = step(behind, second)
+            if first_done is None and second_done is None:
+                first, second = lax.optimization_barrier((first, second))
+    return first_done, second_done
 
 
 def last_body(count, *refs):
@@ -500,16 +591,13 @@
         [((cx, cy, cz, c), BF16), ((count, 1, c), jnp.int32)],
         [pltpu.VMEM((cx * cy * bz, c), F32)],
     )
-    face = ((by + 2, bz, c), BF16)
+    face = (((by + 2) * bz + cy * cz, c), BF16)
     own, ta, tb = call(
-        turn_body,
-        "turn",
-        (field, ya, yb),
-        [((bx, by + 2, bz, c), BF16), face, face],
+        turn_body, "turn", (field, ya, yb, pg), [((bx, by + 2, bz, c), BF16), face, face]
     )
     xa, xb = swap_faces(ta, tb, "grp")
     bias = fine_bias.reshape(1, c)
-    hidden, ds, pooled, wb = call(
+    hidden, ds, pool_in, wb = call(
         inner_body,
         "inner",
         (own, fine_kernel, bias),
@@ -522,32 +610,46 @@
         [pltpu.VMEM((cy * bz, c), F32)],
         6,
     )
-    face = ((3, cy, cz, c), BF16)
-    hid_edge, ds_edge, halo, pooled, pa, pb = call(
-        outer_body,
-        "outer",
-        (own, xa, xb, wb, bias, hidden, pooled, pg),
-        [
-            ((2, by, bz, c), BF16),
-            ((2, by, bz, c), F32),
-            ((2, by + 2, bz, c), BF16),
-            ((cx, cy, cz, c), BF16),
-            face,
-            face,
-        ],
-        [pltpu.VMEM((cy * bz, c), F32)],
+
+    def edge(second, face):
+        return call(
+            functools.partial(edge_body, second),
+            "edge",
+            (own, face, wb, bias, hidden, pool_in),
+            [
+                ((by, bz, c), BF16),
+                ((by, bz, c), F32),
+                ((cy, cz, c), BF16),
+                ((2, cy, cz, c), BF16),
+            ],
+            [pltpu.VMEM((cy * bz, c), F32)],
+            1,
+        )
+
+    hid_a, ds_a, pool_a, pa = edge(False, xa)
+    hid_b, ds_b, pool_b, pb = edge(True, xb)
+    pxa, pxb = swap_faces(pa, pb, "grp")
+    (taps,) = call(taps_body, "taps", (coarse_kernel,), [((9 * c, 3 * c2), BF16)], (), 0.5)
+    pxa, taps = lax.optimization_barrier((pxa, taps))
+    face = ((2 * (cx + 4) + cx + 2, cz, c), BF16)
+    pooled = (pool_in, pool_a, pool_b)
+    qa, qb = call(turn2_body, "turn2", (*pooled, pg, pxa, pxb, xa, xb), [face, face])
+    pya, pyb = swap_faces(qa, qb, "sub")
+    bias2 = coarse_bias.reshape(1, c2)
+    slope_mid, coarse_mid = call(
+        mid_body,
+        "mid",
+        (*pooled, pxa, pxb, xa, xb, pg, taps, bias2, merge_weight),
+        [((cx + 2, cy - 2, cz, c2), BF16), ((cx, cy - 2, cz, c2), BF16)],
+        [pltpu.VMEM((cx + 4, cy, cz, c), BF16), pltpu.VMEM((cx + 2, cy, cz, c), BF16)],
         2,
     )
-    pxa, pxb = swap_faces(pa, pb, "grp")
-    face = ((2 * (cx + 4) + cx + 2, cz, c), BF16)
-    qa, qb = call(turn2_body, "turn2", (pooled, pg, pxa, pxb), [face, face])
-    pya, pyb = swap_faces(qa, qb, "sub")
     cells = cx * cy * cz
     part = (n // 2, 28 * (c2 // n), c)
     slope, coarse, ckeep, csend, cbias = call(
         functools.partial(coarse_body, n),
         "coarse",
-        (pooled, pxa, pxb, pya, pyb, pg, coarse_kernel, coarse_bias.reshape(1, c2), merge_weight),
+        (*pooled, pxa, pxb, pya, pyb, xa, xb, pg, taps, bias2, merge_weight, slope_mid, coarse_mid),
         [
             ((cx + 2, cy + 2, cz, c2), BF16),
             ((cx, cy, cz, c2), BF16),
@@ -558,7 +660,6 @@
         [
             pltpu.VMEM((cx + 4, cy + 4, cz, c), BF16),
             pltpu.VMEM((cx + 2, cy + 2, cz, c), BF16),
-            pltpu.VMEM((9 * c, 3 * c2), BF16),
             pltpu.VMEM((3 * c2, cells), BF16),
             pltpu.VMEM((cells, 10 * c), BF16),
             pltpu.VMEM((3 * c2, 10 * c), BF16),
@@ -570,7 +671,7 @@
     (output,) = call(
         merge_body,
         "merge",
-        (hidden, hid_edge, coarse, merge_weight),
+        (hidden, hid_a, hid_b, coarse, merge_weight),
         [((bx, by, bz, c), BF16)],
         [pltpu.VMEM((cx * cy * bz, c), F32)],
         2,
@@ -584,7 +685,7 @@
     fkeep, fsend = call(
         functools.partial(back_body, n),
         "back",
-        (slope, coarse_kernel, cotangent, ds, ds_edge, own, halo, cbias),
+        (slope, coarse_kernel, cotangent, ds, ds_a, ds_b, own, xa, xb, cbias),
         [(part, BF16), (part, BF16)],
         [
             pltpu.VMEM((cx * cy * bz, c), F32),
@@ -594,13 +695,15 @@
         ],
         10,
     )
-    fsend, cparts = lax.optimization_barrier((fsend, cparts))
-    fgot = cores(fsend)
-    fparts = cross(*spread_sum(fkeep, fgot))
-    coarse_sum = finish_sum(cparts, places, "coarse", ('half', 'sum'))
-    fine_sum = finish_sum(fparts, places, "fine", ('half', 'sum'))
+
+    coarse_sum, fine_sum = side_by_side(
+        finish_sum(cparts, places, "coarse", ("half", "sum")),
+        lambda got: finish_sum(cross(*spread_sum(fkeep, jnp.stack(got))), places, "fine", ("half", "sum")),
+        [cores(part) for part in fsend],
+    )
     per, cper = c // n, c2 // n
     grad_coarse, grad_merge = last(coarse_sum, cper, [((cper, c), F32)], "coarse_last")
+    fine_sum, grad_merge = lax.optimization_barrier((fine_sum, grad_merge))
     biases = [((1, per), F32), ((1, cper), F32)]
     grad_fine, bias, coarse_sums = last(fine_sum, per, biases, "fine_last")
     return (output, grad_fine, bias[0], grad_coarse, coarse_sums[0], grad_merge)

time: 87.5 us -> 83.7 us (0.957)
  starting transfers between devices: 44.4 us -> 41.2 us
    ppermute x4, starting transfers between devices: 10.4 us -> 8.56 us  [swap_faces(): return (lax.ppermute(first, axis, one), got)]
    ppermute x18 -> x19, starting transfers between devices: 31.3 us -> 30 us  [partners(): return lax.ppermute(value, ('grp', 'sub'), pairs)]
    pallas_call x16 -> x19, Pallas kernels: 25.7 us -> 25.1 us  [call(): pl.pallas_call(body, name=name, out_shape=[jax.ShapeDtypeStruct(s, t) for...]
    ppermute x18 -> x19, waiting for transfers between devices: 11.6 us -> 11.4 us  [partners(): return lax.ppermute(value, ('grp', 'sub'), pairs)]
  transfers between devices with their start and end apart: 26 -> 27, of which waited for: 13 -> 14; matrix products, arithmetic and copies ran while one was open for 0% -> 0% of each run, Pallas kernels for 20% -> 24%
where the time goes in v6:
time: 83.7 us; the launch traced here: 83.4 us
  starting transfers between devices  41.2 us (49%)
  Pallas kernels  25.1 us (30%)
  waiting for transfers between devices  14 us (17%)
  local copies, waits for them, and re-layouts  1.32 us (2%)
  other arithmetic  0.99 us (1%)
  between operations  0.89 us (1%)
    ppermute x19, starting transfers between devices, partners(): return lax.ppermute(value, ('grp', 'sub'), pairs)  30 us
    pallas_call x19, Pallas kernels, call(): pl.pallas_call(body, name=name, out_shape=[jax.ShapeDtypeStruct(s, t) for...  25.1 us
    ppermute x19, waiting for transfers between devices, partners(): return lax.ppermute(value, ('grp', 'sub'), pairs)  11.4 us
    ppermute x4, starting transfers between devices, swap_faces(): return (lax.ppermute(first, axis, one), got)  8.56 us
    ppermute x4, starting transfers between devices, swap_faces(): got = lax.ppermute(second, axis, two)  2.66 us
    ppermute x4, waiting for transfers between devices, swap_faces(): return (lax.ppermute(first, axis, one), got)  2.57 us
  transfers between devices with their start and end apart: 27, of which 14 were waited for; matrix products, arithmetic and copies ran while one was open for 0% of the time, Pallas kernels for 24%

profile of v6, /device:TPU:0, one launch (start us, length us, event | category | flops | bytes accessed | tf_op | source)
XLA Modules:
  0.0 83.4 jit_solution(2618337402600886748)
XLA Ops:
  0.6 0.9 %fusion.1 = (bf16[8,32,128]{2,1,0:T(8,128)(2,1)S(1)}, bf16[8,32,128]{2,1,0:T(8,128)(2,1)S(1)}) fusion(pred[]{:T(512)S(6)} %eq.3, bf16[8,16,32,128]{3,2,1,0:T(8,128)(2,1)} %field.1), kind=kLoop, calls=%fused_computation.8 | loop fusion | flops 65536 | bytes 262145 | tf_op jit(solution)/shard_map/jit(_where)/select_n | solution.py:584
  1.5 0.7 collective-permute-start.1
  2.2 0.0 copy-start.1
  2.2 4.4 %collective-permute-start = (bf16[8,32,128]{2,1,0:T(8,128)(2,1)S(1)}, bf16[8,32,128]{2,1,0:T(8,128)(2,1)S(1)}, u32[]{:S(2)}, u32[]{:S(2)}) collective-permute-start(bf16[8,32,128]{2,1,0:T(8,128)(2,1)S(1)} %get-tuple-element.139), channel_id=1, source_target_pairs={{0,1},{1,0},{2,3},{3,2},{4,5},{5,4},{6,7},{7,6},{8,9},{9,8},{10,11... | collective-permute-start | bytes 196616 | tf_op jit(solution)/shard_map/ppermute | solution.py:396
  6.6 1.2 %copy-done.2 = bf16[8,16,32,128]{3,2,1,0:T(8,128)(2,1)S(1)} copy-done((bf16[8,16,32,128]{3,2,1,0:T(8,128)(2,1)S(1)}, bf16[8,16,32,128]{3,2,1,0:T(8,128)(2,1)}, u32[]{:S(2)}) %copy-start.2) | copy-done | bytes 1048600
  7.8 0.8 cubes.1
  8.6 0.0 copy-start.4
  8.6 0.0 copy-start.7
  8.7 0.2 turn.1
  8.8 1.6 %collective-permute-start.2 = (bf16[704,128]{1,0:T(8,128)(2,1)S(1)}, bf16[704,128]{1,0:T(8,128)(2,1)S(1)}, u32[]{:S(2)}, u32[]{:S(2)}) collective-permute-start(bf16[704,128]{1,0:T(8,128)(2,1)S(1)} %get-tuple-element.75), channel_id=1, source_target_pairs={{0,4},{4,0},{8,12},{12,8},{16,20},{20,16},{24,28},{28,24},{1,5},{5... | collective-permute-start | bytes 540680 | tf_op jit(solution)/shard_map/ppermute | solution.py:396
  10.4 0.7 collective-permute-start.3
  11.1 5.1 %inner.1 = (bf16[6,16,32,128]{3,2,1,0:T(8,128)(2,1)S(1)}, f32[6,16,32,128]{3,2,1,0:T(8,128)S(1)}, bf16[2,8,16,128]{3,2,1,0:T(8,128)(2,1)S(1)}, bf16[1152,384]{1,0:T(8,128)(2,1)S(1)}) custom-call(bf16[8,18,32,128]{3,2,1,0:T(8,128)(2,1)S(1)} %get-tuple-element.73.own, bf16[3,3,3,128,128]{4,3,2,1,0:T(8,128)(2,1)S(1)} %copy-done.4, f32[1,128]{1,0:T(1,128)S(1)} %bitcast.46), custom_call_target="tpu_custom_call" | custom-call | flops 6000000000 | tf_op jit(solution)/shard_map/inner/pallas_call | solution.py:20
  16.2 2.1 %collective-permute-done.2.face.xa = bf16[704,128]{1,0:T(8,128)(2,1)S(1)} collective-permute-done((bf16[704,128]{1,0:T(8,128)(2,1)S(1)}, bf16[704,128]{1,0:T(8,128)(2,1)S(1)}, u32[]{:S(2)}, u32[]{:S(2)}) %collective-permute-start.2) | collective-permute-done | bytes 180256 | tf_op jit(solution)/shard_map/ppermute | solution.py:396
  18.3 1.0 %edge.2 = (bf16[16,32,128]{2,1,0:T(8,128)(2,1)S(1)}, f32[16,32,128]{2,1,0:T(8,128)S(1)}, bf16[8,16,128]{2,1,0:T(8,128)(2,1)S(1)}, bf16[2,8,16,128]{3,2,1,0:T(8,128)(2,1)S(1)}) custom-call(bf16[8,18,32,128]{3,2,1,0:T(8,128)(2,1)S(1)} %get-tuple-element.73.own, bf16[704,128]{1,0:T(8,128)(2,1)S(1)} %collective-permute-done.2.face.xa, ...), custom_call_target="tpu_custom_call" | custom-call | flops 1000000000 | tf_op jit(solution)/shard_map/edge/pallas_call | solution.py:20
  19.3 0.0 copy-start
  19.3 2.5 %collective-permute-start.4 = (bf16[2,8,16,128]{3,2,1,0:T(8,128)(2,1)S(1)}, bf16[2,8,16,128]{3,2,1,0:T(8,128)(2,1)S(1)}, u32[]{:S(2)}, u32[]{:S(2)}) collective-permute-start(bf16[2,8,16,128]{3,2,1,0:T(8,128)(2,1)S(1)} %get-tuple-element.83), channel_id=1, source_target_pairs={{0,4},{4,0},{8,12},{12,8},{16,20},{20,16},{24,28},{28,24},{1,5},{5... | collective-permute-start | bytes 196616 | tf_op jit(solution)/shard_map/ppermute | solution.py:396
  21.9 0.0 collective-permute-done.3.face.xb
  21.9 1.0 %edge.3 = (bf16[16,32,128]{2,1,0:T(8,128)(2,1)S(1)}, f32[16,32,128]{2,1,0:T(8,128)S(1)}, bf16[8,16,128]{2,1,0:T(8,128)(2,1)S(1)}, bf16[2,8,16,128]{3,2,1,0:T(8,128)(2,1)S(1)}) custom-call(bf16[8,18,32,128]{3,2,1,0:T(8,128)(2,1)S(1)} %get-tuple-element.73.own, bf16[704,128]{1,0:T(8,128)(2,1)S(1)} %collective-permute-done.3.face.xb, ...), custom_call_target="tpu_custom_call" | custom-call | flops 1000000000 | tf_op jit(solution)/shard_map/edge/pallas_call | solution.py:20
  22.8 0.7 collective-permute-start.5
  23.5 0.1 taps.1.wb
  23.6 0.5 collective-permute-done.4.ra
  24.2 0.1 collective-permute-start.6
  24.2 0.7 collective-permute-start.7
  24.9 0.0 copy-done.5
  24.9 1.5 %mid.1 = (bf16[6,6,16,256]{3,2,1,0:T(8,128)(2,1)S(1)}, bf16[4,6,16,256]{3,2,1,0:T(8,128)(2,1)S(1)}) custom-call(bf16[2,8,16,128]{3,2,1,0:T(8,128)(2,1)S(1)} %get-tuple-element.77.pool_in, bf16[8,16,128]{2,1,0:T(8,128)(2,1)S(1)} %get-tuple-element.81.pool_a, bf16[8,16,128]{2,1,0:T(8,128)(2,1)S(1)} %get-tuple-element.82.pool_b, ...), custom_call_target="tpu_custom_call" | custom-call | flops 2000000000 | tf_op jit(solution)/shard_map/mid/pallas_call | solution.py:20
  26.5 3.4 %coarse.1 = (bf16[6,10,16,256]{3,2,1,0:T(8,128)(2,1)S(1)}, bf16[4,8,16,256]{3,2,1,0:T(8,128)(2,1)S(1)}, bf16[2,1792,128]{2,1,0:T(8,128)(2,1)S(1)}, bf16[2,1792,128]{2,1,0:T(8,128)(2,1)S(1)}, bf16[256,128]{1,0:T(8,128)(2,1)S(1)}) custom-call(bf16[2,8,16,128]{3,2,1,0:T(8,128)(2,1)S(1)} %get-tuple-element.77.pool_in, ...), custom_call_target="tpu_custom_call" | custom-call | flops 6000000000 | tf_op jit(solution)/shard_map/coarse/pallas_call | solution.py:20
  29.9 4.1 %collective-permute-start.8 = (bf16[2,1792,128]{2,1,0:T(8,128)(2,1)S(1)}, bf16[2,1792,128]{2,1,0:T(8,128)(2,1)S(1)}, u32[]{:S(2)}, u32[]{:S(2)}) collective-permute-start(bf16[2,1792,128]{2,1,0:T(8,128)(2,1)S(1)} %get-tuple-element.92), channel_id=1, source_target_pairs={{0,1},{1,0},{2,3},{3,2},{4,5},{5,4},{6,7},{7,6},{8,9},{9,8},{10,11... | collective-permute-start | bytes 2752520 | tf_op jit(solution)/shard_map/ppermute | solution.py:426
  34.1 1.3 %merge.1 = bf16[8,16,32,128]{3,2,1,0:T(8,128)(2,1)} custom-call(bf16[6,16,32,128]{3,2,1,0:T(8,128)(2,1)S(1)} %get-tuple-element.74.hid_in.hidden, bf16[16,32,128]{2,1,0:T(8,128)(2,1)S(1)} %get-tuple-element.78.hid_a, bf16[16,32,128]{2,1,0:T(8,128)(2,1)S(1)} %get-tuple-element.80.hid_b, bf16[4,8,16,256]{3,2,1,0:T(8,128)(2,1)S(1)} %get-tuple-element.91.coarse, ...), custom_call_target="tpu_custom_call" | custom-call | flops 2000000000 | tf_op jit(solution)/shard_map/merge/pallas_call | solution.py:20
  35.4 0.8 collective-permute-done.8
  36.2 0.2 split.2
  36.4 6.4 %collective-permute-start.9 = (bf16[1,896,128]{2,1,0:T(8,128)(2,1)S(1)}, bf16[1,896,128]{2,1,0:T(8,128)(2,1)S(1)}, u32[]{:S(2)}, u32[]{:S(2)}) collective-permute-start(bf16[1,896,128]{2,1,0:T(8,128)(2,1)S(1)} %get-tuple-element.102), channel_id=1, source_target_pairs={{0,6},{1,7},{2,4},{3,5},{4,2},{5,3},{6,0},{7,1},{8,14},{9,15},{10,... | collective-permute-start | bytes 688136 | tf_op jit(solution)/shard_map/ppermute | solution.py:426
  42.8 1.0 %collective-permute-start.10 = (bf16[1,896,128]{2,1,0:T(8,128)(2,1)S(1)}, bf16[1,896,128]{2,1,0:T(8,128)(2,1)S(1)}, u32[]{:S(2)}, u32[]{:S(2)}) collective-permute-start(bf16[1,896,128]{2,1,0:T(8,128)(2,1)S(1)} %get-tuple-element.103), channel_id=1, source_target_pairs={{0,2},{1,3},{2,0},{3,1},{4,6},{5,7},{6,4},{7,5},{8,10},{9,11},{10,... | collective-permute-start | bytes 688136 | tf_op jit(solution)/shard_map/ppermute | solution.py:426
  43.9 8.2 %back.1 = (bf16[2,896,128]{2,1,0:T(8,128)(2,1)S(1)}, bf16[2,896,128]{2,1,0:T(8,128)(2,1)S(1)}) custom-call(bf16[6,10,16,256]{3,2,1,0:T(8,128)(2,1)S(1)} %get-tuple-element.107.slope, bf16[3,3,3,128,256]{4,3,2,1,0:T(8,128)(2,1)S(1)} %copy-done, bf16[8,16,32,128]{3,2,1,0:T(8,128)(2,1)S(1)} %copy-done.3, f32[6,16,32,128]{3,2,1,0:T(8,128)S(1)} %get-tuple-element.108.ds, ...), custom_call_target="tpu_custom_call" | custom-call | flops 10000000000 | tf_op jit(solution)/shard_map/back/pallas_call | solution.py:20
  52.1 0.1 collective-permute-start.13
  52.2 0.5 collective-permute-start.12
  52.7 1.0 %collective-permute-done.10 = bf16[1,896,128]{2,1,0:T(8,128)(2,1)S(1)} collective-permute-done((bf16[1,896,128]{2,1,0:T(8,128)(2,1)S(1)}, bf16[1,896,128]{2,1,0:T(8,128)(2,1)S(1)}, u32[]{:S(2)}, u32[]{:S(2)}) %collective-permute-start.10) | collective-permute-done | bytes 229408 | tf_op jit(solution)/shard_map/ppermute | solution.py:426
  53.7 0.1 coarse_half.1
  53.8 0.2 collective-permute-done.12
  54.0 3.5 %collective-permute-start.14 = (bf16[448,128]{1,0:T(8,128)(2,1)S(1)}, bf16[448,128]{1,0:T(8,128)(2,1)S(1)}, u32[]{:S(2)}, u32[]{:S(2)}) collective-permute-start(bf16[448,128]{1,0:T(8,128)(2,1)S(1)} %get-tuple-element.114), channel_id=1, source_target_pairs={{0,8},{1,9},{2,10},{3,11},{4,12},{5,13},{6,14},{7,15},{8,0},{9,1},... | collective-permute-start | bytes 344072 | tf_op jit(solution)/shard_map/ppermute | solution.py:426
  57.5 0.1 split.3
  57.6 0.7 collective-permute-start.16
  58.3 1.2 %collective-permute-start.17 = (bf16[1,448,128]{2,1,0:T(8,128)(2,1)S(1)}, bf16[1,448,128]{2,1,0:T(8,128)(2,1)S(1)}, u32[]{:S(2)}, u32[]{:S(2)}) collective-permute-start(bf16[1,448,128]{2,1,0:T(8,128)(2,1)S(1)} %get-tuple-element.120), channel_id=1, source_target_pairs={{0,2},{1,3},{2,0},{3,1},{4,6},{5,7},{6,4},{7,5},{8,10},{9,11},{10,... | collective-permute-start | bytes 344072 | tf_op jit(solution)/shard_map/ppermute | solution.py:426
  59.6 1.6 %collective-permute-start.18 = (bf16[1,448,128]{2,1,0:T(8,128)(2,1)S(1)}, bf16[1,448,128]{2,1,0:T(8,128)(2,1)S(1)}, u32[]{:S(2)}, u32[]{:S(2)}) collective-permute-start(bf16[1,448,128]{2,1,0:T(8,128)(2,1)S(1)} %get-tuple-element.121), channel_id=1, source_target_pairs={{0,4},{1,5},{2,6},{3,7},{4,0},{5,1},{6,2},{7,3},{8,12},{9,13},{10,... | collective-permute-start | bytes 344072 | tf_op jit(solution)/shard_map/ppermute | solution.py:426
  61.2 2.6 %collective-permute-start.15 = (bf16[448,128]{1,0:T(8,128)(2,1)S(1)}, bf16[448,128]{1,0:T(8,128)(2,1)S(1)}, u32[]{:S(2)}, u32[]{:S(2)}) collective-permute-start(bf16[448,128]{1,0:T(8,128)(2,1)S(1)} %coarse_sum.1), channel_id=1, source_target_pairs={{0,16},{1,17},{2,18},{3,19},{4,20},{5,21},{6,22},{7,23},{8,24},{9,... | collective-permute-start | bytes 344072 | tf_op jit(solution)/shard_map/ppermute | solution.py:426
  63.8 0.8 collective-permute-done.16
  64.6 0.8 collective-permute-done.17
  65.4 0.2 collective-permute-done.18
  65.6 0.1 fine_half.1
  65.7 0.3 collective-permute-start.19
  66.0 3.9 %collective-permute-done.19.refs_1_ = bf16[224,128]{1,0:T(8,128)(2,1)S(1)} collective-permute-done((bf16[224,128]{1,0:T(8,128)(2,1)S(1)}, bf16[224,128]{1,0:T(8,128)(2,1)S(1)}, u32[]{:S(2)}, u32[]{:S(2)}) %collective-permute-start.19) | collective-permute-done | bytes 57376 | tf_op jit(solution)/shard_map/ppermute | solution.py:426
  69.9 1.4 %collective-permute-start.20 = (bf16[224,128]{1,0:T(8,128)(2,1)S(1)}, bf16[224,128]{1,0:T(8,128)(2,1)S(1)}, u32[]{:S(2)}, u32[]{:S(2)}) collective-permute-start(bf16[224,128]{1,0:T(8,128)(2,1)S(1)} %fine_sum.1), channel_id=1, source_target_pairs={{0,16},{1,17},{2,18},{3,19},{4,20},{5,21},{6,22},{7,23},{8,24},{9,... | collective-permute-start | bytes 172040 | tf_op jit(solution)/shard_map/ppermute | solution.py:426
  71.3 1.8 %collective-permute-start.26 = (bf16[448,128]{1,0:T(8,128)(2,1)S(1)}, bf16[448,128]{1,0:T(8,128)(2,1)S(1)}, u32[]{:S(2)}, u32[]{:S(2)}) collective-permute-start(bf16[448,128]{1,0:T(8,128)(2,1)S(1)} %add_convert_fusion.refs_0_), channel_id=1, source_target_pairs={{0,12},{1,13},{2,14},{3,15},{4,8},{5,9},{6,10},{7,11},{8,4},{9,5},... | collective-permute-start | bytes 344072 | tf_op jit(solution)/shard_map/ppermute | solution.py:426
  73.1 0.3 collective-permute-start.25
  73.4 1.5 %collective-permute-start.24 = (bf16[448,128]{1,0:T(8,128)(2,1)S(1)}, bf16[448,128]{1,0:T(8,128)(2,1)S(1)}, u32[]{:S(2)}, u32[]{:S(2)}) collective-permute-start(bf16[448,128]{1,0:T(8,128)(2,1)S(1)} %add_convert_fusion.refs_0_), channel_id=1, source_target_pairs={{0,4},{1,5},{2,6},{3,7},{4,0},{5,1},{6,2},{7,3},{8,12},{9,13},{10,... | collective-permute-start | bytes 344072 | tf_op jit(solution)/shard_map/ppermute | solution.py:426
  74.9 0.8 collective-permute-done.20
  75.7 1.0 %collective-permute-start.23 = (bf16[224,128]{1,0:T(8,128)(2,1)S(1)}, bf16[224,128]{1,0:T(8,128)(2,1)S(1)}, u32[]{:S(2)}, u32[]{:S(2)}) collective-permute-start(bf16[224,128]{1,0:T(8,128)(2,1)S(1)} %add_convert_fusion.1.refs_0_), channel_id=1, source_target_pairs={{0,12},{1,13},{2,14},{3,15},{4,8},{5,9},{6,10},{7,11},{8,4},{9,5},... | collective-permute-start | bytes 172040 | tf_op jit(solution)/shard_map/ppermute | solution.py:426
  76.7 1.0 %collective-permute-start.22 = (bf16[224,128]{1,0:T(8,128)(2,1)S(1)}, bf16[224,128]{1,0:T(8,128)(2,1)S(1)}, u32[]{:S(2)}, u32[]{:S(2)}) collective-permute-start(bf16[224,128]{1,0:T(8,128)(2,1)S(1)} %add_convert_fusion.1.refs_0_), channel_id=1, source_target_pairs={{0,8},{1,9},{2,10},{3,11},{4,12},{5,13},{6,14},{7,15},{8,0},{9,1},... | collective-permute-start | bytes 172040 | tf_op jit(solution)/shard_map/ppermute | solution.py:426
  77.7 0.7 collective-permute-done.26.refs_3_
  78.4 0.9 %collective-permute-start.21 = (bf16[224,128]{1,0:T(8,128)(2,1)S(1)}, bf16[224,128]{1,0:T(8,128)(2,1)S(1)}, u32[]{:S(2)}, u32[]{:S(2)}) collective-permute-start(bf16[224,128]{1,0:T(8,128)(2,1)S(1)} %add_convert_fusion.1.refs_0_), channel_id=1, source_target_pairs={{0,4},{1,5},{2,6},{3,7},{4,0},{5,1},{6,2},{7,3},{8,12},{9,13},{10,... | collective-permute-start | bytes 172040 | tf_op jit(solution)/shard_map/ppermute | solution.py:426
  79.3 1.0 %collective-permute-done.25.refs_2_ = bf16[448,128]{1,0:T(8,128)(2,1)S(1)} collective-permute-done((bf16[448,128]{1,0:T(8,128)(2,1)S(1)}, bf16[448,128]{1,0:T(8,128)(2,1)S(1)}, u32[]{:S(2)}, u32[]{:S(2)}) %collective-permute-start.25) | collective-permute-done | bytes 114720 | tf_op jit(solution)/shard_map/ppermute | solution.py:426
  80.3 1.0 %coarse_last.1 = (f32[3,3,3,64,128]{4,3,2,1,0:T(8,128)}, f32[64,128]{1,0:T(8,128)}) custom-call(bf16[448,128]{1,0:T(8,128)(2,1)S(1)} %add_convert_fusion.refs_0_, bf16[448,128]{1,0:T(8,128)(2,1)S(1)} %collective-permute-done.24.refs_1_, bf16[448,128]{1,0:T(8,128)(2,1)S(1)} %collective-permute-done.25.refs_2_, ...), custom_call_target="tpu_custom_call" | custom-call | flops 1000000000 | tf_op jit(solution)/shard_map/coarse_last/pallas_call | solution.py:20
  81.3 0.3 collective-permute-done.22.refs_2_
  81.6 0.9 %collective-permute-done.21.refs_1_ = bf16[224,128]{1,0:T(8,128)(2,1)S(1)} collective-permute-done((bf16[224,128]{1,0:T(8,128)(2,1)S(1)}, bf16[224,128]{1,0:T(8,128)(2,1)S(1)}, u32[]{:S(2)}, u32[]{:S(2)}) %collective-permute-start.21) | collective-permute-done | bytes 57376 | tf_op jit(solution)/shard_map/ppermute | solution.py:426
  82.6 0.9 %fine_last.1 = (f32[3,3,3,32,128]{4,3,2,1,0:T(8,128)}, f32[1,32]{1,0:T(1,128)}, f32[1,64]{1,0:T(1,128)}) custom-call(bf16[224,128]{1,0:T(8,128)(2,1)S(1)} %add_convert_fusion.1.refs_0_, bf16[224,128]{1,0:T(8,128)(2,1)S(1)} %collective-permute-done.21.refs_1_, bf16[224,128]{1,0:T(8,128)(2,1)S(1)} %collective-permute-done.22.refs_2_, ...), custom_call_target="tpu_custom_call" | custom-call | flops 1000000000 | tf_op jit(solution)/shard_map/fine_last/pallas_call | solution.py:20
  (30 shorter events, 0.3 us)
Async XLA Ops:
  1.5 7.1 %collective-permute-start.1 = (bf16[8,32,128]{2,1,0:T(8,128)(2,1)S(1)}, bf16[8,32,128]{2,1,0:T(8,128)(2,1)S(1)}, u32[]{:S(2)}, u32[]{:S(2)}) collective-permute-start(bf16[8,32,128]{2,1,0:T(8,128)(2,1)S(1)} %get-tuple-element.138), channel_id=1, source_target_pairs={{1,2},{2,1},{5,6},{6,5},{9,10},{10,9},{13,14},{14,13},{17,18},{18,... | collective-permute-start | bytes 196616 | tf_op jit(solution)/shard_map/ppermute | solution.py:395
  2.2 6.4 %copy-start.1 = (bf16[8,16,32,128]{3,2,1,0:T(8,128)(2,1)S(1)}, bf16[8,16,32,128]{3,2,1,0:T(8,128)(2,1)}, u32[]{:S(2)}) copy-start(bf16[8,16,32,128]{3,2,1,0:T(8,128)(2,1)} %field.1) | copy-start | bytes 3145732
  2.2 6.4 %collective-permute-start = (bf16[8,32,128]{2,1,0:T(8,128)(2,1)S(1)}, bf16[8,32,128]{2,1,0:T(8,128)(2,1)S(1)}, u32[]{:S(2)}, u32[]{:S(2)}) collective-permute-start(bf16[8,32,128]{2,1,0:T(8,128)(2,1)S(1)} %get-tuple-element.139), channel_id=1, source_target_pairs={{0,1},{1,0},{2,3},{3,2},{4,5},{5,4},{6,7},{7,6},{8,9},{9,8},{10,11... | collective-permute-start | bytes 196616 | tf_op jit(solution)/shard_map/ppermute | solution.py:396
  6.6 1.2 %copy-start.2 = (bf16[8,16,32,128]{3,2,1,0:T(8,128)(2,1)S(1)}, bf16[8,16,32,128]{3,2,1,0:T(8,128)(2,1)}, u32[]{:S(2)}) copy-start(bf16[8,16,32,128]{3,2,1,0:T(8,128)(2,1)} %cot.3) | copy-start | bytes 3145732
  8.6 2.4 %copy-start.4 = (bf16[3,3,3,128,128]{4,3,2,1,0:T(8,128)(2,1)S(1)}, bf16[3,3,3,128,128]{4,3,2,1,0:T(8,128)(2,1)}, u32[]{:S(2)}) copy-start(bf16[3,3,3,128,128]{4,3,2,1,0:T(8,128)(2,1)} %w.3) | copy-start | bytes 2654212
  8.6 2.4 %copy-start.7 = (f32[128]{0:T(128)S(1)}, f32[128]{0:T(128)}, u32[]{:S(2)}) copy-start(f32[128]{0:T(128)} %param.10) | copy-start | bytes 1540
  8.8 9.5 %collective-permute-start.2 = (bf16[704,128]{1,0:T(8,128)(2,1)S(1)}, bf16[704,128]{1,0:T(8,128)(2,1)S(1)}, u32[]{:S(2)}, u32[]{:S(2)}) collective-permute-start(bf16[704,128]{1,0:T(8,128)(2,1)S(1)} %get-tuple-element.75), channel_id=1, source_target_pairs={{0,4},{4,0},{8,12},{12,8},{16,20},{20,16},{24,28},{28,24},{1,5},{5... | collective-permute-start | bytes 540680 | tf_op jit(solution)/shard_map/ppermute | solution.py:396
  10.4 11.5 %collective-permute-start.3 = (bf16[704,128]{1,0:T(8,128)(2,1)S(1)}, bf16[704,128]{1,0:T(8,128)(2,1)S(1)}, u32[]{:S(2)}, u32[]{:S(2)}) collective-permute-start(bf16[704,128]{1,0:T(8,128)(2,1)S(1)} %get-tuple-element.79), channel_id=1, source_target_pairs={{4,8},{8,4},{12,16},{16,12},{20,24},{24,20},{5,9},{9,5},{13,17},{1... | collective-permute-start | bytes 540680 | tf_op jit(solution)/shard_map/ppermute | solution.py:395
  19.3 4.2 %copy-start = (bf16[3,3,3,128,256]{4,3,2,1,0:T(8,128)(2,1)S(1)}, bf16[3,3,3,128,256]{4,3,2,1,0:T(8,128)(2,1)}, u32[]{:S(2)}) copy-start(bf16[3,3,3,128,256]{4,3,2,1,0:T(8,128)(2,1)} %w.5) | copy-start | bytes 5308420
  19.3 4.8 %collective-permute-start.4 = (bf16[2,8,16,128]{3,2,1,0:T(8,128)(2,1)S(1)}, bf16[2,8,16,128]{3,2,1,0:T(8,128)(2,1)S(1)}, u32[]{:S(2)}, u32[]{:S(2)}) collective-permute-start(bf16[2,8,16,128]{3,2,1,0:T(8,128)(2,1)S(1)} %get-tuple-element.83), channel_id=1, source_target_pairs={{0,4},{4,0},{8,12},{12,8},{16,20},{20,16},{24,28},{28,24},{1,5},{5... | collective-permute-start | bytes 196616 | tf_op jit(solution)/shard_map/ppermute | solution.py:396
  22.8 1.3 %collective-permute-start.5 = (bf16[2,8,16,128]{3,2,1,0:T(8,128)(2,1)S(1)}, bf16[2,8,16,128]{3,2,1,0:T(8,128)(2,1)S(1)}, u32[]{:S(2)}, u32[]{:S(2)}) collective-permute-start(bf16[2,8,16,128]{3,2,1,0:T(8,128)(2,1)S(1)} %get-tuple-element.85), channel_id=1, source_target_pairs={{4,8},{8,4},{12,16},{16,12},{20,24},{24,20},{5,9},{9,5},{13,17},{1... | collective-permute-start | bytes 196616 | tf_op jit(solution)/shard_map/ppermute | solution.py:395
  24.1 0.8 %copy-start.5 = (bf16[256,128]{1,0:T(8,128)(2,1)S(1)}, bf16[256,128]{1,0:T(8,128)(2,1)}, u32[]{:S(2)}) copy-start(bf16[256,128]{1,0:T(8,128)(2,1)} %wm.5) | copy-start | bytes 196612
  24.1 0.8 %copy-start.6 = (f32[256]{0:T(256)S(1)}, f32[256]{0:T(256)}, u32[]{:S(2)}) copy-start(f32[256]{0:T(256)} %param.12) | copy-start | bytes 3076
  24.2 2.3 %collective-permute-start.6 = (bf16[22,16,128]{2,1,0:T(8,128)(2,1)S(1)}, bf16[22,16,128]{2,1,0:T(8,128)(2,1)S(1)}, u32[]{:S(2)}, u32[]{:S(2)}) collective-permute-start(bf16[22,16,128]{2,1,0:T(8,128)(2,1)S(1)} %get-tuple-element.86), channel_id=1, source_target_pairs={{0,1},{1,0},{2,3},{3,2},{4,5},{5,4},{6,7},{7,6},{8,9},{9,8},{10,11... | collective-permute-start | bytes 270344 | tf_op jit(solution)/shard_map/ppermute | solution.py:396
  24.2 2.3 %collective-permute-start.7 = (bf16[22,16,128]{2,1,0:T(8,128)(2,1)S(1)}, bf16[22,16,128]{2,1,0:T(8,128)(2,1)S(1)}, u32[]{:S(2)}, u32[]{:S(2)}) collective-permute-start(bf16[22,16,128]{2,1,0:T(8,128)(2,1)S(1)} %get-tuple-element.87), channel_id=1, source_target_pairs={{1,2},{2,1},{5,6},{6,5},{9,10},{10,9},{13,14},{14,13},{17,18},{18,... | collective-permute-start | bytes 270344 | tf_op jit(solution)/shard_map/ppermute | solution.py:395
  29.9 6.2 %collective-permute-start.8 = (bf16[2,1792,128]{2,1,0:T(8,128)(2,1)S(1)}, bf16[2,1792,128]{2,1,0:T(8,128)(2,1)S(1)}, u32[]{:S(2)}, u32[]{:S(2)}) collective-permute-start(bf16[2,1792,128]{2,1,0:T(8,128)(2,1)S(1)} %get-tuple-element.92), channel_id=1, source_target_pairs={{0,1},{1,0},{2,3},{3,2},{4,5},{5,4},{6,7},{7,6},{8,9},{9,8},{10,11... | collective-permute-start | bytes 2752520 | tf_op jit(solution)/shard_map/ppermute | solution.py:426
  36.2 7.7 %copy-start.3 = (bf16[8,16,32,128]{3,2,1,0:T(8,128)(2,1)S(1)}, bf16[8,16,32,128]{3,2,1,0:T(8,128)(2,1)}, u32[]{:S(2)}) copy-start(bf16[8,16,32,128]{3,2,1,0:T(8,128)(2,1)} %cot.3) | copy-start | bytes 3145732
  36.4 16.3 %collective-permute-start.9 = (bf16[1,896,128]{2,1,0:T(8,128)(2,1)S(1)}, bf16[1,896,128]{2,1,0:T(8,128)(2,1)S(1)}, u32[]{:S(2)}, u32[]{:S(2)}) collective-permute-start(bf16[1,896,128]{2,1,0:T(8,128)(2,1)S(1)} %get-tuple-element.102), channel_id=1, source_target_pairs={{0,6},{1,7},{2,4},{3,5},{4,2},{5,3},{6,0},{7,1},{8,14},{9,15},{10,... | collective-permute-start | bytes 688136 | tf_op jit(solution)/shard_map/ppermute | solution.py:426
  42.8 10.8 %collective-permute-start.10 = (bf16[1,896,128]{2,1,0:T(8,128)(2,1)S(1)}, bf16[1,896,128]{2,1,0:T(8,128)(2,1)S(1)}, u32[]{:S(2)}, u32[]{:S(2)}) collective-permute-start(bf16[1,896,128]{2,1,0:T(8,128)(2,1)S(1)} %get-tuple-element.103), channel_id=1, source_target_pairs={{0,2},{1,3},{2,0},{3,1},{4,6},{5,7},{6,4},{7,5},{8,10},{9,11},{10,... | collective-permute-start | bytes 688136 | tf_op jit(solution)/shard_map/ppermute | solution.py:426
  43.9 9.8 %collective-permute-start.11 = (bf16[1,896,128]{2,1,0:T(8,128)(2,1)S(1)}, bf16[1,896,128]{2,1,0:T(8,128)(2,1)S(1)}, u32[]{:S(2)}, u32[]{:S(2)}) collective-permute-start(bf16[1,896,128]{2,1,0:T(8,128)(2,1)S(1)} %get-tuple-element.104), channel_id=1, source_target_pairs={{0,4},{1,5},{2,6},{3,7},{4,0},{5,1},{6,2},{7,3},{8,12},{9,13},{10,... | collective-permute-start | bytes 688136 | tf_op jit(solution)/shard_map/ppermute | solution.py:426
  52.1 1.7 %collective-permute-start.13 = (bf16[896,128]{1,0:T(8,128)(2,1)S(1)}, bf16[896,128]{1,0:T(8,128)(2,1)S(1)}, u32[]{:S(2)}, u32[]{:S(2)}) collective-permute-start(bf16[896,128]{1,0:T(8,128)(2,1)S(1)} %get-tuple-element.140), channel_id=1, source_target_pairs={{0,1},{1,0},{2,3},{3,2},{4,5},{5,4},{6,7},{7,6},{8,9},{9,8},{10,11... | collective-permute-start | bytes 688136 | tf_op jit(solution)/shard_map/ppermute | solution.py:426
  52.2 1.8 %collective-permute-start.12 = (bf16[896,128]{1,0:T(8,128)(2,1)S(1)}, bf16[896,128]{1,0:T(8,128)(2,1)S(1)}, u32[]{:S(2)}, u32[]{:S(2)}) collective-permute-start(bf16[896,128]{1,0:T(8,128)(2,1)S(1)} %get-tuple-element.141), channel_id=1, source_target_pairs={{0,1},{1,0},{2,3},{3,2},{4,5},{5,4},{6,7},{7,6},{8,9},{9,8},{10,11... | collective-permute-start | bytes 688136 | tf_op jit(solution)/shard_map/ppermute | solution.py:426
  54.0 7.2 %collective-permute-start.14 = (bf16[448,128]{1,0:T(8,128)(2,1)S(1)}, bf16[448,128]{1,0:T(8,128)(2,1)S(1)}, u32[]{:S(2)}, u32[]{:S(2)}) collective-permute-start(bf16[448,128]{1,0:T(8,128)(2,1)S(1)} %get-tuple-element.114), channel_id=1, source_target_pairs={{0,8},{1,9},{2,10},{3,11},{4,12},{5,13},{6,14},{7,15},{8,0},{9,1},... | collective-permute-start | bytes 344072 | tf_op jit(solution)/shard_map/ppermute | solution.py:426
  57.6 7.0 %collective-permute-start.16 = (bf16[1,448,128]{2,1,0:T(8,128)(2,1)S(1)}, bf16[1,448,128]{2,1,0:T(8,128)(2,1)S(1)}, u32[]{:S(2)}, u32[]{:S(2)}) collective-permute-start(bf16[1,448,128]{2,1,0:T(8,128)(2,1)S(1)} %get-tuple-element.119), channel_id=1, source_target_pairs={{0,6},{1,7},{2,4},{3,5},{4,2},{5,3},{6,0},{7,1},{8,14},{9,15},{10,... | collective-permute-start | bytes 344072 | tf_op jit(solution)/shard_map/ppermute | solution.py:426
  58.3 7.1 %collective-permute-start.17 = (bf16[1,448,128]{2,1,0:T(8,128)(2,1)S(1)}, bf16[1,448,128]{2,1,0:T(8,128)(2,1)S(1)}, u32[]{:S(2)}, u32[]{:S(2)}) collective-permute-start(bf16[1,448,128]{2,1,0:T(8,128)(2,1)S(1)} %get-tuple-element.120), channel_id=1, source_target_pairs={{0,2},{1,3},{2,0},{3,1},{4,6},{5,7},{6,4},{7,5},{8,10},{9,11},{10,... | collective-permute-start | bytes 344072 | tf_op jit(solution)/shard_map/ppermute | solution.py:426
  59.6 6.0 %collective-permute-start.18 = (bf16[1,448,128]{2,1,0:T(8,128)(2,1)S(1)}, bf16[1,448,128]{2,1,0:T(8,128)(2,1)S(1)}, u32[]{:S(2)}, u32[]{:S(2)}) collective-permute-start(bf16[1,448,128]{2,1,0:T(8,128)(2,1)S(1)} %get-tuple-element.121), channel_id=1, source_target_pairs={{0,4},{1,5},{2,6},{3,7},{4,0},{5,1},{6,2},{7,3},{8,12},{9,13},{10,... | collective-permute-start | bytes 344072 | tf_op jit(solution)/shard_map/ppermute | solution.py:426
  61.2 8.7 %collective-permute-start.15 = (bf16[448,128]{1,0:T(8,128)(2,1)S(1)}, bf16[448,128]{1,0:T(8,128)(2,1)S(1)}, u32[]{:S(2)}, u32[]{:S(2)}) collective-permute-start(bf16[448,128]{1,0:T(8,128)(2,1)S(1)} %coarse_sum.1), channel_id=1, source_target_pairs={{0,16},{1,17},{2,18},{3,19},{4,20},{5,21},{6,22},{7,23},{8,24},{9,... | collective-permute-start | bytes 344072 | tf_op jit(solution)/shard_map/ppermute | solution.py:426
  65.7 4.2 %collective-permute-start.19 = (bf16[224,128]{1,0:T(8,128)(2,1)S(1)}, bf16[224,128]{1,0:T(8,128)(2,1)S(1)}, u32[]{:S(2)}, u32[]{:S(2)}) collective-permute-start(bf16[224,128]{1,0:T(8,128)(2,1)S(1)} %get-tuple-element.123), channel_id=1, source_target_pairs={{0,8},{1,9},{2,10},{3,11},{4,12},{5,13},{6,14},{7,15},{8,0},{9,1},... | collective-permute-start | bytes 172040 | tf_op jit(solution)/shard_map/ppermute | solution.py:426
  69.9 5.7 %collective-permute-start.20 = (bf16[224,128]{1,0:T(8,128)(2,1)S(1)}, bf16[224,128]{1,0:T(8,128)(2,1)S(1)}, u32[]{:S(2)}, u32[]{:S(2)}) collective-permute-start(bf16[224,128]{1,0:T(8,128)(2,1)S(1)} %fine_sum.1), channel_id=1, source_target_pairs={{0,16},{1,17},{2,18},{3,19},{4,20},{5,21},{6,22},{7,23},{8,24},{9,... | collective-permute-start | bytes 172040 | tf_op jit(solution)/shard_map/ppermute | solution.py:426
  71.3 7.1 %collective-permute-start.26 = (bf16[448,128]{1,0:T(8,128)(2,1)S(1)}, bf16[448,128]{1,0:T(8,128)(2,1)S(1)}, u32[]{:S(2)}, u32[]{:S(2)}) collective-permute-start(bf16[448,128]{1,0:T(8,128)(2,1)S(1)} %add_convert_fusion.refs_0_), channel_id=1, source_target_pairs={{0,12},{1,13},{2,14},{3,15},{4,8},{5,9},{6,10},{7,11},{8,4},{9,5},... | collective-permute-start | bytes 344072 | tf_op jit(solution)/shard_map/ppermute | solution.py:426
  73.1 7.2 %collective-permute-start.25 = (bf16[448,128]{1,0:T(8,128)(2,1)S(1)}, bf16[448,128]{1,0:T(8,128)(2,1)S(1)}, u32[]{:S(2)}, u32[]{:S(2)}) collective-permute-start(bf16[448,128]{1,0:T(8,128)(2,1)S(1)} %add_convert_fusion.refs_0_), channel_id=1, source_target_pairs={{0,8},{1,9},{2,10},{3,11},{4,12},{5,13},{6,14},{7,15},{8,0},{9,1},... | collective-permute-start | bytes 344072 | tf_op jit(solution)/shard_map/ppermute | solution.py:426
  73.4 6.9 %collective-permute-start.24 = (bf16[448,128]{1,0:T(8,128)(2,1)S(1)}, bf16[448,128]{1,0:T(8,128)(2,1)S(1)}, u32[]{:S(2)}, u32[]{:S(2)}) collective-permute-start(bf16[448,128]{1,0:T(8,128)(2,1)S(1)} %add_convert_fusion.refs_0_), channel_id=1, source_target_pairs={{0,4},{1,5},{2,6},{3,7},{4,0},{5,1},{6,2},{7,3},{8,12},{9,13},{10,... | collective-permute-start | bytes 344072 | tf_op jit(solution)/shard_map/ppermute | solution.py:426
  75.7 5.7 %collective-permute-start.23 = (bf16[224,128]{1,0:T(8,128)(2,1)S(1)}, bf16[224,128]{1,0:T(8,128)(2,1)S(1)}, u32[]{:S(2)}, u32[]{:S(2)}) collective-permute-start(bf16[224,128]{1,0:T(8,128)(2,1)S(1)} %add_convert_fusion.1.refs_0_), channel_id=1, source_target_pairs={{0,12},{1,13},{2,14},{3,15},{4,8},{5,9},{6,10},{7,11},{8,4},{9,5},... | collective-permute-start | bytes 172040 | tf_op jit(solution)/shard_map/ppermute | solution.py:426
  76.7 4.9 %collective-permute-start.22 = (bf16[224,128]{1,0:T(8,128)(2,1)S(1)}, bf16[224,128]{1,0:T(8,128)(2,1)S(1)}, u32[]{:S(2)}, u32[]{:S(2)}) collective-permute-start(bf16[224,128]{1,0:T(8,128)(2,1)S(1)} %add_convert_fusion.1.refs_0_), channel_id=1, source_target_pairs={{0,8},{1,9},{2,10},{3,11},{4,12},{5,13},{6,14},{7,15},{8,0},{9,1},... | collective-permute-start | bytes 172040 | tf_op jit(solution)/shard_map/ppermute | solution.py:426
  78.4 4.2 %collective-permute-start.21 = (bf16[224,128]{1,0:T(8,128)(2,1)S(1)}, bf16[224,128]{1,0:T(8,128)(2,1)S(1)}, u32[]{:S(2)}, u32[]{:S(2)}) collective-permute-start(bf16[224,128]{1,0:T(8,128)(2,1)S(1)} %add_convert_fusion.1.refs_0_), channel_id=1, source_target_pairs={{0,4},{1,5},{2,6},{3,7},{4,0},{5,1},{6,2},{7,3},{8,12},{9,13},{10,... | collective-permute-start | bytes 172040 | tf_op jit(solution)/shard_map/ppermute | solution.py:426

commit v7 on v6

--- a/solution.py
+++ b/solution.py
@@ -243,7 +243,7 @@
 
 def coarse_body(
     n, pool_in, pool_a, pool_b, ra, rb, ua, ub, xa, xb, pg, wb, bias, wm, slope_mid, coarse_mid,
-    slope, coarse, keep, send, cbias, qpad, gpad, st, rhs, acc, ct,
+    slope, coarse, keep, send, cbias, qpad, gpad, st, acc, ct,
 ):
     cx, cy, cz, c = pg.shape
     c2 = wm.shape[0]
@@ -284,13 +284,17 @@
     st[pl.ds(0, c2), :] = shift_rows(wide_mid, -1, cz).astype(BF16).T
     st[pl.ds(c2, c2), :] = mid.T
     st[pl.ds(2 * c2, c2), :] = shift_rows(wide_mid, 1, cz).astype(BF16).T
-    for i in range(3):
-        for j in range(3):
-            rhs[:, pl.ds((3 * i + j) * c, c)] = qpad[
-                1 + i : 1 + i + cx, 1 + j : 1 + j + cy
-            ].reshape(cells, c)
-    rhs[:, pl.ds(9 * c, c)] = jnp.ones((cells, c), BF16)
-    acc[...] = jnp.dot(st[...], rhs[...], preferred_element_type=F32).astype(BF16)
+
+    def window(t):
+        if t == 9:
+            return jnp.ones((cells, c), BF16)
+        i, j = 1 + t // 3, 1 + t % 3
+        return qpad[i : i + cx, j : j + cy].reshape(cells, c)
+
+    for t in range(0, 10, 2):
+        acc[:, pl.ds(t * c, 2 * c)] = jnp.dot(
+            st[...], jnp.concatenate([window(t), window(t + 1)], axis=1), preferred_element_type=F32
+        ).astype(BF16)
     ct[...] = jnp.dot(
         coarse[...].reshape(cells, c2).T, pg[...].reshape(cells, c), preferred_element_type=F32
     ).astype(BF16)
@@ -306,7 +310,7 @@
     spread(keep, send, n, 28, piece)
 
 
-def back_body(n, slope, w, cot, ds, ds_a, ds_b, own, xa, xb, cbias, keep, send, up, st, rhs, acc):
+def back_body(n, slope, w, cot, ds, ds_a, ds_b, own, xa, xb, cbias, keep, send, up, st, acc):
     bx, by, bz, c = cot.shape
     cx, cy, cz = bx // 2, by // 2, bz // 2
     c2 = slope.shape[3]
@@ -340,23 +344,24 @@
         st[pl.ds(0, c), pl.ds(x * rows, rows)] = shift_rows(wide, -1, bz).astype(BF16).T
         st[pl.ds(c, c), pl.ds(x * rows, rows)] = fs.T
         st[pl.ds(2 * c, c), pl.ds(x * rows, rows)] = shift_rows(wide, 1, bz).astype(BF16).T
-    voxels = bx * rows
+
+    def window(t, x):
+        if t == 9:
+            return jnp.ones((rows, c), BF16)
+        x, j = x + t // 3 - 1, t % 3
+        plane = own[x, j : j + by] if 0 <= x < bx else halo[int(x == bx)][j : j + by]
+        return plane.reshape(rows, c)
+
     for t in range(0, 10, 2):
-        for h in (0, 1):
-            i, j = (t + h) // 3, (t + h) % 3
-            if t + h == 9:
-                rhs[:, pl.ds(h * c, c)] = jnp.ones((voxels, c), BF16)
-            else:
-                first, past = max(i - 1, 0), min(i - 1 + bx, bx)
-                at = (first - i + 1) * rows
-                size = (past - first) * rows
-                rhs[pl.ds(at, size), pl.ds(h * c, c)] = own[first:past, j : j + by].reshape(size, c)
-                if i != 1:
-                    edge = halo[i // 2][j : j + by].reshape(rows, c)
-                    rhs[pl.ds(0 if i == 0 else size, rows), pl.ds(h * c, c)] = edge
-        acc[:, pl.ds(t * c, 2 * c)] = jnp.dot(
-            st[...], rhs[...], preferred_element_type=F32
-        ).astype(BF16)
+        total = jnp.zeros((3 * c, 2 * c), F32)
+        for first in range(0, bx, 1):
+            pairs = [jnp.concatenate([window(t, x), window(t + 1, x)], axis=1) for x in range(first, first + 1)]
+            total = total + jnp.dot(
+                st[:, pl.ds(first * rows, 1 * rows)],
+                jnp.concatenate(pairs, axis=0),
+                preferred_element_type=F32,
+            )
+        acc[:, pl.ds(t * c, 2 * c)] = total.astype(BF16)
     per, cper = c // n, c2 // n
     lane = lax.broadcasted_iota(jnp.int32, (per, c), 1)
 
@@ -636,6 +641,7 @@
     qa, qb = call(turn2_body, "turn2", (*pooled, pg, pxa, pxb, xa, xb), [face, face])
     pya, pyb = swap_faces(qa, qb, "sub")
     bias2 = coarse_bias.reshape(1, c2)
+    pyb, pya = lax.optimization_barrier((pyb, pya))
     slope_mid, coarse_mid = call(
         mid_body,
         "mid",
@@ -661,7 +667,6 @@
             pltpu.VMEM((cx + 4, cy + 4, cz, c), BF16),
             pltpu.VMEM((cx + 2, cy + 2, cz, c), BF16),
             pltpu.VMEM((3 * c2, cells), BF16),
-            pltpu.VMEM((cells, 10 * c), BF16),
             pltpu.VMEM((3 * c2, 10 * c), BF16),
             pltpu.VMEM((c2, c), BF16),
         ],
@@ -690,7 +695,6 @@
         [
             pltpu.VMEM((cx * cy * bz, c), F32),
             pltpu.VMEM((3 * c, voxels), BF16),
-            pltpu.VMEM((voxels, 2 * c), BF16),
             pltpu.VMEM((3 * c, 10 * c), BF16),
         ],
         10,

time: 83.7 us -> 83.2 us (level)
  waiting for transfers between devices: 14 us -> 15.5 us
  starting transfers between devices: 41.2 us -> 40.1 us
  Pallas kernels: 25.1 us -> 24.2 us
    ppermute x19, starting transfers between devices: 30 us -> 26.3 us  [partners(): return lax.ppermute(value, ('grp', 'sub'), pairs)]
    ppermute x4, starting transfers between devices: 8.56 us -> 11.1 us  [swap_faces(): return (lax.ppermute(first, axis, one), got)]
    ppermute x19, waiting for transfers between devices: 11.4 us -> 12.9 us  [partners(): return lax.ppermute(value, ('grp', 'sub'), pairs)]
    pallas_call x19, Pallas kernels: 25.1 us -> 24.2 us  [call(): pl.pallas_call(body, name=name, out_shape=[jax.ShapeDtypeStruct(s, t) for...]
  transfers between devices with their start and end apart: 27 -> 27, of which waited for: 14 -> 12; matrix products, arithmetic and copies ran while one was open for 0% -> 0% of each run, Pallas kernels for 24% -> 24%
where the time goes in v7:
time: 83.2 us; the launch traced here: 82.9 us
  starting transfers between devices  40.1 us (48%)
  Pallas kernels  24.2 us (29%)
  waiting for transfers between devices  15.5 us (19%)
  local copies, waits for them, and re-layouts  1.29 us (2%)
  other arithmetic  0.99 us (1%)
  between operations  0.89 us (1%)
    ppermute x19, starting transfers between devices, partners(): return lax.ppermute(value, ('grp', 'sub'), pairs)  26.3 us
    pallas_call x19, Pallas kernels, call(): pl.pallas_call(body, name=name, out_shape=[jax.ShapeDtypeStruct(s, t) for...  24.2 us
    ppermute x19, waiting for transfers between devices, partners(): return lax.ppermute(value, ('grp', 'sub'), pairs)  12.9 us
    ppermute x4, starting transfers between devices, swap_faces(): return (lax.ppermute(first, axis, one), got)  11.1 us
    ppermute x4, starting transfers between devices, swap_faces(): got = lax.ppermute(second, axis, two)  2.66 us
    ppermute x4, waiting for transfers between devices, swap_faces(): return (lax.ppermute(first, axis, one), got)  2.57 us
  transfers between devices with their start and end apart: 27, of which 12 were waited for; matrix products, arithmetic and copies ran while one was open for 0% of the time, Pallas kernels for 24%

profile of v7, /device:TPU:0, one launch (start us, length us, event | category | flops | bytes accessed | tf_op | source)
XLA Modules:
  0.0 82.9 jit_solution(12891280373225784377)
XLA Ops:
  0.6 0.9 %fusion.1 = (bf16[8,32,128]{2,1,0:T(8,128)(2,1)S(1)}, bf16[8,32,128]{2,1,0:T(8,128)(2,1)S(1)}) fusion(pred[]{:T(512)S(6)} %eq.3, bf16[8,16,32,128]{3,2,1,0:T(8,128)(2,1)} %field.1), kind=kLoop, calls=%fused_computation.8 | loop fusion | flops 65536 | bytes 262145 | tf_op jit(solution)/shard_map/jit(_where)/select_n | solution.py:589
  1.5 0.7 collective-permute-start.1
  2.2 0.0 copy-start.1
  2.2 4.4 %collective-permute-start = (bf16[8,32,128]{2,1,0:T(8,128)(2,1)S(1)}, bf16[8,32,128]{2,1,0:T(8,128)(2,1)S(1)}, u32[]{:S(2)}, u32[]{:S(2)}) collective-permute-start(bf16[8,32,128]{2,1,0:T(8,128)(2,1)S(1)} %get-tuple-element.143), channel_id=1, source_target_pairs={{0,1},{1,0},{2,3},{3,2},{4,5},{5,4},{6,7},{7,6},{8,9},{9,8},{10,11... | collective-permute-start | bytes 196616 | tf_op jit(solution)/shard_map/ppermute | solution.py:401
  6.6 1.2 %copy-done.2 = bf16[8,16,32,128]{3,2,1,0:T(8,128)(2,1)S(1)} copy-done((bf16[8,16,32,128]{3,2,1,0:T(8,128)(2,1)S(1)}, bf16[8,16,32,128]{3,2,1,0:T(8,128)(2,1)}, u32[]{:S(2)}) %copy-start.2) | copy-done | bytes 1048600
  7.8 0.8 cubes.1
  8.6 0.0 collective-permute-done.1.yb
  8.6 0.0 copy-start.4
  8.6 0.0 copy-start.7
  8.7 0.2 turn.1
  8.8 1.6 %collective-permute-start.2 = (bf16[704,128]{1,0:T(8,128)(2,1)S(1)}, bf16[704,128]{1,0:T(8,128)(2,1)S(1)}, u32[]{:S(2)}, u32[]{:S(2)}) collective-permute-start(bf16[704,128]{1,0:T(8,128)(2,1)S(1)} %get-tuple-element.77), channel_id=1, source_target_pairs={{0,4},{4,0},{8,12},{12,8},{16,20},{20,16},{24,28},{28,24},{1,5},{5... | collective-permute-start | bytes 540680 | tf_op jit(solution)/shard_map/ppermute | solution.py:401
  10.4 0.7 collective-permute-start.3
  11.1 5.1 %inner.1 = (bf16[6,16,32,128]{3,2,1,0:T(8,128)(2,1)S(1)}, f32[6,16,32,128]{3,2,1,0:T(8,128)S(1)}, bf16[2,8,16,128]{3,2,1,0:T(8,128)(2,1)S(1)}, bf16[1152,384]{1,0:T(8,128)(2,1)S(1)}) custom-call(bf16[8,18,32,128]{3,2,1,0:T(8,128)(2,1)S(1)} %get-tuple-element.75.own, bf16[3,3,3,128,128]{4,3,2,1,0:T(8,128)(2,1)S(1)} %copy-done.4, f32[1,128]{1,0:T(1,128)S(1)} %bitcast.46), custom_call_target="tpu_custom_call" | custom-call | flops 6000000000 | tf_op jit(solution)/shard_map/inner/pallas_call | solution.py:20
  16.2 2.1 %collective-permute-done.2.face.xa = bf16[704,128]{1,0:T(8,128)(2,1)S(1)} collective-permute-done((bf16[704,128]{1,0:T(8,128)(2,1)S(1)}, bf16[704,128]{1,0:T(8,128)(2,1)S(1)}, u32[]{:S(2)}, u32[]{:S(2)}) %collective-permute-start.2) | collective-permute-done | bytes 180256 | tf_op jit(solution)/shard_map/ppermute | solution.py:401
  18.3 1.0 %edge.2 = (bf16[16,32,128]{2,1,0:T(8,128)(2,1)S(1)}, f32[16,32,128]{2,1,0:T(8,128)S(1)}, bf16[8,16,128]{2,1,0:T(8,128)(2,1)S(1)}, bf16[2,8,16,128]{3,2,1,0:T(8,128)(2,1)S(1)}) custom-call(bf16[8,18,32,128]{3,2,1,0:T(8,128)(2,1)S(1)} %get-tuple-element.75.own, bf16[704,128]{1,0:T(8,128)(2,1)S(1)} %collective-permute-done.2.face.xa, ...), custom_call_target="tpu_custom_call" | custom-call | flops 1000000000 | tf_op jit(solution)/shard_map/edge/pallas_call | solution.py:20
  19.3 0.0 copy-start
  19.3 2.5 %collective-permute-start.4 = (bf16[2,8,16,128]{3,2,1,0:T(8,128)(2,1)S(1)}, bf16[2,8,16,128]{3,2,1,0:T(8,128)(2,1)S(1)}, u32[]{:S(2)}, u32[]{:S(2)}) collective-permute-start(bf16[2,8,16,128]{3,2,1,0:T(8,128)(2,1)S(1)} %get-tuple-element.85), channel_id=1, source_target_pairs={{0,4},{4,0},{8,12},{12,8},{16,20},{20,16},{24,28},{28,24},{1,5},{5... | collective-permute-start | bytes 196616 | tf_op jit(solution)/shard_map/ppermute | solution.py:401
  21.9 0.0 collective-permute-done.3.face.xb
  21.9 1.0 %edge.3 = (bf16[16,32,128]{2,1,0:T(8,128)(2,1)S(1)}, f32[16,32,128]{2,1,0:T(8,128)S(1)}, bf16[8,16,128]{2,1,0:T(8,128)(2,1)S(1)}, bf16[2,8,16,128]{3,2,1,0:T(8,128)(2,1)S(1)}) custom-call(bf16[8,18,32,128]{3,2,1,0:T(8,128)(2,1)S(1)} %get-tuple-element.75.own, bf16[704,128]{1,0:T(8,128)(2,1)S(1)} %collective-permute-done.3.face.xb, ...), custom_call_target="tpu_custom_call" | custom-call | flops 1000000000 | tf_op jit(solution)/shard_map/edge/pallas_call | solution.py:20
  22.8 0.7 collective-permute-start.5
  23.5 0.1 taps.1.wb
  23.6 0.5 collective-permute-done.4.ra
  24.2 0.7 collective-permute-start.6
  24.8 2.6 %collective-permute-start.7 = (bf16[22,16,128]{2,1,0:T(8,128)(2,1)S(1)}, bf16[22,16,128]{2,1,0:T(8,128)(2,1)S(1)}, u32[]{:S(2)}, u32[]{:S(2)}) collective-permute-start(bf16[22,16,128]{2,1,0:T(8,128)(2,1)S(1)} %get-tuple-element.89), channel_id=1, source_target_pairs={{0,1},{1,0},{2,3},{3,2},{4,5},{5,4},{6,7},{7,6},{8,9},{9,8},{10,11... | collective-permute-start | bytes 270344 | tf_op jit(solution)/shard_map/ppermute | solution.py:401
  27.4 1.5 %mid.1 = (bf16[6,6,16,256]{3,2,1,0:T(8,128)(2,1)S(1)}, bf16[4,6,16,256]{3,2,1,0:T(8,128)(2,1)S(1)}) custom-call(bf16[2,8,16,128]{3,2,1,0:T(8,128)(2,1)S(1)} %get-tuple-element.79.pool_in, bf16[8,16,128]{2,1,0:T(8,128)(2,1)S(1)} %get-tuple-element.83.pool_a, bf16[8,16,128]{2,1,0:T(8,128)(2,1)S(1)} %get-tuple-element.84.pool_b, ...), custom_call_target="tpu_custom_call" | custom-call | flops 2000000000 | tf_op jit(solution)/shard_map/mid/pallas_call | solution.py:20
  28.9 0.0 collective-permute-done.6.ub
  29.0 3.3 %coarse.1 = (bf16[6,10,16,256]{3,2,1,0:T(8,128)(2,1)S(1)}, bf16[4,8,16,256]{3,2,1,0:T(8,128)(2,1)S(1)}, bf16[2,1792,128]{2,1,0:T(8,128)(2,1)S(1)}, bf16[2,1792,128]{2,1,0:T(8,128)(2,1)S(1)}, bf16[256,128]{1,0:T(8,128)(2,1)S(1)}) custom-call(bf16[2,8,16,128]{3,2,1,0:T(8,128)(2,1)S(1)} %get-tuple-element.79.pool_in, ...), custom_call_target="tpu_custom_call" | custom-call | flops 6000000000 | tf_op jit(solution)/shard_map/coarse/pallas_call | solution.py:20
  32.3 0.7 collective-permute-start.8
  32.9 1.3 %merge.1 = bf16[8,16,32,128]{3,2,1,0:T(8,128)(2,1)} custom-call(bf16[6,16,32,128]{3,2,1,0:T(8,128)(2,1)S(1)} %get-tuple-element.76.hid_in.hidden, bf16[16,32,128]{2,1,0:T(8,128)(2,1)S(1)} %get-tuple-element.80.hid_a, bf16[16,32,128]{2,1,0:T(8,128)(2,1)S(1)} %get-tuple-element.82.hid_b, bf16[4,8,16,256]{3,2,1,0:T(8,128)(2,1)S(1)} %get-tuple-element.95.coarse, ...), custom_call_target="tpu_custom_call" | custom-call | flops 2000000000 | tf_op jit(solution)/shard_map/merge/pallas_call | solution.py:20
  34.3 0.8 collective-permute-done.8
  35.0 0.2 split.2
  35.3 7.4 %collective-permute-start.9 = (bf16[1,896,128]{2,1,0:T(8,128)(2,1)S(1)}, bf16[1,896,128]{2,1,0:T(8,128)(2,1)S(1)}, u32[]{:S(2)}, u32[]{:S(2)}) collective-permute-start(bf16[1,896,128]{2,1,0:T(8,128)(2,1)S(1)} %get-tuple-element.106), channel_id=1, source_target_pairs={{0,6},{1,7},{2,4},{3,5},{4,2},{5,3},{6,0},{7,1},{8,14},{9,15},{10,... | collective-permute-start | bytes 688136 | tf_op jit(solution)/shard_map/ppermute | solution.py:431
  42.7 0.1 collective-permute-start.10
  42.7 0.6 collective-permute-start.11
  43.3 7.4 %back.1 = (bf16[2,896,128]{2,1,0:T(8,128)(2,1)S(1)}, bf16[2,896,128]{2,1,0:T(8,128)(2,1)S(1)}) custom-call(bf16[6,10,16,256]{3,2,1,0:T(8,128)(2,1)S(1)} %get-tuple-element.111.slope, bf16[3,3,3,128,256]{4,3,2,1,0:T(8,128)(2,1)S(1)} %copy-done, bf16[8,16,32,128]{3,2,1,0:T(8,128)(2,1)S(1)} %copy-done.3, f32[6,16,32,128]{3,2,1,0:T(8,128)S(1)} %get-tuple-element.112.ds, ...), custom_call_target="tpu_custom_call" | custom-call | flops 10000000000 | tf_op jit(solution)/shard_map/back/pallas_call | solution.py:20
  50.8 0.1 collective-permute-start.13
  50.9 0.5 collective-permute-start.12
  51.4 2.1 %collective-permute-done.10 = bf16[1,896,128]{2,1,0:T(8,128)(2,1)S(1)} collective-permute-done((bf16[1,896,128]{2,1,0:T(8,128)(2,1)S(1)}, bf16[1,896,128]{2,1,0:T(8,128)(2,1)S(1)}, u32[]{:S(2)}, u32[]{:S(2)}) %collective-permute-start.10) | collective-permute-done | bytes 229408 | tf_op jit(solution)/shard_map/ppermute | solution.py:431
  53.5 0.1 coarse_half.1
  53.6 3.3 %collective-permute-start.14 = (bf16[448,128]{1,0:T(8,128)(2,1)S(1)}, bf16[448,128]{1,0:T(8,128)(2,1)S(1)}, u32[]{:S(2)}, u32[]{:S(2)}) collective-permute-start(bf16[448,128]{1,0:T(8,128)(2,1)S(1)} %get-tuple-element.118), channel_id=1, source_target_pairs={{0,8},{1,9},{2,10},{3,11},{4,12},{5,13},{6,14},{7,15},{8,0},{9,1},... | collective-permute-start | bytes 344072 | tf_op jit(solution)/shard_map/ppermute | solution.py:431
  57.0 0.1 split.3
  57.1 1.0 %collective-permute-start.16 = (bf16[1,448,128]{2,1,0:T(8,128)(2,1)S(1)}, bf16[1,448,128]{2,1,0:T(8,128)(2,1)S(1)}, u32[]{:S(2)}, u32[]{:S(2)}) collective-permute-start(bf16[1,448,128]{2,1,0:T(8,128)(2,1)S(1)} %get-tuple-element.123), channel_id=1, source_target_pairs={{0,6},{1,7},{2,4},{3,5},{4,2},{5,3},{6,0},{7,1},{8,14},{9,15},{10,... | collective-permute-start | bytes 344072 | tf_op jit(solution)/shard_map/ppermute | solution.py:431
  58.1 0.7 collective-permute-start.17
  58.9 1.8 %collective-permute-start.18 = (bf16[1,448,128]{2,1,0:T(8,128)(2,1)S(1)}, bf16[1,448,128]{2,1,0:T(8,128)(2,1)S(1)}, u32[]{:S(2)}, u32[]{:S(2)}) collective-permute-start(bf16[1,448,128]{2,1,0:T(8,128)(2,1)S(1)} %get-tuple-element.125), channel_id=1, source_target_pairs={{0,4},{1,5},{2,6},{3,7},{4,0},{5,1},{6,2},{7,3},{8,12},{9,13},{10,... | collective-permute-start | bytes 344072 | tf_op jit(solution)/shard_map/ppermute | solution.py:431
  60.7 2.1 %collective-permute-start.15 = (bf16[448,128]{1,0:T(8,128)(2,1)S(1)}, bf16[448,128]{1,0:T(8,128)(2,1)S(1)}, u32[]{:S(2)}, u32[]{:S(2)}) collective-permute-start(bf16[448,128]{1,0:T(8,128)(2,1)S(1)} %coarse_sum.1), channel_id=1, source_target_pairs={{0,16},{1,17},{2,18},{3,19},{4,20},{5,21},{6,22},{7,23},{8,24},{9,... | collective-permute-start | bytes 344072 | tf_op jit(solution)/shard_map/ppermute | solution.py:431
  62.8 1.0 %collective-permute-done.16 = bf16[1,448,128]{2,1,0:T(8,128)(2,1)S(1)} collective-permute-done((bf16[1,448,128]{2,1,0:T(8,128)(2,1)S(1)}, bf16[1,448,128]{2,1,0:T(8,128)(2,1)S(1)}, u32[]{:S(2)}, u32[]{:S(2)}) %collective-permute-start.16) | collective-permute-done | bytes 114720 | tf_op jit(solution)/shard_map/ppermute | solution.py:431
  63.9 1.1 %collective-permute-done.17 = bf16[1,448,128]{2,1,0:T(8,128)(2,1)S(1)} collective-permute-done((bf16[1,448,128]{2,1,0:T(8,128)(2,1)S(1)}, bf16[1,448,128]{2,1,0:T(8,128)(2,1)S(1)}, u32[]{:S(2)}, u32[]{:S(2)}) %collective-permute-start.17) | collective-permute-done | bytes 114720 | tf_op jit(solution)/shard_map/ppermute | solution.py:431
  65.0 0.1 fine_half.1
  65.0 0.4 collective-permute-start.19
  65.4 3.9 %collective-permute-done.19.refs_1_ = bf16[224,128]{1,0:T(8,128)(2,1)S(1)} collective-permute-done((bf16[224,128]{1,0:T(8,128)(2,1)S(1)}, bf16[224,128]{1,0:T(8,128)(2,1)S(1)}, u32[]{:S(2)}, u32[]{:S(2)}) %collective-permute-start.19) | collective-permute-done | bytes 57376 | tf_op jit(solution)/shard_map/ppermute | solution.py:431
  69.3 1.4 %collective-permute-start.20 = (bf16[224,128]{1,0:T(8,128)(2,1)S(1)}, bf16[224,128]{1,0:T(8,128)(2,1)S(1)}, u32[]{:S(2)}, u32[]{:S(2)}) collective-permute-start(bf16[224,128]{1,0:T(8,128)(2,1)S(1)} %fine_sum.1), channel_id=1, source_target_pairs={{0,16},{1,17},{2,18},{3,19},{4,20},{5,21},{6,22},{7,23},{8,24},{9,... | collective-permute-start | bytes 172040 | tf_op jit(solution)/shard_map/ppermute | solution.py:431
  70.7 1.8 %collective-permute-start.26 = (bf16[448,128]{1,0:T(8,128)(2,1)S(1)}, bf16[448,128]{1,0:T(8,128)(2,1)S(1)}, u32[]{:S(2)}, u32[]{:S(2)}) collective-permute-start(bf16[448,128]{1,0:T(8,128)(2,1)S(1)} %add_convert_fusion.refs_0_), channel_id=1, source_target_pairs={{0,12},{1,13},{2,14},{3,15},{4,8},{5,9},{6,10},{7,11},{8,4},{9,5},... | collective-permute-start | bytes 344072 | tf_op jit(solution)/shard_map/ppermute | solution.py:431
  72.5 0.3 collective-permute-start.25
  72.8 1.5 %collective-permute-start.24 = (bf16[448,128]{1,0:T(8,128)(2,1)S(1)}, bf16[448,128]{1,0:T(8,128)(2,1)S(1)}, u32[]{:S(2)}, u32[]{:S(2)}) collective-permute-start(bf16[448,128]{1,0:T(8,128)(2,1)S(1)} %add_convert_fusion.refs_0_), channel_id=1, source_target_pairs={{0,4},{1,5},{2,6},{3,7},{4,0},{5,1},{6,2},{7,3},{8,12},{9,13},{10,... | collective-permute-start | bytes 344072 | tf_op jit(solution)/shard_map/ppermute | solution.py:431
  74.3 0.7 collective-permute-done.20
  75.0 1.1 %collective-permute-start.23 = (bf16[224,128]{1,0:T(8,128)(2,1)S(1)}, bf16[224,128]{1,0:T(8,128)(2,1)S(1)}, u32[]{:S(2)}, u32[]{:S(2)}) collective-permute-start(bf16[224,128]{1,0:T(8,128)(2,1)S(1)} %add_convert_fusion.1.refs_0_), channel_id=1, source_target_pairs={{0,12},{1,13},{2,14},{3,15},{4,8},{5,9},{6,10},{7,11},{8,4},{9,5},... | collective-permute-start | bytes 172040 | tf_op jit(solution)/shard_map/ppermute | solution.py:431
  76.1 0.8 collective-permute-start.22
  76.9 1.0 %collective-permute-done.26.refs_3_ = bf16[448,128]{1,0:T(8,128)(2,1)S(1)} collective-permute-done((bf16[448,128]{1,0:T(8,128)(2,1)S(1)}, bf16[448,128]{1,0:T(8,128)(2,1)S(1)}, u32[]{:S(2)}, u32[]{:S(2)}) %collective-permute-start.26) | collective-permute-done | bytes 114720 | tf_op jit(solution)/shard_map/ppermute | solution.py:431
  77.9 0.9 %collective-permute-start.21 = (bf16[224,128]{1,0:T(8,128)(2,1)S(1)}, bf16[224,128]{1,0:T(8,128)(2,1)S(1)}, u32[]{:S(2)}, u32[]{:S(2)}) collective-permute-start(bf16[224,128]{1,0:T(8,128)(2,1)S(1)} %add_convert_fusion.1.refs_0_), channel_id=1, source_target_pairs={{0,4},{1,5},{2,6},{3,7},{4,0},{5,1},{6,2},{7,3},{8,12},{9,13},{10,... | collective-permute-start | bytes 172040 | tf_op jit(solution)/shard_map/ppermute | solution.py:431
  78.8 0.5 collective-permute-done.25.refs_2_
  79.3 0.2 collective-permute-done.24.refs_1_
  79.5 1.0 %coarse_last.1 = (f32[3,3,3,64,128]{4,3,2,1,0:T(8,128)}, f32[64,128]{1,0:T(8,128)}) custom-call(bf16[448,128]{1,0:T(8,128)(2,1)S(1)} %add_convert_fusion.refs_0_, bf16[448,128]{1,0:T(8,128)(2,1)S(1)} %collective-permute-done.24.refs_1_, bf16[448,128]{1,0:T(8,128)(2,1)S(1)} %collective-permute-done.25.refs_2_, ...), custom_call_target="tpu_custom_call" | custom-call | flops 1000000000 | tf_op jit(solution)/shard_map/coarse_last/pallas_call | solution.py:20
  80.6 1.5 %collective-permute-done.21.refs_1_ = bf16[224,128]{1,0:T(8,128)(2,1)S(1)} collective-permute-done((bf16[224,128]{1,0:T(8,128)(2,1)S(1)}, bf16[224,128]{1,0:T(8,128)(2,1)S(1)}, u32[]{:S(2)}, u32[]{:S(2)}) %collective-permute-start.21) | collective-permute-done | bytes 57376 | tf_op jit(solution)/shard_map/ppermute | solution.py:431
  82.1 0.9 %fine_last.1 = (f32[3,3,3,32,128]{4,3,2,1,0:T(8,128)}, f32[1,32]{1,0:T(1,128)}, f32[1,64]{1,0:T(1,128)}) custom-call(bf16[224,128]{1,0:T(8,128)(2,1)S(1)} %add_convert_fusion.1.refs_0_, bf16[224,128]{1,0:T(8,128)(2,1)S(1)} %collective-permute-done.21.refs_1_, bf16[224,128]{1,0:T(8,128)(2,1)S(1)} %collective-permute-done.22.refs_2_, ...), custom_call_target="tpu_custom_call" | custom-call | flops 1000000000 | tf_op jit(solution)/shard_map/fine_last/pallas_call | solution.py:20
  (30 shorter events, 0.3 us)
Async XLA Ops:
  1.5 7.1 %collective-permute-start.1 = (bf16[8,32,128]{2,1,0:T(8,128)(2,1)S(1)}, bf16[8,32,128]{2,1,0:T(8,128)(2,1)S(1)}, u32[]{:S(2)}, u32[]{:S(2)}) collective-permute-start(bf16[8,32,128]{2,1,0:T(8,128)(2,1)S(1)} %get-tuple-element.142), channel_id=1, source_target_pairs={{1,2},{2,1},{5,6},{6,5},{9,10},{10,9},{13,14},{14,13},{17,18},{18,... | collective-permute-start | bytes 196616 | tf_op jit(solution)/shard_map/ppermute | solution.py:400
  2.2 6.4 %copy-start.1 = (bf16[8,16,32,128]{3,2,1,0:T(8,128)(2,1)S(1)}, bf16[8,16,32,128]{3,2,1,0:T(8,128)(2,1)}, u32[]{:S(2)}) copy-start(bf16[8,16,32,128]{3,2,1,0:T(8,128)(2,1)} %field.1) | copy-start | bytes 3145732
  2.2 6.4 %collective-permute-start = (bf16[8,32,128]{2,1,0:T(8,128)(2,1)S(1)}, bf16[8,32,128]{2,1,0:T(8,128)(2,1)S(1)}, u32[]{:S(2)}, u32[]{:S(2)}) collective-permute-start(bf16[8,32,128]{2,1,0:T(8,128)(2,1)S(1)} %get-tuple-element.143), channel_id=1, source_target_pairs={{0,1},{1,0},{2,3},{3,2},{4,5},{5,4},{6,7},{7,6},{8,9},{9,8},{10,11... | collective-permute-start | bytes 196616 | tf_op jit(solution)/shard_map/ppermute | solution.py:401
  6.6 1.2 %copy-start.2 = (bf16[8,16,32,128]{3,2,1,0:T(8,128)(2,1)S(1)}, bf16[8,16,32,128]{3,2,1,0:T(8,128)(2,1)}, u32[]{:S(2)}) copy-start(bf16[8,16,32,128]{3,2,1,0:T(8,128)(2,1)} %cot.3) | copy-start | bytes 3145732
  8.6 2.4 %copy-start.4 = (bf16[3,3,3,128,128]{4,3,2,1,0:T(8,128)(2,1)S(1)}, bf16[3,3,3,128,128]{4,3,2,1,0:T(8,128)(2,1)}, u32[]{:S(2)}) copy-start(bf16[3,3,3,128,128]{4,3,2,1,0:T(8,128)(2,1)} %w.3) | copy-start | bytes 2654212
  8.6 2.4 %copy-start.7 = (f32[128]{0:T(128)S(1)}, f32[128]{0:T(128)}, u32[]{:S(2)}) copy-start(f32[128]{0:T(128)} %param.10) | copy-start | bytes 1540
  8.8 9.5 %collective-permute-start.2 = (bf16[704,128]{1,0:T(8,128)(2,1)S(1)}, bf16[704,128]{1,0:T(8,128)(2,1)S(1)}, u32[]{:S(2)}, u32[]{:S(2)}) collective-permute-start(bf16[704,128]{1,0:T(8,128)(2,1)S(1)} %get-tuple-element.77), channel_id=1, source_target_pairs={{0,4},{4,0},{8,12},{12,8},{16,20},{20,16},{24,28},{28,24},{1,5},{5... | collective-permute-start | bytes 540680 | tf_op jit(solution)/shard_map/ppermute | solution.py:401
  10.4 11.5 %collective-permute-start.3 = (bf16[704,128]{1,0:T(8,128)(2,1)S(1)}, bf16[704,128]{1,0:T(8,128)(2,1)S(1)}, u32[]{:S(2)}, u32[]{:S(2)}) collective-permute-start(bf16[704,128]{1,0:T(8,128)(2,1)S(1)} %get-tuple-element.81), channel_id=1, source_target_pairs={{4,8},{8,4},{12,16},{16,12},{20,24},{24,20},{5,9},{9,5},{13,17},{1... | collective-permute-start | bytes 540680 | tf_op jit(solution)/shard_map/ppermute | solution.py:400
  19.3 4.2 %copy-start = (bf16[3,3,3,128,256]{4,3,2,1,0:T(8,128)(2,1)S(1)}, bf16[3,3,3,128,256]{4,3,2,1,0:T(8,128)(2,1)}, u32[]{:S(2)}) copy-start(bf16[3,3,3,128,256]{4,3,2,1,0:T(8,128)(2,1)} %w.5) | copy-start | bytes 5308420
  19.3 4.8 %collective-permute-start.4 = (bf16[2,8,16,128]{3,2,1,0:T(8,128)(2,1)S(1)}, bf16[2,8,16,128]{3,2,1,0:T(8,128)(2,1)S(1)}, u32[]{:S(2)}, u32[]{:S(2)}) collective-permute-start(bf16[2,8,16,128]{3,2,1,0:T(8,128)(2,1)S(1)} %get-tuple-element.85), channel_id=1, source_target_pairs={{0,4},{4,0},{8,12},{12,8},{16,20},{20,16},{24,28},{28,24},{1,5},{5... | collective-permute-start | bytes 196616 | tf_op jit(solution)/shard_map/ppermute | solution.py:401
  22.8 1.3 %collective-permute-start.5 = (bf16[2,8,16,128]{3,2,1,0:T(8,128)(2,1)S(1)}, bf16[2,8,16,128]{3,2,1,0:T(8,128)(2,1)S(1)}, u32[]{:S(2)}, u32[]{:S(2)}) collective-permute-start(bf16[2,8,16,128]{3,2,1,0:T(8,128)(2,1)S(1)} %get-tuple-element.87), channel_id=1, source_target_pairs={{4,8},{8,4},{12,16},{16,12},{20,24},{24,20},{5,9},{9,5},{13,17},{1... | collective-permute-start | bytes 196616 | tf_op jit(solution)/shard_map/ppermute | solution.py:400
  24.1 3.3 %copy-start.5 = (bf16[256,128]{1,0:T(8,128)(2,1)S(1)}, bf16[256,128]{1,0:T(8,128)(2,1)}, u32[]{:S(2)}) copy-start(bf16[256,128]{1,0:T(8,128)(2,1)} %wm.5) | copy-start | bytes 196612
  24.1 3.3 %copy-start.6 = (f32[256]{0:T(256)S(1)}, f32[256]{0:T(256)}, u32[]{:S(2)}) copy-start(f32[256]{0:T(256)} %param.12) | copy-start | bytes 3076
  24.2 4.8 %collective-permute-start.6 = (bf16[22,16,128]{2,1,0:T(8,128)(2,1)S(1)}, bf16[22,16,128]{2,1,0:T(8,128)(2,1)S(1)}, u32[]{:S(2)}, u32[]{:S(2)}) collective-permute-start(bf16[22,16,128]{2,1,0:T(8,128)(2,1)S(1)} %get-tuple-element.88), channel_id=1, source_target_pairs={{1,2},{2,1},{5,6},{6,5},{9,10},{10,9},{13,14},{14,13},{17,18},{18,... | collective-permute-start | bytes 270344 | tf_op jit(solution)/shard_map/ppermute | solution.py:400
  24.8 4.1 %collective-permute-start.7 = (bf16[22,16,128]{2,1,0:T(8,128)(2,1)S(1)}, bf16[22,16,128]{2,1,0:T(8,128)(2,1)S(1)}, u32[]{:S(2)}, u32[]{:S(2)}) collective-permute-start(bf16[22,16,128]{2,1,0:T(8,128)(2,1)S(1)} %get-tuple-element.89), channel_id=1, source_target_pairs={{0,1},{1,0},{2,3},{3,2},{4,5},{5,4},{6,7},{7,6},{8,9},{9,8},{10,11... | collective-permute-start | bytes 270344 | tf_op jit(solution)/shard_map/ppermute | solution.py:401
  32.3 2.8 %collective-permute-start.8 = (bf16[2,1792,128]{2,1,0:T(8,128)(2,1)S(1)}, bf16[2,1792,128]{2,1,0:T(8,128)(2,1)S(1)}, u32[]{:S(2)}, u32[]{:S(2)}) collective-permute-start(bf16[2,1792,128]{2,1,0:T(8,128)(2,1)S(1)} %get-tuple-element.96), channel_id=1, source_target_pairs={{0,1},{1,0},{2,3},{3,2},{4,5},{5,4},{6,7},{7,6},{8,9},{9,8},{10,11... | collective-permute-start | bytes 2752520 | tf_op jit(solution)/shard_map/ppermute | solution.py:431
  35.0 8.3 %copy-start.3 = (bf16[8,16,32,128]{3,2,1,0:T(8,128)(2,1)S(1)}, bf16[8,16,32,128]{3,2,1,0:T(8,128)(2,1)}, u32[]{:S(2)}) copy-start(bf16[8,16,32,128]{3,2,1,0:T(8,128)(2,1)} %cot.3) | copy-start | bytes 3145732
  35.3 16.1 %collective-permute-start.9 = (bf16[1,896,128]{2,1,0:T(8,128)(2,1)S(1)}, bf16[1,896,128]{2,1,0:T(8,128)(2,1)S(1)}, u32[]{:S(2)}, u32[]{:S(2)}) collective-permute-start(bf16[1,896,128]{2,1,0:T(8,128)(2,1)S(1)} %get-tuple-element.106), channel_id=1, source_target_pairs={{0,6},{1,7},{2,4},{3,5},{4,2},{5,3},{6,0},{7,1},{8,14},{9,15},{10,... | collective-permute-start | bytes 688136 | tf_op jit(solution)/shard_map/ppermute | solution.py:431
  42.7 10.8 %collective-permute-start.10 = (bf16[1,896,128]{2,1,0:T(8,128)(2,1)S(1)}, bf16[1,896,128]{2,1,0:T(8,128)(2,1)S(1)}, u32[]{:S(2)}, u32[]{:S(2)}) collective-permute-start(bf16[1,896,128]{2,1,0:T(8,128)(2,1)S(1)} %get-tuple-element.107), channel_id=1, source_target_pairs={{0,2},{1,3},{2,0},{3,1},{4,6},{5,7},{6,4},{7,5},{8,10},{9,11},{10,... | collective-permute-start | bytes 688136 | tf_op jit(solution)/shard_map/ppermute | solution.py:431
  42.7 10.8 %collective-permute-start.11 = (bf16[1,896,128]{2,1,0:T(8,128)(2,1)S(1)}, bf16[1,896,128]{2,1,0:T(8,128)(2,1)S(1)}, u32[]{:S(2)}, u32[]{:S(2)}) collective-permute-start(bf16[1,896,128]{2,1,0:T(8,128)(2,1)S(1)} %get-tuple-element.108), channel_id=1, source_target_pairs={{0,4},{1,5},{2,6},{3,7},{4,0},{5,1},{6,2},{7,3},{8,12},{9,13},{10,... | collective-permute-start | bytes 688136 | tf_op jit(solution)/shard_map/ppermute | solution.py:431
  50.8 2.8 %collective-permute-start.13 = (bf16[896,128]{1,0:T(8,128)(2,1)S(1)}, bf16[896,128]{1,0:T(8,128)(2,1)S(1)}, u32[]{:S(2)}, u32[]{:S(2)}) collective-permute-start(bf16[896,128]{1,0:T(8,128)(2,1)S(1)} %get-tuple-element.144), channel_id=1, source_target_pairs={{0,1},{1,0},{2,3},{3,2},{4,5},{5,4},{6,7},{7,6},{8,9},{9,8},{10,11... | collective-permute-start | bytes 688136 | tf_op jit(solution)/shard_map/ppermute | solution.py:431
  50.9 2.8 %collective-permute-start.12 = (bf16[896,128]{1,0:T(8,128)(2,1)S(1)}, bf16[896,128]{1,0:T(8,128)(2,1)S(1)}, u32[]{:S(2)}, u32[]{:S(2)}) collective-permute-start(bf16[896,128]{1,0:T(8,128)(2,1)S(1)} %get-tuple-element.145), channel_id=1, source_target_pairs={{0,1},{1,0},{2,3},{3,2},{4,5},{5,4},{6,7},{7,6},{8,9},{9,8},{10,11... | collective-permute-start | bytes 688136 | tf_op jit(solution)/shard_map/ppermute | solution.py:431
  53.6 7.0 %collective-permute-start.14 = (bf16[448,128]{1,0:T(8,128)(2,1)S(1)}, bf16[448,128]{1,0:T(8,128)(2,1)S(1)}, u32[]{:S(2)}, u32[]{:S(2)}) collective-permute-start(bf16[448,128]{1,0:T(8,128)(2,1)S(1)} %get-tuple-element.118), channel_id=1, source_target_pairs={{0,8},{1,9},{2,10},{3,11},{4,12},{5,13},{6,14},{7,15},{8,0},{9,1},... | collective-permute-start | bytes 344072 | tf_op jit(solution)/shard_map/ppermute | solution.py:431
  57.1 6.8 %collective-permute-start.16 = (bf16[1,448,128]{2,1,0:T(8,128)(2,1)S(1)}, bf16[1,448,128]{2,1,0:T(8,128)(2,1)S(1)}, u32[]{:S(2)}, u32[]{:S(2)}) collective-permute-start(bf16[1,448,128]{2,1,0:T(8,128)(2,1)S(1)} %get-tuple-element.123), channel_id=1, source_target_pairs={{0,6},{1,7},{2,4},{3,5},{4,2},{5,3},{6,0},{7,1},{8,14},{9,15},{10,... | collective-permute-start | bytes 344072 | tf_op jit(solution)/shard_map/ppermute | solution.py:431
  58.1 6.8 %collective-permute-start.17 = (bf16[1,448,128]{2,1,0:T(8,128)(2,1)S(1)}, bf16[1,448,128]{2,1,0:T(8,128)(2,1)S(1)}, u32[]{:S(2)}, u32[]{:S(2)}) collective-permute-start(bf16[1,448,128]{2,1,0:T(8,128)(2,1)S(1)} %get-tuple-element.124), channel_id=1, source_target_pairs={{0,2},{1,3},{2,0},{3,1},{4,6},{5,7},{6,4},{7,5},{8,10},{9,11},{10,... | collective-permute-start | bytes 344072 | tf_op jit(solution)/shard_map/ppermute | solution.py:431
  58.9 6.1 %collective-permute-start.18 = (bf16[1,448,128]{2,1,0:T(8,128)(2,1)S(1)}, bf16[1,448,128]{2,1,0:T(8,128)(2,1)S(1)}, u32[]{:S(2)}, u32[]{:S(2)}) collective-permute-start(bf16[1,448,128]{2,1,0:T(8,128)(2,1)S(1)} %get-tuple-element.125), channel_id=1, source_target_pairs={{0,4},{1,5},{2,6},{3,7},{4,0},{5,1},{6,2},{7,3},{8,12},{9,13},{10,... | collective-permute-start | bytes 344072 | tf_op jit(solution)/shard_map/ppermute | solution.py:431
  60.7 8.6 %collective-permute-start.15 = (bf16[448,128]{1,0:T(8,128)(2,1)S(1)}, bf16[448,128]{1,0:T(8,128)(2,1)S(1)}, u32[]{:S(2)}, u32[]{:S(2)}) collective-permute-start(bf16[448,128]{1,0:T(8,128)(2,1)S(1)} %coarse_sum.1), channel_id=1, source_target_pairs={{0,16},{1,17},{2,18},{3,19},{4,20},{5,21},{6,22},{7,23},{8,24},{9,... | collective-permute-start | bytes 344072 | tf_op jit(solution)/shard_map/ppermute | solution.py:431
  65.0 4.2 %collective-permute-start.19 = (bf16[224,128]{1,0:T(8,128)(2,1)S(1)}, bf16[224,128]{1,0:T(8,128)(2,1)S(1)}, u32[]{:S(2)}, u32[]{:S(2)}) collective-permute-start(bf16[224,128]{1,0:T(8,128)(2,1)S(1)} %get-tuple-element.127), channel_id=1, source_target_pairs={{0,8},{1,9},{2,10},{3,11},{4,12},{5,13},{6,14},{7,15},{8,0},{9,1},... | collective-permute-start | bytes 172040 | tf_op jit(solution)/shard_map/ppermute | solution.py:431
  69.3 5.7 %collective-permute-start.20 = (bf16[224,128]{1,0:T(8,128)(2,1)S(1)}, bf16[224,128]{1,0:T(8,128)(2,1)S(1)}, u32[]{:S(2)}, u32[]{:S(2)}) collective-permute-start(bf16[224,128]{1,0:T(8,128)(2,1)S(1)} %fine_sum.1), channel_id=1, source_target_pairs={{0,16},{1,17},{2,18},{3,19},{4,20},{5,21},{6,22},{7,23},{8,24},{9,... | collective-permute-start | bytes 172040 | tf_op jit(solution)/shard_map/ppermute | solution.py:431
  70.7 7.1 %collective-permute-start.26 = (bf16[448,128]{1,0:T(8,128)(2,1)S(1)}, bf16[448,128]{1,0:T(8,128)(2,1)S(1)}, u32[]{:S(2)}, u32[]{:S(2)}) collective-permute-start(bf16[448,128]{1,0:T(8,128)(2,1)S(1)} %add_convert_fusion.refs_0_), channel_id=1, source_target_pairs={{0,12},{1,13},{2,14},{3,15},{4,8},{5,9},{6,10},{7,11},{8,4},{9,5},... | collective-permute-start | bytes 344072 | tf_op jit(solution)/shard_map/ppermute | solution.py:431
  72.5 6.8 %collective-permute-start.25 = (bf16[448,128]{1,0:T(8,128)(2,1)S(1)}, bf16[448,128]{1,0:T(8,128)(2,1)S(1)}, u32[]{:S(2)}, u32[]{:S(2)}) collective-permute-start(bf16[448,128]{1,0:T(8,128)(2,1)S(1)} %add_convert_fusion.refs_0_), channel_id=1, source_target_pairs={{0,8},{1,9},{2,10},{3,11},{4,12},{5,13},{6,14},{7,15},{8,0},{9,1},... | collective-permute-start | bytes 344072 | tf_op jit(solution)/shard_map/ppermute | solution.py:431
  72.8 6.7 %collective-permute-start.24 = (bf16[448,128]{1,0:T(8,128)(2,1)S(1)}, bf16[448,128]{1,0:T(8,128)(2,1)S(1)}, u32[]{:S(2)}, u32[]{:S(2)}) collective-permute-start(bf16[448,128]{1,0:T(8,128)(2,1)S(1)} %add_convert_fusion.refs_0_), channel_id=1, source_target_pairs={{0,4},{1,5},{2,6},{3,7},{4,0},{5,1},{6,2},{7,3},{8,12},{9,13},{10,... | collective-permute-start | bytes 344072 | tf_op jit(solution)/shard_map/ppermute | solution.py:431
  75.0 5.5 %collective-permute-start.23 = (bf16[224,128]{1,0:T(8,128)(2,1)S(1)}, bf16[224,128]{1,0:T(8,128)(2,1)S(1)}, u32[]{:S(2)}, u32[]{:S(2)}) collective-permute-start(bf16[224,128]{1,0:T(8,128)(2,1)S(1)} %add_convert_fusion.1.refs_0_), channel_id=1, source_target_pairs={{0,12},{1,13},{2,14},{3,15},{4,8},{5,9},{6,10},{7,11},{8,4},{9,5},... | collective-permute-start | bytes 172040 | tf_op jit(solution)/shard_map/ppermute | solution.py:431
  76.1 4.5 %collective-permute-start.22 = (bf16[224,128]{1,0:T(8,128)(2,1)S(1)}, bf16[224,128]{1,0:T(8,128)(2,1)S(1)}, u32[]{:S(2)}, u32[]{:S(2)}) collective-permute-start(bf16[224,128]{1,0:T(8,128)(2,1)S(1)} %add_convert_fusion.1.refs_0_), channel_id=1, source_target_pairs={{0,8},{1,9},{2,10},{3,11},{4,12},{5,13},{6,14},{7,15},{8,0},{9,1},... | collective-permute-start | bytes 172040 | tf_op jit(solution)/shard_map/ppermute | solution.py:431
  77.9 4.2 %collective-permute-start.21 = (bf16[224,128]{1,0:T(8,128)(2,1)S(1)}, bf16[224,128]{1,0:T(8,128)(2,1)S(1)}, u32[]{:S(2)}, u32[]{:S(2)}) collective-permute-start(bf16[224,128]{1,0:T(8,128)(2,1)S(1)} %add_convert_fusion.1.refs_0_), channel_id=1, source_target_pairs={{0,4},{1,5},{2,6},{3,7},{4,0},{5,1},{6,2},{7,3},{8,12},{9,13},{10,... | collective-permute-start | bytes 172040 | tf_op jit(solution)/shard_map/ppermute | solution.py:431

commit v8 on v7

--- a/solution.py
+++ b/solution.py
@@ -453,7 +453,7 @@
 
 
 def cross(own, over_sub, over_grp, over_both):
-    return [own, partners(over_both, 1, 2), partners(over_sub, 0, 2), partners(over_grp, 1, 0)]
+    return [own, partners(over_sub, 0, 2), partners(over_both, 1, 2), partners(over_grp, 1, 0)]
 
 
 def split_body(count, axis, bit, *refs):

time: 83.2 us -> 82.7 us (level)
  transfers between devices with their start and end apart: 27 -> 27, of which waited for: 12 -> 14; matrix products, arithmetic and copies ran while one was open for 0% -> 0% of each run, Pallas kernels for 24% -> 24%
where the time goes in v8:
time: 82.7 us; the launch traced here: 82.4 us
  starting transfers between devices  40.2 us (49%)
  Pallas kernels  24.2 us (29%)
  waiting for transfers between devices  14.9 us (18%)
  local copies, waits for them, and re-layouts  1.29 us (2%)
  other arithmetic  0.99 us (1%)
  between operations  0.89 us (1%)
    ppermute x19, starting transfers between devices, partners(): return lax.ppermute(value, ('grp', 'sub'), pairs)  26.5 us
    pallas_call x19, Pallas kernels, call(): pl.pallas_call(body, name=name, out_shape=[jax.ShapeDtypeStruct(s, t) for...  24.2 us
    ppermute x19, waiting for transfers between devices, partners(): return lax.ppermute(value, ('grp', 'sub'), pairs)  12.3 us
    ppermute x4, starting transfers between devices, swap_faces(): return (lax.ppermute(first, axis, one), got)  11.1 us
    ppermute x4, starting transfers between devices, swap_faces(): got = lax.ppermute(second, axis, two)  2.66 us
    ppermute x4, waiting for transfers between devices, swap_faces(): return (lax.ppermute(first, axis, one), got)  2.57 us
  transfers between devices with their start and end apart: 27, of which 14 were waited for; matrix products, arithmetic and copies ran while one was open for 0% of the time, Pallas kernels for 24%

profile of v8, /device:TPU:0, one launch (start us, length us, event | category | flops | bytes accessed | tf_op | source)
XLA Modules:
  0.0 82.4 jit_solution(4294094321678932227)
XLA Ops:
  0.6 0.9 %fusion.1 = (bf16[8,32,128]{2,1,0:T(8,128)(2,1)S(1)}, bf16[8,32,128]{2,1,0:T(8,128)(2,1)S(1)}) fusion(pred[]{:T(512)S(6)} %eq.3, bf16[8,16,32,128]{3,2,1,0:T(8,128)(2,1)} %field.1), kind=kLoop, calls=%fused_computation.8 | loop fusion | flops 65536 | bytes 262145 | tf_op jit(solution)/shard_map/jit(_where)/select_n | solution.py:589
  1.5 0.7 collective-permute-start.1
  2.2 0.0 copy-start.1
  2.2 4.4 %collective-permute-start = (bf16[8,32,128]{2,1,0:T(8,128)(2,1)S(1)}, bf16[8,32,128]{2,1,0:T(8,128)(2,1)S(1)}, u32[]{:S(2)}, u32[]{:S(2)}) collective-permute-start(bf16[8,32,128]{2,1,0:T(8,128)(2,1)S(1)} %get-tuple-element.143), channel_id=1, source_target_pairs={{0,1},{1,0},{2,3},{3,2},{4,5},{5,4},{6,7},{7,6},{8,9},{9,8},{10,11... | collective-permute-start | bytes 196616 | tf_op jit(solution)/shard_map/ppermute | solution.py:401
  6.6 1.2 %copy-done.2 = bf16[8,16,32,128]{3,2,1,0:T(8,128)(2,1)S(1)} copy-done((bf16[8,16,32,128]{3,2,1,0:T(8,128)(2,1)S(1)}, bf16[8,16,32,128]{3,2,1,0:T(8,128)(2,1)}, u32[]{:S(2)}) %copy-start.2) | copy-done | bytes 1048600
  7.8 0.8 cubes.1
  8.6 0.0 collective-permute-done.1.yb
  8.6 0.0 copy-start.4
  8.6 0.0 copy-start.7
  8.7 0.2 turn.1
  8.8 1.6 %collective-permute-start.2 = (bf16[704,128]{1,0:T(8,128)(2,1)S(1)}, bf16[704,128]{1,0:T(8,128)(2,1)S(1)}, u32[]{:S(2)}, u32[]{:S(2)}) collective-permute-start(bf16[704,128]{1,0:T(8,128)(2,1)S(1)} %get-tuple-element.77), channel_id=1, source_target_pairs={{0,4},{4,0},{8,12},{12,8},{16,20},{20,16},{24,28},{28,24},{1,5},{5... | collective-permute-start | bytes 540680 | tf_op jit(solution)/shard_map/ppermute | solution.py:401
  10.4 0.7 collective-permute-start.3
  11.1 5.1 %inner.1 = (bf16[6,16,32,128]{3,2,1,0:T(8,128)(2,1)S(1)}, f32[6,16,32,128]{3,2,1,0:T(8,128)S(1)}, bf16[2,8,16,128]{3,2,1,0:T(8,128)(2,1)S(1)}, bf16[1152,384]{1,0:T(8,128)(2,1)S(1)}) custom-call(bf16[8,18,32,128]{3,2,1,0:T(8,128)(2,1)S(1)} %get-tuple-element.75.own, bf16[3,3,3,128,128]{4,3,2,1,0:T(8,128)(2,1)S(1)} %copy-done.4, f32[1,128]{1,0:T(1,128)S(1)} %bitcast.46), custom_call_target="tpu_custom_call" | custom-call | flops 6000000000 | tf_op jit(solution)/shard_map/inner/pallas_call | solution.py:20
  16.2 2.1 %collective-permute-done.2.face.xa = bf16[704,128]{1,0:T(8,128)(2,1)S(1)} collective-permute-done((bf16[704,128]{1,0:T(8,128)(2,1)S(1)}, bf16[704,128]{1,0:T(8,128)(2,1)S(1)}, u32[]{:S(2)}, u32[]{:S(2)}) %collective-permute-start.2) | collective-permute-done | bytes 180256 | tf_op jit(solution)/shard_map/ppermute | solution.py:401
  18.3 1.0 %edge.2 = (bf16[16,32,128]{2,1,0:T(8,128)(2,1)S(1)}, f32[16,32,128]{2,1,0:T(8,128)S(1)}, bf16[8,16,128]{2,1,0:T(8,128)(2,1)S(1)}, bf16[2,8,16,128]{3,2,1,0:T(8,128)(2,1)S(1)}) custom-call(bf16[8,18,32,128]{3,2,1,0:T(8,128)(2,1)S(1)} %get-tuple-element.75.own, bf16[704,128]{1,0:T(8,128)(2,1)S(1)} %collective-permute-done.2.face.xa, ...), custom_call_target="tpu_custom_call" | custom-call | flops 1000000000 | tf_op jit(solution)/shard_map/edge/pallas_call | solution.py:20
  19.3 0.0 copy-start
  19.3 2.5 %collective-permute-start.4 = (bf16[2,8,16,128]{3,2,1,0:T(8,128)(2,1)S(1)}, bf16[2,8,16,128]{3,2,1,0:T(8,128)(2,1)S(1)}, u32[]{:S(2)}, u32[]{:S(2)}) collective-permute-start(bf16[2,8,16,128]{3,2,1,0:T(8,128)(2,1)S(1)} %get-tuple-element.85), channel_id=1, source_target_pairs={{0,4},{4,0},{8,12},{12,8},{16,20},{20,16},{24,28},{28,24},{1,5},{5... | collective-permute-start | bytes 196616 | tf_op jit(solution)/shard_map/ppermute | solution.py:401
  21.9 1.0 %edge.3 = (bf16[16,32,128]{2,1,0:T(8,128)(2,1)S(1)}, f32[16,32,128]{2,1,0:T(8,128)S(1)}, bf16[8,16,128]{2,1,0:T(8,128)(2,1)S(1)}, bf16[2,8,16,128]{3,2,1,0:T(8,128)(2,1)S(1)}) custom-call(bf16[8,18,32,128]{3,2,1,0:T(8,128)(2,1)S(1)} %get-tuple-element.75.own, bf16[704,128]{1,0:T(8,128)(2,1)S(1)} %collective-permute-done.3.face.xb, ...), custom_call_target="tpu_custom_call" | custom-call | flops 1000000000 | tf_op jit(solution)/shard_map/edge/pallas_call | solution.py:20
  22.8 0.7 collective-permute-start.5
  23.5 0.1 taps.1.wb
  23.6 0.5 collective-permute-done.4.ra
  24.2 0.7 collective-permute-start.6
  24.8 2.6 %collective-permute-start.7 = (bf16[22,16,128]{2,1,0:T(8,128)(2,1)S(1)}, bf16[22,16,128]{2,1,0:T(8,128)(2,1)S(1)}, u32[]{:S(2)}, u32[]{:S(2)}) collective-permute-start(bf16[22,16,128]{2,1,0:T(8,128)(2,1)S(1)} %get-tuple-element.89), channel_id=1, source_target_pairs={{0,1},{1,0},{2,3},{3,2},{4,5},{5,4},{6,7},{7,6},{8,9},{9,8},{10,11... | collective-permute-start | bytes 270344 | tf_op jit(solution)/shard_map/ppermute | solution.py:401
  27.4 1.5 %mid.1 = (bf16[6,6,16,256]{3,2,1,0:T(8,128)(2,1)S(1)}, bf16[4,6,16,256]{3,2,1,0:T(8,128)(2,1)S(1)}) custom-call(bf16[2,8,16,128]{3,2,1,0:T(8,128)(2,1)S(1)} %get-tuple-element.79.pool_in, bf16[8,16,128]{2,1,0:T(8,128)(2,1)S(1)} %get-tuple-element.83.pool_a, bf16[8,16,128]{2,1,0:T(8,128)(2,1)S(1)} %get-tuple-element.84.pool_b, ...), custom_call_target="tpu_custom_call" | custom-call | flops 2000000000 | tf_op jit(solution)/shard_map/mid/pallas_call | solution.py:20
  29.0 3.3 %coarse.1 = (bf16[6,10,16,256]{3,2,1,0:T(8,128)(2,1)S(1)}, bf16[4,8,16,256]{3,2,1,0:T(8,128)(2,1)S(1)}, bf16[2,1792,128]{2,1,0:T(8,128)(2,1)S(1)}, bf16[2,1792,128]{2,1,0:T(8,128)(2,1)S(1)}, bf16[256,128]{1,0:T(8,128)(2,1)S(1)}) custom-call(bf16[2,8,16,128]{3,2,1,0:T(8,128)(2,1)S(1)} %get-tuple-element.79.pool_in, ...), custom_call_target="tpu_custom_call" | custom-call | flops 6000000000 | tf_op jit(solution)/shard_map/coarse/pallas_call | solution.py:20
  32.3 0.7 collective-permute-start.8
  32.9 1.3 %merge.1 = bf16[8,16,32,128]{3,2,1,0:T(8,128)(2,1)} custom-call(bf16[6,16,32,128]{3,2,1,0:T(8,128)(2,1)S(1)} %get-tuple-element.76.hid_in.hidden, bf16[16,32,128]{2,1,0:T(8,128)(2,1)S(1)} %get-tuple-element.80.hid_a, bf16[16,32,128]{2,1,0:T(8,128)(2,1)S(1)} %get-tuple-element.82.hid_b, bf16[4,8,16,256]{3,2,1,0:T(8,128)(2,1)S(1)} %get-tuple-element.95.coarse, ...), custom_call_target="tpu_custom_call" | custom-call | flops 2000000000 | tf_op jit(solution)/shard_map/merge/pallas_call | solution.py:20
  34.3 0.8 collective-permute-done.8
  35.0 0.2 split.2
  35.3 2.0 %collective-permute-start.9 = (bf16[1,896,128]{2,1,0:T(8,128)(2,1)S(1)}, bf16[1,896,128]{2,1,0:T(8,128)(2,1)S(1)}, u32[]{:S(2)}, u32[]{:S(2)}) collective-permute-start(bf16[1,896,128]{2,1,0:T(8,128)(2,1)S(1)} %get-tuple-element.106), channel_id=1, source_target_pairs={{0,2},{1,3},{2,0},{3,1},{4,6},{5,7},{6,4},{7,5},{8,10},{9,11},{10,... | collective-permute-start | bytes 688136 | tf_op jit(solution)/shard_map/ppermute | solution.py:431
  37.3 5.4 %collective-permute-start.10 = (bf16[1,896,128]{2,1,0:T(8,128)(2,1)S(1)}, bf16[1,896,128]{2,1,0:T(8,128)(2,1)S(1)}, u32[]{:S(2)}, u32[]{:S(2)}) collective-permute-start(bf16[1,896,128]{2,1,0:T(8,128)(2,1)S(1)} %get-tuple-element.107), channel_id=1, source_target_pairs={{0,6},{1,7},{2,4},{3,5},{4,2},{5,3},{6,0},{7,1},{8,14},{9,15},{10,... | collective-permute-start | bytes 688136 | tf_op jit(solution)/shard_map/ppermute | solution.py:431
  42.7 0.5 collective-permute-start.11
  43.2 7.4 %back.1 = (bf16[2,896,128]{2,1,0:T(8,128)(2,1)S(1)}, bf16[2,896,128]{2,1,0:T(8,128)(2,1)S(1)}) custom-call(bf16[6,10,16,256]{3,2,1,0:T(8,128)(2,1)S(1)} %get-tuple-element.111.slope, bf16[3,3,3,128,256]{4,3,2,1,0:T(8,128)(2,1)S(1)} %copy-done, bf16[8,16,32,128]{3,2,1,0:T(8,128)(2,1)S(1)} %copy-done.3, f32[6,16,32,128]{3,2,1,0:T(8,128)S(1)} %get-tuple-element.112.ds, ...), custom_call_target="tpu_custom_call" | custom-call | flops 10000000000 | tf_op jit(solution)/shard_map/back/pallas_call | solution.py:20
  50.7 0.1 collective-permute-start.13
  50.8 0.5 collective-permute-start.12
  51.3 2.5 %collective-permute-done.11 = bf16[1,896,128]{2,1,0:T(8,128)(2,1)S(1)} collective-permute-done((bf16[1,896,128]{2,1,0:T(8,128)(2,1)S(1)}, bf16[1,896,128]{2,1,0:T(8,128)(2,1)S(1)}, u32[]{:S(2)}, u32[]{:S(2)}) %collective-permute-start.11) | collective-permute-done | bytes 229408 | tf_op jit(solution)/shard_map/ppermute | solution.py:431
  53.8 0.1 coarse_half.1
  53.9 3.1 %collective-permute-start.14 = (bf16[448,128]{1,0:T(8,128)(2,1)S(1)}, bf16[448,128]{1,0:T(8,128)(2,1)S(1)}, u32[]{:S(2)}, u32[]{:S(2)}) collective-permute-start(bf16[448,128]{1,0:T(8,128)(2,1)S(1)} %get-tuple-element.118), channel_id=1, source_target_pairs={{0,8},{1,9},{2,10},{3,11},{4,12},{5,13},{6,14},{7,15},{8,0},{9,1},... | collective-permute-start | bytes 344072 | tf_op jit(solution)/shard_map/ppermute | solution.py:431
  57.0 0.1 split.3
  57.2 1.7 %collective-permute-start.16 = (bf16[1,448,128]{2,1,0:T(8,128)(2,1)S(1)}, bf16[1,448,128]{2,1,0:T(8,128)(2,1)S(1)}, u32[]{:S(2)}, u32[]{:S(2)}) collective-permute-start(bf16[1,448,128]{2,1,0:T(8,128)(2,1)S(1)} %get-tuple-element.123), channel_id=1, source_target_pairs={{0,2},{1,3},{2,0},{3,1},{4,6},{5,7},{6,4},{7,5},{8,10},{9,11},{10,... | collective-permute-start | bytes 344072 | tf_op jit(solution)/shard_map/ppermute | solution.py:431
  58.9 0.3 collective-permute-start.17
  59.2 1.5 %collective-permute-start.18 = (bf16[1,448,128]{2,1,0:T(8,128)(2,1)S(1)}, bf16[1,448,128]{2,1,0:T(8,128)(2,1)S(1)}, u32[]{:S(2)}, u32[]{:S(2)}) collective-permute-start(bf16[1,448,128]{2,1,0:T(8,128)(2,1)S(1)} %get-tuple-element.125), channel_id=1, source_target_pairs={{0,4},{1,5},{2,6},{3,7},{4,0},{5,1},{6,2},{7,3},{8,12},{9,13},{10,... | collective-permute-start | bytes 344072 | tf_op jit(solution)/shard_map/ppermute | solution.py:431
  60.8 2.1 %collective-permute-start.15 = (bf16[448,128]{1,0:T(8,128)(2,1)S(1)}, bf16[448,128]{1,0:T(8,128)(2,1)S(1)}, u32[]{:S(2)}, u32[]{:S(2)}) collective-permute-start(bf16[448,128]{1,0:T(8,128)(2,1)S(1)} %coarse_sum.1), channel_id=1, source_target_pairs={{0,16},{1,17},{2,18},{3,19},{4,20},{5,21},{6,22},{7,23},{8,24},{9,... | collective-permute-start | bytes 344072 | tf_op jit(solution)/shard_map/ppermute | solution.py:431
  62.9 0.4 collective-permute-done.16
  63.3 1.3 %collective-permute-done.17 = bf16[1,448,128]{2,1,0:T(8,128)(2,1)S(1)} collective-permute-done((bf16[1,448,128]{2,1,0:T(8,128)(2,1)S(1)}, bf16[1,448,128]{2,1,0:T(8,128)(2,1)S(1)}, u32[]{:S(2)}, u32[]{:S(2)}) %collective-permute-start.17) | collective-permute-done | bytes 114720 | tf_op jit(solution)/shard_map/ppermute | solution.py:431
  64.6 0.4 collective-permute-done.18
  65.0 0.1 fine_half.1
  65.0 0.4 collective-permute-start.19
  65.4 3.9 %collective-permute-done.19.refs_1_ = bf16[224,128]{1,0:T(8,128)(2,1)S(1)} collective-permute-done((bf16[224,128]{1,0:T(8,128)(2,1)S(1)}, bf16[224,128]{1,0:T(8,128)(2,1)S(1)}, u32[]{:S(2)}, u32[]{:S(2)}) %collective-permute-start.19) | collective-permute-done | bytes 57376 | tf_op jit(solution)/shard_map/ppermute | solution.py:431
  69.3 1.4 %collective-permute-start.20 = (bf16[224,128]{1,0:T(8,128)(2,1)S(1)}, bf16[224,128]{1,0:T(8,128)(2,1)S(1)}, u32[]{:S(2)}, u32[]{:S(2)}) collective-permute-start(bf16[224,128]{1,0:T(8,128)(2,1)S(1)} %fine_sum.1), channel_id=1, source_target_pairs={{0,16},{1,17},{2,18},{3,19},{4,20},{5,21},{6,22},{7,23},{8,24},{9,... | collective-permute-start | bytes 172040 | tf_op jit(solution)/shard_map/ppermute | solution.py:431
  70.7 1.8 %collective-permute-start.26 = (bf16[448,128]{1,0:T(8,128)(2,1)S(1)}, bf16[448,128]{1,0:T(8,128)(2,1)S(1)}, u32[]{:S(2)}, u32[]{:S(2)}) collective-permute-start(bf16[448,128]{1,0:T(8,128)(2,1)S(1)} %add_convert_fusion.refs_0_), channel_id=1, source_target_pairs={{0,12},{1,13},{2,14},{3,15},{4,8},{5,9},{6,10},{7,11},{8,4},{9,5},... | collective-permute-start | bytes 344072 | tf_op jit(solution)/shard_map/ppermute | solution.py:431
  72.5 0.3 collective-permute-start.25
  72.7 1.5 %collective-permute-start.24 = (bf16[448,128]{1,0:T(8,128)(2,1)S(1)}, bf16[448,128]{1,0:T(8,128)(2,1)S(1)}, u32[]{:S(2)}, u32[]{:S(2)}) collective-permute-start(bf16[448,128]{1,0:T(8,128)(2,1)S(1)} %add_convert_fusion.refs_0_), channel_id=1, source_target_pairs={{0,4},{1,5},{2,6},{3,7},{4,0},{5,1},{6,2},{7,3},{8,12},{9,13},{10,... | collective-permute-start | bytes 344072 | tf_op jit(solution)/shard_map/ppermute | solution.py:431
  74.3 0.7 collective-permute-done.20
  75.0 1.1 %collective-permute-start.23 = (bf16[224,128]{1,0:T(8,128)(2,1)S(1)}, bf16[224,128]{1,0:T(8,128)(2,1)S(1)}, u32[]{:S(2)}, u32[]{:S(2)}) collective-permute-start(bf16[224,128]{1,0:T(8,128)(2,1)S(1)} %add_convert_fusion.1.refs_0_), channel_id=1, source_target_pairs={{0,12},{1,13},{2,14},{3,15},{4,8},{5,9},{6,10},{7,11},{8,4},{9,5},... | collective-permute-start | bytes 172040 | tf_op jit(solution)/shard_map/ppermute | solution.py:431
  76.1 0.9 %collective-permute-start.22 = (bf16[224,128]{1,0:T(8,128)(2,1)S(1)}, bf16[224,128]{1,0:T(8,128)(2,1)S(1)}, u32[]{:S(2)}, u32[]{:S(2)}) collective-permute-start(bf16[224,128]{1,0:T(8,128)(2,1)S(1)} %add_convert_fusion.1.refs_0_), channel_id=1, source_target_pairs={{0,8},{1,9},{2,10},{3,11},{4,12},{5,13},{6,14},{7,15},{8,0},{9,1},... | collective-permute-start | bytes 172040 | tf_op jit(solution)/shard_map/ppermute | solution.py:431
  77.0 0.4 collective-permute-done.26.refs_3_
  77.4 1.1 %collective-permute-start.21 = (bf16[224,128]{1,0:T(8,128)(2,1)S(1)}, bf16[224,128]{1,0:T(8,128)(2,1)S(1)}, u32[]{:S(2)}, u32[]{:S(2)}) collective-permute-start(bf16[224,128]{1,0:T(8,128)(2,1)S(1)} %add_convert_fusion.1.refs_0_), channel_id=1, source_target_pairs={{0,4},{1,5},{2,6},{3,7},{4,0},{5,1},{6,2},{7,3},{8,12},{9,13},{10,... | collective-permute-start | bytes 172040 | tf_op jit(solution)/shard_map/ppermute | solution.py:431
  78.5 0.1 collective-permute-done.24.refs_1_
  78.6 1.0 %coarse_last.1 = (f32[3,3,3,64,128]{4,3,2,1,0:T(8,128)}, f32[64,128]{1,0:T(8,128)}) custom-call(bf16[448,128]{1,0:T(8,128)(2,1)S(1)} %add_convert_fusion.refs_0_, bf16[448,128]{1,0:T(8,128)(2,1)S(1)} %collective-permute-done.24.refs_1_, bf16[448,128]{1,0:T(8,128)(2,1)S(1)} %collective-permute-done.25.refs_2_, ...), custom_call_target="tpu_custom_call" | custom-call | flops 1000000000 | tf_op jit(solution)/shard_map/coarse_last/pallas_call | solution.py:20
  79.6 0.5 collective-permute-done.23.refs_3_
  80.1 0.1 collective-permute-done.22.refs_2_
  80.2 1.3 %collective-permute-done.21.refs_1_ = bf16[224,128]{1,0:T(8,128)(2,1)S(1)} collective-permute-done((bf16[224,128]{1,0:T(8,128)(2,1)S(1)}, bf16[224,128]{1,0:T(8,128)(2,1)S(1)}, u32[]{:S(2)}, u32[]{:S(2)}) %collective-permute-start.21) | collective-permute-done | bytes 57376 | tf_op jit(solution)/shard_map/ppermute | solution.py:431
  81.6 0.9 %fine_last.1 = (f32[3,3,3,32,128]{4,3,2,1,0:T(8,128)}, f32[1,32]{1,0:T(1,128)}, f32[1,64]{1,0:T(1,128)}) custom-call(bf16[224,128]{1,0:T(8,128)(2,1)S(1)} %add_convert_fusion.1.refs_0_, bf16[224,128]{1,0:T(8,128)(2,1)S(1)} %collective-permute-done.21.refs_1_, bf16[224,128]{1,0:T(8,128)(2,1)S(1)} %collective-permute-done.22.refs_2_, ...), custom_call_target="tpu_custom_call" | custom-call | flops 1000000000 | tf_op jit(solution)/shard_map/fine_last/pallas_call | solution.py:20
  (30 shorter events, 0.3 us)
Async XLA Ops:
  1.5 7.1 %collective-permute-start.1 = (bf16[8,32,128]{2,1,0:T(8,128)(2,1)S(1)}, bf16[8,32,128]{2,1,0:T(8,128)(2,1)S(1)}, u32[]{:S(2)}, u32[]{:S(2)}) collective-permute-start(bf16[8,32,128]{2,1,0:T(8,128)(2,1)S(1)} %get-tuple-element.142), channel_id=1, source_target_pairs={{1,2},{2,1},{5,6},{6,5},{9,10},{10,9},{13,14},{14,13},{17,18},{18,... | collective-permute-start | bytes 196616 | tf_op jit(solution)/shard_map/ppermute | solution.py:400
  2.2 6.4 %copy-start.1 = (bf16[8,16,32,128]{3,2,1,0:T(8,128)(2,1)S(1)}, bf16[8,16,32,128]{3,2,1,0:T(8,128)(2,1)}, u32[]{:S(2)}) copy-start(bf16[8,16,32,128]{3,2,1,0:T(8,128)(2,1)} %field.1) | copy-start | bytes 3145732
  2.2 6.4 %collective-permute-start = (bf16[8,32,128]{2,1,0:T(8,128)(2,1)S(1)}, bf16[8,32,128]{2,1,0:T(8,128)(2,1)S(1)}, u32[]{:S(2)}, u32[]{:S(2)}) collective-permute-start(bf16[8,32,128]{2,1,0:T(8,128)(2,1)S(1)} %get-tuple-element.143), channel_id=1, source_target_pairs={{0,1},{1,0},{2,3},{3,2},{4,5},{5,4},{6,7},{7,6},{8,9},{9,8},{10,11... | collective-permute-start | bytes 196616 | tf_op jit(solution)/shard_map/ppermute | solution.py:401
  6.6 1.2 %copy-start.2 = (bf16[8,16,32,128]{3,2,1,0:T(8,128)(2,1)S(1)}, bf16[8,16,32,128]{3,2,1,0:T(8,128)(2,1)}, u32[]{:S(2)}) copy-start(bf16[8,16,32,128]{3,2,1,0:T(8,128)(2,1)} %cot.3) | copy-start | bytes 3145732
  8.6 2.4 %copy-start.4 = (bf16[3,3,3,128,128]{4,3,2,1,0:T(8,128)(2,1)S(1)}, bf16[3,3,3,128,128]{4,3,2,1,0:T(8,128)(2,1)}, u32[]{:S(2)}) copy-start(bf16[3,3,3,128,128]{4,3,2,1,0:T(8,128)(2,1)} %w.3) | copy-start | bytes 2654212
  8.6 2.4 %copy-start.7 = (f32[128]{0:T(128)S(1)}, f32[128]{0:T(128)}, u32[]{:S(2)}) copy-start(f32[128]{0:T(128)} %param.10) | copy-start | bytes 1540
  8.8 9.5 %collective-permute-start.2 = (bf16[704,128]{1,0:T(8,128)(2,1)S(1)}, bf16[704,128]{1,0:T(8,128)(2,1)S(1)}, u32[]{:S(2)}, u32[]{:S(2)}) collective-permute-start(bf16[704,128]{1,0:T(8,128)(2,1)S(1)} %get-tuple-element.77), channel_id=1, source_target_pairs={{0,4},{4,0},{8,12},{12,8},{16,20},{20,16},{24,28},{28,24},{1,5},{5... | collective-permute-start | bytes 540680 | tf_op jit(solution)/shard_map/ppermute | solution.py:401
  10.4 11.5 %collective-permute-start.3 = (bf16[704,128]{1,0:T(8,128)(2,1)S(1)}, bf16[704,128]{1,0:T(8,128)(2,1)S(1)}, u32[]{:S(2)}, u32[]{:S(2)}) collective-permute-start(bf16[704,128]{1,0:T(8,128)(2,1)S(1)} %get-tuple-element.81), channel_id=1, source_target_pairs={{4,8},{8,4},{12,16},{16,12},{20,24},{24,20},{5,9},{9,5},{13,17},{1... | collective-permute-start | bytes 540680 | tf_op jit(solution)/shard_map/ppermute | solution.py:400
  19.3 4.2 %copy-start = (bf16[3,3,3,128,256]{4,3,2,1,0:T(8,128)(2,1)S(1)}, bf16[3,3,3,128,256]{4,3,2,1,0:T(8,128)(2,1)}, u32[]{:S(2)}) copy-start(bf16[3,3,3,128,256]{4,3,2,1,0:T(8,128)(2,1)} %w.5) | copy-start | bytes 5308420
  19.3 4.8 %collective-permute-start.4 = (bf16[2,8,16,128]{3,2,1,0:T(8,128)(2,1)S(1)}, bf16[2,8,16,128]{3,2,1,0:T(8,128)(2,1)S(1)}, u32[]{:S(2)}, u32[]{:S(2)}) collective-permute-start(bf16[2,8,16,128]{3,2,1,0:T(8,128)(2,1)S(1)} %get-tuple-element.85), channel_id=1, source_target_pairs={{0,4},{4,0},{8,12},{12,8},{16,20},{20,16},{24,28},{28,24},{1,5},{5... | collective-permute-start | bytes 196616 | tf_op jit(solution)/shard_map/ppermute | solution.py:401
  22.8 1.3 %collective-permute-start.5 = (bf16[2,8,16,128]{3,2,1,0:T(8,128)(2,1)S(1)}, bf16[2,8,16,128]{3,2,1,0:T(8,128)(2,1)S(1)}, u32[]{:S(2)}, u32[]{:S(2)}) collective-permute-start(bf16[2,8,16,128]{3,2,1,0:T(8,128)(2,1)S(1)} %get-tuple-element.87), channel_id=1, source_target_pairs={{4,8},{8,4},{12,16},{16,12},{20,24},{24,20},{5,9},{9,5},{13,17},{1... | collective-permute-start | bytes 196616 | tf_op jit(solution)/shard_map/ppermute | solution.py:400
  24.1 3.3 %copy-start.5 = (bf16[256,128]{1,0:T(8,128)(2,1)S(1)}, bf16[256,128]{1,0:T(8,128)(2,1)}, u32[]{:S(2)}) copy-start(bf16[256,128]{1,0:T(8,128)(2,1)} %wm.5) | copy-start | bytes 196612
  24.1 3.3 %copy-start.6 = (f32[256]{0:T(256)S(1)}, f32[256]{0:T(256)}, u32[]{:S(2)}) copy-start(f32[256]{0:T(256)} %param.12) | copy-start | bytes 3076
  24.2 4.8 %collective-permute-start.6 = (bf16[22,16,128]{2,1,0:T(8,128)(2,1)S(1)}, bf16[22,16,128]{2,1,0:T(8,128)(2,1)S(1)}, u32[]{:S(2)}, u32[]{:S(2)}) collective-permute-start(bf16[22,16,128]{2,1,0:T(8,128)(2,1)S(1)} %get-tuple-element.88), channel_id=1, source_target_pairs={{1,2},{2,1},{5,6},{6,5},{9,10},{10,9},{13,14},{14,13},{17,18},{18,... | collective-permute-start | bytes 270344 | tf_op jit(solution)/shard_map/ppermute | solution.py:400
  24.8 4.1 %collective-permute-start.7 = (bf16[22,16,128]{2,1,0:T(8,128)(2,1)S(1)}, bf16[22,16,128]{2,1,0:T(8,128)(2,1)S(1)}, u32[]{:S(2)}, u32[]{:S(2)}) collective-permute-start(bf16[22,16,128]{2,1,0:T(8,128)(2,1)S(1)} %get-tuple-element.89), channel_id=1, source_target_pairs={{0,1},{1,0},{2,3},{3,2},{4,5},{5,4},{6,7},{7,6},{8,9},{9,8},{10,11... | collective-permute-start | bytes 270344 | tf_op jit(solution)/shard_map/ppermute | solution.py:401
  32.3 2.8 %collective-permute-start.8 = (bf16[2,1792,128]{2,1,0:T(8,128)(2,1)S(1)}, bf16[2,1792,128]{2,1,0:T(8,128)(2,1)S(1)}, u32[]{:S(2)}, u32[]{:S(2)}) collective-permute-start(bf16[2,1792,128]{2,1,0:T(8,128)(2,1)S(1)} %get-tuple-element.96), channel_id=1, source_target_pairs={{0,1},{1,0},{2,3},{3,2},{4,5},{5,4},{6,7},{7,6},{8,9},{9,8},{10,11... | collective-permute-start | bytes 2752520 | tf_op jit(solution)/shard_map/ppermute | solution.py:431
  35.0 8.2 %copy-start.3 = (bf16[8,16,32,128]{3,2,1,0:T(8,128)(2,1)S(1)}, bf16[8,16,32,128]{3,2,1,0:T(8,128)(2,1)}, u32[]{:S(2)}) copy-start(bf16[8,16,32,128]{3,2,1,0:T(8,128)(2,1)} %cot.3) | copy-start | bytes 3145732
  35.3 16.0 %collective-permute-start.9 = (bf16[1,896,128]{2,1,0:T(8,128)(2,1)S(1)}, bf16[1,896,128]{2,1,0:T(8,128)(2,1)S(1)}, u32[]{:S(2)}, u32[]{:S(2)}) collective-permute-start(bf16[1,896,128]{2,1,0:T(8,128)(2,1)S(1)} %get-tuple-element.106), channel_id=1, source_target_pairs={{0,2},{1,3},{2,0},{3,1},{4,6},{5,7},{6,4},{7,5},{8,10},{9,11},{10,... | collective-permute-start | bytes 688136 | tf_op jit(solution)/shard_map/ppermute | solution.py:431
  37.3 14.0 %collective-permute-start.10 = (bf16[1,896,128]{2,1,0:T(8,128)(2,1)S(1)}, bf16[1,896,128]{2,1,0:T(8,128)(2,1)S(1)}, u32[]{:S(2)}, u32[]{:S(2)}) collective-permute-start(bf16[1,896,128]{2,1,0:T(8,128)(2,1)S(1)} %get-tuple-element.107), channel_id=1, source_target_pairs={{0,6},{1,7},{2,4},{3,5},{4,2},{5,3},{6,0},{7,1},{8,14},{9,15},{10,... | collective-permute-start | bytes 688136 | tf_op jit(solution)/shard_map/ppermute | solution.py:431
  42.7 11.0 %collective-permute-start.11 = (bf16[1,896,128]{2,1,0:T(8,128)(2,1)S(1)}, bf16[1,896,128]{2,1,0:T(8,128)(2,1)S(1)}, u32[]{:S(2)}, u32[]{:S(2)}) collective-permute-start(bf16[1,896,128]{2,1,0:T(8,128)(2,1)S(1)} %get-tuple-element.108), channel_id=1, source_target_pairs={{0,4},{1,5},{2,6},{3,7},{4,0},{5,1},{6,2},{7,3},{8,12},{9,13},{10,... | collective-permute-start | bytes 688136 | tf_op jit(solution)/shard_map/ppermute | solution.py:431
  50.7 3.2 %collective-permute-start.13 = (bf16[896,128]{1,0:T(8,128)(2,1)S(1)}, bf16[896,128]{1,0:T(8,128)(2,1)S(1)}, u32[]{:S(2)}, u32[]{:S(2)}) collective-permute-start(bf16[896,128]{1,0:T(8,128)(2,1)S(1)} %get-tuple-element.144), channel_id=1, source_target_pairs={{0,1},{1,0},{2,3},{3,2},{4,5},{5,4},{6,7},{7,6},{8,9},{9,8},{10,11... | collective-permute-start | bytes 688136 | tf_op jit(solution)/shard_map/ppermute | solution.py:431
  50.8 3.1 %collective-permute-start.12 = (bf16[896,128]{1,0:T(8,128)(2,1)S(1)}, bf16[896,128]{1,0:T(8,128)(2,1)S(1)}, u32[]{:S(2)}, u32[]{:S(2)}) collective-permute-start(bf16[896,128]{1,0:T(8,128)(2,1)S(1)} %get-tuple-element.145), channel_id=1, source_target_pairs={{0,1},{1,0},{2,3},{3,2},{4,5},{5,4},{6,7},{7,6},{8,9},{9,8},{10,11... | collective-permute-start | bytes 688136 | tf_op jit(solution)/shard_map/ppermute | solution.py:431
  53.9 6.8 %collective-permute-start.14 = (bf16[448,128]{1,0:T(8,128)(2,1)S(1)}, bf16[448,128]{1,0:T(8,128)(2,1)S(1)}, u32[]{:S(2)}, u32[]{:S(2)}) collective-permute-start(bf16[448,128]{1,0:T(8,128)(2,1)S(1)} %get-tuple-element.118), channel_id=1, source_target_pairs={{0,8},{1,9},{2,10},{3,11},{4,12},{5,13},{6,14},{7,15},{8,0},{9,1},... | collective-permute-start | bytes 344072 | tf_op jit(solution)/shard_map/ppermute | solution.py:431
  57.2 6.1 %collective-permute-start.16 = (bf16[1,448,128]{2,1,0:T(8,128)(2,1)S(1)}, bf16[1,448,128]{2,1,0:T(8,128)(2,1)S(1)}, u32[]{:S(2)}, u32[]{:S(2)}) collective-permute-start(bf16[1,448,128]{2,1,0:T(8,128)(2,1)S(1)} %get-tuple-element.123), channel_id=1, source_target_pairs={{0,2},{1,3},{2,0},{3,1},{4,6},{5,7},{6,4},{7,5},{8,10},{9,11},{10,... | collective-permute-start | bytes 344072 | tf_op jit(solution)/shard_map/ppermute | solution.py:431
  58.9 5.7 %collective-permute-start.17 = (bf16[1,448,128]{2,1,0:T(8,128)(2,1)S(1)}, bf16[1,448,128]{2,1,0:T(8,128)(2,1)S(1)}, u32[]{:S(2)}, u32[]{:S(2)}) collective-permute-start(bf16[1,448,128]{2,1,0:T(8,128)(2,1)S(1)} %get-tuple-element.124), channel_id=1, source_target_pairs={{0,6},{1,7},{2,4},{3,5},{4,2},{5,3},{6,0},{7,1},{8,14},{9,15},{10,... | collective-permute-start | bytes 344072 | tf_op jit(solution)/shard_map/ppermute | solution.py:431
  59.2 5.8 %collective-permute-start.18 = (bf16[1,448,128]{2,1,0:T(8,128)(2,1)S(1)}, bf16[1,448,128]{2,1,0:T(8,128)(2,1)S(1)}, u32[]{:S(2)}, u32[]{:S(2)}) collective-permute-start(bf16[1,448,128]{2,1,0:T(8,128)(2,1)S(1)} %get-tuple-element.125), channel_id=1, source_target_pairs={{0,4},{1,5},{2,6},{3,7},{4,0},{5,1},{6,2},{7,3},{8,12},{9,13},{10,... | collective-permute-start | bytes 344072 | tf_op jit(solution)/shard_map/ppermute | solution.py:431
  60.8 8.5 %collective-permute-start.15 = (bf16[448,128]{1,0:T(8,128)(2,1)S(1)}, bf16[448,128]{1,0:T(8,128)(2,1)S(1)}, u32[]{:S(2)}, u32[]{:S(2)}) collective-permute-start(bf16[448,128]{1,0:T(8,128)(2,1)S(1)} %coarse_sum.1), channel_id=1, source_target_pairs={{0,16},{1,17},{2,18},{3,19},{4,20},{5,21},{6,22},{7,23},{8,24},{9,... | collective-permute-start | bytes 344072 | tf_op jit(solution)/shard_map/ppermute | solution.py:431
  65.0 4.2 %collective-permute-start.19 = (bf16[224,128]{1,0:T(8,128)(2,1)S(1)}, bf16[224,128]{1,0:T(8,128)(2,1)S(1)}, u32[]{:S(2)}, u32[]{:S(2)}) collective-permute-start(bf16[224,128]{1,0:T(8,128)(2,1)S(1)} %get-tuple-element.127), channel_id=1, source_target_pairs={{0,8},{1,9},{2,10},{3,11},{4,12},{5,13},{6,14},{7,15},{8,0},{9,1},... | collective-permute-start | bytes 172040 | tf_op jit(solution)/shard_map/ppermute | solution.py:431
  69.3 5.7 %collective-permute-start.20 = (bf16[224,128]{1,0:T(8,128)(2,1)S(1)}, bf16[224,128]{1,0:T(8,128)(2,1)S(1)}, u32[]{:S(2)}, u32[]{:S(2)}) collective-permute-start(bf16[224,128]{1,0:T(8,128)(2,1)S(1)} %fine_sum.1), channel_id=1, source_target_pairs={{0,16},{1,17},{2,18},{3,19},{4,20},{5,21},{6,22},{7,23},{8,24},{9,... | collective-permute-start | bytes 172040 | tf_op jit(solution)/shard_map/ppermute | solution.py:431
  70.7 6.7 %collective-permute-start.26 = (bf16[448,128]{1,0:T(8,128)(2,1)S(1)}, bf16[448,128]{1,0:T(8,128)(2,1)S(1)}, u32[]{:S(2)}, u32[]{:S(2)}) collective-permute-start(bf16[448,128]{1,0:T(8,128)(2,1)S(1)} %add_convert_fusion.refs_0_), channel_id=1, source_target_pairs={{0,12},{1,13},{2,14},{3,15},{4,8},{5,9},{6,10},{7,11},{8,4},{9,5},... | collective-permute-start | bytes 344072 | tf_op jit(solution)/shard_map/ppermute | solution.py:431
  72.5 6.0 %collective-permute-start.25 = (bf16[448,128]{1,0:T(8,128)(2,1)S(1)}, bf16[448,128]{1,0:T(8,128)(2,1)S(1)}, u32[]{:S(2)}, u32[]{:S(2)}) collective-permute-start(bf16[448,128]{1,0:T(8,128)(2,1)S(1)} %add_convert_fusion.refs_0_), channel_id=1, source_target_pairs={{0,8},{1,9},{2,10},{3,11},{4,12},{5,13},{6,14},{7,15},{8,0},{9,1},... | collective-permute-start | bytes 344072 | tf_op jit(solution)/shard_map/ppermute | solution.py:431
  72.7 5.8 %collective-permute-start.24 = (bf16[448,128]{1,0:T(8,128)(2,1)S(1)}, bf16[448,128]{1,0:T(8,128)(2,1)S(1)}, u32[]{:S(2)}, u32[]{:S(2)}) collective-permute-start(bf16[448,128]{1,0:T(8,128)(2,1)S(1)} %add_convert_fusion.refs_0_), channel_id=1, source_target_pairs={{0,4},{1,5},{2,6},{3,7},{4,0},{5,1},{6,2},{7,3},{8,12},{9,13},{10,... | collective-permute-start | bytes 344072 | tf_op jit(solution)/shard_map/ppermute | solution.py:431
  75.0 5.1 %collective-permute-start.23 = (bf16[224,128]{1,0:T(8,128)(2,1)S(1)}, bf16[224,128]{1,0:T(8,128)(2,1)S(1)}, u32[]{:S(2)}, u32[]{:S(2)}) collective-permute-start(bf16[224,128]{1,0:T(8,128)(2,1)S(1)} %add_convert_fusion.1.refs_0_), channel_id=1, source_target_pairs={{0,12},{1,13},{2,14},{3,15},{4,8},{5,9},{6,10},{7,11},{8,4},{9,5},... | collective-permute-start | bytes 172040 | tf_op jit(solution)/shard_map/ppermute | solution.py:431
  76.1 4.2 %collective-permute-start.22 = (bf16[224,128]{1,0:T(8,128)(2,1)S(1)}, bf16[224,128]{1,0:T(8,128)(2,1)S(1)}, u32[]{:S(2)}, u32[]{:S(2)}) collective-permute-start(bf16[224,128]{1,0:T(8,128)(2,1)S(1)} %add_convert_fusion.1.refs_0_), channel_id=1, source_target_pairs={{0,8},{1,9},{2,10},{3,11},{4,12},{5,13},{6,14},{7,15},{8,0},{9,1},... | collective-permute-start | bytes 172040 | tf_op jit(solution)/shard_map/ppermute | solution.py:431
  77.4 4.2 %collective-permute-start.21 = (bf16[224,128]{1,0:T(8,128)(2,1)S(1)}, bf16[224,128]{1,0:T(8,128)(2,1)S(1)}, u32[]{:S(2)}, u32[]{:S(2)}) collective-permute-start(bf16[224,128]{1,0:T(8,128)(2,1)S(1)} %add_convert_fusion.1.refs_0_), channel_id=1, source_target_pairs={{0,4},{1,5},{2,6},{3,7},{4,0},{5,1},{6,2},{7,3},{8,12},{9,13},{10,... | collective-permute-start | bytes 172040 | tf_op jit(solution)/shard_map/ppermute | solution.py:431

commit v9 on v8

--- a/solution.py
+++ b/solution.py
@@ -56,7 +56,7 @@
 
 
 def sigmoid(value):
-    return 1.0 / (1.0 + jnp.exp(-value))
+    return 0.5 + 0.5 * jnp.tanh(0.5 * value)
 
 
 def turn_body(field, ya, yb, pg, own, out_a, out_b):
@@ -631,8 +631,9 @@
             1,
         )
 
+    hid_b, ds_b, pool_b, pb = edge(True, xb)
+    xa, pb = lax.optimization_barrier((xa, pb))
     hid_a, ds_a, pool_a, pa = edge(False, xa)
-    hid_b, ds_b, pool_b, pb = edge(True, xb)
     pxa, pxb = swap_faces(pa, pb, "grp")
     (taps,) = call(taps_body, "taps", (coarse_kernel,), [((9 * c, 3 * c2), BF16)], (), 0.5)
     pxa, taps = lax.optimization_barrier((pxa, taps))

time: 82.7 us -> 82.6 us (level)
    ppermute x19, starting transfers between devices: 26.5 us -> 25.1 us  [partners(): return lax.ppermute(value, ('grp', 'sub'), pairs)]
    ppermute x4, starting transfers between devices: 11.1 us -> 12.3 us  [swap_faces(): return (lax.ppermute(first, axis, one), got)]
  transfers between devices with their start and end apart: 27 -> 27, of which waited for: 14 -> 14; matrix products, arithmetic and copies ran while one was open for 0% -> 0% of each run, Pallas kernels for 24% -> 22%
where the time goes in v9:
time: 82.6 us; the launch traced here: 82.3 us
  starting transfers between devices  40 us (48%)
  Pallas kernels  24.1 us (29%)
  waiting for transfers between devices  15 us (18%)
  local copies, waits for them, and re-layouts  1.29 us (2%)
  other arithmetic  0.99 us (1%)
  between operations  0.88 us (1%)
    ppermute x19, starting transfers between devices, partners(): return lax.ppermute(value, ('grp', 'sub'), pairs)  25.1 us
    pallas_call x19, Pallas kernels, call(): pl.pallas_call(body, name=name, out_shape=[jax.ShapeDtypeStruct(s, t) for...  24.1 us
    ppermute x19, waiting for transfers between devices, partners(): return lax.ppermute(value, ('grp', 'sub'), pairs)  12.4 us
    ppermute x4, starting transfers between devices, swap_faces(): return (lax.ppermute(first, axis, one), got)  12.3 us
    ppermute x4, waiting for transfers between devices, swap_faces(): return (lax.ppermute(first, axis, one), got)  2.66 us
    ppermute x4, starting transfers between devices, swap_faces(): got = lax.ppermute(second, axis, two)  2.64 us
  transfers between devices with their start and end apart: 27, of which 14 were waited for; matrix products, arithmetic and copies ran while one was open for 0% of the time, Pallas kernels for 22%

profile of v9, /device:TPU:0, one launch (start us, length us, event | category | flops | bytes accessed | tf_op | source)
XLA Modules:
  0.0 82.3 jit_solution(750346003330774356)
XLA Ops:
  0.6 0.9 %fusion.1 = (bf16[8,32,128]{2,1,0:T(8,128)(2,1)S(1)}, bf16[8,32,128]{2,1,0:T(8,128)(2,1)S(1)}) fusion(pred[]{:T(512)S(6)} %eq.3, bf16[8,16,32,128]{3,2,1,0:T(8,128)(2,1)} %field.1), kind=kLoop, calls=%fused_computation.8 | loop fusion | flops 65536 | bytes 262145 | tf_op jit(solution)/shard_map/jit(_where)/select_n | solution.py:589
  1.5 0.7 collective-permute-start.1
  2.2 0.0 copy-start.1
  2.2 4.4 %collective-permute-start = (bf16[8,32,128]{2,1,0:T(8,128)(2,1)S(1)}, bf16[8,32,128]{2,1,0:T(8,128)(2,1)S(1)}, u32[]{:S(2)}, u32[]{:S(2)}) collective-permute-start(bf16[8,32,128]{2,1,0:T(8,128)(2,1)S(1)} %get-tuple-element.147), channel_id=1, source_target_pairs={{0,1},{1,0},{2,3},{3,2},{4,5},{5,4},{6,7},{7,6},{8,9},{9,8},{10,11... | collective-permute-start | bytes 196616 | tf_op jit(solution)/shard_map/ppermute | solution.py:401
  6.6 1.2 %copy-done.2 = bf16[8,16,32,128]{3,2,1,0:T(8,128)(2,1)S(1)} copy-done((bf16[8,16,32,128]{3,2,1,0:T(8,128)(2,1)S(1)}, bf16[8,16,32,128]{3,2,1,0:T(8,128)(2,1)}, u32[]{:S(2)}) %copy-start.2) | copy-done | bytes 1048600
  7.8 0.8 cubes.1
  8.6 0.0 copy-start.4
  8.6 0.0 copy-start.7
  8.7 0.2 turn.1
  8.8 1.6 %collective-permute-start.2 = (bf16[704,128]{1,0:T(8,128)(2,1)S(1)}, bf16[704,128]{1,0:T(8,128)(2,1)S(1)}, u32[]{:S(2)}, u32[]{:S(2)}) collective-permute-start(bf16[704,128]{1,0:T(8,128)(2,1)S(1)} %get-tuple-element.79), channel_id=1, source_target_pairs={{0,4},{4,0},{8,12},{12,8},{16,20},{20,16},{24,28},{28,24},{1,5},{5... | collective-permute-start | bytes 540680 | tf_op jit(solution)/shard_map/ppermute | solution.py:401
  10.4 0.7 collective-permute-start.3
  11.1 5.1 %inner.1 = (bf16[6,16,32,128]{3,2,1,0:T(8,128)(2,1)S(1)}, f32[6,16,32,128]{3,2,1,0:T(8,128)S(1)}, bf16[2,8,16,128]{3,2,1,0:T(8,128)(2,1)S(1)}, bf16[1152,384]{1,0:T(8,128)(2,1)S(1)}) custom-call(bf16[8,18,32,128]{3,2,1,0:T(8,128)(2,1)S(1)} %get-tuple-element.77.own, bf16[3,3,3,128,128]{4,3,2,1,0:T(8,128)(2,1)S(1)} %copy-done.4, f32[1,128]{1,0:T(1,128)S(1)} %bitcast.46), custom_call_target="tpu_custom_call" | custom-call | flops 6000000000 | tf_op jit(solution)/shard_map/inner/pallas_call | solution.py:20
  16.1 1.0 %edge.2 = (bf16[16,32,128]{2,1,0:T(8,128)(2,1)S(1)}, f32[16,32,128]{2,1,0:T(8,128)S(1)}, bf16[8,16,128]{2,1,0:T(8,128)(2,1)S(1)}, bf16[2,8,16,128]{3,2,1,0:T(8,128)(2,1)S(1)}) custom-call(bf16[8,18,32,128]{3,2,1,0:T(8,128)(2,1)S(1)} %get-tuple-element.77.own, bf16[704,128]{1,0:T(8,128)(2,1)S(1)} %collective-permute-done.3.face.xb, ...), custom_call_target="tpu_custom_call" | custom-call | flops 1000000000 | tf_op jit(solution)/shard_map/edge/pallas_call | solution.py:20
  17.1 1.2 %collective-permute-done.2.face.xa = bf16[704,128]{1,0:T(8,128)(2,1)S(1)} collective-permute-done((bf16[704,128]{1,0:T(8,128)(2,1)S(1)}, bf16[704,128]{1,0:T(8,128)(2,1)S(1)}, u32[]{:S(2)}, u32[]{:S(2)}) %collective-permute-start.2) | collective-permute-done | bytes 180256 | tf_op jit(solution)/shard_map/ppermute | solution.py:401
  18.3 1.0 %edge.3 = (bf16[16,32,128]{2,1,0:T(8,128)(2,1)S(1)}, f32[16,32,128]{2,1,0:T(8,128)S(1)}, bf16[8,16,128]{2,1,0:T(8,128)(2,1)S(1)}, bf16[2,8,16,128]{3,2,1,0:T(8,128)(2,1)S(1)}) custom-call(bf16[8,18,32,128]{3,2,1,0:T(8,128)(2,1)S(1)} %get-tuple-element.77.own, bf16[704,128]{1,0:T(8,128)(2,1)S(1)} %collective-permute-done.2.face.xa, ...), custom_call_target="tpu_custom_call" | custom-call | flops 1000000000 | tf_op jit(solution)/shard_map/edge/pallas_call | solution.py:20
  19.3 3.2 %collective-permute-start.4 = (bf16[2,8,16,128]{3,2,1,0:T(8,128)(2,1)S(1)}, bf16[2,8,16,128]{3,2,1,0:T(8,128)(2,1)S(1)}, u32[]{:S(2)}, u32[]{:S(2)}) collective-permute-start(bf16[2,8,16,128]{3,2,1,0:T(8,128)(2,1)S(1)} %get-tuple-element.89), channel_id=1, source_target_pairs={{0,4},{4,0},{8,12},{12,8},{16,20},{20,16},{24,28},{28,24},{1,5},{5... | collective-permute-start | bytes 196616 | tf_op jit(solution)/shard_map/ppermute | solution.py:401
  22.4 0.7 collective-permute-start.5
  23.1 0.1 taps.1.wb
  23.2 1.5 %collective-permute-done.4.ra = bf16[2,8,16,128]{3,2,1,0:T(8,128)(2,1)S(1)} collective-permute-done((bf16[2,8,16,128]{3,2,1,0:T(8,128)(2,1)S(1)}, bf16[2,8,16,128]{3,2,1,0:T(8,128)(2,1)S(1)}, u32[]{:S(2)}, u32[]{:S(2)}) %collective-permute-start.4) | collective-permute-done | bytes 65568 | tf_op jit(solution)/shard_map/ppermute | solution.py:401
  24.7 0.7 collective-permute-start.6
  25.4 3.1 %collective-permute-start.7 = (bf16[22,16,128]{2,1,0:T(8,128)(2,1)S(1)}, bf16[22,16,128]{2,1,0:T(8,128)(2,1)S(1)}, u32[]{:S(2)}, u32[]{:S(2)}) collective-permute-start(bf16[22,16,128]{2,1,0:T(8,128)(2,1)S(1)} %get-tuple-element.93), channel_id=1, source_target_pairs={{0,1},{1,0},{2,3},{3,2},{4,5},{5,4},{6,7},{7,6},{8,9},{9,8},{10,11... | collective-permute-start | bytes 270344 | tf_op jit(solution)/shard_map/ppermute | solution.py:401
  28.6 1.5 %mid.1 = (bf16[6,6,16,256]{3,2,1,0:T(8,128)(2,1)S(1)}, bf16[4,6,16,256]{3,2,1,0:T(8,128)(2,1)S(1)}) custom-call(bf16[2,8,16,128]{3,2,1,0:T(8,128)(2,1)S(1)} %get-tuple-element.82.pool_in, bf16[8,16,128]{2,1,0:T(8,128)(2,1)S(1)} %get-tuple-element.87.pool_a, bf16[8,16,128]{2,1,0:T(8,128)(2,1)S(1)} %get-tuple-element.88.pool_b, ...), custom_call_target="tpu_custom_call" | custom-call | flops 2000000000 | tf_op jit(solution)/shard_map/mid/pallas_call | solution.py:20
  30.1 0.0 collective-permute-done.6.ub
  30.1 0.0 collective-permute-done.7.ua
  30.1 3.3 %coarse.1 = (bf16[6,10,16,256]{3,2,1,0:T(8,128)(2,1)S(1)}, bf16[4,8,16,256]{3,2,1,0:T(8,128)(2,1)S(1)}, bf16[2,1792,128]{2,1,0:T(8,128)(2,1)S(1)}, bf16[2,1792,128]{2,1,0:T(8,128)(2,1)S(1)}, bf16[256,128]{1,0:T(8,128)(2,1)S(1)}) custom-call(bf16[2,8,16,128]{3,2,1,0:T(8,128)(2,1)S(1)} %get-tuple-element.82.pool_in, ...), custom_call_target="tpu_custom_call" | custom-call | flops 6000000000 | tf_op jit(solution)/shard_map/coarse/pallas_call | solution.py:20
  33.4 0.7 collective-permute-start.8
  34.1 1.3 %merge.1 = bf16[8,16,32,128]{3,2,1,0:T(8,128)(2,1)} custom-call(bf16[6,16,32,128]{3,2,1,0:T(8,128)(2,1)S(1)} %get-tuple-element.78.hid_in.hidden, bf16[16,32,128]{2,1,0:T(8,128)(2,1)S(1)} %get-tuple-element.85.hid_a, bf16[16,32,128]{2,1,0:T(8,128)(2,1)S(1)} %get-tuple-element.86.hid_b, bf16[4,8,16,256]{3,2,1,0:T(8,128)(2,1)S(1)} %get-tuple-element.99.coarse, ...), custom_call_target="tpu_custom_call" | custom-call | flops 2000000000 | tf_op jit(solution)/shard_map/merge/pallas_call | solution.py:20
  35.4 0.8 collective-permute-done.8
  36.2 0.2 split.2
  36.4 2.0 %collective-permute-start.9 = (bf16[1,896,128]{2,1,0:T(8,128)(2,1)S(1)}, bf16[1,896,128]{2,1,0:T(8,128)(2,1)S(1)}, u32[]{:S(2)}, u32[]{:S(2)}) collective-permute-start(bf16[1,896,128]{2,1,0:T(8,128)(2,1)S(1)} %get-tuple-element.110), channel_id=1, source_target_pairs={{0,2},{1,3},{2,0},{3,1},{4,6},{5,7},{6,4},{7,5},{8,10},{9,11},{10,... | collective-permute-start | bytes 688136 | tf_op jit(solution)/shard_map/ppermute | solution.py:431
  38.4 4.2 %collective-permute-start.10 = (bf16[1,896,128]{2,1,0:T(8,128)(2,1)S(1)}, bf16[1,896,128]{2,1,0:T(8,128)(2,1)S(1)}, u32[]{:S(2)}, u32[]{:S(2)}) collective-permute-start(bf16[1,896,128]{2,1,0:T(8,128)(2,1)S(1)} %get-tuple-element.111), channel_id=1, source_target_pairs={{0,6},{1,7},{2,4},{3,5},{4,2},{5,3},{6,0},{7,1},{8,14},{9,15},{10,... | collective-permute-start | bytes 688136 | tf_op jit(solution)/shard_map/ppermute | solution.py:431
  42.6 0.5 collective-permute-start.11
  43.1 7.4 %back.1 = (bf16[2,896,128]{2,1,0:T(8,128)(2,1)S(1)}, bf16[2,896,128]{2,1,0:T(8,128)(2,1)S(1)}) custom-call(bf16[6,10,16,256]{3,2,1,0:T(8,128)(2,1)S(1)} %get-tuple-element.115.slope, bf16[3,3,3,128,256]{4,3,2,1,0:T(8,128)(2,1)S(1)} %copy-done, bf16[8,16,32,128]{3,2,1,0:T(8,128)(2,1)S(1)} %copy-done.3, f32[6,16,32,128]{3,2,1,0:T(8,128)S(1)} %get-tuple-element.116.ds, ...), custom_call_target="tpu_custom_call" | custom-call | flops 10000000000 | tf_op jit(solution)/shard_map/back/pallas_call | solution.py:20
  50.5 0.1 collective-permute-start.13
  50.6 0.5 collective-permute-start.12
  51.1 2.5 %collective-permute-done.11 = bf16[1,896,128]{2,1,0:T(8,128)(2,1)S(1)} collective-permute-done((bf16[1,896,128]{2,1,0:T(8,128)(2,1)S(1)}, bf16[1,896,128]{2,1,0:T(8,128)(2,1)S(1)}, u32[]{:S(2)}, u32[]{:S(2)}) %collective-permute-start.11) | collective-permute-done | bytes 229408 | tf_op jit(solution)/shard_map/ppermute | solution.py:431
  53.7 0.1 coarse_half.1
  53.8 3.1 %collective-permute-start.14 = (bf16[448,128]{1,0:T(8,128)(2,1)S(1)}, bf16[448,128]{1,0:T(8,128)(2,1)S(1)}, u32[]{:S(2)}, u32[]{:S(2)}) collective-permute-start(bf16[448,128]{1,0:T(8,128)(2,1)S(1)} %get-tuple-element.122), channel_id=1, source_target_pairs={{0,8},{1,9},{2,10},{3,11},{4,12},{5,13},{6,14},{7,15},{8,0},{9,1},... | collective-permute-start | bytes 344072 | tf_op jit(solution)/shard_map/ppermute | solution.py:431
  56.9 0.1 split.3
  57.0 1.7 %collective-permute-start.16 = (bf16[1,448,128]{2,1,0:T(8,128)(2,1)S(1)}, bf16[1,448,128]{2,1,0:T(8,128)(2,1)S(1)}, u32[]{:S(2)}, u32[]{:S(2)}) collective-permute-start(bf16[1,448,128]{2,1,0:T(8,128)(2,1)S(1)} %get-tuple-element.127), channel_id=1, source_target_pairs={{0,2},{1,3},{2,0},{3,1},{4,6},{5,7},{6,4},{7,5},{8,10},{9,11},{10,... | collective-permute-start | bytes 344072 | tf_op jit(solution)/shard_map/ppermute | solution.py:431
  58.8 0.3 collective-permute-start.17
  59.1 1.5 %collective-permute-start.18 = (bf16[1,448,128]{2,1,0:T(8,128)(2,1)S(1)}, bf16[1,448,128]{2,1,0:T(8,128)(2,1)S(1)}, u32[]{:S(2)}, u32[]{:S(2)}) collective-permute-start(bf16[1,448,128]{2,1,0:T(8,128)(2,1)S(1)} %get-tuple-element.129), channel_id=1, source_target_pairs={{0,4},{1,5},{2,6},{3,7},{4,0},{5,1},{6,2},{7,3},{8,12},{9,13},{10,... | collective-permute-start | bytes 344072 | tf_op jit(solution)/shard_map/ppermute | solution.py:431
  60.6 2.1 %collective-permute-start.15 = (bf16[448,128]{1,0:T(8,128)(2,1)S(1)}, bf16[448,128]{1,0:T(8,128)(2,1)S(1)}, u32[]{:S(2)}, u32[]{:S(2)}) collective-permute-start(bf16[448,128]{1,0:T(8,128)(2,1)S(1)} %coarse_sum.1), channel_id=1, source_target_pairs={{0,16},{1,17},{2,18},{3,19},{4,20},{5,21},{6,22},{7,23},{8,24},{9,... | collective-permute-start | bytes 344072 | tf_op jit(solution)/shard_map/ppermute | solution.py:431
  62.8 0.4 collective-permute-done.16
  63.1 1.3 %collective-permute-done.17 = bf16[1,448,128]{2,1,0:T(8,128)(2,1)S(1)} collective-permute-done((bf16[1,448,128]{2,1,0:T(8,128)(2,1)S(1)}, bf16[1,448,128]{2,1,0:T(8,128)(2,1)S(1)}, u32[]{:S(2)}, u32[]{:S(2)}) %collective-permute-start.17) | collective-permute-done | bytes 114720 | tf_op jit(solution)/shard_map/ppermute | solution.py:431
  64.5 0.4 collective-permute-done.18
  64.8 0.1 fine_half.1
  64.9 0.4 collective-permute-start.19
  65.2 3.9 %collective-permute-done.19.refs_1_ = bf16[224,128]{1,0:T(8,128)(2,1)S(1)} collective-permute-done((bf16[224,128]{1,0:T(8,128)(2,1)S(1)}, bf16[224,128]{1,0:T(8,128)(2,1)S(1)}, u32[]{:S(2)}, u32[]{:S(2)}) %collective-permute-start.19) | collective-permute-done | bytes 57376 | tf_op jit(solution)/shard_map/ppermute | solution.py:431
  69.2 1.4 %collective-permute-start.20 = (bf16[224,128]{1,0:T(8,128)(2,1)S(1)}, bf16[224,128]{1,0:T(8,128)(2,1)S(1)}, u32[]{:S(2)}, u32[]{:S(2)}) collective-permute-start(bf16[224,128]{1,0:T(8,128)(2,1)S(1)} %fine_sum.1), channel_id=1, source_target_pairs={{0,16},{1,17},{2,18},{3,19},{4,20},{5,21},{6,22},{7,23},{8,24},{9,... | collective-permute-start | bytes 172040 | tf_op jit(solution)/shard_map/ppermute | solution.py:431
  70.6 1.8 %collective-permute-start.26 = (bf16[448,128]{1,0:T(8,128)(2,1)S(1)}, bf16[448,128]{1,0:T(8,128)(2,1)S(1)}, u32[]{:S(2)}, u32[]{:S(2)}) collective-permute-start(bf16[448,128]{1,0:T(8,128)(2,1)S(1)} %add_convert_fusion.refs_0_), channel_id=1, source_target_pairs={{0,12},{1,13},{2,14},{3,15},{4,8},{5,9},{6,10},{7,11},{8,4},{9,5},... | collective-permute-start | bytes 344072 | tf_op jit(solution)/shard_map/ppermute | solution.py:431
  72.4 0.3 collective-permute-start.25
  72.6 1.5 %collective-permute-start.24 = (bf16[448,128]{1,0:T(8,128)(2,1)S(1)}, bf16[448,128]{1,0:T(8,128)(2,1)S(1)}, u32[]{:S(2)}, u32[]{:S(2)}) collective-permute-start(bf16[448,128]{1,0:T(8,128)(2,1)S(1)} %add_convert_fusion.refs_0_), channel_id=1, source_target_pairs={{0,4},{1,5},{2,6},{3,7},{4,0},{5,1},{6,2},{7,3},{8,12},{9,13},{10,... | collective-permute-start | bytes 344072 | tf_op jit(solution)/shard_map/ppermute | solution.py:431
  74.1 0.7 collective-permute-done.20
  74.8 1.1 %collective-permute-start.23 = (bf16[224,128]{1,0:T(8,128)(2,1)S(1)}, bf16[224,128]{1,0:T(8,128)(2,1)S(1)}, u32[]{:S(2)}, u32[]{:S(2)}) collective-permute-start(bf16[224,128]{1,0:T(8,128)(2,1)S(1)} %add_convert_fusion.1.refs_0_), channel_id=1, source_target_pairs={{0,12},{1,13},{2,14},{3,15},{4,8},{5,9},{6,10},{7,11},{8,4},{9,5},... | collective-permute-start | bytes 172040 | tf_op jit(solution)/shard_map/ppermute | solution.py:431
  75.9 0.9 %collective-permute-start.22 = (bf16[224,128]{1,0:T(8,128)(2,1)S(1)}, bf16[224,128]{1,0:T(8,128)(2,1)S(1)}, u32[]{:S(2)}, u32[]{:S(2)}) collective-permute-start(bf16[224,128]{1,0:T(8,128)(2,1)S(1)} %add_convert_fusion.1.refs_0_), channel_id=1, source_target_pairs={{0,8},{1,9},{2,10},{3,11},{4,12},{5,13},{6,14},{7,15},{8,0},{9,1},... | collective-permute-start | bytes 172040 | tf_op jit(solution)/shard_map/ppermute | solution.py:431
  76.9 0.4 collective-permute-done.26.refs_3_
  77.3 1.1 %collective-permute-start.21 = (bf16[224,128]{1,0:T(8,128)(2,1)S(1)}, bf16[224,128]{1,0:T(8,128)(2,1)S(1)}, u32[]{:S(2)}, u32[]{:S(2)}) collective-permute-start(bf16[224,128]{1,0:T(8,128)(2,1)S(1)} %add_convert_fusion.1.refs_0_), channel_id=1, source_target_pairs={{0,4},{1,5},{2,6},{3,7},{4,0},{5,1},{6,2},{7,3},{8,12},{9,13},{10,... | collective-permute-start | bytes 172040 | tf_op jit(solution)/shard_map/ppermute | solution.py:431
  78.4 0.1 collective-permute-done.24.refs_1_
  78.5 1.0 %coarse_last.1 = (f32[3,3,3,64,128]{4,3,2,1,0:T(8,128)}, f32[64,128]{1,0:T(8,128)}) custom-call(bf16[448,128]{1,0:T(8,128)(2,1)S(1)} %add_convert_fusion.refs_0_, bf16[448,128]{1,0:T(8,128)(2,1)S(1)} %collective-permute-done.24.refs_1_, bf16[448,128]{1,0:T(8,128)(2,1)S(1)} %collective-permute-done.25.refs_2_, ...), custom_call_target="tpu_custom_call" | custom-call | flops 1000000000 | tf_op jit(solution)/shard_map/coarse_last/pallas_call | solution.py:20
  79.5 0.5 collective-permute-done.23.refs_3_
  80.0 0.1 collective-permute-done.22.refs_2_
  80.1 1.3 %collective-permute-done.21.refs_1_ = bf16[224,128]{1,0:T(8,128)(2,1)S(1)} collective-permute-done((bf16[224,128]{1,0:T(8,128)(2,1)S(1)}, bf16[224,128]{1,0:T(8,128)(2,1)S(1)}, u32[]{:S(2)}, u32[]{:S(2)}) %collective-permute-start.21) | collective-permute-done | bytes 57376 | tf_op jit(solution)/shard_map/ppermute | solution.py:431
  81.4 0.9 %fine_last.1 = (f32[3,3,3,32,128]{4,3,2,1,0:T(8,128)}, f32[1,32]{1,0:T(1,128)}, f32[1,64]{1,0:T(1,128)}) custom-call(bf16[224,128]{1,0:T(8,128)(2,1)S(1)} %add_convert_fusion.1.refs_0_, bf16[224,128]{1,0:T(8,128)(2,1)S(1)} %collective-permute-done.21.refs_1_, bf16[224,128]{1,0:T(8,128)(2,1)S(1)} %collective-permute-done.22.refs_2_, ...), custom_call_target="tpu_custom_call" | custom-call | flops 1000000000 | tf_op jit(solution)/shard_map/fine_last/pallas_call | solution.py:20
  (30 shorter events, 0.3 us)
Async XLA Ops:
  1.5 7.1 %collective-permute-start.1 = (bf16[8,32,128]{2,1,0:T(8,128)(2,1)S(1)}, bf16[8,32,128]{2,1,0:T(8,128)(2,1)S(1)}, u32[]{:S(2)}, u32[]{:S(2)}) collective-permute-start(bf16[8,32,128]{2,1,0:T(8,128)(2,1)S(1)} %get-tuple-element.146), channel_id=1, source_target_pairs={{1,2},{2,1},{5,6},{6,5},{9,10},{10,9},{13,14},{14,13},{17,18},{18,... | collective-permute-start | bytes 196616 | tf_op jit(solution)/shard_map/ppermute | solution.py:400
  2.2 6.4 %copy-start.1 = (bf16[8,16,32,128]{3,2,1,0:T(8,128)(2,1)S(1)}, bf16[8,16,32,128]{3,2,1,0:T(8,128)(2,1)}, u32[]{:S(2)}) copy-start(bf16[8,16,32,128]{3,2,1,0:T(8,128)(2,1)} %field.1) | copy-start | bytes 3145732
  2.2 6.4 %collective-permute-start = (bf16[8,32,128]{2,1,0:T(8,128)(2,1)S(1)}, bf16[8,32,128]{2,1,0:T(8,128)(2,1)S(1)}, u32[]{:S(2)}, u32[]{:S(2)}) collective-permute-start(bf16[8,32,128]{2,1,0:T(8,128)(2,1)S(1)} %get-tuple-element.147), channel_id=1, source_target_pairs={{0,1},{1,0},{2,3},{3,2},{4,5},{5,4},{6,7},{7,6},{8,9},{9,8},{10,11... | collective-permute-start | bytes 196616 | tf_op jit(solution)/shard_map/ppermute | solution.py:401
  6.6 1.2 %copy-start.2 = (bf16[8,16,32,128]{3,2,1,0:T(8,128)(2,1)S(1)}, bf16[8,16,32,128]{3,2,1,0:T(8,128)(2,1)}, u32[]{:S(2)}) copy-start(bf16[8,16,32,128]{3,2,1,0:T(8,128)(2,1)} %cot.3) | copy-start | bytes 3145732
  8.6 2.4 %copy-start.4 = (bf16[3,3,3,128,128]{4,3,2,1,0:T(8,128)(2,1)S(1)}, bf16[3,3,3,128,128]{4,3,2,1,0:T(8,128)(2,1)}, u32[]{:S(2)}) copy-start(bf16[3,3,3,128,128]{4,3,2,1,0:T(8,128)(2,1)} %w.3) | copy-start | bytes 2654212
  8.6 2.4 %copy-start.7 = (f32[128]{0:T(128)S(1)}, f32[128]{0:T(128)}, u32[]{:S(2)}) copy-start(f32[128]{0:T(128)} %param.10) | copy-start | bytes 1540
  8.8 9.5 %collective-permute-start.2 = (bf16[704,128]{1,0:T(8,128)(2,1)S(1)}, bf16[704,128]{1,0:T(8,128)(2,1)S(1)}, u32[]{:S(2)}, u32[]{:S(2)}) collective-permute-start(bf16[704,128]{1,0:T(8,128)(2,1)S(1)} %get-tuple-element.79), channel_id=1, source_target_pairs={{0,4},{4,0},{8,12},{12,8},{16,20},{20,16},{24,28},{28,24},{1,5},{5... | collective-permute-start | bytes 540680 | tf_op jit(solution)/shard_map/ppermute | solution.py:401
  10.4 5.7 %collective-permute-start.3 = (bf16[704,128]{1,0:T(8,128)(2,1)S(1)}, bf16[704,128]{1,0:T(8,128)(2,1)S(1)}, u32[]{:S(2)}, u32[]{:S(2)}) collective-permute-start(bf16[704,128]{1,0:T(8,128)(2,1)S(1)} %get-tuple-element.80), channel_id=1, source_target_pairs={{4,8},{8,4},{12,16},{16,12},{20,24},{24,20},{5,9},{9,5},{13,17},{1... | collective-permute-start | bytes 540680 | tf_op jit(solution)/shard_map/ppermute | solution.py:400
  18.3 4.8 %copy-start = (bf16[3,3,3,128,256]{4,3,2,1,0:T(8,128)(2,1)S(1)}, bf16[3,3,3,128,256]{4,3,2,1,0:T(8,128)(2,1)}, u32[]{:S(2)}) copy-start(bf16[3,3,3,128,256]{4,3,2,1,0:T(8,128)(2,1)} %w.5) | copy-start | bytes 5308420
  19.3 5.4 %collective-permute-start.4 = (bf16[2,8,16,128]{3,2,1,0:T(8,128)(2,1)S(1)}, bf16[2,8,16,128]{3,2,1,0:T(8,128)(2,1)S(1)}, u32[]{:S(2)}, u32[]{:S(2)}) collective-permute-start(bf16[2,8,16,128]{3,2,1,0:T(8,128)(2,1)S(1)} %get-tuple-element.89), channel_id=1, source_target_pairs={{0,4},{4,0},{8,12},{12,8},{16,20},{20,16},{24,28},{28,24},{1,5},{5... | collective-permute-start | bytes 196616 | tf_op jit(solution)/shard_map/ppermute | solution.py:401
  22.4 2.2 %collective-permute-start.5 = (bf16[2,8,16,128]{3,2,1,0:T(8,128)(2,1)S(1)}, bf16[2,8,16,128]{3,2,1,0:T(8,128)(2,1)S(1)}, u32[]{:S(2)}, u32[]{:S(2)}) collective-permute-start(bf16[2,8,16,128]{3,2,1,0:T(8,128)(2,1)S(1)} %get-tuple-element.91), channel_id=1, source_target_pairs={{4,8},{8,4},{12,16},{16,12},{20,24},{24,20},{5,9},{9,5},{13,17},{1... | collective-permute-start | bytes 196616 | tf_op jit(solution)/shard_map/ppermute | solution.py:400
  24.7 3.9 %copy-start.5 = (bf16[256,128]{1,0:T(8,128)(2,1)S(1)}, bf16[256,128]{1,0:T(8,128)(2,1)}, u32[]{:S(2)}) copy-start(bf16[256,128]{1,0:T(8,128)(2,1)} %wm.5) | copy-start | bytes 196612
  24.7 3.9 %copy-start.6 = (f32[256]{0:T(256)S(1)}, f32[256]{0:T(256)}, u32[]{:S(2)}) copy-start(f32[256]{0:T(256)} %param.12) | copy-start | bytes 3076
  24.7 5.4 %collective-permute-start.6 = (bf16[22,16,128]{2,1,0:T(8,128)(2,1)S(1)}, bf16[22,16,128]{2,1,0:T(8,128)(2,1)S(1)}, u32[]{:S(2)}, u32[]{:S(2)}) collective-permute-start(bf16[22,16,128]{2,1,0:T(8,128)(2,1)S(1)} %get-tuple-element.92), channel_id=1, source_target_pairs={{1,2},{2,1},{5,6},{6,5},{9,10},{10,9},{13,14},{14,13},{17,18},{18,... | collective-permute-start | bytes 270344 | tf_op jit(solution)/shard_map/ppermute | solution.py:400
  25.4 4.7 %collective-permute-start.7 = (bf16[22,16,128]{2,1,0:T(8,128)(2,1)S(1)}, bf16[22,16,128]{2,1,0:T(8,128)(2,1)S(1)}, u32[]{:S(2)}, u32[]{:S(2)}) collective-permute-start(bf16[22,16,128]{2,1,0:T(8,128)(2,1)S(1)} %get-tuple-element.93), channel_id=1, source_target_pairs={{0,1},{1,0},{2,3},{3,2},{4,5},{5,4},{6,7},{7,6},{8,9},{9,8},{10,11... | collective-permute-start | bytes 270344 | tf_op jit(solution)/shard_map/ppermute | solution.py:401
  33.4 2.8 %collective-permute-start.8 = (bf16[2,1792,128]{2,1,0:T(8,128)(2,1)S(1)}, bf16[2,1792,128]{2,1,0:T(8,128)(2,1)S(1)}, u32[]{:S(2)}, u32[]{:S(2)}) collective-permute-start(bf16[2,1792,128]{2,1,0:T(8,128)(2,1)S(1)} %get-tuple-element.100), channel_id=1, source_target_pairs={{0,1},{1,0},{2,3},{3,2},{4,5},{5,4},{6,7},{7,6},{8,9},{9,8},{10,11... | collective-permute-start | bytes 2752520 | tf_op jit(solution)/shard_map/ppermute | solution.py:431
  36.2 6.9 %copy-start.3 = (bf16[8,16,32,128]{3,2,1,0:T(8,128)(2,1)S(1)}, bf16[8,16,32,128]{3,2,1,0:T(8,128)(2,1)}, u32[]{:S(2)}) copy-start(bf16[8,16,32,128]{3,2,1,0:T(8,128)(2,1)} %cot.3) | copy-start | bytes 3145732
  36.4 14.7 %collective-permute-start.9 = (bf16[1,896,128]{2,1,0:T(8,128)(2,1)S(1)}, bf16[1,896,128]{2,1,0:T(8,128)(2,1)S(1)}, u32[]{:S(2)}, u32[]{:S(2)}) collective-permute-start(bf16[1,896,128]{2,1,0:T(8,128)(2,1)S(1)} %get-tuple-element.110), channel_id=1, source_target_pairs={{0,2},{1,3},{2,0},{3,1},{4,6},{5,7},{6,4},{7,5},{8,10},{9,11},{10,... | collective-permute-start | bytes 688136 | tf_op jit(solution)/shard_map/ppermute | solution.py:431
  38.4 12.7 %collective-permute-start.10 = (bf16[1,896,128]{2,1,0:T(8,128)(2,1)S(1)}, bf16[1,896,128]{2,1,0:T(8,128)(2,1)S(1)}, u32[]{:S(2)}, u32[]{:S(2)}) collective-permute-start(bf16[1,896,128]{2,1,0:T(8,128)(2,1)S(1)} %get-tuple-element.111), channel_id=1, source_target_pairs={{0,6},{1,7},{2,4},{3,5},{4,2},{5,3},{6,0},{7,1},{8,14},{9,15},{10,... | collective-permute-start | bytes 688136 | tf_op jit(solution)/shard_map/ppermute | solution.py:431
  42.6 11.1 %collective-permute-start.11 = (bf16[1,896,128]{2,1,0:T(8,128)(2,1)S(1)}, bf16[1,896,128]{2,1,0:T(8,128)(2,1)S(1)}, u32[]{:S(2)}, u32[]{:S(2)}) collective-permute-start(bf16[1,896,128]{2,1,0:T(8,128)(2,1)S(1)} %get-tuple-element.112), channel_id=1, source_target_pairs={{0,4},{1,5},{2,6},{3,7},{4,0},{5,1},{6,2},{7,3},{8,12},{9,13},{10,... | collective-permute-start | bytes 688136 | tf_op jit(solution)/shard_map/ppermute | solution.py:431
  50.5 3.2 %collective-permute-start.13 = (bf16[896,128]{1,0:T(8,128)(2,1)S(1)}, bf16[896,128]{1,0:T(8,128)(2,1)S(1)}, u32[]{:S(2)}, u32[]{:S(2)}) collective-permute-start(bf16[896,128]{1,0:T(8,128)(2,1)S(1)} %get-tuple-element.148), channel_id=1, source_target_pairs={{0,1},{1,0},{2,3},{3,2},{4,5},{5,4},{6,7},{7,6},{8,9},{9,8},{10,11... | collective-permute-start | bytes 688136 | tf_op jit(solution)/shard_map/ppermute | solution.py:431
  50.6 3.2 %collective-permute-start.12 = (bf16[896,128]{1,0:T(8,128)(2,1)S(1)}, bf16[896,128]{1,0:T(8,128)(2,1)S(1)}, u32[]{:S(2)}, u32[]{:S(2)}) collective-permute-start(bf16[896,128]{1,0:T(8,128)(2,1)S(1)} %get-tuple-element.149), channel_id=1, source_target_pairs={{0,1},{1,0},{2,3},{3,2},{4,5},{5,4},{6,7},{7,6},{8,9},{9,8},{10,11... | collective-permute-start | bytes 688136 | tf_op jit(solution)/shard_map/ppermute | solution.py:431
  53.8 6.8 %collective-permute-start.14 = (bf16[448,128]{1,0:T(8,128)(2,1)S(1)}, bf16[448,128]{1,0:T(8,128)(2,1)S(1)}, u32[]{:S(2)}, u32[]{:S(2)}) collective-permute-start(bf16[448,128]{1,0:T(8,128)(2,1)S(1)} %get-tuple-element.122), channel_id=1, source_target_pairs={{0,8},{1,9},{2,10},{3,11},{4,12},{5,13},{6,14},{7,15},{8,0},{9,1},... | collective-permute-start | bytes 344072 | tf_op jit(solution)/shard_map/ppermute | solution.py:431
  57.0 6.1 %collective-permute-start.16 = (bf16[1,448,128]{2,1,0:T(8,128)(2,1)S(1)}, bf16[1,448,128]{2,1,0:T(8,128)(2,1)S(1)}, u32[]{:S(2)}, u32[]{:S(2)}) collective-permute-start(bf16[1,448,128]{2,1,0:T(8,128)(2,1)S(1)} %get-tuple-element.127), channel_id=1, source_target_pairs={{0,2},{1,3},{2,0},{3,1},{4,6},{5,7},{6,4},{7,5},{8,10},{9,11},{10,... | collective-permute-start | bytes 344072 | tf_op jit(solution)/shard_map/ppermute | solution.py:431
  58.8 5.7 %collective-permute-start.17 = (bf16[1,448,128]{2,1,0:T(8,128)(2,1)S(1)}, bf16[1,448,128]{2,1,0:T(8,128)(2,1)S(1)}, u32[]{:S(2)}, u32[]{:S(2)}) collective-permute-start(bf16[1,448,128]{2,1,0:T(8,128)(2,1)S(1)} %get-tuple-element.128), channel_id=1, source_target_pairs={{0,6},{1,7},{2,4},{3,5},{4,2},{5,3},{6,0},{7,1},{8,14},{9,15},{10,... | collective-permute-start | bytes 344072 | tf_op jit(solution)/shard_map/ppermute | solution.py:431
  59.1 5.8 %collective-permute-start.18 = (bf16[1,448,128]{2,1,0:T(8,128)(2,1)S(1)}, bf16[1,448,128]{2,1,0:T(8,128)(2,1)S(1)}, u32[]{:S(2)}, u32[]{:S(2)}) collective-permute-start(bf16[1,448,128]{2,1,0:T(8,128)(2,1)S(1)} %get-tuple-element.129), channel_id=1, source_target_pairs={{0,4},{1,5},{2,6},{3,7},{4,0},{5,1},{6,2},{7,3},{8,12},{9,13},{10,... | collective-permute-start | bytes 344072 | tf_op jit(solution)/shard_map/ppermute | solution.py:431
  60.6 8.5 %collective-permute-start.15 = (bf16[448,128]{1,0:T(8,128)(2,1)S(1)}, bf16[448,128]{1,0:T(8,128)(2,1)S(1)}, u32[]{:S(2)}, u32[]{:S(2)}) collective-permute-start(bf16[448,128]{1,0:T(8,128)(2,1)S(1)} %coarse_sum.1), channel_id=1, source_target_pairs={{0,16},{1,17},{2,18},{3,19},{4,20},{5,21},{6,22},{7,23},{8,24},{9,... | collective-permute-start | bytes 344072 | tf_op jit(solution)/shard_map/ppermute | solution.py:431
  64.9 4.2 %collective-permute-start.19 = (bf16[224,128]{1,0:T(8,128)(2,1)S(1)}, bf16[224,128]{1,0:T(8,128)(2,1)S(1)}, u32[]{:S(2)}, u32[]{:S(2)}) collective-permute-start(bf16[224,128]{1,0:T(8,128)(2,1)S(1)} %get-tuple-element.131), channel_id=1, source_target_pairs={{0,8},{1,9},{2,10},{3,11},{4,12},{5,13},{6,14},{7,15},{8,0},{9,1},... | collective-permute-start | bytes 172040 | tf_op jit(solution)/shard_map/ppermute | solution.py:431
  69.2 5.7 %collective-permute-start.20 = (bf16[224,128]{1,0:T(8,128)(2,1)S(1)}, bf16[224,128]{1,0:T(8,128)(2,1)S(1)}, u32[]{:S(2)}, u32[]{:S(2)}) collective-permute-start(bf16[224,128]{1,0:T(8,128)(2,1)S(1)} %fine_sum.1), channel_id=1, source_target_pairs={{0,16},{1,17},{2,18},{3,19},{4,20},{5,21},{6,22},{7,23},{8,24},{9,... | collective-permute-start | bytes 172040 | tf_op jit(solution)/shard_map/ppermute | solution.py:431
  70.6 6.7 %collective-permute-start.26 = (bf16[448,128]{1,0:T(8,128)(2,1)S(1)}, bf16[448,128]{1,0:T(8,128)(2,1)S(1)}, u32[]{:S(2)}, u32[]{:S(2)}) collective-permute-start(bf16[448,128]{1,0:T(8,128)(2,1)S(1)} %add_convert_fusion.refs_0_), channel_id=1, source_target_pairs={{0,12},{1,13},{2,14},{3,15},{4,8},{5,9},{6,10},{7,11},{8,4},{9,5},... | collective-permute-start | bytes 344072 | tf_op jit(solution)/shard_map/ppermute | solution.py:431
  72.4 6.0 %collective-permute-start.25 = (bf16[448,128]{1,0:T(8,128)(2,1)S(1)}, bf16[448,128]{1,0:T(8,128)(2,1)S(1)}, u32[]{:S(2)}, u32[]{:S(2)}) collective-permute-start(bf16[448,128]{1,0:T(8,128)(2,1)S(1)} %add_convert_fusion.refs_0_), channel_id=1, source_target_pairs={{0,8},{1,9},{2,10},{3,11},{4,12},{5,13},{6,14},{7,15},{8,0},{9,1},... | collective-permute-start | bytes 344072 | tf_op jit(solution)/shard_map/ppermute | solution.py:431
  72.6 5.8 %collective-permute-start.24 = (bf16[448,128]{1,0:T(8,128)(2,1)S(1)}, bf16[448,128]{1,0:T(8,128)(2,1)S(1)}, u32[]{:S(2)}, u32[]{:S(2)}) collective-permute-start(bf16[448,128]{1,0:T(8,128)(2,1)S(1)} %add_convert_fusion.refs_0_), channel_id=1, source_target_pairs={{0,4},{1,5},{2,6},{3,7},{4,0},{5,1},{6,2},{7,3},{8,12},{9,13},{10,... | collective-permute-start | bytes 344072 | tf_op jit(solution)/shard_map/ppermute | solution.py:431
  74.8 5.1 %collective-permute-start.23 = (bf16[224,128]{1,0:T(8,128)(2,1)S(1)}, bf16[224,128]{1,0:T(8,128)(2,1)S(1)}, u32[]{:S(2)}, u32[]{:S(2)}) collective-permute-start(bf16[224,128]{1,0:T(8,128)(2,1)S(1)} %add_convert_fusion.1.refs_0_), channel_id=1, source_target_pairs={{0,12},{1,13},{2,14},{3,15},{4,8},{5,9},{6,10},{7,11},{8,4},{9,5},... | collective-permute-start | bytes 172040 | tf_op jit(solution)/shard_map/ppermute | solution.py:431
  75.9 4.2 %collective-permute-start.22 = (bf16[224,128]{1,0:T(8,128)(2,1)S(1)}, bf16[224,128]{1,0:T(8,128)(2,1)S(1)}, u32[]{:S(2)}, u32[]{:S(2)}) collective-permute-start(bf16[224,128]{1,0:T(8,128)(2,1)S(1)} %add_convert_fusion.1.refs_0_), channel_id=1, source_target_pairs={{0,8},{1,9},{2,10},{3,11},{4,12},{5,13},{6,14},{7,15},{8,0},{9,1},... | collective-permute-start | bytes 172040 | tf_op jit(solution)/shard_map/ppermute | solution.py:431
  77.3 4.2 %collective-permute-start.21 = (bf16[224,128]{1,0:T(8,128)(2,1)S(1)}, bf16[224,128]{1,0:T(8,128)(2,1)S(1)}, u32[]{:S(2)}, u32[]{:S(2)}) collective-permute-start(bf16[224,128]{1,0:T(8,128)(2,1)S(1)} %add_convert_fusion.1.refs_0_), channel_id=1, source_target_pairs={{0,4},{1,5},{2,6},{3,7},{4,0},{5,1},{6,2},{7,3},{8,12},{9,13},{10,... | collective-permute-start | bytes 172040 | tf_op jit(solution)/shard_map/ppermute | solution.py:431
